TPU v7x, 256 devices: a whole 4x4x8 slice. The times are simulated.
256 devices in a mesh: gx: 64 (over z, y, core), gy: 2 (over x_hi), gz: 2 (over x_lo).
Axes of the slice: x: 4 (x_hi: 2, x_lo: 2; x = x_hi * 2 + x_lo), y: 4, z: 8, core: 2. Of those that a mesh axis runs over, the one named last changes fastest.
Arguments:
- fields: float32 [2, 2, 1024, 2048], P(None, 'gz', 'gx', 'gy'), may hold values from -5.5 to 8
- kappa: float32 [2, 2, 1024, 2048], P(None, 'gz', 'gx', 'gy'), may hold values from 100 to 800000
- vertical: float32 [2, 2, 1024, 2048], P(None, 'gz', 'gx', 'gy'), may hold values from 0.03 to 0.4
Outputs:
- advanced: float32 [2, 2, 1024, 2048], P(None, 'gz', 'gx', 'gy')
All inputs are finite; a program needn't handle non-finite values.
Results may differ from a plain program's by a relative error of at most 0.005.
Values sent between devices are 32-bit elements; how exact they have to be, the bound alone decides.
No kernel may reach another device: no remote copies, remote signals or barrier semaphores. Data moves between devices by JAX's collectives and lax.ppermute only.
A program may use at most 128 MiB of HBM per device.

v0:
```python
import functools

import jax
import jax.numpy as jnp
from jax import lax
from jax.experimental import pallas as pl
from jax.experimental.pallas import tpu as pltpu
from jax.sharding import PartitionSpec as P

F32 = jnp.float32
ROWS = 16
COLS = 1024
ALL = 2 * ROWS
VMEM = pl.BlockSpec(memory_space=pltpu.VMEM)
SMEM = pl.BlockSpec(memory_space=pltpu.SMEM)
X_STEPS = (1, 2, 4, 8)
Y_STEPS = (1, 2, 4, 8, 16, 32, 64, 128, 256, 512)
PARAMS = pltpu.CompilerParams(vmem_limit_bytes=40 * 1024 * 1024)


def shape(*dims):
    return jax.ShapeDtypeStruct(dims, F32)


def turn(x, k, axis):
    n = x.shape[axis]
    k = k % n
    unit = 128 if axis == 1 else 8
    if k == 0:
        return x
    if k % unit == 0:
        low = lax.slice_in_dim(x, n - k, n, axis=axis)
        high = lax.slice_in_dim(x, 0, n - k, axis=axis)
        return jnp.concatenate([low, high], axis=axis)
    return pltpu.roll(x, k, axis)


def reduce_matrix(low, excess, rights, steps, axis, keep):
    for index, k in enumerate(steps):
        high = turn(low, -k, axis)
        inverse = 1.0 / (low + high + excess)
        a = low * turn(inverse, k, axis)
        b = high * turn(inverse, -k, axis)
        keep(index, a, b)
        excess = excess + a * turn(excess, k, axis) + b * turn(excess, -k, axis)
        rights = [r + a * turn(r, k, axis) + b * turn(r, -k, axis) for r in rights]
        low = a * turn(low, k, axis)
    inverse = 1.0 / excess
    return inverse, [r * inverse for r in rights]


def reduce_right(right, steps, axis, load):
    for index, k in enumerate(steps):
        a, b = load(index)
        right = right + a * turn(right, k, axis) + b * turn(right, -k, axis)
    return right


def dense(row):
    return jnp.concatenate([row[:, 128 * i : 128 * (i + 1)] for i in range(8)], axis=0)


def natural(tile, rows):
    return jnp.concatenate(
        [jnp.broadcast_to(tile[i : i + 1, :], (rows, 128)) for i in range(8)], axis=1
    )


def factor_kernel(place, kappa, ax, bx, qx, h1, h2, ay, by, qy, hy, parts, edge):
    gy = place[0]
    half = 512
    rows = lax.broadcasted_iota(jnp.int32, (ROWS, half), 0)
    for f in range(2):
        mine = pl.ds(f * ROWS, ROWS)
        for c in range(COLS // half):
            cols = pl.ds(c * half, half)
            k = kappa[mine, cols]
            face = (k + turn(k, 1, 0)) * 0.5
            low = jnp.where((rows >= 2) & (rows <= 14), face, 0.0)
            first = jnp.where(rows == 1, face, 0.0)
            last = jnp.where(rows == 14, turn(face, -1, 0), 0.0)

            def keep(index, a, b, mine=mine, cols=cols):
                ax[index, mine, cols] = a
                bx[index, mine, cols] = b

            inverse, (one, two) = reduce_matrix(
                low, 1.0 + first + last, [first, last], X_STEPS, 0, keep
            )
            qx[mine, cols] = jnp.where((rows >= 1) & (rows <= 14), inverse, 0.0)
            one = jnp.where(rows == 0, 1.0, one)
            two = jnp.where(rows == ROWS - 1, 1.0, two)
            h1[mine, cols] = one
            h2[mine, cols] = two
            for n, row in enumerate(
                (
                    jnp.sum(first * two, axis=0, keepdims=True),
                    jnp.sum(one, axis=0, keepdims=True),
                    jnp.sum(two, axis=0, keepdims=True),
                )
            ):
                for i in range(half // 128):
                    parts[n, f, pl.ds(c * (half // 128) + i, 1), :] = row[:, 128 * i : 128 * (i + 1)]
    lanes = lax.broadcasted_iota(jnp.int32, (8, COLS), 1)
    wide = lax.broadcasted_iota(jnp.int32, (8, 128), 1)
    low_side = gy == 0
    terminal = lanes == jnp.where(low_side, COLS - 1, 0)
    cut = lanes == jnp.where(low_side, COLS - 1, 1)
    outer = lanes == jnp.where(low_side, 0, COLS - 1)
    beside = lanes == jnp.where(low_side, COLS - 2, 1)
    for g in range(ALL // 8):
        mine = pl.ds(g * 8, 8)
        k = kappa[mine, :]
        face = (k + turn(k, 1, 1)) * 0.5
        low = jnp.where((lanes == 0) | cut, 0.0, face)
        link = jnp.where(beside, jnp.where(low_side, turn(face, -1, 1), face), 0.0)
        ground = jnp.where(outer, 1.0 + 0.5 * k, 1.0)

        def keep(index, a, b, mine=mine):
            ay[index, mine, :] = a
            by[index, mine, :] = b

        inverse, (profile,) = reduce_matrix(low, ground + link, [link], Y_STEPS, 1, keep)
        qy[mine, :] = jnp.where(terminal, 0.0, inverse)
        profile = jnp.where(terminal, 1.0, profile)
        hy[mine, :] = profile
        total = jnp.sum(profile * ground, axis=1, keepdims=True)
        rim = jnp.sum(jnp.where(terminal, k, 0.0), axis=1, keepdims=True)
        edge[mine, :] = jnp.where(wide == 0, total, jnp.where(wide == 1, rim, 0.0))


def source_kernel(place, fields, fields_far, vertical, vertical_far, kappa, halo, h1, h2, parts, source, sums, message):
    gx = place[1]
    here = fields[...]
    v = vertical[...]
    s = here + (v + vertical_far[...]) * 0.5 * (fields_far[...] - here) - v * 0.5 * here
    source[...] = s
    for f in range(2):
        mine = slice(f * ROWS, (f + 1) * ROWS)
        first = dense(jnp.sum(h1[mine, :] * s[mine, :], axis=0, keepdims=True))
        last = dense(jnp.sum(h2[mine, :] * s[mine, :], axis=0, keepdims=True))
        west = (dense(kappa[f * ROWS : f * ROWS + 1, :]) + dense(halo[f : f + 1, :])) * 0.5
        east = dense(kappa[f * ROWS + ROWS - 1 : f * ROWS + ROWS, :]) * 0.5
        g, s_first, s_last = parts[0, f], parts[1, f], parts[2, f]
        inverse = 1.0 / (west + g + s_first)
        a = west * inverse
        b = g * inverse
        sums[0, f] = a
        sums[1, f] = b
        sums[2, f] = first * inverse
        element = (
            a * g,
            a * s_first,
            jnp.where(gx == 63, s_last + east, s_last) + b * s_first,
            a * first,
            last + b * first,
        )
        for n, value in enumerate(element):
            for j in range(4):
                message[2 * j + f, n] = value


def local_x_kernel(source, ax, bx, qx, out):
    half = 512
    for f in range(2):
        mine = pl.ds(f * ROWS, ROWS)
        for c in range(COLS // half):
            cols = pl.ds(c * half, half)
            r = source[mine, cols]
            r = reduce_right(r, X_STEPS, 0, lambda i: (ax[i, mine, cols], bx[i, mine, cols]))
            out[mine, cols] = r * qx[mine, cols]


def slab_kernel(got, message, chain):
    g, sl, sr, rl, rr = (got[0, n] for n in range(5))
    for k in range(7):
        g2, sl2, sr2, rl2, rr2 = (got[k + 1, n] for n in range(5))
        s = sr + sl2
        r = rr + rl2
        inverse = 1.0 / (g + g2 + s)
        a = g * inverse
        b = g2 * inverse
        chain[k, 0] = a
        chain[k, 1] = b
        chain[k, 2] = r * inverse
        sl = sl + a * s
        rl = rl + a * r
        sr = sr2 + b * s
        rr = rr2 + b * r
        g = a * g2
    for n, value in enumerate((g, sl, sr, rl, rr)):
        for j in range(8):
            message[j, n] = value


def ends_kernel(place, got, chain, mine, other):
    gx = place[1]
    slab = gx // 8
    seat = gx % 8
    zero = jnp.zeros((8, 128), F32)
    conduct = got[0, 0] + got[0, 2]
    right = got[0, 4]
    ratios, offsets = [], []
    for k in range(7):
        conduct = conduct + got[k + 1, 1]
        right = right + got[k + 1, 3]
        inverse = 1.0 / (conduct + got[k + 1, 0])
        f = got[k + 1, 0] * inverse
        ratios.append(f)
        offsets.append(right * inverse)
        conduct = got[k + 1, 2] + f * conduct
        right = got[k + 1, 4] + f * right
    value = right / conduct
    values = [value]
    for k in range(6, -1, -1):
        value = ratios[k] * value + offsets[k]
        values.append(value)
    values = [zero] + values[::-1]
    left, last = zero, zero
    for z in range(8):
        left = jnp.where(slab == z, values[z], left)
        last = jnp.where(slab == z, values[z + 1], last)
    nodes = [last]
    for k in range(6, -1, -1):
        nodes.append(chain[k, 0] * left + chain[k, 1] * nodes[-1] + chain[k, 2])
    nodes = [left] + nodes[::-1]
    even = seat % 2 == 0
    trio = [zero, zero, zero]
    for j in range(4):
        for n in range(3):
            trio[n] = jnp.where(seat // 2 == j, nodes[2 * j + n], trio[n])
    mine[0] = jnp.where(even, trio[0], trio[1])
    mine[1] = jnp.where(even, trio[1], trio[2])
    other[0] = jnp.where(even, trio[1], trio[0])
    other[1] = jnp.where(even, trio[2], trio[1])


def section_kernel(place, mine, other, sums, local, h1, h2, hy, edge, section, message):
    core = place[1] % 2
    wide = lax.broadcasted_iota(jnp.int32, (8, 128), 1)
    for f in range(2):
        left = jnp.where(core == f, mine[0], other[0])
        last = jnp.where(core == f, mine[1], other[1])
        first = sums[0, f] * left + sums[1, f] * last + sums[2, f]
        rows = slice(f * ROWS, (f + 1) * ROWS)
        s = local[rows, :] + h1[rows, :] * natural(first, ROWS) + h2[rows, :] * natural(last, ROWS)
        section[rows, :] = s
        total = jnp.sum(hy[rows, :] * s, axis=1, keepdims=True)
        for g in range(2):
            part = slice(f * ROWS + g * 8, f * ROWS + g * 8 + 8)
            message[part, :] = jnp.where(wide == 2, total[g * 8 : g * 8 + 8], edge[part, :])


def local_y_kernel(section, ay, by, qy, out):
    for g in range(ALL // 8):
        mine = pl.ds(g * 8, 8)
        r = section[mine, :]
        r = reduce_right(r, Y_STEPS, 1, lambda i: (ay[i, mine, :], by[i, mine, :]))
        out[mine, :] = r * qy[mine, :]


def output_kernel(message, far, local, hy, out):
    e, k, r = (message[:, n : n + 1] for n in range(3))
    e2, k2, r2 = (far[:, n : n + 1] for n in range(3))
    c = (k + k2) * 0.5
    value = ((e2 + c) * r + c * r2) / (e * e2 + c * (e + e2))
    out[...] = local[...] + hy[...] * value


def call(kernel, outs, specs, flops=0, size=0):
    return pl.pallas_call(
        kernel,
        out_shape=outs,
        in_specs=specs,
        out_specs=jax.tree.map(lambda _: VMEM, outs),
        compiler_params=PARAMS,
        cost_estimate=pl.CostEstimate(flops=flops, bytes_accessed=size, transcendentals=0),
    )


PLANE_GROUPS = [[8 * a + b for b in range(8)] for a in range(8)]
SLAB_GROUPS = [[8 * b + a for b in range(8)] for a in range(8)]


def local(fields, kappa, vertical):
    gx = lax.axis_index("gx")
    gy = lax.axis_index("gy")
    place = jnp.stack([gy, gx]).astype(jnp.int32)
    grid = (ALL, COLS)
    swap = [(0, 1), (1, 0)]
    fields_far = lax.ppermute(fields, "gz", swap)
    vertical_far = lax.ppermute(vertical, "gz", swap)
    halo = lax.ppermute(kappa[:, 0, ROWS - 1], "gx", [(i, i + 1) for i in range(63)])
    k = kappa.reshape(grid)
    full = shape(*grid)
    ax, bx, qx, h1, h2, ay, by, qy, hy, parts, edge = call(
        factor_kernel,
        (
            shape(4, *grid), shape(4, *grid), full, full, full,
            shape(10, *grid), shape(10, *grid), full, full,
            shape(3, 2, 8, 128), shape(ALL, 128),
        ),
        [SMEM, VMEM],
        flops=20_000_000,
        size=4_000_000,
    )(place, k)
    source, sums, message = call(
        source_kernel,
        (full, shape(3, 2, 8, 128), shape(8, 5, 8, 128)),
        [SMEM] + [VMEM] * 9,
    )(
        place, fields.reshape(grid), fields_far.reshape(grid), vertical.reshape(grid),
        vertical_far.reshape(grid), k, halo, h1, h2, parts,
    )
    got = lax.all_to_all(message, "gx", 0, 0, axis_index_groups=PLANE_GROUPS, tiled=True)
    local_x = call(local_x_kernel, full, [VMEM] * 4, flops=1_000_000, size=1_000_000)(source, ax, bx, qx)
    message, chain = call(
        slab_kernel, (shape(8, 5, 8, 128), shape(7, 3, 8, 128)), [VMEM]
    )(got)
    got = lax.all_to_all(message, "gx", 0, 0, axis_index_groups=SLAB_GROUPS, tiled=True)
    mine, other = call(
        ends_kernel, (shape(2, 8, 128), shape(2, 8, 128)), [SMEM, VMEM, VMEM]
    )(place, got, chain)
    other = lax.ppermute(other, "gx", [(i, i ^ 1) for i in range(64)])
    section, message = call(
        section_kernel, (full, shape(ALL, 128)), [SMEM] + [VMEM] * 8
    )(place, mine, other, sums, local_x, h1, h2, hy, edge)
    far = lax.ppermute(message, "gy", swap)
    local_y = call(local_y_kernel, full, [VMEM] * 4, flops=4_000_000, size=3_000_000)(section, ay, by, qy)
    out = call(output_kernel, full, [VMEM] * 4)(message, far, local_y, hy)
    return out.reshape(fields.shape)


def solution(mesh):
    spec = P(None, "gz", "gx", "gy")
    return jax.shard_map(
        local, mesh=mesh, in_specs=(spec, spec, spec), out_specs=spec, check_vma=False
    )
```

profile of v0, /device:TPU:1, one launch (start us, length us, event | category | flops | bytes accessed | tf_op | source)
XLA Modules:
  0.0 51.8 jit_solution(4258267636317174859)
XLA Ops:
  0.0 2.0 %collective-permute-start = (f32[2,1,16,1024]{3,2,1,0:T(8,128)}, f32[2,1,16,1024]{3,2,1,0:T(8,128)S(1)}, u32[]{:S(2)}, u32[]{:S(2)}) collective-permute-start(f32[2,1,16,1024]{3,2,1,0:T(8,128)} %param.3), channel_id=1, source_target_pairs={{0,1},{1,0},{2,3},{3,2},{4,5},{5,4},{6,7},{7,6},{8,9},{9,8},{10,11... | collective-permute-start | bytes 393224 | tf_op jit(solution)/shard_map/ppermute | solution.py:291
  2.0 0.0 collective-permute-start.1
  2.1 0.8 %slice.3 = f32[2,1,1,1024]{3,2,1,0:T(1,128)S(1)} slice(f32[2,1,16,1024]{3,2,1,0:T(8,128)} %param.4), slice={[0:2], [0:1], [15:16], [0:1024]} | slice | bytes 16384 | tf_op jit(solution)/shard_map/slice | solution.py:293
  2.9 4.5 %collective-permute-start.2 = (f32[2,1024]{1,0:T(2,128)S(1)}, f32[2,1024]{1,0:T(2,128)S(1)}, u32[]{:S(2)}, u32[]{:S(2)}) collective-permute-start(f32[2,1024]{1,0:T(2,128)S(1)} %bitcast.19), channel_id=1, source_target_pairs={{0,4},{4,8},{8,12},{12,16},{16,20},{20,24},{24,28},{28,32},{32,36}... | collective-permute-start | bytes 24584 | tf_op jit(solution)/shard_map/ppermute | solution.py:293
  7.5 0.1 pad_add_fusion.place
  7.6 0.0 copy-start
  7.6 0.9 %copy-done = f32[2,1,16,1024]{3,2,1,0:T(8,128)S(1)} copy-done((f32[2,1,16,1024]{3,2,1,0:T(8,128)S(1)}, f32[2,1,16,1024]{3,2,1,0:T(8,128)}, u32[]{:S(2)}) %copy-start) | copy-done | bytes 131096
  8.5 5.2 %shard_map.37 = (f32[4,32,1024]{2,1,0:T(8,128)S(1)}, f32[4,32,1024]{2,1,0:T(8,128)S(1)}, f32[32,1024]{1,0:T(8,128)S(1)}, f32[32,1024]{1,0:T(8,128)S(1)}, f32[32,...) custom-call(s32[2]{0:T(128)S(1)} %pad_add_fusion.place, ...), custom_call_target="tpu_custom_call" | custom-call | flops 20000000 | bytes 4000000 | tf_op jit(solution)/shard_map/pallas_call | solution.py:296
  13.6 0.0 collective-permute-done.2.halo
  13.6 0.0 collective-permute-done
  13.6 0.0 collective-permute-done.1
  13.6 0.0 copy-start.1
  13.7 0.9 %copy-done.1 = f32[2,1,16,1024]{3,2,1,0:T(8,128)S(1)} copy-done((f32[2,1,16,1024]{3,2,1,0:T(8,128)S(1)}, f32[2,1,16,1024]{3,2,1,0:T(8,128)}, u32[]{:S(2)}) %copy-start.1) | copy-done | bytes 131096
  14.6 0.0 copy-start.2
  14.6 0.9 %copy-done.2 = f32[2,1,16,1024]{3,2,1,0:T(8,128)S(1)} copy-done((f32[2,1,16,1024]{3,2,1,0:T(8,128)S(1)}, f32[2,1,16,1024]{3,2,1,0:T(8,128)}, u32[]{:S(2)}) %copy-start.2) | copy-done | bytes 131096
  15.5 0.7 %shard_map.38 = (f32[32,1024]{1,0:T(8,128)S(1)}, f32[3,2,8,128]{3,2,1,0:T(8,128)S(1)}, f32[8,5,8,128]{3,2,1,0:T(8,128)S(1)}) custom-call(s32[2]{0:T(128)S(1)} %pad_add_fusion.place, f32[32,1024]{1,0:T(8,128)S(1)} %bitcast.15, f32[32,1024]{1,0:T(8,128)S(1)} %bitcast.17, f32[32,1024]{1,0:T(8,128)S(1)} %bitcast.16, f32[32,1024]{1,0:T(8,128)S(1)} %bitcast.18, ...), custom_call_target="tpu_custom_call" | custom-call | tf_op jit(solution)/shard_map/pallas_call | solution.py:307
  16.1 9.8 %all_to_all.10.got = f32[8,5,8,128]{3,2,1,0:T(8,128)S(1)} all-to-all(f32[8,5,8,128]{3,2,1,0:T(8,128)S(1)} %get-tuple-element.28), channel_id=1, replica_groups={{0,4,8,12,16,20,24,28},{32,36,40,44,48,52,56,60},{64,68,72,76,80,84,88,..., dimensions={0} | all-to-all | bytes 327680 | tf_op jit(solution)/shard_map/all_to_all | solution.py:315
  25.9 0.1 shard_map.39
  26.0 15.9 %all_to_all.11.got = f32[8,5,8,128]{3,2,1,0:T(8,128)S(1)} all-to-all(f32[8,5,8,128]{3,2,1,0:T(8,128)S(1)} %get-tuple-element.29), channel_id=1, replica_groups={{0,32,64,96,128,160,192,224},{4,36,68,100,132,164,196,228},{8,40,72,104..., dimensions={0} | all-to-all | bytes 327680 | tf_op jit(solution)/shard_map/all_to_all | solution.py:320
  41.9 0.7 %shard_map.40 = (f32[2,8,128]{2,1,0:T(8,128)S(1)}, f32[2,8,128]{2,1,0:T(8,128)S(1)}) custom-call(s32[2]{0:T(128)S(1)} %pad_add_fusion.place, f32[8,5,8,128]{3,2,1,0:T(8,128)S(1)} %all_to_all.11.got, f32[7,3,8,128]{3,2,1,0:T(8,128)S(1)} %get-tuple-element.30.chain), custom_call_target="tpu_custom_call" | custom-call | tf_op jit(solution)/shard_map/pallas_call | solution.py:321
  42.6 2.7 %collective-permute-start.3 = (f32[2,8,128]{2,1,0:T(8,128)S(1)}, f32[2,8,128]{2,1,0:T(8,128)S(1)}, u32[]{:S(2)}, u32[]{:S(2)}) collective-permute-start(f32[2,8,128]{2,1,0:T(8,128)S(1)} %get-tuple-element.32), channel_id=1, source_target_pairs={{0,4},{4,0},{8,12},{12,8},{16,20},{20,16},{24,28},{28,24},{32,36},... | collective-permute-start | bytes 24584 | tf_op jit(solution)/shard_map/ppermute | solution.py:324
  45.3 0.1 shard_map.41.local
  45.5 0.7 %collective-permute-done.3.other = f32[2,8,128]{2,1,0:T(8,128)S(1)} collective-permute-done((f32[2,8,128]{2,1,0:T(8,128)S(1)}, f32[2,8,128]{2,1,0:T(8,128)S(1)}, u32[]{:S(2)}, u32[]{:S(2)}) %collective-permute-start.3) | collective-permute-done | bytes 8224 | tf_op jit(solution)/shard_map/ppermute | solution.py:324
  46.2 0.7 %shard_map.42 = (f32[32,1024]{1,0:T(8,128)S(1)}, f32[32,128]{1,0:T(8,128)S(1)}) custom-call(s32[2]{0:T(128)S(1)} %pad_add_fusion.place, f32[2,8,128]{2,1,0:T(8,128)S(1)} %get-tuple-element.31.mine, f32[2,8,128]{2,1,0:T(8,128)S(1)} %collective-permute-done.3.other, f32[3,2,8,128]{3,2,1,0:T(8,128)S(1)} %get-tuple-element.33.sums, ...), custom_call_target="tpu_custom_call" | custom-call | tf_op jit(solution)/shard_map/pallas_call | solution.py:325
  46.8 2.8 %collective-permute-start.4 = (f32[32,128]{1,0:T(8,128)S(1)}, f32[32,128]{1,0:T(8,128)S(1)}, u32[]{:S(2)}, u32[]{:S(2)}) collective-permute-start(f32[32,128]{1,0:T(8,128)S(1)} %get-tuple-element.40.message), channel_id=1, source_target_pairs={{0,2},{2,0},{1,3},{3,1},{4,6},{6,4},{5,7},{7,5},{8,10},{10,8},{9,1... | collective-permute-start | bytes 49160 | tf_op jit(solution)/shard_map/ppermute | solution.py:328
  49.6 0.9 %shard_map.43.local = f32[32,1024]{1,0:T(8,128)S(1)} custom-call(f32[32,1024]{1,0:T(8,128)S(1)} %get-tuple-element.41.section, f32[10,32,1024]{2,1,0:T(8,128)S(1)} %get-tuple-element.42.ay, f32[10,32,1024]{2,1,0:T(8,128)S(1)} %get-tuple-element.43.by, f32[32,1024]{1,0:T(8,128)S(1)} %get-tuple-element.44.qy), custom_call_target="tpu_custom_call" | custom-call | flops 4000000 | bytes 3000000 | tf_op jit(solution)/shard_map/pallas_call | solution.py:329
  50.5 0.5 collective-permute-done.4.far
  50.9 0.9 %shard_map.44 = f32[32,1024]{1,0:T(8,128)} custom-call(f32[32,128]{1,0:T(8,128)S(1)} %get-tuple-element.40.message, f32[32,128]{1,0:T(8,128)S(1)} %collective-permute-done.4.far, f32[32,1024]{1,0:T(8,128)S(1)} %shard_map.43.local, f32[32,1024]{1,0:T(8,128)S(1)} %get-tuple-element.38.hy), custom_call_target="tpu_custom_call" | custom-call | tf_op jit(solution)/shard_map/pallas_call | solution.py:330
  (1 shorter events, 0.0 us)
Async XLA Ops:
  0.0 13.6 %collective-permute-start = (f32[2,1,16,1024]{3,2,1,0:T(8,128)}, f32[2,1,16,1024]{3,2,1,0:T(8,128)S(1)}, u32[]{:S(2)}, u32[]{:S(2)}) collective-permute-start(f32[2,1,16,1024]{3,2,1,0:T(8,128)} %param.3), channel_id=1, source_target_pairs={{0,1},{1,0},{2,3},{3,2},{4,5},{5,4},{6,7},{7,6},{8,9},{9,8},{10,11... | collective-permute-start | bytes 393224 | tf_op jit(solution)/shard_map/ppermute | solution.py:291
  2.0 11.6 %collective-permute-start.1 = (f32[2,1,16,1024]{3,2,1,0:T(8,128)}, f32[2,1,16,1024]{3,2,1,0:T(8,128)S(1)}, u32[]{:S(2)}, u32[]{:S(2)}) collective-permute-start(f32[2,1,16,1024]{3,2,1,0:T(8,128)} %param.5), channel_id=1, source_target_pairs={{0,1},{1,0},{2,3},{3,2},{4,5},{5,4},{6,7},{7,6},{8,9},{9,8},{10,11... | collective-permute-start | bytes 393224 | tf_op jit(solution)/shard_map/ppermute | solution.py:292
  2.9 10.7 %collective-permute-start.2 = (f32[2,1024]{1,0:T(2,128)S(1)}, f32[2,1024]{1,0:T(2,128)S(1)}, u32[]{:S(2)}, u32[]{:S(2)}) collective-permute-start(f32[2,1024]{1,0:T(2,128)S(1)} %bitcast.19), channel_id=1, source_target_pairs={{0,4},{4,8},{8,12},{12,16},{16,20},{20,24},{24,28},{28,32},{32,36}... | collective-permute-start | bytes 24584 | tf_op jit(solution)/shard_map/ppermute | solution.py:293
  7.6 0.9 %copy-start = (f32[2,1,16,1024]{3,2,1,0:T(8,128)S(1)}, f32[2,1,16,1024]{3,2,1,0:T(8,128)}, u32[]{:S(2)}) copy-start(f32[2,1,16,1024]{3,2,1,0:T(8,128)} %param.4) | copy-start | bytes 393220
  13.6 0.9 %copy-start.1 = (f32[2,1,16,1024]{3,2,1,0:T(8,128)S(1)}, f32[2,1,16,1024]{3,2,1,0:T(8,128)}, u32[]{:S(2)}) copy-start(f32[2,1,16,1024]{3,2,1,0:T(8,128)} %param.3) | copy-start | bytes 393220
  14.6 0.9 %copy-start.2 = (f32[2,1,16,1024]{3,2,1,0:T(8,128)S(1)}, f32[2,1,16,1024]{3,2,1,0:T(8,128)}, u32[]{:S(2)}) copy-start(f32[2,1,16,1024]{3,2,1,0:T(8,128)} %param.5) | copy-start | bytes 393220
  42.6 3.6 %collective-permute-start.3 = (f32[2,8,128]{2,1,0:T(8,128)S(1)}, f32[2,8,128]{2,1,0:T(8,128)S(1)}, u32[]{:S(2)}, u32[]{:S(2)}) collective-permute-start(f32[2,8,128]{2,1,0:T(8,128)S(1)} %get-tuple-element.32), channel_id=1, source_target_pairs={{0,4},{4,0},{8,12},{12,8},{16,20},{20,16},{24,28},{28,24},{32,36},... | collective-permute-start | bytes 24584 | tf_op jit(solution)/shard_map/ppermute | solution.py:324
  46.8 4.1 %collective-permute-start.4 = (f32[32,128]{1,0:T(8,128)S(1)}, f32[32,128]{1,0:T(8,128)S(1)}, u32[]{:S(2)}, u32[]{:S(2)}) collective-permute-start(f32[32,128]{1,0:T(8,128)S(1)} %get-tuple-element.40.message), channel_id=1, source_target_pairs={{0,2},{2,0},{1,3},{3,1},{4,6},{6,4},{5,7},{7,5},{8,10},{10,8},{9,1... | collective-permute-start | bytes 49160 | tf_op jit(solution)/shard_map/ppermute | solution.py:328
where the time goes:
time: 52.1 us; the launch traced here: 51.8 us
  blocking collectives  25.7 us (49%)
  starting transfers between devices  12.1 us (23%)
  Pallas kernels  9.08 us (17%)
  local copies, waits for them, and re-layouts  3.56 us (7%)
  waiting for transfers between devices  1.2 us (2%)
    all_to_all x1, blocking collectives, local(): lax.all_to_all(message, 'gx', 0, 0, axis_index_groups=SLAB_GROUPS, tiled=...  15.9 us
    all_to_all x1, blocking collectives, local(): lax.all_to_all(message, 'gx', 0, 0, axis_index_groups=PLANE_GROUPS, tiled...  9.78 us
    pallas_call x1, Pallas kernels, local(): call(factor_kernel, (shape(4, *grid), shape(4, *grid), full, full, full,...  5.15 us
    ppermute x1, starting transfers between devices, local(): lax.ppermute(kappa[:, 0, ROWS - 1], 'gx', [(i, i + 1) for i in range(63)])  4.55 us
    ppermute x1, starting transfers between devices, local(): far = lax.ppermute(message, 'gy', swap)  2.76 us
    ppermute x1, starting transfers between devices, local(): other = lax.ppermute(other, 'gx', [(i, i ^ 1) for i in range(64)])  2.74 us
    unnamed x7, local copies, waits for them, and re-layouts  2.71 us
    ppermute x1, starting transfers between devices, local(): fields_far = lax.ppermute(fields, 'gz', swap)  2.04 us
  transfers between devices with their start and end apart: 5, of which 2 were waited for; matrix products, arithmetic and copies ran while one was open for 2% of the time, Pallas kernels for 12%

commit v1 on v0

--- a/solution.py
+++ b/solution.py
@@ -12,7 +12,7 @@
 COLS = 1024
 ALL = 2 * ROWS
 VMEM = pl.BlockSpec(memory_space=pltpu.VMEM)
-SMEM = pl.BlockSpec(memory_space=pltpu.SMEM)
+HBM = pl.BlockSpec(memory_space=pltpu.HBM)
 X_STEPS = (1, 2, 4, 8)
 Y_STEPS = (1, 2, 4, 8, 16, 32, 64, 128, 256, 512)
 PARAMS = pltpu.CompilerParams(vmem_limit_bytes=40 * 1024 * 1024)
@@ -66,8 +66,16 @@
     )
 
 
-def factor_kernel(place, kappa, ax, bx, qx, h1, h2, ay, by, qy, hy, parts, edge):
-    gy = place[0]
+def factor_kernel(
+    fields_arg, vertical_arg, kappa_arg,
+    fields, vertical, kappa, ax, bx, qx, h1, h2, ay, by, qy, hy, parts, edge, done,
+):
+    pairs = ((kappa_arg, kappa), (fields_arg, fields), (vertical_arg, vertical))
+    copies = [pltpu.make_async_copy(a, b, done.at[n]) for n, (a, b) in enumerate(pairs)]
+    for copy in copies:
+        copy.start()
+    copies[0].wait()
+    gy = lax.axis_index("gy")
     half = 512
     rows = lax.broadcasted_iota(jnp.int32, (ROWS, half), 0)
     for f in range(2):
@@ -127,10 +135,12 @@
         total = jnp.sum(profile * ground, axis=1, keepdims=True)
         rim = jnp.sum(jnp.where(terminal, k, 0.0), axis=1, keepdims=True)
         edge[mine, :] = jnp.where(wide == 0, total, jnp.where(wide == 1, rim, 0.0))
-
-
-def source_kernel(place, fields, fields_far, vertical, vertical_far, kappa, halo, h1, h2, parts, source, sums, message):
-    gx = place[1]
+    copies[1].wait()
+    copies[2].wait()
+
+
+def source_kernel(fields, fields_far, vertical, vertical_far, kappa, halo, h1, h2, parts, source, sums, message):
+    gx = lax.axis_index("gx")
     here = fields[...]
     v = vertical[...]
     s = here + (v + vertical_far[...]) * 0.5 * (fields_far[...] - here) - v * 0.5 * here
@@ -139,7 +149,7 @@
         mine = slice(f * ROWS, (f + 1) * ROWS)
         first = dense(jnp.sum(h1[mine, :] * s[mine, :], axis=0, keepdims=True))
         last = dense(jnp.sum(h2[mine, :] * s[mine, :], axis=0, keepdims=True))
-        west = (dense(kappa[f * ROWS : f * ROWS + 1, :]) + dense(halo[f : f + 1, :])) * 0.5
+        west = (dense(kappa[f * ROWS : f * ROWS + 1, :]) + dense(halo[f * ROWS + ROWS - 1 : f * ROWS + ROWS, :])) * 0.5
         east = dense(kappa[f * ROWS + ROWS - 1 : f * ROWS + ROWS, :]) * 0.5
         g, s_first, s_last = parts[0, f], parts[1, f], parts[2, f]
         inverse = 1.0 / (west + g + s_first)
@@ -193,8 +203,8 @@
             message[j, n] = value
 
 
-def ends_kernel(place, got, chain, mine, other):
-    gx = place[1]
+def ends_kernel(got, chain, mine, other):
+    gx = lax.axis_index("gx")
     slab = gx // 8
     seat = gx % 8
     zero = jnp.zeros((8, 128), F32)
@@ -235,8 +245,8 @@
     other[1] = jnp.where(even, trio[2], trio[1])
 
 
-def section_kernel(place, mine, other, sums, local, h1, h2, hy, edge, section, message):
-    core = place[1] % 2
+def section_kernel(mine, other, sums, local, h1, h2, hy, edge, section, message):
+    core = lax.axis_index("gx") % 2
     wide = lax.broadcasted_iota(jnp.int32, (8, 128), 1)
     for f in range(2):
         left = jnp.where(core == f, mine[0], other[0])
@@ -267,12 +277,13 @@
     out[...] = local[...] + hy[...] * value
 
 
-def call(kernel, outs, specs, flops=0, size=0):
+def call(kernel, outs, specs, flops=0, size=0, scratch=()):
     return pl.pallas_call(
         kernel,
         out_shape=outs,
         in_specs=specs,
         out_specs=jax.tree.map(lambda _: VMEM, outs),
+        scratch_shapes=scratch,
         compiler_params=PARAMS,
         cost_estimate=pl.CostEstimate(flops=flops, bytes_accessed=size, transcendentals=0),
     )
@@ -283,34 +294,32 @@
 
 
 def local(fields, kappa, vertical):
-    gx = lax.axis_index("gx")
-    gy = lax.axis_index("gy")
-    place = jnp.stack([gy, gx]).astype(jnp.int32)
     grid = (ALL, COLS)
     swap = [(0, 1), (1, 0)]
     fields_far = lax.ppermute(fields, "gz", swap)
     vertical_far = lax.ppermute(vertical, "gz", swap)
-    halo = lax.ppermute(kappa[:, 0, ROWS - 1], "gx", [(i, i + 1) for i in range(63)])
-    k = kappa.reshape(grid)
+    halo = lax.ppermute(kappa, "gx", [(i, i + 1) for i in range(63)])
     full = shape(*grid)
-    ax, bx, qx, h1, h2, ay, by, qy, hy, parts, edge = call(
+    fields_here, vertical_here, kappa_here, ax, bx, qx, h1, h2, ay, by, qy, hy, parts, edge = call(
         factor_kernel,
         (
+            full, full, full,
             shape(4, *grid), shape(4, *grid), full, full, full,
             shape(10, *grid), shape(10, *grid), full, full,
             shape(3, 2, 8, 128), shape(ALL, 128),
         ),
-        [SMEM, VMEM],
+        [HBM] * 3,
         flops=20_000_000,
         size=4_000_000,
-    )(place, k)
+        scratch=[pltpu.SemaphoreType.DMA((3,))],
+    )(*(pltpu.with_memory_space_constraint(x.reshape(grid), pltpu.HBM) for x in (fields, vertical, kappa)))
     source, sums, message = call(
         source_kernel,
         (full, shape(3, 2, 8, 128), shape(8, 5, 8, 128)),
-        [SMEM] + [VMEM] * 9,
+        [VMEM] * 9,
     )(
-        place, fields.reshape(grid), fields_far.reshape(grid), vertical.reshape(grid),
-        vertical_far.reshape(grid), k, halo, h1, h2, parts,
+        fields_here, fields_far.reshape(grid), vertical_here, vertical_far.reshape(grid),
+        kappa_here, halo.reshape(grid), h1, h2, parts,
     )
     got = lax.all_to_all(message, "gx", 0, 0, axis_index_groups=PLANE_GROUPS, tiled=True)
     local_x = call(local_x_kernel, full, [VMEM] * 4, flops=1_000_000, size=1_000_000)(source, ax, bx, qx)
@@ -319,12 +328,12 @@
     )(got)
     got = lax.all_to_all(message, "gx", 0, 0, axis_index_groups=SLAB_GROUPS, tiled=True)
     mine, other = call(
-        ends_kernel, (shape(2, 8, 128), shape(2, 8, 128)), [SMEM, VMEM, VMEM]
-    )(place, got, chain)
+        ends_kernel, (shape(2, 8, 128), shape(2, 8, 128)), [VMEM, VMEM]
+    )(got, chain)
     other = lax.ppermute(other, "gx", [(i, i ^ 1) for i in range(64)])
     section, message = call(
-        section_kernel, (full, shape(ALL, 128)), [SMEM] + [VMEM] * 8
-    )(place, mine, other, sums, local_x, h1, h2, hy, edge)
+        section_kernel, (full, shape(ALL, 128)), [VMEM] * 8
+    )(mine, other, sums, local_x, h1, h2, hy, edge)
     far = lax.ppermute(message, "gy", swap)
     local_y = call(local_y_kernel, full, [VMEM] * 4, flops=4_000_000, size=3_000_000)(section, ay, by, qy)
     out = call(output_kernel, full, [VMEM] * 4)(message, far, local_y, hy)

time: 52.1 us -> 46.9 us (0.900)
  local copies, waits for them, and re-layouts: 3.56 us -> 0 us
  Pallas kernels: 9.08 us -> 7.81 us
    unnamed x7 -> x0, local copies, waits for them, and re-layouts: 2.71 us -> none
    pallas_call x4, Pallas kernels: 7.14 us -> 5.86 us  [the longest x1 5.49 us: local(): call(factor_kernel, (full, full, full, shape(4, *grid), shape(4, *grid),...]
    slice x1 -> x0, local copies, waits for them, and re-layouts: 0.85 us -> none  [local(): kappa[:, 0, ROWS - 1]]
  transfers between devices with their start and end apart: 5 -> 5, of which waited for: 2 -> 2; matrix products, arithmetic and copies ran while one was open for 2% -> 0% of each run, Pallas kernels for 12% -> 14%
where the time goes in v1:
time: 46.9 us; the launch traced here: 46.7 us
  blocking collectives  25.7 us (55%)
  starting transfers between devices  11.9 us (25%)
  Pallas kernels  7.81 us (17%)
  waiting for transfers between devices  1.19 us (3%)
    all_to_all x1, blocking collectives, local(): lax.all_to_all(message, 'gx', 0, 0, axis_index_groups=SLAB_GROUPS, tiled=...  15.9 us
    all_to_all x1, blocking collectives, local(): lax.all_to_all(message, 'gx', 0, 0, axis_index_groups=PLANE_GROUPS, tiled...  9.78 us
    pallas_call x1, Pallas kernels, local(): call(factor_kernel, (full, full, full, shape(4, *grid), shape(4, *grid),...  5.49 us
    ppermute x1, starting transfers between devices, local(): halo = lax.ppermute(kappa, 'gx', [(i, i + 1) for i in range(63)])  4.03 us
    ppermute x1, starting transfers between devices, local(): far = lax.ppermute(message, 'gy', swap)  2.76 us
    ppermute x1, starting transfers between devices, local(): other = lax.ppermute(other, 'gx', [(i, i ^ 1) for i in range(64)])  2.74 us
    ppermute x1, starting transfers between devices, local(): fields_far = lax.ppermute(fields, 'gz', swap)  2.04 us
  transfers between devices with their start and end apart: 5, of which 2 were waited for; matrix products, arithmetic and copies ran while one was open for 0% of the time, Pallas kernels for 14%

profile of v1, /device:TPU:1, one launch (start us, length us, event | category | flops | bytes accessed | tf_op | source)
XLA Modules:
  0.0 46.7 jit_solution(14777256714263711894)
XLA Ops:
  0.0 2.0 %collective-permute-start = (f32[2,1,16,1024]{3,2,1,0:T(8,128)}, f32[2,1,16,1024]{3,2,1,0:T(8,128)S(1)}, u32[]{:S(2)}, u32[]{:S(2)}) collective-permute-start(f32[2,1,16,1024]{3,2,1,0:T(8,128)} %param.3), channel_id=1, source_target_pairs={{0,1},{1,0},{2,3},{3,2},{4,5},{5,4},{6,7},{7,6},{8,9},{9,8},{10,11... | collective-permute-start | bytes 393224 | tf_op jit(solution)/shard_map/ppermute | solution.py:299
  2.0 4.0 %collective-permute-start.2 = (f32[2,1,16,1024]{3,2,1,0:T(8,128)}, f32[2,1,16,1024]{3,2,1,0:T(8,128)S(1)}, u32[]{:S(2)}, u32[]{:S(2)}) collective-permute-start(f32[2,1,16,1024]{3,2,1,0:T(8,128)} %param.4), channel_id=1, source_target_pairs={{0,4},{4,8},{8,12},{12,16},{16,20},{20,24},{24,28},{28,32},{32,36}... | collective-permute-start | bytes 393224 | tf_op jit(solution)/shard_map/ppermute | solution.py:301
  6.1 0.3 collective-permute-start.1
  6.4 5.5 %shard_map.37 = (f32[32,1024]{1,0:T(8,128)S(1)}, f32[32,1024]{1,0:T(8,128)S(1)}, f32[32,1024]{1,0:T(8,128)S(1)}, f32[4,32,1024]{2,1,0:T(8,128)S(1)}, f32[4,32,10...) custom-call(f32[32,1024]{1,0:T(8,128)} %bitcast.12, ...), custom_call_target="tpu_custom_call" | custom-call | flops 20000000 | bytes 4000000 | tf_op jit(solution)/shard_map/pallas_call | solution.py:303
  11.9 0.0 collective-permute-done
  11.9 0.0 collective-permute-done.2
  11.9 0.0 collective-permute-done.1
  12.0 0.1 shard_map.38
  12.1 9.8 %all_to_all.10.got = f32[8,5,8,128]{3,2,1,0:T(8,128)S(1)} all-to-all(f32[8,5,8,128]{3,2,1,0:T(8,128)S(1)} %get-tuple-element.34), channel_id=1, replica_groups={{0,4,8,12,16,20,24,28},{32,36,40,44,48,52,56,60},{64,68,72,76,80,84,88,..., dimensions={0} | all-to-all | bytes 327680 | tf_op jit(solution)/shard_map/all_to_all | solution.py:324
  21.9 0.1 shard_map.39
  21.9 15.9 %all_to_all.11.got = f32[8,5,8,128]{3,2,1,0:T(8,128)S(1)} all-to-all(f32[8,5,8,128]{3,2,1,0:T(8,128)S(1)} %get-tuple-element.35), channel_id=1, replica_groups={{0,32,64,96,128,160,192,224},{4,36,68,100,132,164,196,228},{8,40,72,104..., dimensions={0} | all-to-all | bytes 327680 | tf_op jit(solution)/shard_map/all_to_all | solution.py:329
  37.9 0.1 shard_map.40
  38.0 2.7 %collective-permute-start.3 = (f32[2,8,128]{2,1,0:T(8,128)S(1)}, f32[2,8,128]{2,1,0:T(8,128)S(1)}, u32[]{:S(2)}, u32[]{:S(2)}) collective-permute-start(f32[2,8,128]{2,1,0:T(8,128)S(1)} %get-tuple-element.38), channel_id=1, source_target_pairs={{0,4},{4,0},{8,12},{12,8},{16,20},{20,16},{24,28},{28,24},{32,36},... | collective-permute-start | bytes 24584 | tf_op jit(solution)/shard_map/ppermute | solution.py:333
  40.8 0.1 shard_map.41.local
  40.9 0.7 %collective-permute-done.3.other = f32[2,8,128]{2,1,0:T(8,128)S(1)} collective-permute-done((f32[2,8,128]{2,1,0:T(8,128)S(1)}, f32[2,8,128]{2,1,0:T(8,128)S(1)}, u32[]{:S(2)}, u32[]{:S(2)}) %collective-permute-start.3) | collective-permute-done | bytes 8224 | tf_op jit(solution)/shard_map/ppermute | solution.py:333
  41.6 0.1 shard_map.42
  41.7 2.8 %collective-permute-start.4 = (f32[32,128]{1,0:T(8,128)S(1)}, f32[32,128]{1,0:T(8,128)S(1)}, u32[]{:S(2)}, u32[]{:S(2)}) collective-permute-start(f32[32,128]{1,0:T(8,128)S(1)} %get-tuple-element.46.message), channel_id=1, source_target_pairs={{0,2},{2,0},{1,3},{3,1},{4,6},{6,4},{5,7},{7,5},{8,10},{10,8},{9,1... | collective-permute-start | bytes 49160 | tf_op jit(solution)/shard_map/ppermute | solution.py:337
  44.5 0.9 %shard_map.43.local = f32[32,1024]{1,0:T(8,128)S(1)} custom-call(f32[32,1024]{1,0:T(8,128)S(1)} %get-tuple-element.47.section, f32[10,32,1024]{2,1,0:T(8,128)S(1)} %get-tuple-element.48.ay, f32[10,32,1024]{2,1,0:T(8,128)S(1)} %get-tuple-element.49.by, f32[32,1024]{1,0:T(8,128)S(1)} %get-tuple-element.50.qy), custom_call_target="tpu_custom_call" | custom-call | flops 4000000 | bytes 3000000 | tf_op jit(solution)/shard_map/pallas_call | solution.py:338
  45.3 0.5 %collective-permute-done.4.far = f32[32,128]{1,0:T(8,128)S(1)} collective-permute-done((f32[32,128]{1,0:T(8,128)S(1)}, f32[32,128]{1,0:T(8,128)S(1)}, u32[]{:S(2)}, u32[]{:S(2)}) %collective-permute-start.4) | collective-permute-done | bytes 16416 | tf_op jit(solution)/shard_map/ppermute | solution.py:337
  45.8 0.9 %shard_map.44 = f32[32,1024]{1,0:T(8,128)} custom-call(f32[32,128]{1,0:T(8,128)S(1)} %get-tuple-element.46.message, f32[32,128]{1,0:T(8,128)S(1)} %collective-permute-done.4.far, f32[32,1024]{1,0:T(8,128)S(1)} %shard_map.43.local, f32[32,1024]{1,0:T(8,128)S(1)} %get-tuple-element.44.hy), custom_call_target="tpu_custom_call" | custom-call | tf_op jit(solution)/shard_map/pallas_call | solution.py:339
Async XLA Ops:
  0.0 11.9 %collective-permute-start = (f32[2,1,16,1024]{3,2,1,0:T(8,128)}, f32[2,1,16,1024]{3,2,1,0:T(8,128)S(1)}, u32[]{:S(2)}, u32[]{:S(2)}) collective-permute-start(f32[2,1,16,1024]{3,2,1,0:T(8,128)} %param.3), channel_id=1, source_target_pairs={{0,1},{1,0},{2,3},{3,2},{4,5},{5,4},{6,7},{7,6},{8,9},{9,8},{10,11... | collective-permute-start | bytes 393224 | tf_op jit(solution)/shard_map/ppermute | solution.py:299
  2.0 9.9 %collective-permute-start.2 = (f32[2,1,16,1024]{3,2,1,0:T(8,128)}, f32[2,1,16,1024]{3,2,1,0:T(8,128)S(1)}, u32[]{:S(2)}, u32[]{:S(2)}) collective-permute-start(f32[2,1,16,1024]{3,2,1,0:T(8,128)} %param.4), channel_id=1, source_target_pairs={{0,4},{4,8},{8,12},{12,16},{16,20},{20,24},{24,28},{28,32},{32,36}... | collective-permute-start | bytes 393224 | tf_op jit(solution)/shard_map/ppermute | solution.py:301
  6.1 5.9 %collective-permute-start.1 = (f32[2,1,16,1024]{3,2,1,0:T(8,128)}, f32[2,1,16,1024]{3,2,1,0:T(8,128)S(1)}, u32[]{:S(2)}, u32[]{:S(2)}) collective-permute-start(f32[2,1,16,1024]{3,2,1,0:T(8,128)} %param.5), channel_id=1, source_target_pairs={{0,1},{1,0},{2,3},{3,2},{4,5},{5,4},{6,7},{7,6},{8,9},{9,8},{10,11... | collective-permute-start | bytes 393224 | tf_op jit(solution)/shard_map/ppermute | solution.py:300
  38.0 3.6 %collective-permute-start.3 = (f32[2,8,128]{2,1,0:T(8,128)S(1)}, f32[2,8,128]{2,1,0:T(8,128)S(1)}, u32[]{:S(2)}, u32[]{:S(2)}) collective-permute-start(f32[2,8,128]{2,1,0:T(8,128)S(1)} %get-tuple-element.38), channel_id=1, source_target_pairs={{0,4},{4,0},{8,12},{12,8},{16,20},{20,16},{24,28},{28,24},{32,36},... | collective-permute-start | bytes 24584 | tf_op jit(solution)/shard_map/ppermute | solution.py:333
  41.7 4.1 %collective-permute-start.4 = (f32[32,128]{1,0:T(8,128)S(1)}, f32[32,128]{1,0:T(8,128)S(1)}, u32[]{:S(2)}, u32[]{:S(2)}) collective-permute-start(f32[32,128]{1,0:T(8,128)S(1)} %get-tuple-element.46.message), channel_id=1, source_target_pairs={{0,2},{2,0},{1,3},{3,1},{4,6},{6,4},{5,7},{7,5},{8,10},{10,8},{9,1... | collective-permute-start | bytes 49160 | tf_op jit(solution)/shard_map/ppermute | solution.py:337

commit v2 on v1

--- a/solution.py
+++ b/solution.py
@@ -66,16 +66,14 @@
     )
 
 
-def factor_kernel(
-    fields_arg, vertical_arg, kappa_arg,
-    fields, vertical, kappa, ax, bx, qx, h1, h2, ay, by, qy, hy, parts, edge, done,
+def factor_x_kernel(
+    fields_arg, vertical_arg, kappa_arg, fields, vertical, kappa, ax, bx, qx, h1, h2, parts, done
 ):
     pairs = ((kappa_arg, kappa), (fields_arg, fields), (vertical_arg, vertical))
     copies = [pltpu.make_async_copy(a, b, done.at[n]) for n, (a, b) in enumerate(pairs)]
     for copy in copies:
         copy.start()
     copies[0].wait()
-    gy = lax.axis_index("gy")
     half = 512
     rows = lax.broadcasted_iota(jnp.int32, (ROWS, half), 0)
     for f in range(2):
@@ -109,6 +107,13 @@
             ):
                 for i in range(half // 128):
                     parts[n, f, pl.ds(c * (half // 128) + i, 1), :] = row[:, 128 * i : 128 * (i + 1)]
+    copies[1].wait()
+    copies[2].wait()
+
+
+def factor_y_kernel(kappa, after, ay, by, qy, hy, edge):
+    del after
+    gy = lax.axis_index("gy")
     lanes = lax.broadcasted_iota(jnp.int32, (8, COLS), 1)
     wide = lax.broadcasted_iota(jnp.int32, (8, 128), 1)
     low_side = gy == 0
@@ -135,12 +140,12 @@
         total = jnp.sum(profile * ground, axis=1, keepdims=True)
         rim = jnp.sum(jnp.where(terminal, k, 0.0), axis=1, keepdims=True)
         edge[mine, :] = jnp.where(wide == 0, total, jnp.where(wide == 1, rim, 0.0))
-    copies[1].wait()
-    copies[2].wait()
-
-
-def source_kernel(fields, fields_far, vertical, vertical_far, kappa, halo, h1, h2, parts, source, sums, message):
+
+
+def source_kernel(fields, fields_far, vertical, vertical_far, kappa, halo, h1, h2, parts, source, sums, keep, send):
     gx = lax.axis_index("gx")
+    even = gx % 2 == 0
+    elements = []
     here = fields[...]
     v = vertical[...]
     s = here + (v + vertical_far[...]) * 0.5 * (fields_far[...] - here) - v * 0.5 * here
@@ -165,9 +170,10 @@
             a * first,
             last + b * first,
         )
-        for n, value in enumerate(element):
-            for j in range(4):
-                message[2 * j + f, n] = value
+        elements.append(element)
+    for n, (one, two) in enumerate(zip(*elements)):
+        keep[n] = jnp.where(even, one, two)
+        send[n] = jnp.where(even, two, one)
 
 
 def local_x_kernel(source, ax, bx, qx, out):
@@ -181,32 +187,79 @@
             out[mine, cols] = r * qx[mine, cols]
 
 
-def slab_kernel(got, message, chain):
-    g, sl, sr, rl, rr = (got[0, n] for n in range(5))
-    for k in range(7):
-        g2, sl2, sr2, rl2, rr2 = (got[k + 1, n] for n in range(5))
-        s = sr + sl2
-        r = rr + rl2
-        inverse = 1.0 / (g + g2 + s)
-        a = g * inverse
-        b = g2 * inverse
-        chain[k, 0] = a
-        chain[k, 1] = b
-        chain[k, 2] = r * inverse
-        sl = sl + a * s
-        rl = rl + a * r
-        sr = sr2 + b * s
-        rr = rr2 + b * r
-        g = a * g2
-    for n, value in enumerate((g, sl, sr, rl, rr)):
+def merge(one, two):
+    g, sl, sr, rl, rr = one
+    g2, sl2, sr2, rl2, rr2 = two
+    s = sr + sl2
+    r = rr + rl2
+    inverse = 1.0 / (g + g2 + s)
+    a = g * inverse
+    b = g2 * inverse
+    return (a * g2, sl + a * s, sr2 + b * s, rl + a * r, rr2 + b * r), (a, b, r * inverse)
+
+
+def load(ref):
+    return tuple(ref[n] for n in range(5))
+
+
+def chip_kernel(keep, got, chip, middle):
+    even = lax.axis_index("gx") % 2 == 0
+    mine, other = load(keep), load(got)
+    first = [jnp.where(even, m, o) for m, o in zip(mine, other)]
+    second = [jnp.where(even, o, m) for m, o in zip(mine, other)]
+    element, node = merge(first, second)
+    for n, value in enumerate(element):
+        chip[n] = value
+    for n, value in enumerate(node):
+        middle[n] = value
+
+
+def slab_kernel(chip, far1, far2, far3, middle, after, message, nodes):
+    del after
+    y = lax.axis_index("gx") // 2 % 4
+    arrived = [load(chip), load(far1), load(far2), load(far3)]
+    chips = []
+    for m in range(4):
+        chosen = arrived[0]
+        for shift in range(1, 4):
+            here = (y + shift) % 4 == m
+            chosen = [jnp.where(here, a, c) for a, c in zip(arrived[shift], chosen)]
+        chips.append(chosen)
+    element = chips[0]
+    inner = []
+    for m in range(1, 4):
+        element, node = merge(element, chips[m])
+        inner.append(node)
+    for n, value in enumerate(element):
         for j in range(8):
             message[j, n] = value
-
-
-def ends_kernel(got, chain, mine, other):
+    zero, one = jnp.zeros((8, 128), F32), jnp.ones((8, 128), F32)
+    ends = [(zero, one, zero)]
+    for a, b, c in inner[::-1]:
+        a2, b2, c2 = ends[-1]
+        ends.append((a + b * a2, b * b2, c + b * c2))
+    ends.append((one, zero, zero))
+    ends = ends[::-1]
+    west, east = ends[0], ends[1]
+    for m in range(1, 4):
+        west = [jnp.where(y == m, e, w) for e, w in zip(ends[m], west)]
+        east = [jnp.where(y == m, e, w) for e, w in zip(ends[m + 1], east)]
+    a, b, c = load3(middle)
+    half = [a * w + b * e for w, e in zip(west, east)]
+    half[2] = half[2] + c
+    for n, trio in enumerate((west, half, east)):
+        for m in range(3):
+            nodes[n, m] = trio[m]
+
+
+def load3(ref):
+    return tuple(ref[n] for n in range(3))
+
+
+def ends_kernel(got, nodes, mine, other):
     gx = lax.axis_index("gx")
     slab = gx // 8
-    seat = gx % 8
+    even = gx % 2 == 0
     zero = jnp.zeros((8, 128), F32)
     conduct = got[0, 0] + got[0, 2]
     right = got[0, 4]
@@ -230,15 +283,7 @@
     for z in range(8):
         left = jnp.where(slab == z, values[z], left)
         last = jnp.where(slab == z, values[z + 1], last)
-    nodes = [last]
-    for k in range(6, -1, -1):
-        nodes.append(chain[k, 0] * left + chain[k, 1] * nodes[-1] + chain[k, 2])
-    nodes = [left] + nodes[::-1]
-    even = seat % 2 == 0
-    trio = [zero, zero, zero]
-    for j in range(4):
-        for n in range(3):
-            trio[n] = jnp.where(seat // 2 == j, nodes[2 * j + n], trio[n])
+    trio = [nodes[n, 0] * left + nodes[n, 1] * last + nodes[n, 2] for n in range(3)]
     mine[0] = jnp.where(even, trio[0], trio[1])
     mine[1] = jnp.where(even, trio[1], trio[2])
     other[0] = jnp.where(even, trio[1], trio[0])
@@ -289,8 +334,12 @@
     )
 
 
-PLANE_GROUPS = [[8 * a + b for b in range(8)] for a in range(8)]
 SLAB_GROUPS = [[8 * b + a for b in range(8)] for a in range(8)]
+CORES = [(i, i ^ 1) for i in range(64)]
+
+
+def chips_on(shift):
+    return [(i // 8 * 8 + (i + 2 * shift) % 8, i) for i in range(64)]
 
 
 def local(fields, kappa, vertical):
@@ -300,37 +349,40 @@
     vertical_far = lax.ppermute(vertical, "gz", swap)
     halo = lax.ppermute(kappa, "gx", [(i, i + 1) for i in range(63)])
     full = shape(*grid)
-    fields_here, vertical_here, kappa_here, ax, bx, qx, h1, h2, ay, by, qy, hy, parts, edge = call(
-        factor_kernel,
-        (
-            full, full, full,
-            shape(4, *grid), shape(4, *grid), full, full, full,
-            shape(10, *grid), shape(10, *grid), full, full,
-            shape(3, 2, 8, 128), shape(ALL, 128),
-        ),
+    half = shape(5, 8, 128)
+    fields_here, vertical_here, kappa_here, ax, bx, qx, h1, h2, parts = call(
+        factor_x_kernel,
+        (full, full, full, shape(4, *grid), shape(4, *grid), full, full, full, shape(3, 2, 8, 128)),
         [HBM] * 3,
-        flops=20_000_000,
-        size=4_000_000,
+        flops=4_000_000,
+        size=2_000_000,
         scratch=[pltpu.SemaphoreType.DMA((3,))],
     )(*(pltpu.with_memory_space_constraint(x.reshape(grid), pltpu.HBM) for x in (fields, vertical, kappa)))
-    source, sums, message = call(
-        source_kernel,
-        (full, shape(3, 2, 8, 128), shape(8, 5, 8, 128)),
-        [VMEM] * 9,
+    source, sums, keep, send = call(
+        source_kernel, (full, shape(3, 2, 8, 128), half, half), [VMEM] * 9
     )(
         fields_here, fields_far.reshape(grid), vertical_here, vertical_far.reshape(grid),
         kappa_here, halo.reshape(grid), h1, h2, parts,
     )
-    got = lax.all_to_all(message, "gx", 0, 0, axis_index_groups=PLANE_GROUPS, tiled=True)
+    got = lax.ppermute(send, "gx", CORES)
     local_x = call(local_x_kernel, full, [VMEM] * 4, flops=1_000_000, size=1_000_000)(source, ax, bx, qx)
-    message, chain = call(
-        slab_kernel, (shape(8, 5, 8, 128), shape(7, 3, 8, 128)), [VMEM]
-    )(got)
+    chip, middle = call(chip_kernel, (half, shape(3, 8, 128)), [VMEM] * 2)(keep, got)
+    far = [lax.ppermute(chip, "gx", chips_on(shift)) for shift in (2, 1, 3)]
+    ay, by, qy, hy, edge = call(
+        factor_y_kernel,
+        (shape(10, *grid), shape(10, *grid), full, full, shape(ALL, 128)),
+        [VMEM] * 2,
+        flops=20_000_000,
+        size=4_000_000,
+    )(kappa_here, middle)
+    message, nodes = call(
+        slab_kernel, (shape(8, 5, 8, 128), shape(3, 3, 8, 128)), [VMEM] * 6
+    )(chip, far[1], far[0], far[2], middle, edge)
     got = lax.all_to_all(message, "gx", 0, 0, axis_index_groups=SLAB_GROUPS, tiled=True)
     mine, other = call(
         ends_kernel, (shape(2, 8, 128), shape(2, 8, 128)), [VMEM, VMEM]
-    )(got, chain)
-    other = lax.ppermute(other, "gx", [(i, i ^ 1) for i in range(64)])
+    )(got, nodes)
+    other = lax.ppermute(other, "gx", CORES)
     section, message = call(
         section_kernel, (full, shape(ALL, 128)), [VMEM] * 8
     )(mine, other, sums, local_x, h1, h2, hy, edge)

time: 46.9 us -> 46.6 us (level)
  blocking collectives: 25.7 us -> 16.3 us
  starting transfers between devices: 11.9 us -> 17.1 us
  waiting for transfers between devices: 1.19 us -> 5.15 us
    all_to_all x1 -> x0, blocking collectives: 9.78 us -> none  [local(): lax.all_to_all(message, 'gx', 0, 0, axis_index_groups=PLANE_GROUPS, tiled...]
    ppermute x1 -> x5, starting transfers between devices: 2.74 us -> 8.18 us  [the longest x3 5.43 us: local(): far = [lax.ppermute(chip, 'gx', chips_on(shift)) for shift in (2, 1, 3)]]
    ppermute x1, waiting for transfers between devices: 0.01 us -> 2.21 us  [local(): vertical_far = lax.ppermute(vertical, 'gz', swap)]
    ppermute x1 -> x5, waiting for transfers between devices: 0.7 us -> 1.87 us  [the longest x1 1.18 us: local(): got = lax.ppermute(send, 'gx', CORES)]
    pallas_call x3 -> x5, Pallas kernels: 5.69 us -> 5.8 us  [the longest x1 4 us: local(): call(factor_y_kernel, (shape(10, *grid), shape(10, *grid), full, full, sh...]
  transfers between devices with their start and end apart: 5 -> 9, of which waited for: 2 -> 5; matrix products, arithmetic and copies ran while one was open for 0% -> 0% of each run, Pallas kernels for 14% -> 14%
where the time goes in v2:
time: 46.6 us; the launch traced here: 46.5 us
  starting transfers between devices  17.1 us (37%)
  blocking collectives  16.3 us (35%)
  Pallas kernels  7.91 us (17%)
  waiting for transfers between devices  5.15 us (11%)
    all_to_all x1, blocking collectives, local(): lax.all_to_all(message, 'gx', 0, 0, axis_index_groups=SLAB_GROUPS, tiled=...  16.3 us
    ppermute x3, starting transfers between devices, local(): far = [lax.ppermute(chip, 'gx', chips_on(shift)) for shift in (2, 1, 3)]  5.43 us
    ppermute x1, starting transfers between devices, local(): halo = lax.ppermute(kappa, 'gx', [(i, i + 1) for i in range(63)])  4.03 us
    pallas_call x1, Pallas kernels, local(): call(factor_y_kernel, (shape(10, *grid), shape(10, *grid), full, full, sh...  4 us
    ppermute x1, starting transfers between devices, local(): other = lax.ppermute(other, 'gx', CORES)  2.67 us
    ppermute x1, starting transfers between devices, local(): far = lax.ppermute(message, 'gy', swap)  2.47 us
    ppermute x1, waiting for transfers between devices, local(): vertical_far = lax.ppermute(vertical, 'gz', swap)  2.21 us
    ppermute x1, starting transfers between devices, local(): fields_far = lax.ppermute(fields, 'gz', swap)  2.04 us
  transfers between devices with their start and end apart: 9, of which 5 were waited for; matrix products, arithmetic and copies ran while one was open for 0% of the time, Pallas kernels for 14%

profile of v2, /device:TPU:1, one launch (start us, length us, event | category | flops | bytes accessed | tf_op | source)
XLA Modules:
  0.0 46.5 jit_solution(12422934786928129592)
XLA Ops:
  0.0 2.0 %collective-permute-start = (f32[2,1,16,1024]{3,2,1,0:T(8,128)}, f32[2,1,16,1024]{3,2,1,0:T(8,128)S(1)}, u32[]{:S(2)}, u32[]{:S(2)}) collective-permute-start(f32[2,1,16,1024]{3,2,1,0:T(8,128)} %param.3), channel_id=1, source_target_pairs={{0,1},{1,0},{2,3},{3,2},{4,5},{5,4},{6,7},{7,6},{8,9},{9,8},{10,11... | collective-permute-start | bytes 393224 | tf_op jit(solution)/shard_map/ppermute | solution.py:348
  2.0 4.0 %collective-permute-start.2 = (f32[2,1,16,1024]{3,2,1,0:T(8,128)}, f32[2,1,16,1024]{3,2,1,0:T(8,128)S(1)}, u32[]{:S(2)}, u32[]{:S(2)}) collective-permute-start(f32[2,1,16,1024]{3,2,1,0:T(8,128)} %param.4), channel_id=1, source_target_pairs={{0,4},{4,8},{8,12},{12,16},{16,20},{20,24},{24,28},{28,32},{32,36}... | collective-permute-start | bytes 393224 | tf_op jit(solution)/shard_map/ppermute | solution.py:350
  6.1 0.3 collective-permute-start.1
  6.4 1.6 %shard_map.37 = (f32[32,1024]{1,0:T(8,128)S(1)}, f32[32,1024]{1,0:T(8,128)S(1)}, f32[32,1024]{1,0:T(8,128)S(1)}, f32[4,32,1024]{2,1,0:T(8,128)S(1)}, f32[4,32,10...) custom-call(f32[32,1024]{1,0:T(8,128)} %bitcast.12, ...), custom_call_target="tpu_custom_call" | custom-call | flops 4000000 | bytes 2000000 | tf_op jit(solution)/shard_map/pallas_call | solution.py:353
  8.0 0.0 collective-permute-done
  8.0 0.3 collective-permute-done.2
  8.3 2.2 %collective-permute-done.1 = f32[2,1,16,1024]{3,2,1,0:T(8,128)S(1)} collective-permute-done((f32[2,1,16,1024]{3,2,1,0:T(8,128)}, f32[2,1,16,1024]{3,2,1,0:T(8,128)S(1)}, u32[]{:S(2)}, u32[]{:S(2)}) %collective-permute-start.1) | collective-permute-done | bytes 131104 | tf_op jit(solution)/shard_map/ppermute | solution.py:349
  10.5 0.1 shard_map.38
  10.6 0.1 collective-permute-start.3
  10.7 1.2 %collective-permute-done.3.got = f32[5,8,128]{2,1,0:T(8,128)S(1)} collective-permute-done((f32[5,8,128]{2,1,0:T(8,128)S(1)}, f32[5,8,128]{2,1,0:T(8,128)S(1)}, u32[]{:S(2)}, u32[]{:S(2)}) %collective-permute-start.3) | collective-permute-done | bytes 20512 | tf_op jit(solution)/shard_map/ppermute | solution.py:367
  11.9 1.7 %collective-permute-start.6 = (f32[5,8,128]{2,1,0:T(8,128)S(1)}, f32[5,8,128]{2,1,0:T(8,128)S(1)}, u32[]{:S(2)}, u32[]{:S(2)}) collective-permute-start(f32[5,8,128]{2,1,0:T(8,128)S(1)} %get-tuple-element.39.chip), channel_id=1, source_target_pairs={{24,0},{28,4},{0,8},{4,12},{8,16},{12,20},{16,24},{20,28},{56,32},... | collective-permute-start | bytes 61448 | tf_op jit(solution)/shard_map/ppermute | solution.py:370
  13.7 2.6 %collective-permute-start.5 = (f32[5,8,128]{2,1,0:T(8,128)S(1)}, f32[5,8,128]{2,1,0:T(8,128)S(1)}, u32[]{:S(2)}, u32[]{:S(2)}) collective-permute-start(f32[5,8,128]{2,1,0:T(8,128)S(1)} %get-tuple-element.39.chip), channel_id=1, source_target_pairs={{16,0},{20,4},{24,8},{28,12},{0,16},{4,20},{8,24},{12,28},{48,32},... | collective-permute-start | bytes 61448 | tf_op jit(solution)/shard_map/ppermute | solution.py:370
  16.3 1.1 %collective-permute-start.4 = (f32[5,8,128]{2,1,0:T(8,128)S(1)}, f32[5,8,128]{2,1,0:T(8,128)S(1)}, u32[]{:S(2)}, u32[]{:S(2)}) collective-permute-start(f32[5,8,128]{2,1,0:T(8,128)S(1)} %get-tuple-element.39.chip), channel_id=1, source_target_pairs={{8,0},{12,4},{16,8},{20,12},{24,16},{28,20},{0,24},{4,28},{40,32},... | collective-permute-start | bytes 61448 | tf_op jit(solution)/shard_map/ppermute | solution.py:370
  17.4 4.0 %shard_map.40 = (f32[10,32,1024]{2,1,0:T(8,128)S(1)}, f32[10,32,1024]{2,1,0:T(8,128)S(1)}, f32[32,1024]{1,0:T(8,128)S(1)}, f32[32,1024]{1,0:T(8,128)S(1)}, f32[32,128]{1,0:T(8,128)S(1)}) custom-call(f32[32,1024]{1,0:T(8,128)S(1)} %get-tuple-element.33.kappa, f32[3,8,128]{2,1,0:T(8,128)S(1)} %get-tuple-element.40.after.middle), custom_call_target="tpu_custom_call" | custom-call | flops 20000000 | bytes 4000000 | tf_op jit(solution)/shard_map/pallas_call | solution.py:371
  21.4 0.0 collective-permute-done.6.far3
  21.4 0.0 collective-permute-done.5.far2
  21.4 0.0 collective-permute-done.4.far1
  21.4 0.1 shard_map.41
  21.5 16.3 %all_to_all.5.got = f32[8,5,8,128]{3,2,1,0:T(8,128)S(1)} all-to-all(f32[8,5,8,128]{3,2,1,0:T(8,128)S(1)} %get-tuple-element.42), channel_id=1, replica_groups={{0,32,64,96,128,160,192,224},{4,36,68,100,132,164,196,228},{8,40,72,104..., dimensions={0} | all-to-all | bytes 327680 | tf_op jit(solution)/shard_map/all_to_all | solution.py:381
  37.8 0.1 shard_map.42
  37.9 2.7 %collective-permute-start.7 = (f32[2,8,128]{2,1,0:T(8,128)S(1)}, f32[2,8,128]{2,1,0:T(8,128)S(1)}, u32[]{:S(2)}, u32[]{:S(2)}) collective-permute-start(f32[2,8,128]{2,1,0:T(8,128)S(1)} %get-tuple-element.45), channel_id=1, source_target_pairs={{0,4},{4,0},{8,12},{12,8},{16,20},{20,16},{24,28},{28,24},{32,36},... | collective-permute-start | bytes 24584 | tf_op jit(solution)/shard_map/ppermute | solution.py:385
  40.5 0.1 shard_map.43.local
  40.7 0.7 %collective-permute-done.7.other = f32[2,8,128]{2,1,0:T(8,128)S(1)} collective-permute-done((f32[2,8,128]{2,1,0:T(8,128)S(1)}, f32[2,8,128]{2,1,0:T(8,128)S(1)}, u32[]{:S(2)}, u32[]{:S(2)}) %collective-permute-start.7) | collective-permute-done | bytes 8224 | tf_op jit(solution)/shard_map/ppermute | solution.py:385
  41.4 0.1 shard_map.44
  41.5 2.5 %collective-permute-start.8 = (f32[32,128]{1,0:T(8,128)S(1)}, f32[32,128]{1,0:T(8,128)S(1)}, u32[]{:S(2)}, u32[]{:S(2)}) collective-permute-start(f32[32,128]{1,0:T(8,128)S(1)} %get-tuple-element.52.message), channel_id=1, source_target_pairs={{0,2},{2,0},{1,3},{3,1},{4,6},{6,4},{5,7},{7,5},{8,10},{10,8},{9,1... | collective-permute-start | bytes 49160 | tf_op jit(solution)/shard_map/ppermute | solution.py:389
  44.0 0.9 %shard_map.45.local = f32[32,1024]{1,0:T(8,128)S(1)} custom-call(f32[32,1024]{1,0:T(8,128)S(1)} %get-tuple-element.53.section, f32[10,32,1024]{2,1,0:T(8,128)S(1)} %get-tuple-element.54.ay, f32[10,32,1024]{2,1,0:T(8,128)S(1)} %get-tuple-element.55.by, f32[32,1024]{1,0:T(8,128)S(1)} %get-tuple-element.56.qy), custom_call_target="tpu_custom_call" | custom-call | flops 4000000 | bytes 3000000 | tf_op jit(solution)/shard_map/pallas_call | solution.py:390
  44.8 0.8 %collective-permute-done.8.far = f32[32,128]{1,0:T(8,128)S(1)} collective-permute-done((f32[32,128]{1,0:T(8,128)S(1)}, f32[32,128]{1,0:T(8,128)S(1)}, u32[]{:S(2)}, u32[]{:S(2)}) %collective-permute-start.8) | collective-permute-done | bytes 16416 | tf_op jit(solution)/shard_map/ppermute | solution.py:389
  45.6 0.9 %shard_map.46 = f32[32,1024]{1,0:T(8,128)} custom-call(f32[32,128]{1,0:T(8,128)S(1)} %get-tuple-element.52.message, f32[32,128]{1,0:T(8,128)S(1)} %collective-permute-done.8.far, f32[32,1024]{1,0:T(8,128)S(1)} %shard_map.45.local, f32[32,1024]{1,0:T(8,128)S(1)} %get-tuple-element.51.hy), custom_call_target="tpu_custom_call" | custom-call | tf_op jit(solution)/shard_map/pallas_call | solution.py:391
  (1 shorter events, 0.0 us)
Async XLA Ops:
  0.0 8.0 %collective-permute-start = (f32[2,1,16,1024]{3,2,1,0:T(8,128)}, f32[2,1,16,1024]{3,2,1,0:T(8,128)S(1)}, u32[]{:S(2)}, u32[]{:S(2)}) collective-permute-start(f32[2,1,16,1024]{3,2,1,0:T(8,128)} %param.3), channel_id=1, source_target_pairs={{0,1},{1,0},{2,3},{3,2},{4,5},{5,4},{6,7},{7,6},{8,9},{9,8},{10,11... | collective-permute-start | bytes 393224 | tf_op jit(solution)/shard_map/ppermute | solution.py:348
  2.0 6.3 %collective-permute-start.2 = (f32[2,1,16,1024]{3,2,1,0:T(8,128)}, f32[2,1,16,1024]{3,2,1,0:T(8,128)S(1)}, u32[]{:S(2)}, u32[]{:S(2)}) collective-permute-start(f32[2,1,16,1024]{3,2,1,0:T(8,128)} %param.4), channel_id=1, source_target_pairs={{0,4},{4,8},{8,12},{12,16},{16,20},{20,24},{24,28},{28,32},{32,36}... | collective-permute-start | bytes 393224 | tf_op jit(solution)/shard_map/ppermute | solution.py:350
  6.1 4.5 %collective-permute-start.1 = (f32[2,1,16,1024]{3,2,1,0:T(8,128)}, f32[2,1,16,1024]{3,2,1,0:T(8,128)S(1)}, u32[]{:S(2)}, u32[]{:S(2)}) collective-permute-start(f32[2,1,16,1024]{3,2,1,0:T(8,128)} %param.5), channel_id=1, source_target_pairs={{0,1},{1,0},{2,3},{3,2},{4,5},{5,4},{6,7},{7,6},{8,9},{9,8},{10,11... | collective-permute-start | bytes 393224 | tf_op jit(solution)/shard_map/ppermute | solution.py:349
  10.6 1.3 %collective-permute-start.3 = (f32[5,8,128]{2,1,0:T(8,128)S(1)}, f32[5,8,128]{2,1,0:T(8,128)S(1)}, u32[]{:S(2)}, u32[]{:S(2)}) collective-permute-start(f32[5,8,128]{2,1,0:T(8,128)S(1)} %get-tuple-element.38), channel_id=1, source_target_pairs={{0,4},{4,0},{8,12},{12,8},{16,20},{20,16},{24,28},{28,24},{32,36},... | collective-permute-start | bytes 61448 | tf_op jit(solution)/shard_map/ppermute | solution.py:367
  11.9 9.4 %collective-permute-start.6 = (f32[5,8,128]{2,1,0:T(8,128)S(1)}, f32[5,8,128]{2,1,0:T(8,128)S(1)}, u32[]{:S(2)}, u32[]{:S(2)}) collective-permute-start(f32[5,8,128]{2,1,0:T(8,128)S(1)} %get-tuple-element.39.chip), channel_id=1, source_target_pairs={{24,0},{28,4},{0,8},{4,12},{8,16},{12,20},{16,24},{20,28},{56,32},... | collective-permute-start | bytes 61448 | tf_op jit(solution)/shard_map/ppermute | solution.py:370
  13.7 7.7 %collective-permute-start.5 = (f32[5,8,128]{2,1,0:T(8,128)S(1)}, f32[5,8,128]{2,1,0:T(8,128)S(1)}, u32[]{:S(2)}, u32[]{:S(2)}) collective-permute-start(f32[5,8,128]{2,1,0:T(8,128)S(1)} %get-tuple-element.39.chip), channel_id=1, source_target_pairs={{16,0},{20,4},{24,8},{28,12},{0,16},{4,20},{8,24},{12,28},{48,32},... | collective-permute-start | bytes 61448 | tf_op jit(solution)/shard_map/ppermute | solution.py:370
  16.3 5.1 %collective-permute-start.4 = (f32[5,8,128]{2,1,0:T(8,128)S(1)}, f32[5,8,128]{2,1,0:T(8,128)S(1)}, u32[]{:S(2)}, u32[]{:S(2)}) collective-permute-start(f32[5,8,128]{2,1,0:T(8,128)S(1)} %get-tuple-element.39.chip), channel_id=1, source_target_pairs={{8,0},{12,4},{16,8},{20,12},{24,16},{28,20},{0,24},{4,28},{40,32},... | collective-permute-start | bytes 61448 | tf_op jit(solution)/shard_map/ppermute | solution.py:370
  37.9 3.5 %collective-permute-start.7 = (f32[2,8,128]{2,1,0:T(8,128)S(1)}, f32[2,8,128]{2,1,0:T(8,128)S(1)}, u32[]{:S(2)}, u32[]{:S(2)}) collective-permute-start(f32[2,8,128]{2,1,0:T(8,128)S(1)} %get-tuple-element.45), channel_id=1, source_target_pairs={{0,4},{4,0},{8,12},{12,8},{16,20},{20,16},{24,28},{28,24},{32,36},... | collective-permute-start | bytes 24584 | tf_op jit(solution)/shard_map/ppermute | solution.py:385
  41.5 4.1 %collective-permute-start.8 = (f32[32,128]{1,0:T(8,128)S(1)}, f32[32,128]{1,0:T(8,128)S(1)}, u32[]{:S(2)}, u32[]{:S(2)}) collective-permute-start(f32[32,128]{1,0:T(8,128)S(1)} %get-tuple-element.52.message), channel_id=1, source_target_pairs={{0,2},{2,0},{1,3},{3,1},{4,6},{6,4},{5,7},{7,5},{8,10},{10,8},{9,1... | collective-permute-start | bytes 49160 | tf_op jit(solution)/shard_map/ppermute | solution.py:389

commit v3 on v2

--- a/solution.py
+++ b/solution.py
@@ -35,24 +35,77 @@
     return pltpu.roll(x, k, axis)
 
 
-def reduce_matrix(low, excess, rights, steps, axis, keep):
+def turn_lines(x, k):
+    lanes = lax.broadcasted_iota(jnp.int32, (1, 128), 1)
+
+    def blocks(pair, n):
+        if n == 4:
+            return pair[::-1]
+        turned = [pltpu.roll(p, 32 * n % 128, 1) for p in pair]
+        over = lanes < 32 * n if n > 0 else lanes >= 128 + 32 * n
+        return [jnp.where(over, turned[1 - h], turned[h]) for h in range(2)]
+
+    pair = [x[:128], x[128:]]
+    size = abs(k)
+    if size >= 128:
+        pair = blocks(pair, 4 if size == 512 else k // 128)
+    elif size >= 8:
+        if k > 0:
+            moved = blocks([p[128 - k :] for p in pair], 1)
+            pair = [jnp.concatenate([m, p[: 128 - k]], axis=0) for m, p in zip(moved, pair)]
+        else:
+            moved = blocks([p[:size] for p in pair], -1)
+            pair = [jnp.concatenate([p[size:], m], axis=0) for m, p in zip(moved, pair)]
+    else:
+        rows = lax.broadcasted_iota(jnp.int32, (8, 128), 0)
+        turned = [pltpu.roll(p, k % 128, 0) for p in pair]
+        if k > 0:
+            ends = [t[:8] for t in turned]
+            ends = [jnp.where(rows < k, m, e) for m, e in zip(blocks(ends, 1), ends)]
+            pair = [jnp.concatenate([e, t[8:]], axis=0) for e, t in zip(ends, turned)]
+        else:
+            ends = [t[120:] for t in turned]
+            ends = [jnp.where(rows >= 8 + k, m, e) for m, e in zip(blocks(ends, -1), ends)]
+            pair = [jnp.concatenate([t[:120], e], axis=0) for e, t in zip(ends, turned)]
+    return jnp.concatenate(pair, axis=0)
+
+
+def stand(x):
+    tiles = [x[:, 128 * j : 128 * (j + 1)] for j in range(8)]
+    return jnp.concatenate(
+        [jnp.concatenate(tiles[4 * h : 4 * h + 4], axis=0).T for h in range(2)], axis=0
+    )
+
+
+def lie(x):
+    tiles = [x[128 * h : 128 * (h + 1)].T for h in range(2)]
+    return jnp.concatenate(
+        [tiles[h][ALL * b : ALL * (b + 1)] for h in range(2) for b in range(4)], axis=1
+    )
+
+
+def turn_rows(x, k):
+    return turn(x, k, 0)
+
+
+def reduce_matrix(low, excess, rights, steps, move, keep):
     for index, k in enumerate(steps):
-        high = turn(low, -k, axis)
+        high = move(low, -k)
         inverse = 1.0 / (low + high + excess)
-        a = low * turn(inverse, k, axis)
-        b = high * turn(inverse, -k, axis)
-        keep(index, a, b)
-        excess = excess + a * turn(excess, k, axis) + b * turn(excess, -k, axis)
-        rights = [r + a * turn(r, k, axis) + b * turn(r, -k, axis) for r in rights]
-        low = a * turn(low, k, axis)
+        up = high * inverse
+        down = low * inverse
+        keep(index, up, down)
+        excess = excess + move(up * excess, k) + move(down * excess, -k)
+        rights = [r + move(up * r, k) + move(down * r, -k) for r in rights]
+        low = move(up * low, k)
     inverse = 1.0 / excess
     return inverse, [r * inverse for r in rights]
 
 
-def reduce_right(right, steps, axis, load):
+def reduce_right(right, steps, move, load):
     for index, k in enumerate(steps):
-        a, b = load(index)
-        right = right + a * turn(right, k, axis) + b * turn(right, -k, axis)
+        up, down = load(index)
+        right = right + move(up * right, k) + move(down * right, -k)
     return right
 
 
@@ -66,14 +119,19 @@
     )
 
 
-def factor_x_kernel(
-    fields_arg, vertical_arg, kappa_arg, fields, vertical, kappa, ax, bx, qx, h1, h2, parts, done
-):
+def input_kernel(fields_arg, vertical_arg, kappa_arg, fields, vertical, kappa, rim, done):
     pairs = ((kappa_arg, kappa), (fields_arg, fields), (vertical_arg, vertical))
     copies = [pltpu.make_async_copy(a, b, done.at[n]) for n, (a, b) in enumerate(pairs)]
     for copy in copies:
         copy.start()
     copies[0].wait()
+    for f in range(2):
+        rim[f] = dense(kappa[f * ROWS + ROWS - 1 : f * ROWS + ROWS, :])
+    copies[1].wait()
+    copies[2].wait()
+
+
+def factor_x_kernel(kappa, ax, bx, qx, h1, h2, parts):
     half = 512
     rows = lax.broadcasted_iota(jnp.int32, (ROWS, half), 0)
     for f in range(2):
@@ -91,7 +149,7 @@
                 bx[index, mine, cols] = b
 
             inverse, (one, two) = reduce_matrix(
-                low, 1.0 + first + last, [first, last], X_STEPS, 0, keep
+                low, 1.0 + first + last, [first, last], X_STEPS, turn_rows, keep
             )
             qx[mine, cols] = jnp.where((rows >= 1) & (rows <= 14), inverse, 0.0)
             one = jnp.where(rows == 0, 1.0, one)
@@ -107,42 +165,42 @@
             ):
                 for i in range(half // 128):
                     parts[n, f, pl.ds(c * (half // 128) + i, 1), :] = row[:, 128 * i : 128 * (i + 1)]
-    copies[1].wait()
-    copies[2].wait()
-
-
-def factor_y_kernel(kappa, after, ay, by, qy, hy, edge):
+
+
+def factor_y_kernel(kappa, ay, by, qy, hy, edge):
+    gy = lax.axis_index("gy")
+    low_side = gy == 0
+    end = jnp.where(low_side, COLS - 1, 0)
+    start = COLS - 1 - end
+    beside = jnp.where(low_side, COLS - 2, 1)
+    cut = jnp.where(low_side, COLS - 1, 1)
+    k = stand(kappa[...])
+    row = lax.broadcasted_iota(jnp.int32, (256, 128), 0)
+    lane = lax.broadcasted_iota(jnp.int32, (256, 128), 1)
+    y = row // 128 * 512 + lane // 32 * 128 + row % 128
+    face = (k + turn_lines(k, 1)) * 0.5
+    low = jnp.where((y == 0) | (y == cut), 0.0, face)
+    link = jnp.where(y == beside, jnp.where(low_side, turn_lines(face, -1), face), 0.0)
+    ground = jnp.where(y == start, 1.0 + 0.5 * k, 1.0)
+
+    def keep(index, up, down):
+        ay[index] = up
+        by[index] = down
+
+    inverse, (profile,) = reduce_matrix(low, ground + link, [link], Y_STEPS, turn_lines, keep)
+    qy[...] = jnp.where(y == end, 0.0, inverse)
+    profile = lie(jnp.where(y == end, 1.0, profile))
+    hy[...] = profile
+    k = kappa[...]
+    column = lax.broadcasted_iota(jnp.int32, (ALL, COLS), 1)
+    total = jnp.sum(profile * jnp.where(column == start, 1.0 + 0.5 * k, 1.0), axis=1, keepdims=True)
+    rim = jnp.sum(jnp.where(column == end, k, 0.0), axis=1, keepdims=True)
+    wide = lax.broadcasted_iota(jnp.int32, (ALL, 128), 1)
+    edge[...] = jnp.where(wide == 0, total, jnp.where(wide == 1, rim, 0.0))
+
+
+def source_kernel(fields, fields_far, vertical, vertical_far, kappa, halo, h1, h2, parts, after, source, sums, keep, send):
     del after
-    gy = lax.axis_index("gy")
-    lanes = lax.broadcasted_iota(jnp.int32, (8, COLS), 1)
-    wide = lax.broadcasted_iota(jnp.int32, (8, 128), 1)
-    low_side = gy == 0
-    terminal = lanes == jnp.where(low_side, COLS - 1, 0)
-    cut = lanes == jnp.where(low_side, COLS - 1, 1)
-    outer = lanes == jnp.where(low_side, 0, COLS - 1)
-    beside = lanes == jnp.where(low_side, COLS - 2, 1)
-    for g in range(ALL // 8):
-        mine = pl.ds(g * 8, 8)
-        k = kappa[mine, :]
-        face = (k + turn(k, 1, 1)) * 0.5
-        low = jnp.where((lanes == 0) | cut, 0.0, face)
-        link = jnp.where(beside, jnp.where(low_side, turn(face, -1, 1), face), 0.0)
-        ground = jnp.where(outer, 1.0 + 0.5 * k, 1.0)
-
-        def keep(index, a, b, mine=mine):
-            ay[index, mine, :] = a
-            by[index, mine, :] = b
-
-        inverse, (profile,) = reduce_matrix(low, ground + link, [link], Y_STEPS, 1, keep)
-        qy[mine, :] = jnp.where(terminal, 0.0, inverse)
-        profile = jnp.where(terminal, 1.0, profile)
-        hy[mine, :] = profile
-        total = jnp.sum(profile * ground, axis=1, keepdims=True)
-        rim = jnp.sum(jnp.where(terminal, k, 0.0), axis=1, keepdims=True)
-        edge[mine, :] = jnp.where(wide == 0, total, jnp.where(wide == 1, rim, 0.0))
-
-
-def source_kernel(fields, fields_far, vertical, vertical_far, kappa, halo, h1, h2, parts, source, sums, keep, send):
     gx = lax.axis_index("gx")
     even = gx % 2 == 0
     elements = []
@@ -154,7 +212,7 @@
         mine = slice(f * ROWS, (f + 1) * ROWS)
         first = dense(jnp.sum(h1[mine, :] * s[mine, :], axis=0, keepdims=True))
         last = dense(jnp.sum(h2[mine, :] * s[mine, :], axis=0, keepdims=True))
-        west = (dense(kappa[f * ROWS : f * ROWS + 1, :]) + dense(halo[f * ROWS + ROWS - 1 : f * ROWS + ROWS, :])) * 0.5
+        west = (dense(kappa[f * ROWS : f * ROWS + 1, :]) + halo[f]) * 0.5
         east = dense(kappa[f * ROWS + ROWS - 1 : f * ROWS + ROWS, :]) * 0.5
         g, s_first, s_last = parts[0, f], parts[1, f], parts[2, f]
         inverse = 1.0 / (west + g + s_first)
@@ -183,7 +241,7 @@
         for c in range(COLS // half):
             cols = pl.ds(c * half, half)
             r = source[mine, cols]
-            r = reduce_right(r, X_STEPS, 0, lambda i: (ax[i, mine, cols], bx[i, mine, cols]))
+            r = reduce_right(r, X_STEPS, turn_rows, lambda i: (ax[i, mine, cols], bx[i, mine, cols]))
             out[mine, cols] = r * qx[mine, cols]
 
 
@@ -214,8 +272,7 @@
         middle[n] = value
 
 
-def slab_kernel(chip, far1, far2, far3, middle, after, message, nodes):
-    del after
+def slab_kernel(chip, far1, far2, far3, middle, message, nodes):
     y = lax.axis_index("gx") // 2 % 4
     arrived = [load(chip), load(far1), load(far2), load(far3)]
     chips = []
@@ -307,11 +364,9 @@
 
 
 def local_y_kernel(section, ay, by, qy, out):
-    for g in range(ALL // 8):
-        mine = pl.ds(g * 8, 8)
-        r = section[mine, :]
-        r = reduce_right(r, Y_STEPS, 1, lambda i: (ay[i, mine, :], by[i, mine, :]))
-        out[mine, :] = r * qy[mine, :]
+    r = stand(section[...])
+    r = reduce_right(r, Y_STEPS, turn_lines, lambda i: (ay[i], by[i]))
+    out[...] = lie(r * qy[...])
 
 
 def output_kernel(message, far, local, hy, out):
@@ -347,37 +402,45 @@
     swap = [(0, 1), (1, 0)]
     fields_far = lax.ppermute(fields, "gz", swap)
     vertical_far = lax.ppermute(vertical, "gz", swap)
-    halo = lax.ppermute(kappa, "gx", [(i, i + 1) for i in range(63)])
     full = shape(*grid)
     half = shape(5, 8, 128)
-    fields_here, vertical_here, kappa_here, ax, bx, qx, h1, h2, parts = call(
+    standing = shape(256, 128)
+    fields_here, vertical_here, kappa_here, rim = call(
+        input_kernel,
+        (full, full, full, shape(2, 8, 128)),
+        [HBM] * 3,
+        flops=1_000_000,
+        size=1_000_000,
+        scratch=[pltpu.SemaphoreType.DMA((3,))],
+    )(*(pltpu.with_memory_space_constraint(x.reshape(grid), pltpu.HBM) for x in (fields, vertical, kappa)))
+    halo = lax.ppermute(rim, "gx", [(i, i + 1) for i in range(63)])
+    ax, bx, qx, h1, h2, parts = call(
         factor_x_kernel,
-        (full, full, full, shape(4, *grid), shape(4, *grid), full, full, full, shape(3, 2, 8, 128)),
-        [HBM] * 3,
+        (shape(4, *grid), shape(4, *grid), full, full, full, shape(3, 2, 8, 128)),
+        [VMEM],
         flops=4_000_000,
         size=2_000_000,
-        scratch=[pltpu.SemaphoreType.DMA((3,))],
-    )(*(pltpu.with_memory_space_constraint(x.reshape(grid), pltpu.HBM) for x in (fields, vertical, kappa)))
+    )(kappa_here)
+    ay, by, qy, hy, edge = call(
+        factor_y_kernel,
+        (shape(10, 256, 128), shape(10, 256, 128), standing, full, shape(ALL, 128)),
+        [VMEM],
+        flops=20_000_000,
+        size=4_000_000,
+    )(kappa_here)
     source, sums, keep, send = call(
-        source_kernel, (full, shape(3, 2, 8, 128), half, half), [VMEM] * 9
+        source_kernel, (full, shape(3, 2, 8, 128), half, half), [VMEM] * 10
     )(
         fields_here, fields_far.reshape(grid), vertical_here, vertical_far.reshape(grid),
-        kappa_here, halo.reshape(grid), h1, h2, parts,
+        kappa_here, halo, h1, h2, parts, edge,
     )
     got = lax.ppermute(send, "gx", CORES)
     local_x = call(local_x_kernel, full, [VMEM] * 4, flops=1_000_000, size=1_000_000)(source, ax, bx, qx)
     chip, middle = call(chip_kernel, (half, shape(3, 8, 128)), [VMEM] * 2)(keep, got)
     far = [lax.ppermute(chip, "gx", chips_on(shift)) for shift in (2, 1, 3)]
-    ay, by, qy, hy, edge = call(
-        factor_y_kernel,
-        (shape(10, *grid), shape(10, *grid), full, full, shape(ALL, 128)),
-        [VMEM] * 2,
-        flops=20_000_000,
-        size=4_000_000,
-    )(kappa_here, middle)
     message, nodes = call(
-        slab_kernel, (shape(8, 5, 8, 128), shape(3, 3, 8, 128)), [VMEM] * 6
-    )(chip, far[1], far[0], far[2], middle, edge)
+        slab_kernel, (shape(8, 5, 8, 128), shape(3, 3, 8, 128)), [VMEM] * 5
+    )(chip, far[1], far[0], far[2], middle)
     got = lax.all_to_all(message, "gx", 0, 0, axis_index_groups=SLAB_GROUPS, tiled=True)
     mine, other = call(
         ends_kernel, (shape(2, 8, 128), shape(2, 8, 128)), [VMEM, VMEM]

time: 46.6 us -> 44.7 us (0.959)
  Pallas kernels: 7.91 us -> 6.19 us
  waiting for transfers between devices: 5.15 us -> 4.27 us
    ppermute x1, waiting for transfers between devices: 2.21 us -> 0.01 us  [local(): vertical_far = lax.ppermute(vertical, 'gz', swap)]
    ppermute x3, waiting for transfers between devices: 0.01 us -> 1.94 us  [local(): far = [lax.ppermute(chip, 'gx', chips_on(shift)) for shift in (2, 1, 3)]]
    pallas_call x4 -> x5, Pallas kernels: 5.79 us -> 4.04 us  [the longest x1 2.14 us: local(): call(factor_y_kernel, (shape(10, 256, 128), shape(10, 256, 128), standing...]
    ppermute x3, starting transfers between devices: 5.43 us -> 4.77 us  [local(): far = [lax.ppermute(chip, 'gx', chips_on(shift)) for shift in (2, 1, 3)]]
    ppermute x1, starting transfers between devices: 4.03 us -> 4.55 us  [local(): halo = lax.ppermute(rim, 'gx', [(i, i + 1) for i in range(63)])]
  transfers between devices with their start and end apart: 9 -> 9, of which waited for: 5 -> 5; matrix products, arithmetic and copies ran while one was open for 0% -> 0% of each run, Pallas kernels for 14% -> 11%
where the time goes in v3:
time: 44.7 us; the launch traced here: 44.3 us
  starting transfers between devices  17.2 us (38%)
  blocking collectives  16.6 us (37%)
  Pallas kernels  6.19 us (14%)
  waiting for transfers between devices  4.27 us (10%)
    all_to_all x1, blocking collectives, local(): lax.all_to_all(message, 'gx', 0, 0, axis_index_groups=SLAB_GROUPS, tiled=...  16.6 us
    ppermute x3, starting transfers between devices, local(): far = [lax.ppermute(chip, 'gx', chips_on(shift)) for shift in (2, 1, 3)]  4.77 us
    ppermute x1, starting transfers between devices, local(): halo = lax.ppermute(rim, 'gx', [(i, i + 1) for i in range(63)])  4.55 us
    ppermute x1, starting transfers between devices, local(): other = lax.ppermute(other, 'gx', CORES)  2.95 us
    ppermute x1, starting transfers between devices, local(): far = lax.ppermute(message, 'gy', swap)  2.76 us
    pallas_call x1, Pallas kernels, local(): call(factor_y_kernel, (shape(10, 256, 128), shape(10, 256, 128), standing...  2.14 us
    ppermute x1, starting transfers between devices, local(): fields_far = lax.ppermute(fields, 'gz', swap)  2.04 us
    ppermute x3, waiting for transfers between devices, local(): far = [lax.ppermute(chip, 'gx', chips_on(shift)) for shift in (2, 1, 3)]  1.94 us
  transfers between devices with their start and end apart: 9, of which 5 were waited for; matrix products, arithmetic and copies ran while one was open for 0% of the time, Pallas kernels for 11%

profile of v3, /device:TPU:1, one launch (start us, length us, event | category | flops | bytes accessed | tf_op | source)
XLA Modules:
  0.0 44.3 jit_solution(7067050657196383677)
XLA Ops:
  0.0 2.0 %collective-permute-start = (f32[2,1,16,1024]{3,2,1,0:T(8,128)}, f32[2,1,16,1024]{3,2,1,0:T(8,128)S(1)}, u32[]{:S(2)}, u32[]{:S(2)}) collective-permute-start(f32[2,1,16,1024]{3,2,1,0:T(8,128)} %param.3), channel_id=1, source_target_pairs={{0,1},{1,0},{2,3},{3,2},{4,5},{5,4},{6,7},{7,6},{8,9},{9,8},{10,11... | collective-permute-start | bytes 393224 | tf_op jit(solution)/shard_map/ppermute | solution.py:403
  2.0 0.0 collective-permute-start.1
  2.1 1.1 %shard_map.37 = (f32[32,1024]{1,0:T(8,128)S(1)}, f32[32,1024]{1,0:T(8,128)S(1)}, f32[32,1024]{1,0:T(8,128)S(1)}, f32[2,8,128]{2,1,0:T(8,128)S(1)}) custom-call(f32[32,1024]{1,0:T(8,128)} %bitcast.11, f32[32,1024]{1,0:T(8,128)} %bitcast.12, f32[32,1024]{1,0:T(8,128)} %bitcast.10), custom_call_target="tpu_custom_call" | custom-call | flops 1000000 | bytes 1000000 | tf_op jit(solution)/shard_map/pallas_call | solution.py:408
  3.1 4.5 %collective-permute-start.2 = (f32[2,8,128]{2,1,0:T(8,128)S(1)}, f32[2,8,128]{2,1,0:T(8,128)S(1)}, u32[]{:S(2)}, u32[]{:S(2)}) collective-permute-start(f32[2,8,128]{2,1,0:T(8,128)S(1)} %get-tuple-element.35), channel_id=1, source_target_pairs={{0,4},{4,8},{8,12},{12,16},{16,20},{20,24},{24,28},{28,32},{32,36}... | collective-permute-start | bytes 24584 | tf_op jit(solution)/shard_map/ppermute | solution.py:416
  7.7 0.7 %shard_map.38 = (f32[4,32,1024]{2,1,0:T(8,128)S(1)}, f32[4,32,1024]{2,1,0:T(8,128)S(1)}, f32[32,1024]{1,0:T(8,128)S(1)}, f32[32,1024]{1,0:T(8,128)S(1)}, f32[32,...) custom-call(f32[32,1024]{1,0:T(8,128)S(1)} %get-tuple-element.34.kappa), custom_call_target="tpu_custom_call" | custom-call | flops 4000000 | bytes 2000000 | tf_op jit(solution)/shard_map/pallas_call | solution.py:417
  8.4 2.1 %shard_map.39 = (f32[10,256,128]{2,1,0:T(8,128)S(1)}, f32[10,256,128]{2,1,0:T(8,128)S(1)}, f32[256,128]{1,0:T(8,128)S(1)}, f32[32,1024]{1,0:T(8,128)S(1)}, f32[32,128]{1,0:T(8,128)S(1)}) custom-call(f32[32,1024]{1,0:T(8,128)S(1)} %get-tuple-element.34.kappa), custom_call_target="tpu_custom_call" | custom-call | flops 20000000 | bytes 4000000 | tf_op jit(solution)/shard_map/pallas_call | solution.py:424
  10.5 0.0 collective-permute-done.2.halo
  10.5 0.0 collective-permute-done
  10.5 0.0 collective-permute-done.1
  10.6 0.1 shard_map.40
  10.7 0.1 collective-permute-start.3
  10.8 1.2 %collective-permute-done.3.got = f32[5,8,128]{2,1,0:T(8,128)S(1)} collective-permute-done((f32[5,8,128]{2,1,0:T(8,128)S(1)}, f32[5,8,128]{2,1,0:T(8,128)S(1)}, u32[]{:S(2)}, u32[]{:S(2)}) %collective-permute-start.3) | collective-permute-done | bytes 20512 | tf_op jit(solution)/shard_map/ppermute | solution.py:437
  12.0 1.4 %collective-permute-start.6 = (f32[5,8,128]{2,1,0:T(8,128)S(1)}, f32[5,8,128]{2,1,0:T(8,128)S(1)}, u32[]{:S(2)}, u32[]{:S(2)}) collective-permute-start(f32[5,8,128]{2,1,0:T(8,128)S(1)} %get-tuple-element.42.chip), channel_id=1, source_target_pairs={{24,0},{28,4},{0,8},{4,12},{8,16},{12,20},{16,24},{20,28},{56,32},... | collective-permute-start | bytes 61448 | tf_op jit(solution)/shard_map/ppermute | solution.py:440
  13.3 2.6 %collective-permute-start.5 = (f32[5,8,128]{2,1,0:T(8,128)S(1)}, f32[5,8,128]{2,1,0:T(8,128)S(1)}, u32[]{:S(2)}, u32[]{:S(2)}) collective-permute-start(f32[5,8,128]{2,1,0:T(8,128)S(1)} %get-tuple-element.42.chip), channel_id=1, source_target_pairs={{16,0},{20,4},{24,8},{28,12},{0,16},{4,20},{8,24},{12,28},{48,32},... | collective-permute-start | bytes 61448 | tf_op jit(solution)/shard_map/ppermute | solution.py:440
  15.9 0.8 %collective-permute-start.4 = (f32[5,8,128]{2,1,0:T(8,128)S(1)}, f32[5,8,128]{2,1,0:T(8,128)S(1)}, u32[]{:S(2)}, u32[]{:S(2)}) collective-permute-start(f32[5,8,128]{2,1,0:T(8,128)S(1)} %get-tuple-element.42.chip), channel_id=1, source_target_pairs={{8,0},{12,4},{16,8},{20,12},{24,16},{28,20},{0,24},{4,28},{40,32},... | collective-permute-start | bytes 61448 | tf_op jit(solution)/shard_map/ppermute | solution.py:440
  16.7 0.0 collective-permute-done.6.far3
  16.7 0.7 %collective-permute-done.5.far2 = f32[5,8,128]{2,1,0:T(8,128)S(1)} collective-permute-done((f32[5,8,128]{2,1,0:T(8,128)S(1)}, f32[5,8,128]{2,1,0:T(8,128)S(1)}, u32[]{:S(2)}, u32[]{:S(2)}) %collective-permute-start.5) | collective-permute-done | bytes 20512 | tf_op jit(solution)/shard_map/ppermute | solution.py:440
  17.5 1.2 %collective-permute-done.4.far1 = f32[5,8,128]{2,1,0:T(8,128)S(1)} collective-permute-done((f32[5,8,128]{2,1,0:T(8,128)S(1)}, f32[5,8,128]{2,1,0:T(8,128)S(1)}, u32[]{:S(2)}, u32[]{:S(2)}) %collective-permute-start.4) | collective-permute-done | bytes 20512 | tf_op jit(solution)/shard_map/ppermute | solution.py:440
  18.7 0.1 shard_map.42
  18.7 16.6 %all_to_all.5.got = f32[8,5,8,128]{3,2,1,0:T(8,128)S(1)} all-to-all(f32[8,5,8,128]{3,2,1,0:T(8,128)S(1)} %get-tuple-element.44), channel_id=1, replica_groups={{0,32,64,96,128,160,192,224},{4,36,68,100,132,164,196,228},{8,40,72,104..., dimensions={0} | all-to-all | bytes 327680 | tf_op jit(solution)/shard_map/all_to_all | solution.py:444
  35.3 0.1 shard_map.43
  35.4 3.0 %collective-permute-start.7 = (f32[2,8,128]{2,1,0:T(8,128)S(1)}, f32[2,8,128]{2,1,0:T(8,128)S(1)}, u32[]{:S(2)}, u32[]{:S(2)}) collective-permute-start(f32[2,8,128]{2,1,0:T(8,128)S(1)} %get-tuple-element.47), channel_id=1, source_target_pairs={{0,4},{4,0},{8,12},{12,8},{16,20},{20,16},{24,28},{28,24},{32,36},... | collective-permute-start | bytes 24584 | tf_op jit(solution)/shard_map/ppermute | solution.py:448
  38.4 0.1 shard_map.44.local
  38.5 0.7 %collective-permute-done.7.other = f32[2,8,128]{2,1,0:T(8,128)S(1)} collective-permute-done((f32[2,8,128]{2,1,0:T(8,128)S(1)}, f32[2,8,128]{2,1,0:T(8,128)S(1)}, u32[]{:S(2)}, u32[]{:S(2)}) %collective-permute-start.7) | collective-permute-done | bytes 8224 | tf_op jit(solution)/shard_map/ppermute | solution.py:448
  39.2 0.1 shard_map.45
  39.3 2.8 %collective-permute-start.8 = (f32[32,128]{1,0:T(8,128)S(1)}, f32[32,128]{1,0:T(8,128)S(1)}, u32[]{:S(2)}, u32[]{:S(2)}) collective-permute-start(f32[32,128]{1,0:T(8,128)S(1)} %get-tuple-element.54.message), channel_id=1, source_target_pairs={{0,2},{2,0},{1,3},{3,1},{4,6},{6,4},{5,7},{7,5},{8,10},{10,8},{9,1... | collective-permute-start | bytes 49160 | tf_op jit(solution)/shard_map/ppermute | solution.py:452
  42.1 0.9 %shard_map.46.local = f32[32,1024]{1,0:T(8,128)S(1)} custom-call(f32[32,1024]{1,0:T(8,128)S(1)} %get-tuple-element.55.section, f32[10,256,128]{2,1,0:T(8,128)S(1)} %get-tuple-element.56.ay, f32[10,256,128]{2,1,0:T(8,128)S(1)} %get-tuple-element.57.by, f32[256,128]{1,0:T(8,128)S(1)} %get-tuple-element.58.qy), custom_call_target="tpu_custom_call" | custom-call | flops 4000000 | bytes 3000000 | tf_op jit(solution)/shard_map/pallas_call | solution.py:453
  43.0 0.5 %collective-permute-done.8.far = f32[32,128]{1,0:T(8,128)S(1)} collective-permute-done((f32[32,128]{1,0:T(8,128)S(1)}, f32[32,128]{1,0:T(8,128)S(1)}, u32[]{:S(2)}, u32[]{:S(2)}) %collective-permute-start.8) | collective-permute-done | bytes 16416 | tf_op jit(solution)/shard_map/ppermute | solution.py:452
  43.5 0.9 %shard_map.47 = f32[32,1024]{1,0:T(8,128)} custom-call(f32[32,128]{1,0:T(8,128)S(1)} %get-tuple-element.54.message, f32[32,128]{1,0:T(8,128)S(1)} %collective-permute-done.8.far, f32[32,1024]{1,0:T(8,128)S(1)} %shard_map.46.local, f32[32,1024]{1,0:T(8,128)S(1)} %get-tuple-element.53.hy), custom_call_target="tpu_custom_call" | custom-call | tf_op jit(solution)/shard_map/pallas_call | solution.py:454
  (1 shorter events, 0.0 us)
Async XLA Ops:
  0.0 10.5 %collective-permute-start = (f32[2,1,16,1024]{3,2,1,0:T(8,128)}, f32[2,1,16,1024]{3,2,1,0:T(8,128)S(1)}, u32[]{:S(2)}, u32[]{:S(2)}) collective-permute-start(f32[2,1,16,1024]{3,2,1,0:T(8,128)} %param.3), channel_id=1, source_target_pairs={{0,1},{1,0},{2,3},{3,2},{4,5},{5,4},{6,7},{7,6},{8,9},{9,8},{10,11... | collective-permute-start | bytes 393224 | tf_op jit(solution)/shard_map/ppermute | solution.py:403
  2.0 8.5 %collective-permute-start.1 = (f32[2,1,16,1024]{3,2,1,0:T(8,128)}, f32[2,1,16,1024]{3,2,1,0:T(8,128)S(1)}, u32[]{:S(2)}, u32[]{:S(2)}) collective-permute-start(f32[2,1,16,1024]{3,2,1,0:T(8,128)} %param.5), channel_id=1, source_target_pairs={{0,1},{1,0},{2,3},{3,2},{4,5},{5,4},{6,7},{7,6},{8,9},{9,8},{10,11... | collective-permute-start | bytes 393224 | tf_op jit(solution)/shard_map/ppermute | solution.py:404
  3.1 7.4 %collective-permute-start.2 = (f32[2,8,128]{2,1,0:T(8,128)S(1)}, f32[2,8,128]{2,1,0:T(8,128)S(1)}, u32[]{:S(2)}, u32[]{:S(2)}) collective-permute-start(f32[2,8,128]{2,1,0:T(8,128)S(1)} %get-tuple-element.35), channel_id=1, source_target_pairs={{0,4},{4,8},{8,12},{12,16},{16,20},{20,24},{24,28},{28,32},{32,36}... | collective-permute-start | bytes 24584 | tf_op jit(solution)/shard_map/ppermute | solution.py:416
  10.7 1.3 %collective-permute-start.3 = (f32[5,8,128]{2,1,0:T(8,128)S(1)}, f32[5,8,128]{2,1,0:T(8,128)S(1)}, u32[]{:S(2)}, u32[]{:S(2)}) collective-permute-start(f32[5,8,128]{2,1,0:T(8,128)S(1)} %get-tuple-element.41), channel_id=1, source_target_pairs={{0,4},{4,0},{8,12},{12,8},{16,20},{20,16},{24,28},{28,24},{32,36},... | collective-permute-start | bytes 61448 | tf_op jit(solution)/shard_map/ppermute | solution.py:437
  12.0 4.8 %collective-permute-start.6 = (f32[5,8,128]{2,1,0:T(8,128)S(1)}, f32[5,8,128]{2,1,0:T(8,128)S(1)}, u32[]{:S(2)}, u32[]{:S(2)}) collective-permute-start(f32[5,8,128]{2,1,0:T(8,128)S(1)} %get-tuple-element.42.chip), channel_id=1, source_target_pairs={{24,0},{28,4},{0,8},{4,12},{8,16},{12,20},{16,24},{20,28},{56,32},... | collective-permute-start | bytes 61448 | tf_op jit(solution)/shard_map/ppermute | solution.py:440
  13.3 4.1 %collective-permute-start.5 = (f32[5,8,128]{2,1,0:T(8,128)S(1)}, f32[5,8,128]{2,1,0:T(8,128)S(1)}, u32[]{:S(2)}, u32[]{:S(2)}) collective-permute-start(f32[5,8,128]{2,1,0:T(8,128)S(1)} %get-tuple-element.42.chip), channel_id=1, source_target_pairs={{16,0},{20,4},{24,8},{28,12},{0,16},{4,20},{8,24},{12,28},{48,32},... | collective-permute-start | bytes 61448 | tf_op jit(solution)/shard_map/ppermute | solution.py:440
  15.9 2.7 %collective-permute-start.4 = (f32[5,8,128]{2,1,0:T(8,128)S(1)}, f32[5,8,128]{2,1,0:T(8,128)S(1)}, u32[]{:S(2)}, u32[]{:S(2)}) collective-permute-start(f32[5,8,128]{2,1,0:T(8,128)S(1)} %get-tuple-element.42.chip), channel_id=1, source_target_pairs={{8,0},{12,4},{16,8},{20,12},{24,16},{28,20},{0,24},{4,28},{40,32},... | collective-permute-start | bytes 61448 | tf_op jit(solution)/shard_map/ppermute | solution.py:440
  35.4 3.8 %collective-permute-start.7 = (f32[2,8,128]{2,1,0:T(8,128)S(1)}, f32[2,8,128]{2,1,0:T(8,128)S(1)}, u32[]{:S(2)}, u32[]{:S(2)}) collective-permute-start(f32[2,8,128]{2,1,0:T(8,128)S(1)} %get-tuple-element.47), channel_id=1, source_target_pairs={{0,4},{4,0},{8,12},{12,8},{16,20},{20,16},{24,28},{28,24},{32,36},... | collective-permute-start | bytes 24584 | tf_op jit(solution)/shard_map/ppermute | solution.py:448
  39.3 4.1 %collective-permute-start.8 = (f32[32,128]{1,0:T(8,128)S(1)}, f32[32,128]{1,0:T(8,128)S(1)}, u32[]{:S(2)}, u32[]{:S(2)}) collective-permute-start(f32[32,128]{1,0:T(8,128)S(1)} %get-tuple-element.54.message), channel_id=1, source_target_pairs={{0,2},{2,0},{1,3},{3,1},{4,6},{6,4},{5,7},{7,5},{8,10},{10,8},{9,1... | collective-permute-start | bytes 49160 | tf_op jit(solution)/shard_map/ppermute | solution.py:452

commit v4 on v3

--- a/solution.py
+++ b/solution.py
@@ -119,19 +119,14 @@
     )
 
 
-def input_kernel(fields_arg, vertical_arg, kappa_arg, fields, vertical, kappa, rim, done):
+def factor_x_kernel(
+    fields_arg, vertical_arg, kappa_arg, fields, vertical, kappa, ax, bx, qx, h1, h2, parts, done
+):
     pairs = ((kappa_arg, kappa), (fields_arg, fields), (vertical_arg, vertical))
     copies = [pltpu.make_async_copy(a, b, done.at[n]) for n, (a, b) in enumerate(pairs)]
     for copy in copies:
         copy.start()
     copies[0].wait()
-    for f in range(2):
-        rim[f] = dense(kappa[f * ROWS + ROWS - 1 : f * ROWS + ROWS, :])
-    copies[1].wait()
-    copies[2].wait()
-
-
-def factor_x_kernel(kappa, ax, bx, qx, h1, h2, parts):
     half = 512
     rows = lax.broadcasted_iota(jnp.int32, (ROWS, half), 0)
     for f in range(2):
@@ -156,15 +151,18 @@
             two = jnp.where(rows == ROWS - 1, 1.0, two)
             h1[mine, cols] = one
             h2[mine, cols] = two
-            for n, row in enumerate(
-                (
-                    jnp.sum(first * two, axis=0, keepdims=True),
-                    jnp.sum(one, axis=0, keepdims=True),
-                    jnp.sum(two, axis=0, keepdims=True),
-                )
-            ):
+            sums = (
+                jnp.sum(first * two, axis=0, keepdims=True),
+                jnp.sum(one, axis=0, keepdims=True),
+                jnp.sum(two, axis=0, keepdims=True),
+                k[:1],
+                k[ROWS - 1 :],
+            )
+            for n, row in enumerate(sums):
                 for i in range(half // 128):
                     parts[n, f, pl.ds(c * (half // 128) + i, 1), :] = row[:, 128 * i : 128 * (i + 1)]
+    copies[1].wait()
+    copies[2].wait()
 
 
 def factor_y_kernel(kappa, ay, by, qy, hy, edge):
@@ -199,36 +197,19 @@
     edge[...] = jnp.where(wide == 0, total, jnp.where(wide == 1, rim, 0.0))
 
 
-def source_kernel(fields, fields_far, vertical, vertical_far, kappa, halo, h1, h2, parts, after, source, sums, keep, send):
+def source_kernel(fields, fields_far, vertical, vertical_far, h1, h2, parts, after, source, keep, send):
     del after
-    gx = lax.axis_index("gx")
-    even = gx % 2 == 0
-    elements = []
+    even = lax.axis_index("gx") % 2 == 0
     here = fields[...]
     v = vertical[...]
     s = here + (v + vertical_far[...]) * 0.5 * (fields_far[...] - here) - v * 0.5 * here
     source[...] = s
+    elements = []
     for f in range(2):
         mine = slice(f * ROWS, (f + 1) * ROWS)
         first = dense(jnp.sum(h1[mine, :] * s[mine, :], axis=0, keepdims=True))
         last = dense(jnp.sum(h2[mine, :] * s[mine, :], axis=0, keepdims=True))
-        west = (dense(kappa[f * ROWS : f * ROWS + 1, :]) + halo[f]) * 0.5
-        east = dense(kappa[f * ROWS + ROWS - 1 : f * ROWS + ROWS, :]) * 0.5
-        g, s_first, s_last = parts[0, f], parts[1, f], parts[2, f]
-        inverse = 1.0 / (west + g + s_first)
-        a = west * inverse
-        b = g * inverse
-        sums[0, f] = a
-        sums[1, f] = b
-        sums[2, f] = first * inverse
-        element = (
-            a * g,
-            a * s_first,
-            jnp.where(gx == 63, s_last + east, s_last) + b * s_first,
-            a * first,
-            last + b * first,
-        )
-        elements.append(element)
+        elements.append((parts[0, f], parts[1, f], parts[2, f], first, last, parts[3, f], parts[4, f]))
     for n, (one, two) in enumerate(zip(*elements)):
         keep[n] = jnp.where(even, one, two)
         send[n] = jnp.where(even, two, one)
@@ -256,8 +237,21 @@
     return (a * g2, sl + a * s, sr2 + b * s, rl + a * r, rr2 + b * r), (a, b, r * inverse)
 
 
+def behind(face, two):
+    g, s, sr, r, rr = two
+    inverse = 1.0 / (face + g + s)
+    a = face * inverse
+    b = g * inverse
+    return (a * g, a * s, sr + b * s, a * r, rr + b * r), (a, b, r * inverse)
+
+
 def load(ref):
-    return tuple(ref[n] for n in range(5))
+    return tuple(ref[n] for n in range(7))
+
+
+def within(node, left, right):
+    a, b, c = node
+    return (a * left[0] + b * right[0], a * left[1] + b * right[1], a * left[2] + b * right[2] + c)
 
 
 def chip_kernel(keep, got, chip, middle):
@@ -265,10 +259,11 @@
     mine, other = load(keep), load(got)
     first = [jnp.where(even, m, o) for m, o in zip(mine, other)]
     second = [jnp.where(even, o, m) for m, o in zip(mine, other)]
-    element, node = merge(first, second)
-    for n, value in enumerate(element):
+    tail, start = behind((first[6] + second[5]) * 0.5, second[:5])
+    element, end = merge(first[:5], tail)
+    for n, value in enumerate((*element, first[5], second[6])):
         chip[n] = value
-    for n, value in enumerate(node):
+    for n, value in enumerate((*end, *start)):
         middle[n] = value
 
 
@@ -282,35 +277,32 @@
             here = (y + shift) % 4 == m
             chosen = [jnp.where(here, a, c) for a, c in zip(arrived[shift], chosen)]
         chips.append(chosen)
-    element = chips[0]
-    inner = []
+    element = chips[0][:5]
+    inner, fronts = [], []
     for m in range(1, 4):
-        element, node = merge(element, chips[m])
+        tail, front = behind((chips[m - 1][6] + chips[m][5]) * 0.5, chips[m][:5])
+        element, node = merge(element, tail)
         inner.append(node)
-    for n, value in enumerate(element):
+        fronts.append(front)
+    for n, value in enumerate((*element, chips[0][5], chips[3][6])):
         for j in range(8):
             message[j, n] = value
     zero, one = jnp.zeros((8, 128), F32), jnp.ones((8, 128), F32)
-    ends = [(zero, one, zero)]
-    for a, b, c in inner[::-1]:
-        a2, b2, c2 = ends[-1]
-        ends.append((a + b * a2, b * b2, c + b * c2))
-    ends.append((one, zero, zero))
-    ends = ends[::-1]
-    west, east = ends[0], ends[1]
+    left = (one, zero, zero)
+    lasts = [(zero, one, zero)]
+    for node in inner[::-1]:
+        lasts.append(within(node, left, lasts[-1]))
+    lasts = lasts[::-1]
+    firsts = [left] + [within(fronts[m - 1], lasts[m - 1], lasts[m]) for m in range(1, 4)]
+    first, last = firsts[0], lasts[0]
     for m in range(1, 4):
-        west = [jnp.where(y == m, e, w) for e, w in zip(ends[m], west)]
-        east = [jnp.where(y == m, e, w) for e, w in zip(ends[m + 1], east)]
-    a, b, c = load3(middle)
-    half = [a * w + b * e for w, e in zip(west, east)]
-    half[2] = half[2] + c
-    for n, trio in enumerate((west, half, east)):
+        first = [jnp.where(y == m, new, old) for new, old in zip(firsts[m], first)]
+        last = [jnp.where(y == m, new, old) for new, old in zip(lasts[m], last)]
+    before = within(tuple(middle[n] for n in range(3)), first, last)
+    second = within(tuple(middle[n] for n in range(3, 6)), before, last)
+    for n, trio in enumerate((first, before, second, last)):
         for m in range(3):
             nodes[n, m] = trio[m]
-
-
-def load3(ref):
-    return tuple(ref[n] for n in range(3))
 
 
 def ends_kernel(got, nodes, mine, other):
@@ -318,42 +310,48 @@
     slab = gx // 8
     even = gx % 2 == 0
     zero = jnp.zeros((8, 128), F32)
-    conduct = got[0, 0] + got[0, 2]
-    right = got[0, 4]
+    slabs, fronts = [], []
+    for z in range(8):
+        face = got[z, 5] * 0.5 if z == 0 else (got[z - 1, 6] + got[z, 5]) * 0.5
+        tail, front = behind(face, tuple(got[z, n] for n in range(5)))
+        slabs.append(tail)
+        fronts.append(front)
+    g, _, conduct, _, right = slabs[0]
+    conduct = conduct + g
     ratios, offsets = [], []
-    for k in range(7):
-        conduct = conduct + got[k + 1, 1]
-        right = right + got[k + 1, 3]
-        inverse = 1.0 / (conduct + got[k + 1, 0])
-        f = got[k + 1, 0] * inverse
+    for z in range(1, 8):
+        g, sl, sr, rl, rr = slabs[z]
+        conduct = conduct + sl
+        right = right + rl
+        inverse = 1.0 / (conduct + g)
+        f = g * inverse
         ratios.append(f)
         offsets.append(right * inverse)
-        conduct = got[k + 1, 2] + f * conduct
-        right = got[k + 1, 4] + f * right
-    value = right / conduct
+        conduct = sr + f * conduct
+        right = rr + f * right
+    value = right / (conduct + got[7, 6] * 0.5)
     values = [value]
     for k in range(6, -1, -1):
         value = ratios[k] * value + offsets[k]
         values.append(value)
     values = [zero] + values[::-1]
-    left, last = zero, zero
+    first, last = zero, zero
     for z in range(8):
-        left = jnp.where(slab == z, values[z], left)
+        a, b, c = fronts[z]
+        first = jnp.where(slab == z, a * values[z] + b * values[z + 1] + c, first)
         last = jnp.where(slab == z, values[z + 1], last)
-    trio = [nodes[n, 0] * left + nodes[n, 1] * last + nodes[n, 2] for n in range(3)]
-    mine[0] = jnp.where(even, trio[0], trio[1])
-    mine[1] = jnp.where(even, trio[1], trio[2])
-    other[0] = jnp.where(even, trio[1], trio[0])
-    other[1] = jnp.where(even, trio[2], trio[1])
-
-
-def section_kernel(mine, other, sums, local, h1, h2, hy, edge, section, message):
+    row = [nodes[n, 0] * first + nodes[n, 1] * last + nodes[n, 2] for n in range(4)]
+    for n in range(2):
+        mine[n] = jnp.where(even, row[n], row[n + 2])
+        other[n] = jnp.where(even, row[n + 2], row[n])
+
+
+def section_kernel(mine, other, local, h1, h2, hy, edge, section, message):
     core = lax.axis_index("gx") % 2
     wide = lax.broadcasted_iota(jnp.int32, (8, 128), 1)
     for f in range(2):
-        left = jnp.where(core == f, mine[0], other[0])
+        first = jnp.where(core == f, mine[0], other[0])
         last = jnp.where(core == f, mine[1], other[1])
-        first = sums[0, f] * left + sums[1, f] * last + sums[2, f]
         rows = slice(f * ROWS, (f + 1) * ROWS)
         s = local[rows, :] + h1[rows, :] * natural(first, ROWS) + h2[rows, :] * natural(last, ROWS)
         section[rows, :] = s
@@ -403,24 +401,16 @@
     fields_far = lax.ppermute(fields, "gz", swap)
     vertical_far = lax.ppermute(vertical, "gz", swap)
     full = shape(*grid)
-    half = shape(5, 8, 128)
+    half = shape(7, 8, 128)
     standing = shape(256, 128)
-    fields_here, vertical_here, kappa_here, rim = call(
-        input_kernel,
-        (full, full, full, shape(2, 8, 128)),
+    fields_here, vertical_here, kappa_here, ax, bx, qx, h1, h2, parts = call(
+        factor_x_kernel,
+        (full, full, full, shape(4, *grid), shape(4, *grid), full, full, full, shape(5, 2, 8, 128)),
         [HBM] * 3,
-        flops=1_000_000,
-        size=1_000_000,
+        flops=4_000_000,
+        size=2_000_000,
         scratch=[pltpu.SemaphoreType.DMA((3,))],
     )(*(pltpu.with_memory_space_constraint(x.reshape(grid), pltpu.HBM) for x in (fields, vertical, kappa)))
-    halo = lax.ppermute(rim, "gx", [(i, i + 1) for i in range(63)])
-    ax, bx, qx, h1, h2, parts = call(
-        factor_x_kernel,
-        (shape(4, *grid), shape(4, *grid), full, full, full, shape(3, 2, 8, 128)),
-        [VMEM],
-        flops=4_000_000,
-        size=2_000_000,
-    )(kappa_here)
     ay, by, qy, hy, edge = call(
         factor_y_kernel,
         (shape(10, 256, 128), shape(10, 256, 128), standing, full, shape(ALL, 128)),
@@ -428,18 +418,16 @@
         flops=20_000_000,
         size=4_000_000,
     )(kappa_here)
-    source, sums, keep, send = call(
-        source_kernel, (full, shape(3, 2, 8, 128), half, half), [VMEM] * 10
-    )(
+    source, keep, send = call(source_kernel, (full, half, half), [VMEM] * 8)(
         fields_here, fields_far.reshape(grid), vertical_here, vertical_far.reshape(grid),
-        kappa_here, halo, h1, h2, parts, edge,
+        h1, h2, parts, edge,
     )
     got = lax.ppermute(send, "gx", CORES)
     local_x = call(local_x_kernel, full, [VMEM] * 4, flops=1_000_000, size=1_000_000)(source, ax, bx, qx)
-    chip, middle = call(chip_kernel, (half, shape(3, 8, 128)), [VMEM] * 2)(keep, got)
+    chip, middle = call(chip_kernel, (half, shape(6, 8, 128)), [VMEM] * 2)(keep, got)
     far = [lax.ppermute(chip, "gx", chips_on(shift)) for shift in (2, 1, 3)]
     message, nodes = call(
-        slab_kernel, (shape(8, 5, 8, 128), shape(3, 3, 8, 128)), [VMEM] * 5
+        slab_kernel, (shape(8, 7, 8, 128), shape(4, 3, 8, 128)), [VMEM] * 5
     )(chip, far[1], far[0], far[2], middle)
     got = lax.all_to_all(message, "gx", 0, 0, axis_index_groups=SLAB_GROUPS, tiled=True)
     mine, other = call(
@@ -447,8 +435,8 @@
     )(got, nodes)
     other = lax.ppermute(other, "gx", CORES)
     section, message = call(
-        section_kernel, (full, shape(ALL, 128)), [VMEM] * 8
-    )(mine, other, sums, local_x, h1, h2, hy, edge)
+        section_kernel, (full, shape(ALL, 128)), [VMEM] * 7
+    )(mine, other, local_x, h1, h2, hy, edge)
     far = lax.ppermute(message, "gy", swap)
     local_y = call(local_y_kernel, full, [VMEM] * 4, flops=4_000_000, size=3_000_000)(section, ay, by, qy)
     out = call(output_kernel, full, [VMEM] * 4)(message, far, local_y, hy)

time: 44.7 us -> 44.4 us (level)
  starting transfers between devices: 17.2 us -> 15.9 us
  waiting for transfers between devices: 4.27 us -> 5.12 us
  blocking collectives: 16.6 us -> 17.1 us
    ppermute x1 -> x0, starting transfers between devices: 4.55 us -> none  [local(): halo = lax.ppermute(rim, 'gx', [(i, i + 1) for i in range(63)])]
    ppermute x1, starting transfers between devices: 0.09 us -> 2.87 us  [local(): got = lax.ppermute(send, 'gx', CORES)]
    ppermute x1, waiting for transfers between devices: 0.01 us -> 1.2 us  [local(): vertical_far = lax.ppermute(vertical, 'gz', swap)]
    all_to_all x1, blocking collectives: 16.6 us -> 17.1 us  [local(): lax.all_to_all(message, 'gx', 0, 0, axis_index_groups=SLAB_GROUPS, tiled=...]
    pallas_call x6 -> x5, Pallas kernels: 2.04 us -> 1.94 us  [the longest x1 1.62 us: local(): call(factor_x_kernel, (full, full, full, shape(4, *grid), shape(4, *grid)...]
  transfers between devices with their start and end apart: 9 -> 8, of which waited for: 5 -> 6; matrix products, arithmetic and copies ran while one was open for 0% -> 0% of each run, Pallas kernels for 11% -> 11%
where the time goes in v4:
time: 44.4 us; the launch traced here: 44.2 us
  blocking collectives  17.1 us (39%)
  starting transfers between devices  15.9 us (36%)
  Pallas kernels  6.11 us (14%)
  waiting for transfers between devices  5.12 us (12%)
    all_to_all x1, blocking collectives, local(): lax.all_to_all(message, 'gx', 0, 0, axis_index_groups=SLAB_GROUPS, tiled=...  17.1 us
    ppermute x3, starting transfers between devices, local(): far = [lax.ppermute(chip, 'gx', chips_on(shift)) for shift in (2, 1, 3)]  5 us
    ppermute x1, starting transfers between devices, local(): other = lax.ppermute(other, 'gx', CORES)  3.2 us
    ppermute x1, starting transfers between devices, local(): got = lax.ppermute(send, 'gx', CORES)  2.87 us
    ppermute x1, starting transfers between devices, local(): far = lax.ppermute(message, 'gy', swap)  2.76 us
    pallas_call x1, Pallas kernels, local(): call(factor_y_kernel, (shape(10, 256, 128), shape(10, 256, 128), standing...  2.14 us
    ppermute x1, starting transfers between devices, local(): fields_far = lax.ppermute(fields, 'gz', swap)  2.04 us
    ppermute x3, waiting for transfers between devices, local(): far = [lax.ppermute(chip, 'gx', chips_on(shift)) for shift in (2, 1, 3)]  1.92 us
  transfers between devices with their start and end apart: 8, of which 6 were waited for; matrix products, arithmetic and copies ran while one was open for 0% of the time, Pallas kernels for 11%

profile of v4, /device:TPU:1, one launch (start us, length us, event | category | flops | bytes accessed | tf_op | source)
XLA Modules:
  0.0 44.2 jit_solution(12882815815505726390)
XLA Ops:
  0.0 2.0 %collective-permute-start = (f32[2,1,16,1024]{3,2,1,0:T(8,128)}, f32[2,1,16,1024]{3,2,1,0:T(8,128)S(1)}, u32[]{:S(2)}, u32[]{:S(2)}) collective-permute-start(f32[2,1,16,1024]{3,2,1,0:T(8,128)} %param.3), channel_id=1, source_target_pairs={{0,1},{1,0},{2,3},{3,2},{4,5},{5,4},{6,7},{7,6},{8,9},{9,8},{10,11... | collective-permute-start | bytes 393224 | tf_op jit(solution)/shard_map/ppermute | solution.py:401
  2.0 0.0 collective-permute-start.1
  2.1 1.6 %shard_map.37 = (f32[32,1024]{1,0:T(8,128)S(1)}, f32[32,1024]{1,0:T(8,128)S(1)}, f32[32,1024]{1,0:T(8,128)S(1)}, f32[4,32,1024]{2,1,0:T(8,128)S(1)}, f32[4,32,10...) custom-call(f32[32,1024]{1,0:T(8,128)} %bitcast.11, ...), custom_call_target="tpu_custom_call" | custom-call | flops 4000000 | bytes 2000000 | tf_op jit(solution)/shard_map/pallas_call | solution.py:406
  3.7 2.1 %shard_map.38 = (f32[10,256,128]{2,1,0:T(8,128)S(1)}, f32[10,256,128]{2,1,0:T(8,128)S(1)}, f32[256,128]{1,0:T(8,128)S(1)}, f32[32,1024]{1,0:T(8,128)S(1)}, f32[32,128]{1,0:T(8,128)S(1)}) custom-call(f32[32,1024]{1,0:T(8,128)S(1)} %get-tuple-element.35.kappa), custom_call_target="tpu_custom_call" | custom-call | flops 20000000 | bytes 4000000 | tf_op jit(solution)/shard_map/pallas_call | solution.py:414
  5.8 0.0 collective-permute-done
  5.8 1.2 %collective-permute-done.1 = f32[2,1,16,1024]{3,2,1,0:T(8,128)S(1)} collective-permute-done((f32[2,1,16,1024]{3,2,1,0:T(8,128)}, f32[2,1,16,1024]{3,2,1,0:T(8,128)S(1)}, u32[]{:S(2)}, u32[]{:S(2)}) %collective-permute-start.1) | collective-permute-done | bytes 131104 | tf_op jit(solution)/shard_map/ppermute | solution.py:402
  7.0 0.1 shard_map.39
  7.1 2.9 %collective-permute-start.2 = (f32[7,8,128]{2,1,0:T(8,128)S(1)}, f32[7,8,128]{2,1,0:T(8,128)S(1)}, u32[]{:S(2)}, u32[]{:S(2)}) collective-permute-start(f32[7,8,128]{2,1,0:T(8,128)S(1)} %get-tuple-element.38), channel_id=1, source_target_pairs={{0,4},{4,0},{8,12},{12,8},{16,20},{20,16},{24,28},{28,24},{32,36},... | collective-permute-start | bytes 86024 | tf_op jit(solution)/shard_map/ppermute | solution.py:425
  10.0 0.9 %collective-permute-done.2.got = f32[7,8,128]{2,1,0:T(8,128)S(1)} collective-permute-done((f32[7,8,128]{2,1,0:T(8,128)S(1)}, f32[7,8,128]{2,1,0:T(8,128)S(1)}, u32[]{:S(2)}, u32[]{:S(2)}) %collective-permute-start.2) | collective-permute-done | bytes 28704 | tf_op jit(solution)/shard_map/ppermute | solution.py:425
  10.9 1.3 %collective-permute-start.5 = (f32[7,8,128]{2,1,0:T(8,128)S(1)}, f32[7,8,128]{2,1,0:T(8,128)S(1)}, u32[]{:S(2)}, u32[]{:S(2)}) collective-permute-start(f32[7,8,128]{2,1,0:T(8,128)S(1)} %get-tuple-element.39.chip), channel_id=1, source_target_pairs={{24,0},{28,4},{0,8},{4,12},{8,16},{12,20},{16,24},{20,28},{56,32},... | collective-permute-start | bytes 86024 | tf_op jit(solution)/shard_map/ppermute | solution.py:428
  12.2 2.6 %collective-permute-start.4 = (f32[7,8,128]{2,1,0:T(8,128)S(1)}, f32[7,8,128]{2,1,0:T(8,128)S(1)}, u32[]{:S(2)}, u32[]{:S(2)}) collective-permute-start(f32[7,8,128]{2,1,0:T(8,128)S(1)} %get-tuple-element.39.chip), channel_id=1, source_target_pairs={{16,0},{20,4},{24,8},{28,12},{0,16},{4,20},{8,24},{12,28},{48,32},... | collective-permute-start | bytes 86024 | tf_op jit(solution)/shard_map/ppermute | solution.py:428
  14.8 1.1 %collective-permute-start.3 = (f32[7,8,128]{2,1,0:T(8,128)S(1)}, f32[7,8,128]{2,1,0:T(8,128)S(1)}, u32[]{:S(2)}, u32[]{:S(2)}) collective-permute-start(f32[7,8,128]{2,1,0:T(8,128)S(1)} %get-tuple-element.39.chip), channel_id=1, source_target_pairs={{8,0},{12,4},{16,8},{20,12},{24,16},{28,20},{0,24},{4,28},{40,32},... | collective-permute-start | bytes 86024 | tf_op jit(solution)/shard_map/ppermute | solution.py:428
  15.9 0.0 collective-permute-done.5.far3
  15.9 0.5 %collective-permute-done.4.far2 = f32[7,8,128]{2,1,0:T(8,128)S(1)} collective-permute-done((f32[7,8,128]{2,1,0:T(8,128)S(1)}, f32[7,8,128]{2,1,0:T(8,128)S(1)}, u32[]{:S(2)}, u32[]{:S(2)}) %collective-permute-start.4) | collective-permute-done | bytes 28704 | tf_op jit(solution)/shard_map/ppermute | solution.py:428
  16.4 1.4 %collective-permute-done.3.far1 = f32[7,8,128]{2,1,0:T(8,128)S(1)} collective-permute-done((f32[7,8,128]{2,1,0:T(8,128)S(1)}, f32[7,8,128]{2,1,0:T(8,128)S(1)}, u32[]{:S(2)}, u32[]{:S(2)}) %collective-permute-start.3) | collective-permute-done | bytes 28704 | tf_op jit(solution)/shard_map/ppermute | solution.py:428
  17.8 0.1 shard_map.41
  17.9 17.1 %all_to_all.5.got = f32[8,7,8,128]{3,2,1,0:T(8,128)S(1)} all-to-all(f32[8,7,8,128]{3,2,1,0:T(8,128)S(1)} %get-tuple-element.41), channel_id=1, replica_groups={{0,32,64,96,128,160,192,224},{4,36,68,100,132,164,196,228},{8,40,72,104..., dimensions={0} | all-to-all | bytes 458752 | tf_op jit(solution)/shard_map/all_to_all | solution.py:432
  35.0 0.1 shard_map.42
  35.1 3.2 %collective-permute-start.6 = (f32[2,8,128]{2,1,0:T(8,128)S(1)}, f32[2,8,128]{2,1,0:T(8,128)S(1)}, u32[]{:S(2)}, u32[]{:S(2)}) collective-permute-start(f32[2,8,128]{2,1,0:T(8,128)S(1)} %get-tuple-element.44), channel_id=1, source_target_pairs={{0,4},{4,0},{8,12},{12,8},{16,20},{20,16},{24,28},{28,24},{32,36},... | collective-permute-start | bytes 24584 | tf_op jit(solution)/shard_map/ppermute | solution.py:436
  38.3 0.1 shard_map.43.local
  38.4 0.7 %collective-permute-done.6.other = f32[2,8,128]{2,1,0:T(8,128)S(1)} collective-permute-done((f32[2,8,128]{2,1,0:T(8,128)S(1)}, f32[2,8,128]{2,1,0:T(8,128)S(1)}, u32[]{:S(2)}, u32[]{:S(2)}) %collective-permute-start.6) | collective-permute-done | bytes 8224 | tf_op jit(solution)/shard_map/ppermute | solution.py:436
  39.1 0.1 shard_map.44
  39.2 2.8 %collective-permute-start.7 = (f32[32,128]{1,0:T(8,128)S(1)}, f32[32,128]{1,0:T(8,128)S(1)}, u32[]{:S(2)}, u32[]{:S(2)}) collective-permute-start(f32[32,128]{1,0:T(8,128)S(1)} %get-tuple-element.50.message), channel_id=1, source_target_pairs={{0,2},{2,0},{1,3},{3,1},{4,6},{6,4},{5,7},{7,5},{8,10},{10,8},{9,1... | collective-permute-start | bytes 49160 | tf_op jit(solution)/shard_map/ppermute | solution.py:440
  42.0 0.9 %shard_map.45.local = f32[32,1024]{1,0:T(8,128)S(1)} custom-call(f32[32,1024]{1,0:T(8,128)S(1)} %get-tuple-element.51.section, f32[10,256,128]{2,1,0:T(8,128)S(1)} %get-tuple-element.52.ay, f32[10,256,128]{2,1,0:T(8,128)S(1)} %get-tuple-element.53.by, f32[256,128]{1,0:T(8,128)S(1)} %get-tuple-element.54.qy), custom_call_target="tpu_custom_call" | custom-call | flops 4000000 | bytes 3000000 | tf_op jit(solution)/shard_map/pallas_call | solution.py:441
  42.9 0.5 %collective-permute-done.7.far = f32[32,128]{1,0:T(8,128)S(1)} collective-permute-done((f32[32,128]{1,0:T(8,128)S(1)}, f32[32,128]{1,0:T(8,128)S(1)}, u32[]{:S(2)}, u32[]{:S(2)}) %collective-permute-start.7) | collective-permute-done | bytes 16416 | tf_op jit(solution)/shard_map/ppermute | solution.py:440
  43.4 0.9 %shard_map.46 = f32[32,1024]{1,0:T(8,128)} custom-call(f32[32,128]{1,0:T(8,128)S(1)} %get-tuple-element.50.message, f32[32,128]{1,0:T(8,128)S(1)} %collective-permute-done.7.far, f32[32,1024]{1,0:T(8,128)S(1)} %shard_map.45.local, f32[32,1024]{1,0:T(8,128)S(1)} %get-tuple-element.49.hy), custom_call_target="tpu_custom_call" | custom-call | tf_op jit(solution)/shard_map/pallas_call | solution.py:442
  (1 shorter events, 0.0 us)
Async XLA Ops:
  0.0 5.8 %collective-permute-start = (f32[2,1,16,1024]{3,2,1,0:T(8,128)}, f32[2,1,16,1024]{3,2,1,0:T(8,128)S(1)}, u32[]{:S(2)}, u32[]{:S(2)}) collective-permute-start(f32[2,1,16,1024]{3,2,1,0:T(8,128)} %param.3), channel_id=1, source_target_pairs={{0,1},{1,0},{2,3},{3,2},{4,5},{5,4},{6,7},{7,6},{8,9},{9,8},{10,11... | collective-permute-start | bytes 393224 | tf_op jit(solution)/shard_map/ppermute | solution.py:401
  2.0 5.0 %collective-permute-start.1 = (f32[2,1,16,1024]{3,2,1,0:T(8,128)}, f32[2,1,16,1024]{3,2,1,0:T(8,128)S(1)}, u32[]{:S(2)}, u32[]{:S(2)}) collective-permute-start(f32[2,1,16,1024]{3,2,1,0:T(8,128)} %param.5), channel_id=1, source_target_pairs={{0,1},{1,0},{2,3},{3,2},{4,5},{5,4},{6,7},{7,6},{8,9},{9,8},{10,11... | collective-permute-start | bytes 393224 | tf_op jit(solution)/shard_map/ppermute | solution.py:402
  7.1 3.7 %collective-permute-start.2 = (f32[7,8,128]{2,1,0:T(8,128)S(1)}, f32[7,8,128]{2,1,0:T(8,128)S(1)}, u32[]{:S(2)}, u32[]{:S(2)}) collective-permute-start(f32[7,8,128]{2,1,0:T(8,128)S(1)} %get-tuple-element.38), channel_id=1, source_target_pairs={{0,4},{4,0},{8,12},{12,8},{16,20},{20,16},{24,28},{28,24},{32,36},... | collective-permute-start | bytes 86024 | tf_op jit(solution)/shard_map/ppermute | solution.py:425
  10.9 5.0 %collective-permute-start.5 = (f32[7,8,128]{2,1,0:T(8,128)S(1)}, f32[7,8,128]{2,1,0:T(8,128)S(1)}, u32[]{:S(2)}, u32[]{:S(2)}) collective-permute-start(f32[7,8,128]{2,1,0:T(8,128)S(1)} %get-tuple-element.39.chip), channel_id=1, source_target_pairs={{24,0},{28,4},{0,8},{4,12},{8,16},{12,20},{16,24},{20,28},{56,32},... | collective-permute-start | bytes 86024 | tf_op jit(solution)/shard_map/ppermute | solution.py:428
  12.2 4.2 %collective-permute-start.4 = (f32[7,8,128]{2,1,0:T(8,128)S(1)}, f32[7,8,128]{2,1,0:T(8,128)S(1)}, u32[]{:S(2)}, u32[]{:S(2)}) collective-permute-start(f32[7,8,128]{2,1,0:T(8,128)S(1)} %get-tuple-element.39.chip), channel_id=1, source_target_pairs={{16,0},{20,4},{24,8},{28,12},{0,16},{4,20},{8,24},{12,28},{48,32},... | collective-permute-start | bytes 86024 | tf_op jit(solution)/shard_map/ppermute | solution.py:428
  14.8 3.0 %collective-permute-start.3 = (f32[7,8,128]{2,1,0:T(8,128)S(1)}, f32[7,8,128]{2,1,0:T(8,128)S(1)}, u32[]{:S(2)}, u32[]{:S(2)}) collective-permute-start(f32[7,8,128]{2,1,0:T(8,128)S(1)} %get-tuple-element.39.chip), channel_id=1, source_target_pairs={{8,0},{12,4},{16,8},{20,12},{24,16},{28,20},{0,24},{4,28},{40,32},... | collective-permute-start | bytes 86024 | tf_op jit(solution)/shard_map/ppermute | solution.py:428
  35.1 4.0 %collective-permute-start.6 = (f32[2,8,128]{2,1,0:T(8,128)S(1)}, f32[2,8,128]{2,1,0:T(8,128)S(1)}, u32[]{:S(2)}, u32[]{:S(2)}) collective-permute-start(f32[2,8,128]{2,1,0:T(8,128)S(1)} %get-tuple-element.44), channel_id=1, source_target_pairs={{0,4},{4,0},{8,12},{12,8},{16,20},{20,16},{24,28},{28,24},{32,36},... | collective-permute-start | bytes 24584 | tf_op jit(solution)/shard_map/ppermute | solution.py:436
  39.2 4.1 %collective-permute-start.7 = (f32[32,128]{1,0:T(8,128)S(1)}, f32[32,128]{1,0:T(8,128)S(1)}, u32[]{:S(2)}, u32[]{:S(2)}) collective-permute-start(f32[32,128]{1,0:T(8,128)S(1)} %get-tuple-element.50.message), channel_id=1, source_target_pairs={{0,2},{2,0},{1,3},{3,1},{4,6},{6,4},{5,7},{7,5},{8,10},{10,8},{9,1... | collective-permute-start | bytes 49160 | tf_op jit(solution)/shard_map/ppermute | solution.py:440

commit v5 on v4

--- a/solution.py
+++ b/solution.py
@@ -254,55 +254,45 @@
     return (a * left[0] + b * right[0], a * left[1] + b * right[1], a * left[2] + b * right[2] + c)
 
 
-def chip_kernel(keep, got, chip, middle):
-    even = lax.axis_index("gx") % 2 == 0
-    mine, other = load(keep), load(got)
-    first = [jnp.where(even, m, o) for m, o in zip(mine, other)]
-    second = [jnp.where(even, o, m) for m, o in zip(mine, other)]
+def join(mine, other, low):
+    first = [jnp.where(low, m, o) for m, o in zip(mine, other)]
+    second = [jnp.where(low, o, m) for m, o in zip(mine, other)]
     tail, start = behind((first[6] + second[5]) * 0.5, second[:5])
     element, end = merge(first[:5], tail)
-    for n, value in enumerate((*element, first[5], second[6])):
-        chip[n] = value
-    for n, value in enumerate((*end, *start)):
-        middle[n] = value
-
-
-def slab_kernel(chip, far1, far2, far3, middle, message, nodes):
-    y = lax.axis_index("gx") // 2 % 4
-    arrived = [load(chip), load(far1), load(far2), load(far3)]
-    chips = []
-    for m in range(4):
-        chosen = arrived[0]
-        for shift in range(1, 4):
-            here = (y + shift) % 4 == m
-            chosen = [jnp.where(here, a, c) for a, c in zip(arrived[shift], chosen)]
-        chips.append(chosen)
-    element = chips[0][:5]
-    inner, fronts = [], []
-    for m in range(1, 4):
-        tail, front = behind((chips[m - 1][6] + chips[m][5]) * 0.5, chips[m][:5])
-        element, node = merge(element, tail)
-        inner.append(node)
-        fronts.append(front)
-    for n, value in enumerate((*element, chips[0][5], chips[3][6])):
+    return (*element, first[5], second[6]), (*end, *start)
+
+
+def join_kernel(bit, mine, other, both, rows):
+    low = lax.axis_index("gx") // bit % 2 == 0
+    element, nodes = join(load(mine), load(other), low)
+    for n, value in enumerate(element):
+        both[n] = value
+    for n, value in enumerate(nodes):
+        rows[n] = value
+
+
+def slab_kernel(mine, other, pair_rows, chip_rows, message, nodes):
+    gx = lax.axis_index("gx")
+    low = gx // 4 % 2 == 0
+    element, rows = join(load(mine), load(other), low)
+    for n, value in enumerate(element):
         for j in range(8):
             message[j, n] = value
     zero, one = jnp.zeros((8, 128), F32), jnp.ones((8, 128), F32)
-    left = (one, zero, zero)
-    lasts = [(zero, one, zero)]
-    for node in inner[::-1]:
-        lasts.append(within(node, left, lasts[-1]))
-    lasts = lasts[::-1]
-    firsts = [left] + [within(fronts[m - 1], lasts[m - 1], lasts[m]) for m in range(1, 4)]
-    first, last = firsts[0], lasts[0]
-    for m in range(1, 4):
-        first = [jnp.where(y == m, new, old) for new, old in zip(firsts[m], first)]
-        last = [jnp.where(y == m, new, old) for new, old in zip(lasts[m], last)]
-    before = within(tuple(middle[n] for n in range(3)), first, last)
-    second = within(tuple(middle[n] for n in range(3, 6)), before, last)
-    for n, trio in enumerate((first, before, second, last)):
-        for m in range(3):
-            nodes[n, m] = trio[m]
+    ends = ((one, zero, zero), (zero, one, zero))
+    parts = [rows, *(tuple(ref[n] for n in range(6)) for ref in (pair_rows, chip_rows))]
+    for n, (rows, low) in enumerate(zip(parts, (low, gx // 2 % 2 == 0, None))):
+        end = within(rows[:3], *ends)
+        start = within(rows[3:], end, ends[1])
+        if n == 2:
+            for m, trio in enumerate((ends[0], end, start, ends[1])):
+                for k in range(3):
+                    nodes[m, k] = trio[k]
+        else:
+            ends = (
+                [jnp.where(low, a, b) for a, b in zip(ends[0], start)],
+                [jnp.where(low, a, b) for a, b in zip(end, ends[1])],
+            )
 
 
 def ends_kernel(got, nodes, mine, other):
@@ -391,8 +381,8 @@
 CORES = [(i, i ^ 1) for i in range(64)]
 
 
-def chips_on(shift):
-    return [(i // 8 * 8 + (i + 2 * shift) % 8, i) for i in range(64)]
+CHIPS = [(i, i ^ 2) for i in range(64)]
+PAIRS = [(i, i ^ 6) for i in range(64)]
 
 
 def local(fields, kappa, vertical):
@@ -424,11 +414,14 @@
     )
     got = lax.ppermute(send, "gx", CORES)
     local_x = call(local_x_kernel, full, [VMEM] * 4, flops=1_000_000, size=1_000_000)(source, ax, bx, qx)
-    chip, middle = call(chip_kernel, (half, shape(6, 8, 128)), [VMEM] * 2)(keep, got)
-    far = [lax.ppermute(chip, "gx", chips_on(shift)) for shift in (2, 1, 3)]
+    rows = shape(6, 8, 128)
+    chip, chip_rows = call(functools.partial(join_kernel, 1), (half, rows), [VMEM] * 2)(keep, got)
+    got = lax.ppermute(chip, "gx", CHIPS)
+    pair, pair_rows = call(functools.partial(join_kernel, 2), (half, rows), [VMEM] * 2)(chip, got)
+    got = lax.ppermute(pair, "gx", PAIRS)
     message, nodes = call(
-        slab_kernel, (shape(8, 7, 8, 128), shape(4, 3, 8, 128)), [VMEM] * 5
-    )(chip, far[1], far[0], far[2], middle)
+        slab_kernel, (shape(8, 7, 8, 128), shape(4, 3, 8, 128)), [VMEM] * 4
+    )(pair, got, pair_rows, chip_rows)
     got = lax.all_to_all(message, "gx", 0, 0, axis_index_groups=SLAB_GROUPS, tiled=True)
     mine, other = call(
         ends_kernel, (shape(2, 8, 128), shape(2, 8, 128)), [VMEM, VMEM]

time: 44.4 us -> 45 us (1.014)
  waiting for transfers between devices: 5.12 us -> 5.95 us
    ppermute x3 -> x2, starting transfers between devices: 5 us -> 4.08 us  [the longest x1 2.76 us: local(): got = lax.ppermute(pair, 'gx', PAIRS)]
    ppermute x1, starting transfers between devices: 3.2 us -> 4.08 us  [local(): other = lax.ppermute(other, 'gx', CORES)]
    ppermute x3 -> x2, waiting for transfers between devices: 1.92 us -> 2.75 us  [the longest x1 1.49 us: local(): got = lax.ppermute(chip, 'gx', CHIPS)]
  transfers between devices with their start and end apart: 8 -> 7, of which waited for: 6 -> 6; matrix products, arithmetic and copies ran while one was open for 0% -> 0% of each run, Pallas kernels for 11% -> 11%
where the time goes in v5:
time: 45 us; the launch traced here: 44.9 us
  blocking collectives  17 us (38%)
  starting transfers between devices  15.9 us (35%)
  Pallas kernels  6.09 us (14%)
  waiting for transfers between devices  5.95 us (13%)
    all_to_all x1, blocking collectives, local(): lax.all_to_all(message, 'gx', 0, 0, axis_index_groups=SLAB_GROUPS, tiled=...  17 us
    ppermute x1, starting transfers between devices, local(): other = lax.ppermute(other, 'gx', CORES)  4.08 us
    ppermute x1, starting transfers between devices, local(): got = lax.ppermute(send, 'gx', CORES)  2.87 us
    ppermute x1, starting transfers between devices, local(): far = lax.ppermute(message, 'gy', swap)  2.76 us
    ppermute x1, starting transfers between devices, local(): got = lax.ppermute(pair, 'gx', PAIRS)  2.76 us
    pallas_call x1, Pallas kernels, local(): call(factor_y_kernel, (shape(10, 256, 128), shape(10, 256, 128), standing...  2.14 us
    ppermute x1, starting transfers between devices, local(): fields_far = lax.ppermute(fields, 'gz', swap)  2.04 us
    pallas_call x1, Pallas kernels, local(): call(factor_x_kernel, (full, full, full, shape(4, *grid), shape(4, *grid)...  1.62 us
  transfers between devices with their start and end apart: 7, of which 6 were waited for; matrix products, arithmetic and copies ran while one was open for 0% of the time, Pallas kernels for 11%

profile of v5, /device:TPU:1, one launch (start us, length us, event | category | flops | bytes accessed | tf_op | source)
XLA Modules:
  0.0 44.9 jit_solution(7668094201666173048)
XLA Ops:
  0.0 2.0 %collective-permute-start = (f32[2,1,16,1024]{3,2,1,0:T(8,128)}, f32[2,1,16,1024]{3,2,1,0:T(8,128)S(1)}, u32[]{:S(2)}, u32[]{:S(2)}) collective-permute-start(f32[2,1,16,1024]{3,2,1,0:T(8,128)} %param.3), channel_id=1, source_target_pairs={{0,1},{1,0},{2,3},{3,2},{4,5},{5,4},{6,7},{7,6},{8,9},{9,8},{10,11... | collective-permute-start | bytes 393224 | tf_op jit(solution)/shard_map/ppermute | solution.py:391
  2.0 0.0 collective-permute-start.1
  2.1 1.6 %shard_map.37 = (f32[32,1024]{1,0:T(8,128)S(1)}, f32[32,1024]{1,0:T(8,128)S(1)}, f32[32,1024]{1,0:T(8,128)S(1)}, f32[4,32,1024]{2,1,0:T(8,128)S(1)}, f32[4,32,10...) custom-call(f32[32,1024]{1,0:T(8,128)} %bitcast.11, ...), custom_call_target="tpu_custom_call" | custom-call | flops 4000000 | bytes 2000000 | tf_op jit(solution)/shard_map/pallas_call | solution.py:396
  3.7 2.1 %shard_map.38 = (f32[10,256,128]{2,1,0:T(8,128)S(1)}, f32[10,256,128]{2,1,0:T(8,128)S(1)}, f32[256,128]{1,0:T(8,128)S(1)}, f32[32,1024]{1,0:T(8,128)S(1)}, f32[32,128]{1,0:T(8,128)S(1)}) custom-call(f32[32,1024]{1,0:T(8,128)S(1)} %get-tuple-element.37.kappa), custom_call_target="tpu_custom_call" | custom-call | flops 20000000 | bytes 4000000 | tf_op jit(solution)/shard_map/pallas_call | solution.py:404
  5.8 0.0 collective-permute-done
  5.8 1.2 %collective-permute-done.1 = f32[2,1,16,1024]{3,2,1,0:T(8,128)S(1)} collective-permute-done((f32[2,1,16,1024]{3,2,1,0:T(8,128)}, f32[2,1,16,1024]{3,2,1,0:T(8,128)S(1)}, u32[]{:S(2)}, u32[]{:S(2)}) %collective-permute-start.1) | collective-permute-done | bytes 131104 | tf_op jit(solution)/shard_map/ppermute | solution.py:392
  7.0 0.1 shard_map.39
  7.1 2.9 %collective-permute-start.2 = (f32[7,8,128]{2,1,0:T(8,128)S(1)}, f32[7,8,128]{2,1,0:T(8,128)S(1)}, u32[]{:S(2)}, u32[]{:S(2)}) collective-permute-start(f32[7,8,128]{2,1,0:T(8,128)S(1)} %get-tuple-element.40), channel_id=1, source_target_pairs={{0,4},{4,0},{8,12},{12,8},{16,20},{20,16},{24,28},{28,24},{32,36},... | collective-permute-start | bytes 86024 | tf_op jit(solution)/shard_map/ppermute | solution.py:415
  10.0 0.9 %collective-permute-done.2.other = f32[7,8,128]{2,1,0:T(8,128)S(1)} collective-permute-done((f32[7,8,128]{2,1,0:T(8,128)S(1)}, f32[7,8,128]{2,1,0:T(8,128)S(1)}, u32[]{:S(2)}, u32[]{:S(2)}) %collective-permute-start.2) | collective-permute-done | bytes 28704 | tf_op jit(solution)/shard_map/ppermute | solution.py:415
  10.9 1.3 %collective-permute-start.3 = (f32[7,8,128]{2,1,0:T(8,128)S(1)}, f32[7,8,128]{2,1,0:T(8,128)S(1)}, u32[]{:S(2)}, u32[]{:S(2)}) collective-permute-start(f32[7,8,128]{2,1,0:T(8,128)S(1)} %get-tuple-element.41.mine), channel_id=1, source_target_pairs={{0,8},{4,12},{8,0},{12,4},{16,24},{20,28},{24,16},{28,20},{32,40},... | collective-permute-start | bytes 86024 | tf_op jit(solution)/shard_map/ppermute | solution.py:419
  12.2 1.5 %collective-permute-done.3.other = f32[7,8,128]{2,1,0:T(8,128)S(1)} collective-permute-done((f32[7,8,128]{2,1,0:T(8,128)S(1)}, f32[7,8,128]{2,1,0:T(8,128)S(1)}, u32[]{:S(2)}, u32[]{:S(2)}) %collective-permute-start.3) | collective-permute-done | bytes 28704 | tf_op jit(solution)/shard_map/ppermute | solution.py:419
  13.7 2.8 %collective-permute-start.4 = (f32[7,8,128]{2,1,0:T(8,128)S(1)}, f32[7,8,128]{2,1,0:T(8,128)S(1)}, u32[]{:S(2)}, u32[]{:S(2)}) collective-permute-start(f32[7,8,128]{2,1,0:T(8,128)S(1)} %get-tuple-element.42.mine), channel_id=1, source_target_pairs={{0,24},{4,28},{8,16},{12,20},{16,8},{20,12},{24,0},{28,4},{32,56},... | collective-permute-start | bytes 86024 | tf_op jit(solution)/shard_map/ppermute | solution.py:421
  16.5 1.3 %collective-permute-done.4.other = f32[7,8,128]{2,1,0:T(8,128)S(1)} collective-permute-done((f32[7,8,128]{2,1,0:T(8,128)S(1)}, f32[7,8,128]{2,1,0:T(8,128)S(1)}, u32[]{:S(2)}, u32[]{:S(2)}) %collective-permute-start.4) | collective-permute-done | bytes 28704 | tf_op jit(solution)/shard_map/ppermute | solution.py:421
  17.8 17.0 %all_to_all.5.got = f32[8,7,8,128]{3,2,1,0:T(8,128)S(1)} all-to-all(f32[8,7,8,128]{3,2,1,0:T(8,128)S(1)} %get-tuple-element.45), channel_id=1, replica_groups={{0,32,64,96,128,160,192,224},{4,36,68,100,132,164,196,228},{8,40,72,104..., dimensions={0} | all-to-all | bytes 458752 | tf_op jit(solution)/shard_map/all_to_all | solution.py:425
  34.8 0.1 shard_map.43
  34.9 4.1 %collective-permute-start.5 = (f32[2,8,128]{2,1,0:T(8,128)S(1)}, f32[2,8,128]{2,1,0:T(8,128)S(1)}, u32[]{:S(2)}, u32[]{:S(2)}) collective-permute-start(f32[2,8,128]{2,1,0:T(8,128)S(1)} %get-tuple-element.48), channel_id=1, source_target_pairs={{0,4},{4,0},{8,12},{12,8},{16,20},{20,16},{24,28},{28,24},{32,36},... | collective-permute-start | bytes 24584 | tf_op jit(solution)/shard_map/ppermute | solution.py:429
  39.0 0.1 shard_map.44.local
  39.1 0.7 %collective-permute-done.5.other = f32[2,8,128]{2,1,0:T(8,128)S(1)} collective-permute-done((f32[2,8,128]{2,1,0:T(8,128)S(1)}, f32[2,8,128]{2,1,0:T(8,128)S(1)}, u32[]{:S(2)}, u32[]{:S(2)}) %collective-permute-start.5) | collective-permute-done | bytes 8224 | tf_op jit(solution)/shard_map/ppermute | solution.py:429
  39.8 0.1 shard_map.45
  39.9 2.8 %collective-permute-start.6 = (f32[32,128]{1,0:T(8,128)S(1)}, f32[32,128]{1,0:T(8,128)S(1)}, u32[]{:S(2)}, u32[]{:S(2)}) collective-permute-start(f32[32,128]{1,0:T(8,128)S(1)} %get-tuple-element.54.message), channel_id=1, source_target_pairs={{0,2},{2,0},{1,3},{3,1},{4,6},{6,4},{5,7},{7,5},{8,10},{10,8},{9,1... | collective-permute-start | bytes 49160 | tf_op jit(solution)/shard_map/ppermute | solution.py:433
  42.7 0.9 %shard_map.46.local = f32[32,1024]{1,0:T(8,128)S(1)} custom-call(f32[32,1024]{1,0:T(8,128)S(1)} %get-tuple-element.55.section, f32[10,256,128]{2,1,0:T(8,128)S(1)} %get-tuple-element.56.ay, f32[10,256,128]{2,1,0:T(8,128)S(1)} %get-tuple-element.57.by, f32[256,128]{1,0:T(8,128)S(1)} %get-tuple-element.58.qy), custom_call_target="tpu_custom_call" | custom-call | flops 4000000 | bytes 3000000 | tf_op jit(solution)/shard_map/pallas_call | solution.py:434
  43.6 0.5 %collective-permute-done.6.far = f32[32,128]{1,0:T(8,128)S(1)} collective-permute-done((f32[32,128]{1,0:T(8,128)S(1)}, f32[32,128]{1,0:T(8,128)S(1)}, u32[]{:S(2)}, u32[]{:S(2)}) %collective-permute-start.6) | collective-permute-done | bytes 16416 | tf_op jit(solution)/shard_map/ppermute | solution.py:433
  44.0 0.9 %shard_map.47 = f32[32,1024]{1,0:T(8,128)} custom-call(f32[32,128]{1,0:T(8,128)S(1)} %get-tuple-element.54.message, f32[32,128]{1,0:T(8,128)S(1)} %collective-permute-done.6.far, f32[32,1024]{1,0:T(8,128)S(1)} %shard_map.46.local, f32[32,1024]{1,0:T(8,128)S(1)} %get-tuple-element.53.hy), custom_call_target="tpu_custom_call" | custom-call | tf_op jit(solution)/shard_map/pallas_call | solution.py:435
  (3 shorter events, 0.1 us)
Async XLA Ops:
  0.0 5.8 %collective-permute-start = (f32[2,1,16,1024]{3,2,1,0:T(8,128)}, f32[2,1,16,1024]{3,2,1,0:T(8,128)S(1)}, u32[]{:S(2)}, u32[]{:S(2)}) collective-permute-start(f32[2,1,16,1024]{3,2,1,0:T(8,128)} %param.3), channel_id=1, source_target_pairs={{0,1},{1,0},{2,3},{3,2},{4,5},{5,4},{6,7},{7,6},{8,9},{9,8},{10,11... | collective-permute-start | bytes 393224 | tf_op jit(solution)/shard_map/ppermute | solution.py:391
  2.0 5.0 %collective-permute-start.1 = (f32[2,1,16,1024]{3,2,1,0:T(8,128)}, f32[2,1,16,1024]{3,2,1,0:T(8,128)S(1)}, u32[]{:S(2)}, u32[]{:S(2)}) collective-permute-start(f32[2,1,16,1024]{3,2,1,0:T(8,128)} %param.5), channel_id=1, source_target_pairs={{0,1},{1,0},{2,3},{3,2},{4,5},{5,4},{6,7},{7,6},{8,9},{9,8},{10,11... | collective-permute-start | bytes 393224 | tf_op jit(solution)/shard_map/ppermute | solution.py:392
  7.1 3.7 %collective-permute-start.2 = (f32[7,8,128]{2,1,0:T(8,128)S(1)}, f32[7,8,128]{2,1,0:T(8,128)S(1)}, u32[]{:S(2)}, u32[]{:S(2)}) collective-permute-start(f32[7,8,128]{2,1,0:T(8,128)S(1)} %get-tuple-element.40), channel_id=1, source_target_pairs={{0,4},{4,0},{8,12},{12,8},{16,20},{20,16},{24,28},{28,24},{32,36},... | collective-permute-start | bytes 86024 | tf_op jit(solution)/shard_map/ppermute | solution.py:415
  10.9 2.8 %collective-permute-start.3 = (f32[7,8,128]{2,1,0:T(8,128)S(1)}, f32[7,8,128]{2,1,0:T(8,128)S(1)}, u32[]{:S(2)}, u32[]{:S(2)}) collective-permute-start(f32[7,8,128]{2,1,0:T(8,128)S(1)} %get-tuple-element.41.mine), channel_id=1, source_target_pairs={{0,8},{4,12},{8,0},{12,4},{16,24},{20,28},{24,16},{28,20},{32,40},... | collective-permute-start | bytes 86024 | tf_op jit(solution)/shard_map/ppermute | solution.py:419
  13.7 4.0 %collective-permute-start.4 = (f32[7,8,128]{2,1,0:T(8,128)S(1)}, f32[7,8,128]{2,1,0:T(8,128)S(1)}, u32[]{:S(2)}, u32[]{:S(2)}) collective-permute-start(f32[7,8,128]{2,1,0:T(8,128)S(1)} %get-tuple-element.42.mine), channel_id=1, source_target_pairs={{0,24},{4,28},{8,16},{12,20},{16,8},{20,12},{24,0},{28,4},{32,56},... | collective-permute-start | bytes 86024 | tf_op jit(solution)/shard_map/ppermute | solution.py:421
  34.9 4.9 %collective-permute-start.5 = (f32[2,8,128]{2,1,0:T(8,128)S(1)}, f32[2,8,128]{2,1,0:T(8,128)S(1)}, u32[]{:S(2)}, u32[]{:S(2)}) collective-permute-start(f32[2,8,128]{2,1,0:T(8,128)S(1)} %get-tuple-element.48), channel_id=1, source_target_pairs={{0,4},{4,0},{8,12},{12,8},{16,20},{20,16},{24,28},{28,24},{32,36},... | collective-permute-start | bytes 24584 | tf_op jit(solution)/shard_map/ppermute | solution.py:429
  39.9 4.1 %collective-permute-start.6 = (f32[32,128]{1,0:T(8,128)S(1)}, f32[32,128]{1,0:T(8,128)S(1)}, u32[]{:S(2)}, u32[]{:S(2)}) collective-permute-start(f32[32,128]{1,0:T(8,128)S(1)} %get-tuple-element.54.message), channel_id=1, source_target_pairs={{0,2},{2,0},{1,3},{3,1},{4,6},{6,4},{5,7},{7,5},{8,10},{10,8},{9,1... | collective-permute-start | bytes 49160 | tf_op jit(solution)/shard_map/ppermute | solution.py:433

commit v6 on v4

--- a/solution.py
+++ b/solution.py
@@ -254,20 +254,44 @@
     return (a * left[0] + b * right[0], a * left[1] + b * right[1], a * left[2] + b * right[2] + c)
 
 
-def chip_kernel(keep, got, chip, middle):
-    even = lax.axis_index("gx") % 2 == 0
-    mine, other = load(keep), load(got)
-    first = [jnp.where(even, m, o) for m, o in zip(mine, other)]
-    second = [jnp.where(even, o, m) for m, o in zip(mine, other)]
+def join(first, second):
     tail, start = behind((first[6] + second[5]) * 0.5, second[:5])
     element, end = merge(first[:5], tail)
-    for n, value in enumerate((*element, first[5], second[6])):
-        chip[n] = value
-    for n, value in enumerate((*end, *start)):
-        middle[n] = value
-
-
-def slab_kernel(chip, far1, far2, far3, middle, message, nodes):
+    return (*element, first[5], second[6]), (*end, *start)
+
+
+def ordered(low, mine, other):
+    first = [jnp.where(low, m, o) for m, o in zip(mine, other)]
+    second = [jnp.where(low, o, m) for m, o in zip(mine, other)]
+    return first, second
+
+
+def join_kernel(bit, mine, other, both, rows):
+    low = lax.axis_index("gx") // bit % 2 == 0
+    element, nodes = join(*ordered(low, load(mine), load(other)))
+    for n, value in enumerate(element):
+        both[n] = value
+    for n, value in enumerate(nodes):
+        rows[n] = value
+
+
+def above_kernel(first_up, second_up, both):
+    two, one = ordered(lax.axis_index("gx") < 16, load(first_up), load(second_up))
+    element, _ = join(one, two)
+    for n, value in enumerate(element):
+        both[n] = value
+
+
+def half_kernel(mine, other, after, both, again):
+    del after
+    low = lax.axis_index("gx") // 16 % 2 == 0
+    element, _ = join(*ordered(low, load(mine), load(other)))
+    for n, value in enumerate(element):
+        both[n] = value
+    again[...] = mine[...]
+
+
+def slab_kernel(chip, far1, far2, far3, middle, slab, nodes):
     y = lax.axis_index("gx") // 2 % 4
     arrived = [load(chip), load(far1), load(far2), load(far3)]
     chips = []
@@ -285,8 +309,7 @@
         inner.append(node)
         fronts.append(front)
     for n, value in enumerate((*element, chips[0][5], chips[3][6])):
-        for j in range(8):
-            message[j, n] = value
+        slab[n] = value
     zero, one = jnp.zeros((8, 128), F32), jnp.ones((8, 128), F32)
     left = (one, zero, zero)
     lasts = [(zero, one, zero)]
@@ -305,22 +328,31 @@
             nodes[n, m] = trio[m]
 
 
-def ends_kernel(got, nodes, mine, other):
+def ends_kernel(pair, inner_low, half_down, inner_high, half_up, pair_rows, nodes, mine, other):
     gx = lax.axis_index("gx")
-    slab = gx // 8
+    z = gx // 8
     even = gx % 2 == 0
-    zero = jnp.zeros((8, 128), F32)
-    slabs, fronts = [], []
-    for z in range(8):
-        face = got[z, 5] * 0.5 if z == 0 else (got[z - 1, 6] + got[z, 5]) * 0.5
-        tail, front = behind(face, tuple(got[z, n] for n in range(5)))
-        slabs.append(tail)
+    lower = z < 4
+    own = load(pair)
+    inner = [jnp.where(lower, a, b) for a, b in zip(load(inner_low), load(inner_high))]
+    one, two = ordered(z // 2 % 2 == 0, own, inner)
+    below, above = load(half_down), load(half_up)
+    chain = [
+        [jnp.where(lower, a, b) for a, b in zip(one, below)],
+        [jnp.where(lower, a, b) for a, b in zip(two, one)],
+        [jnp.where(lower, a, b) for a, b in zip(above, two)],
+    ]
+    tails, fronts = [], []
+    for k in range(3):
+        face = chain[k][5] * 0.5 if k == 0 else (chain[k - 1][6] + chain[k][5]) * 0.5
+        tail, front = behind(face, chain[k][:5])
+        tails.append(tail)
         fronts.append(front)
-    g, _, conduct, _, right = slabs[0]
+    g, _, conduct, _, right = tails[0]
     conduct = conduct + g
     ratios, offsets = [], []
-    for z in range(1, 8):
-        g, sl, sr, rl, rr = slabs[z]
+    for k in (1, 2):
+        g, sl, sr, rl, rr = tails[k]
         conduct = conduct + sl
         right = right + rl
         inverse = 1.0 / (conduct + g)
@@ -329,17 +361,23 @@
         offsets.append(right * inverse)
         conduct = sr + f * conduct
         right = rr + f * right
-    value = right / (conduct + got[7, 6] * 0.5)
-    values = [value]
-    for k in range(6, -1, -1):
-        value = ratios[k] * value + offsets[k]
-        values.append(value)
-    values = [zero] + values[::-1]
-    first, last = zero, zero
-    for z in range(8):
-        a, b, c = fronts[z]
-        first = jnp.where(slab == z, a * values[z] + b * values[z + 1] + c, first)
-        last = jnp.where(slab == z, values[z + 1], last)
+    last2 = right / (conduct + chain[2][6] * 0.5)
+    last1 = ratios[1] * last2 + offsets[1]
+    last0 = ratios[0] * last1 + offsets[0]
+    lasts = (last0, last1, last2)
+    firsts = []
+    for k in range(3):
+        a, b, c = fronts[k]
+        firsts.append(b * lasts[k] + c if k == 0 else a * lasts[k - 1] + b * lasts[k] + c)
+    place = z // 2 % 2 + jnp.where(lower, 0, 1)
+    first, last = firsts[0], lasts[0]
+    for k in (1, 2):
+        first = jnp.where(place == k, firsts[k], first)
+        last = jnp.where(place == k, lasts[k], last)
+    end = pair_rows[0] * first + pair_rows[1] * last + pair_rows[2]
+    start = pair_rows[3] * end + pair_rows[4] * last + pair_rows[5]
+    left = z % 2 == 0
+    first, last = jnp.where(left, first, start), jnp.where(left, end, last)
     row = [nodes[n, 0] * first + nodes[n, 1] * last + nodes[n, 2] for n in range(4)]
     for n in range(2):
         mine[n] = jnp.where(even, row[n], row[n + 2])
@@ -387,12 +425,23 @@
     )
 
 
-SLAB_GROUPS = [[8 * b + a for b in range(8)] for a in range(8)]
 CORES = [(i, i ^ 1) for i in range(64)]
 
 
 def chips_on(shift):
     return [(i // 8 * 8 + (i + 2 * shift) % 8, i) for i in range(64)]
+
+
+def slabs(pairs):
+    return [(8 * a + i, 8 * b + i) for a, b in pairs for i in range(8)]
+
+
+SLABS = slabs([(z, z ^ 1) for z in range(8)])
+LOWER = slabs([(z, z ^ 2) for z in range(4)])
+UPPER = slabs([(z, z ^ 2) for z in range(4, 8)])
+UP_FIRST = slabs([(7, 0), (6, 1), (5, 2), (4, 3)])
+UP_SECOND = slabs([(5, 0), (4, 1), (7, 2), (6, 3)])
+DOWN = slabs([(0, 5), (1, 4), (2, 7), (3, 6)])
 
 
 def local(fields, kappa, vertical):
@@ -424,15 +473,24 @@
     )
     got = lax.ppermute(send, "gx", CORES)
     local_x = call(local_x_kernel, full, [VMEM] * 4, flops=1_000_000, size=1_000_000)(source, ax, bx, qx)
-    chip, middle = call(chip_kernel, (half, shape(6, 8, 128)), [VMEM] * 2)(keep, got)
+    rows = shape(6, 8, 128)
+    chip, middle = call(functools.partial(join_kernel, 1), (half, rows), [VMEM] * 2)(keep, got)
     far = [lax.ppermute(chip, "gx", chips_on(shift)) for shift in (2, 1, 3)]
-    message, nodes = call(
-        slab_kernel, (shape(8, 7, 8, 128), shape(4, 3, 8, 128)), [VMEM] * 5
-    )(chip, far[1], far[0], far[2], middle)
-    got = lax.all_to_all(message, "gx", 0, 0, axis_index_groups=SLAB_GROUPS, tiled=True)
+    slab, nodes = call(slab_kernel, (half, shape(4, 3, 8, 128)), [VMEM] * 5)(
+        chip, far[1], far[0], far[2], middle
+    )
+    got = lax.ppermute(slab, "gx", SLABS)
+    pair, pair_rows = call(functools.partial(join_kernel, 8), (half, rows), [VMEM] * 2)(slab, got)
+    first_up = lax.ppermute(pair, "gx", UP_FIRST)
+    second_up = lax.ppermute(pair, "gx", UP_SECOND)
+    inner_low = lax.ppermute(pair, "gx", LOWER)
+    half_up = call(above_kernel, half, [VMEM] * 2)(first_up, second_up)
+    lower, again = call(half_kernel, (half, half), [VMEM] * 3)(pair, inner_low, half_up)
+    half_down = lax.ppermute(lower, "gx", DOWN)
+    inner_high = lax.ppermute(again, "gx", UPPER)
     mine, other = call(
-        ends_kernel, (shape(2, 8, 128), shape(2, 8, 128)), [VMEM, VMEM]
-    )(got, nodes)
+        ends_kernel, (shape(2, 8, 128), shape(2, 8, 128)), [VMEM] * 7
+    )(pair, inner_low, half_down, inner_high, half_up, pair_rows, nodes)
     other = lax.ppermute(other, "gx", CORES)
     section, message = call(
         section_kernel, (full, shape(ALL, 128)), [VMEM] * 7

time: 44.4 us -> 45.1 us (1.016)
  blocking collectives: 17.1 us -> 0 us
  starting transfers between devices: 15.9 us -> 29.7 us
  waiting for transfers between devices: 5.12 us -> 9 us
    all_to_all x1 -> x0, blocking collectives: 17.1 us -> none  [local(): lax.all_to_all(message, 'gx', 0, 0, axis_index_groups=SLAB_GROUPS, tiled=...]
    ppermute x0 -> x6, starting transfers between devices: none -> 12.4 us  [the longest x1 4.9 us: local(): inner_low = lax.ppermute(pair, 'gx', LOWER)]
    ppermute x0 -> x6, waiting for transfers between devices: none -> 3.89 us  [the longest x1 1.33 us: local(): second_up = lax.ppermute(pair, 'gx', UP_SECOND)]
    ppermute x1, starting transfers between devices: 3.2 us -> 4.55 us  [local(): other = lax.ppermute(other, 'gx', CORES)]
  transfers between devices with their start and end apart: 8 -> 14, of which waited for: 6 -> 10; matrix products, arithmetic and copies ran while one was open for 0% -> 0% of each run, Pallas kernels for 11% -> 11%
where the time goes in v6:
time: 45.1 us; the launch traced here: 44.9 us
  starting transfers between devices  29.7 us (66%)
  waiting for transfers between devices  9 us (20%)
  Pallas kernels  6.15 us (14%)
    ppermute x3, starting transfers between devices, local(): far = [lax.ppermute(chip, 'gx', chips_on(shift)) for shift in (2, 1, 3)]  5 us
    ppermute x1, starting transfers between devices, local(): inner_low = lax.ppermute(pair, 'gx', LOWER)  4.9 us
    ppermute x1, starting transfers between devices, local(): other = lax.ppermute(other, 'gx', CORES)  4.55 us
    ppermute x1, starting transfers between devices, local(): got = lax.ppermute(send, 'gx', CORES)  2.87 us
    ppermute x1, starting transfers between devices, local(): far = lax.ppermute(message, 'gy', swap)  2.76 us
    ppermute x1, starting transfers between devices, local(): half_down = lax.ppermute(lower, 'gx', DOWN)  2.55 us
    pallas_call x1, Pallas kernels, local(): call(factor_y_kernel, (shape(10, 256, 128), shape(10, 256, 128), standing...  2.14 us
    ppermute x1, starting transfers between devices, local(): fields_far = lax.ppermute(fields, 'gz', swap)  2.04 us
  transfers between devices with their start and end apart: 14, of which 10 were waited for; matrix products, arithmetic and copies ran while one was open for 0% of the time, Pallas kernels for 11%

profile of v6, /device:TPU:1, one launch (start us, length us, event | category | flops | bytes accessed | tf_op | source)
XLA Modules:
  0.0 44.9 jit_solution(4974286360439602695)
XLA Ops:
  0.0 2.0 %collective-permute-start = (f32[2,1,16,1024]{3,2,1,0:T(8,128)}, f32[2,1,16,1024]{3,2,1,0:T(8,128)S(1)}, u32[]{:S(2)}, u32[]{:S(2)}) collective-permute-start(f32[2,1,16,1024]{3,2,1,0:T(8,128)} %param.3), channel_id=1, source_target_pairs={{0,1},{1,0},{2,3},{3,2},{4,5},{5,4},{6,7},{7,6},{8,9},{9,8},{10,11... | collective-permute-start | bytes 393224 | tf_op jit(solution)/shard_map/ppermute | solution.py:450
  2.0 0.0 collective-permute-start.1
  2.1 1.6 %shard_map.37 = (f32[32,1024]{1,0:T(8,128)S(1)}, f32[32,1024]{1,0:T(8,128)S(1)}, f32[32,1024]{1,0:T(8,128)S(1)}, f32[4,32,1024]{2,1,0:T(8,128)S(1)}, f32[4,32,10...) custom-call(f32[32,1024]{1,0:T(8,128)} %bitcast.11, ...), custom_call_target="tpu_custom_call" | custom-call | flops 4000000 | bytes 2000000 | tf_op jit(solution)/shard_map/pallas_call | solution.py:455
  3.7 2.1 %shard_map.38 = (f32[10,256,128]{2,1,0:T(8,128)S(1)}, f32[10,256,128]{2,1,0:T(8,128)S(1)}, f32[256,128]{1,0:T(8,128)S(1)}, f32[32,1024]{1,0:T(8,128)S(1)}, f32[32,128]{1,0:T(8,128)S(1)}) custom-call(f32[32,1024]{1,0:T(8,128)S(1)} %get-tuple-element.39.kappa), custom_call_target="tpu_custom_call" | custom-call | flops 20000000 | bytes 4000000 | tf_op jit(solution)/shard_map/pallas_call | solution.py:463
  5.8 0.0 collective-permute-done
  5.8 1.2 %collective-permute-done.1 = f32[2,1,16,1024]{3,2,1,0:T(8,128)S(1)} collective-permute-done((f32[2,1,16,1024]{3,2,1,0:T(8,128)}, f32[2,1,16,1024]{3,2,1,0:T(8,128)S(1)}, u32[]{:S(2)}, u32[]{:S(2)}) %collective-permute-start.1) | collective-permute-done | bytes 131104 | tf_op jit(solution)/shard_map/ppermute | solution.py:451
  7.0 0.1 shard_map.39
  7.1 2.9 %collective-permute-start.2 = (f32[7,8,128]{2,1,0:T(8,128)S(1)}, f32[7,8,128]{2,1,0:T(8,128)S(1)}, u32[]{:S(2)}, u32[]{:S(2)}) collective-permute-start(f32[7,8,128]{2,1,0:T(8,128)S(1)} %get-tuple-element.42), channel_id=1, source_target_pairs={{0,4},{4,0},{8,12},{12,8},{16,20},{20,16},{24,28},{28,24},{32,36},... | collective-permute-start | bytes 86024 | tf_op jit(solution)/shard_map/ppermute | solution.py:474
  10.0 0.9 %collective-permute-done.2.other = f32[7,8,128]{2,1,0:T(8,128)S(1)} collective-permute-done((f32[7,8,128]{2,1,0:T(8,128)S(1)}, f32[7,8,128]{2,1,0:T(8,128)S(1)}, u32[]{:S(2)}, u32[]{:S(2)}) %collective-permute-start.2) | collective-permute-done | bytes 28704 | tf_op jit(solution)/shard_map/ppermute | solution.py:474
  10.9 1.3 %collective-permute-start.5 = (f32[7,8,128]{2,1,0:T(8,128)S(1)}, f32[7,8,128]{2,1,0:T(8,128)S(1)}, u32[]{:S(2)}, u32[]{:S(2)}) collective-permute-start(f32[7,8,128]{2,1,0:T(8,128)S(1)} %get-tuple-element.43.chip), channel_id=1, source_target_pairs={{24,0},{28,4},{0,8},{4,12},{8,16},{12,20},{16,24},{20,28},{56,32},... | collective-permute-start | bytes 86024 | tf_op jit(solution)/shard_map/ppermute | solution.py:478
  12.2 2.6 %collective-permute-start.4 = (f32[7,8,128]{2,1,0:T(8,128)S(1)}, f32[7,8,128]{2,1,0:T(8,128)S(1)}, u32[]{:S(2)}, u32[]{:S(2)}) collective-permute-start(f32[7,8,128]{2,1,0:T(8,128)S(1)} %get-tuple-element.43.chip), channel_id=1, source_target_pairs={{16,0},{20,4},{24,8},{28,12},{0,16},{4,20},{8,24},{12,28},{48,32},... | collective-permute-start | bytes 86024 | tf_op jit(solution)/shard_map/ppermute | solution.py:478
  14.8 1.1 %collective-permute-start.3 = (f32[7,8,128]{2,1,0:T(8,128)S(1)}, f32[7,8,128]{2,1,0:T(8,128)S(1)}, u32[]{:S(2)}, u32[]{:S(2)}) collective-permute-start(f32[7,8,128]{2,1,0:T(8,128)S(1)} %get-tuple-element.43.chip), channel_id=1, source_target_pairs={{8,0},{12,4},{16,8},{20,12},{24,16},{28,20},{0,24},{4,28},{40,32},... | collective-permute-start | bytes 86024 | tf_op jit(solution)/shard_map/ppermute | solution.py:478
  15.9 0.0 collective-permute-done.5.far3
  15.9 0.5 %collective-permute-done.4.far2 = f32[7,8,128]{2,1,0:T(8,128)S(1)} collective-permute-done((f32[7,8,128]{2,1,0:T(8,128)S(1)}, f32[7,8,128]{2,1,0:T(8,128)S(1)}, u32[]{:S(2)}, u32[]{:S(2)}) %collective-permute-start.4) | collective-permute-done | bytes 28704 | tf_op jit(solution)/shard_map/ppermute | solution.py:478
  16.4 1.4 %collective-permute-done.3.far1 = f32[7,8,128]{2,1,0:T(8,128)S(1)} collective-permute-done((f32[7,8,128]{2,1,0:T(8,128)S(1)}, f32[7,8,128]{2,1,0:T(8,128)S(1)}, u32[]{:S(2)}, u32[]{:S(2)}) %collective-permute-start.3) | collective-permute-done | bytes 28704 | tf_op jit(solution)/shard_map/ppermute | solution.py:478
  17.8 0.1 shard_map.41
  17.9 1.7 %collective-permute-start.6 = (f32[7,8,128]{2,1,0:T(8,128)S(1)}, f32[7,8,128]{2,1,0:T(8,128)S(1)}, u32[]{:S(2)}, u32[]{:S(2)}) collective-permute-start(f32[7,8,128]{2,1,0:T(8,128)S(1)} %get-tuple-element.45.mine), channel_id=1, source_target_pairs={{0,32},{4,36},{8,40},{12,44},{16,48},{20,52},{24,56},{28,60},{32,0... | collective-permute-start | bytes 86024 | tf_op jit(solution)/shard_map/ppermute | solution.py:482
  19.6 1.3 %collective-permute-done.6.other = f32[7,8,128]{2,1,0:T(8,128)S(1)} collective-permute-done((f32[7,8,128]{2,1,0:T(8,128)S(1)}, f32[7,8,128]{2,1,0:T(8,128)S(1)}, u32[]{:S(2)}, u32[]{:S(2)}) %collective-permute-start.6) | collective-permute-done | bytes 28704 | tf_op jit(solution)/shard_map/ppermute | solution.py:482
  20.9 1.3 %collective-permute-start.9 = (f32[7,8,128]{2,1,0:T(8,128)S(1)}, f32[7,8,128]{2,1,0:T(8,128)S(1)}, u32[]{:S(2)}, u32[]{:S(2)}) collective-permute-start(f32[7,8,128]{2,1,0:T(8,128)S(1)} %get-tuple-element.46.mine.pair), channel_id=1, source_target_pairs={{160,0},{164,4},{168,8},{172,12},{176,16},{180,20},{184,24},{188,2... | collective-permute-start | bytes 86024 | tf_op jit(solution)/shard_map/ppermute | solution.py:485
  22.2 1.3 %collective-permute-start.8 = (f32[7,8,128]{2,1,0:T(8,128)S(1)}, f32[7,8,128]{2,1,0:T(8,128)S(1)}, u32[]{:S(2)}, u32[]{:S(2)}) collective-permute-start(f32[7,8,128]{2,1,0:T(8,128)S(1)} %get-tuple-element.46.mine.pair), channel_id=1, source_target_pairs={{224,0},{228,4},{232,8},{236,12},{240,16},{244,20},{248,24},{252,2... | collective-permute-start | bytes 86024 | tf_op jit(solution)/shard_map/ppermute | solution.py:484
  23.5 4.9 %collective-permute-start.7 = (f32[7,8,128]{2,1,0:T(8,128)S(1)}, f32[7,8,128]{2,1,0:T(8,128)S(1)}, u32[]{:S(2)}, u32[]{:S(2)}) collective-permute-start(f32[7,8,128]{2,1,0:T(8,128)S(1)} %get-tuple-element.46.mine.pair), channel_id=1, source_target_pairs={{0,64},{4,68},{8,72},{12,76},{16,80},{20,84},{24,88},{28,92},{32,9... | collective-permute-start | bytes 86024 | tf_op jit(solution)/shard_map/ppermute | solution.py:486
  28.4 1.3 %collective-permute-done.9.second_up = f32[7,8,128]{2,1,0:T(8,128)S(1)} collective-permute-done((f32[7,8,128]{2,1,0:T(8,128)S(1)}, f32[7,8,128]{2,1,0:T(8,128)S(1)}, u32[]{:S(2)}, u32[]{:S(2)}) %collective-permute-start.9) | collective-permute-done | bytes 28704 | tf_op jit(solution)/shard_map/ppermute | solution.py:485
  29.7 1.0 %collective-permute-done.8.first_up = f32[7,8,128]{2,1,0:T(8,128)S(1)} collective-permute-done((f32[7,8,128]{2,1,0:T(8,128)S(1)}, f32[7,8,128]{2,1,0:T(8,128)S(1)}, u32[]{:S(2)}, u32[]{:S(2)}) %collective-permute-start.8) | collective-permute-done | bytes 28704 | tf_op jit(solution)/shard_map/ppermute | solution.py:484
  30.7 0.0 collective-permute-done.7.other.inner_low
  30.8 2.5 %collective-permute-start.10 = (f32[7,8,128]{2,1,0:T(8,128)S(1)}, f32[7,8,128]{2,1,0:T(8,128)S(1)}, u32[]{:S(2)}, u32[]{:S(2)}) collective-permute-start(f32[7,8,128]{2,1,0:T(8,128)S(1)} %get-tuple-element.47), channel_id=1, source_target_pairs={{0,160},{4,164},{8,168},{12,172},{16,176},{20,180},{24,184},{28,18... | collective-permute-start | bytes 86024 | tf_op jit(solution)/shard_map/ppermute | solution.py:489
  33.4 0.7 %collective-permute-start.11 = (f32[7,8,128]{2,1,0:T(8,128)S(1)}, f32[7,8,128]{2,1,0:T(8,128)S(1)}, u32[]{:S(2)}, u32[]{:S(2)}) collective-permute-start(f32[7,8,128]{2,1,0:T(8,128)S(1)} %get-tuple-element.48), channel_id=1, source_target_pairs={{128,192},{132,196},{136,200},{140,204},{144,208},{148,212},{152,2... | collective-permute-start | bytes 86024 | tf_op jit(solution)/shard_map/ppermute | solution.py:490
  34.0 0.3 collective-permute-done.10.half_down
  34.3 0.0 collective-permute-done.11.inner_high
  34.3 0.1 shard_map.45
  34.4 4.5 %collective-permute-start.12 = (f32[2,8,128]{2,1,0:T(8,128)S(1)}, f32[2,8,128]{2,1,0:T(8,128)S(1)}, u32[]{:S(2)}, u32[]{:S(2)}) collective-permute-start(f32[2,8,128]{2,1,0:T(8,128)S(1)} %get-tuple-element.52), channel_id=1, source_target_pairs={{0,4},{4,0},{8,12},{12,8},{16,20},{20,16},{24,28},{28,24},{32,36},... | collective-permute-start | bytes 24584 | tf_op jit(solution)/shard_map/ppermute | solution.py:494
  39.0 0.1 shard_map.46.local
  39.1 0.7 %collective-permute-done.12.other = f32[2,8,128]{2,1,0:T(8,128)S(1)} collective-permute-done((f32[2,8,128]{2,1,0:T(8,128)S(1)}, f32[2,8,128]{2,1,0:T(8,128)S(1)}, u32[]{:S(2)}, u32[]{:S(2)}) %collective-permute-start.12) | collective-permute-done | bytes 8224 | tf_op jit(solution)/shard_map/ppermute | solution.py:494
  39.8 0.1 shard_map.47
  39.9 2.8 %collective-permute-start.13 = (f32[32,128]{1,0:T(8,128)S(1)}, f32[32,128]{1,0:T(8,128)S(1)}, u32[]{:S(2)}, u32[]{:S(2)}) collective-permute-start(f32[32,128]{1,0:T(8,128)S(1)} %get-tuple-element.58.message), channel_id=1, source_target_pairs={{0,2},{2,0},{1,3},{3,1},{4,6},{6,4},{5,7},{7,5},{8,10},{10,8},{9,1... | collective-permute-start | bytes 49160 | tf_op jit(solution)/shard_map/ppermute | solution.py:498
  42.7 0.9 %shard_map.48.local = f32[32,1024]{1,0:T(8,128)S(1)} custom-call(f32[32,1024]{1,0:T(8,128)S(1)} %get-tuple-element.59.section, f32[10,256,128]{2,1,0:T(8,128)S(1)} %get-tuple-element.60.ay, f32[10,256,128]{2,1,0:T(8,128)S(1)} %get-tuple-element.61.by, f32[256,128]{1,0:T(8,128)S(1)} %get-tuple-element.62.qy), custom_call_target="tpu_custom_call" | custom-call | flops 4000000 | bytes 3000000 | tf_op jit(solution)/shard_map/pallas_call | solution.py:499
  43.6 0.5 %collective-permute-done.13.far = f32[32,128]{1,0:T(8,128)S(1)} collective-permute-done((f32[32,128]{1,0:T(8,128)S(1)}, f32[32,128]{1,0:T(8,128)S(1)}, u32[]{:S(2)}, u32[]{:S(2)}) %collective-permute-start.13) | collective-permute-done | bytes 16416 | tf_op jit(solution)/shard_map/ppermute | solution.py:498
  44.0 0.9 %shard_map.49 = f32[32,1024]{1,0:T(8,128)} custom-call(f32[32,128]{1,0:T(8,128)S(1)} %get-tuple-element.58.message, f32[32,128]{1,0:T(8,128)S(1)} %collective-permute-done.13.far, f32[32,1024]{1,0:T(8,128)S(1)} %shard_map.48.local, f32[32,1024]{1,0:T(8,128)S(1)} %get-tuple-element.57.hy), custom_call_target="tpu_custom_call" | custom-call | tf_op jit(solution)/shard_map/pallas_call | solution.py:500
  (4 shorter events, 0.1 us)
Async XLA Ops:
  0.0 5.8 %collective-permute-start = (f32[2,1,16,1024]{3,2,1,0:T(8,128)}, f32[2,1,16,1024]{3,2,1,0:T(8,128)S(1)}, u32[]{:S(2)}, u32[]{:S(2)}) collective-permute-start(f32[2,1,16,1024]{3,2,1,0:T(8,128)} %param.3), channel_id=1, source_target_pairs={{0,1},{1,0},{2,3},{3,2},{4,5},{5,4},{6,7},{7,6},{8,9},{9,8},{10,11... | collective-permute-start | bytes 393224 | tf_op jit(solution)/shard_map/ppermute | solution.py:450
  2.0 5.0 %collective-permute-start.1 = (f32[2,1,16,1024]{3,2,1,0:T(8,128)}, f32[2,1,16,1024]{3,2,1,0:T(8,128)S(1)}, u32[]{:S(2)}, u32[]{:S(2)}) collective-permute-start(f32[2,1,16,1024]{3,2,1,0:T(8,128)} %param.5), channel_id=1, source_target_pairs={{0,1},{1,0},{2,3},{3,2},{4,5},{5,4},{6,7},{7,6},{8,9},{9,8},{10,11... | collective-permute-start | bytes 393224 | tf_op jit(solution)/shard_map/ppermute | solution.py:451
  7.1 3.7 %collective-permute-start.2 = (f32[7,8,128]{2,1,0:T(8,128)S(1)}, f32[7,8,128]{2,1,0:T(8,128)S(1)}, u32[]{:S(2)}, u32[]{:S(2)}) collective-permute-start(f32[7,8,128]{2,1,0:T(8,128)S(1)} %get-tuple-element.42), channel_id=1, source_target_pairs={{0,4},{4,0},{8,12},{12,8},{16,20},{20,16},{24,28},{28,24},{32,36},... | collective-permute-start | bytes 86024 | tf_op jit(solution)/shard_map/ppermute | solution.py:474
  10.9 5.0 %collective-permute-start.5 = (f32[7,8,128]{2,1,0:T(8,128)S(1)}, f32[7,8,128]{2,1,0:T(8,128)S(1)}, u32[]{:S(2)}, u32[]{:S(2)}) collective-permute-start(f32[7,8,128]{2,1,0:T(8,128)S(1)} %get-tuple-element.43.chip), channel_id=1, source_target_pairs={{24,0},{28,4},{0,8},{4,12},{8,16},{12,20},{16,24},{20,28},{56,32},... | collective-permute-start | bytes 86024 | tf_op jit(solution)/shard_map/ppermute | solution.py:478
  12.2 4.2 %collective-permute-start.4 = (f32[7,8,128]{2,1,0:T(8,128)S(1)}, f32[7,8,128]{2,1,0:T(8,128)S(1)}, u32[]{:S(2)}, u32[]{:S(2)}) collective-permute-start(f32[7,8,128]{2,1,0:T(8,128)S(1)} %get-tuple-element.43.chip), channel_id=1, source_target_pairs={{16,0},{20,4},{24,8},{28,12},{0,16},{4,20},{8,24},{12,28},{48,32},... | collective-permute-start | bytes 86024 | tf_op jit(solution)/shard_map/ppermute | solution.py:478
  14.8 3.0 %collective-permute-start.3 = (f32[7,8,128]{2,1,0:T(8,128)S(1)}, f32[7,8,128]{2,1,0:T(8,128)S(1)}, u32[]{:S(2)}, u32[]{:S(2)}) collective-permute-start(f32[7,8,128]{2,1,0:T(8,128)S(1)} %get-tuple-element.43.chip), channel_id=1, source_target_pairs={{8,0},{12,4},{16,8},{20,12},{24,16},{28,20},{0,24},{4,28},{40,32},... | collective-permute-start | bytes 86024 | tf_op jit(solution)/shard_map/ppermute | solution.py:478
  17.9 3.0 %collective-permute-start.6 = (f32[7,8,128]{2,1,0:T(8,128)S(1)}, f32[7,8,128]{2,1,0:T(8,128)S(1)}, u32[]{:S(2)}, u32[]{:S(2)}) collective-permute-start(f32[7,8,128]{2,1,0:T(8,128)S(1)} %get-tuple-element.45.mine), channel_id=1, source_target_pairs={{0,32},{4,36},{8,40},{12,44},{16,48},{20,52},{24,56},{28,60},{32,0... | collective-permute-start | bytes 86024 | tf_op jit(solution)/shard_map/ppermute | solution.py:482
  20.9 8.8 %collective-permute-start.9 = (f32[7,8,128]{2,1,0:T(8,128)S(1)}, f32[7,8,128]{2,1,0:T(8,128)S(1)}, u32[]{:S(2)}, u32[]{:S(2)}) collective-permute-start(f32[7,8,128]{2,1,0:T(8,128)S(1)} %get-tuple-element.46.mine.pair), channel_id=1, source_target_pairs={{160,0},{164,4},{168,8},{172,12},{176,16},{180,20},{184,24},{188,2... | collective-permute-start | bytes 86024 | tf_op jit(solution)/shard_map/ppermute | solution.py:485
  22.2 8.5 %collective-permute-start.8 = (f32[7,8,128]{2,1,0:T(8,128)S(1)}, f32[7,8,128]{2,1,0:T(8,128)S(1)}, u32[]{:S(2)}, u32[]{:S(2)}) collective-permute-start(f32[7,8,128]{2,1,0:T(8,128)S(1)} %get-tuple-element.46.mine.pair), channel_id=1, source_target_pairs={{224,0},{228,4},{232,8},{236,12},{240,16},{244,20},{248,24},{252,2... | collective-permute-start | bytes 86024 | tf_op jit(solution)/shard_map/ppermute | solution.py:484
  23.5 7.3 %collective-permute-start.7 = (f32[7,8,128]{2,1,0:T(8,128)S(1)}, f32[7,8,128]{2,1,0:T(8,128)S(1)}, u32[]{:S(2)}, u32[]{:S(2)}) collective-permute-start(f32[7,8,128]{2,1,0:T(8,128)S(1)} %get-tuple-element.46.mine.pair), channel_id=1, source_target_pairs={{0,64},{4,68},{8,72},{12,76},{16,80},{20,84},{24,88},{28,92},{32,9... | collective-permute-start | bytes 86024 | tf_op jit(solution)/shard_map/ppermute | solution.py:486
  30.8 3.5 %collective-permute-start.10 = (f32[7,8,128]{2,1,0:T(8,128)S(1)}, f32[7,8,128]{2,1,0:T(8,128)S(1)}, u32[]{:S(2)}, u32[]{:S(2)}) collective-permute-start(f32[7,8,128]{2,1,0:T(8,128)S(1)} %get-tuple-element.47), channel_id=1, source_target_pairs={{0,160},{4,164},{8,168},{12,172},{16,176},{20,180},{24,184},{28,18... | collective-permute-start | bytes 86024 | tf_op jit(solution)/shard_map/ppermute | solution.py:489
  33.4 1.0 %collective-permute-start.11 = (f32[7,8,128]{2,1,0:T(8,128)S(1)}, f32[7,8,128]{2,1,0:T(8,128)S(1)}, u32[]{:S(2)}, u32[]{:S(2)}) collective-permute-start(f32[7,8,128]{2,1,0:T(8,128)S(1)} %get-tuple-element.48), channel_id=1, source_target_pairs={{128,192},{132,196},{136,200},{140,204},{144,208},{148,212},{152,2... | collective-permute-start | bytes 86024 | tf_op jit(solution)/shard_map/ppermute | solution.py:490
  34.4 5.4 %collective-permute-start.12 = (f32[2,8,128]{2,1,0:T(8,128)S(1)}, f32[2,8,128]{2,1,0:T(8,128)S(1)}, u32[]{:S(2)}, u32[]{:S(2)}) collective-permute-start(f32[2,8,128]{2,1,0:T(8,128)S(1)} %get-tuple-element.52), channel_id=1, source_target_pairs={{0,4},{4,0},{8,12},{12,8},{16,20},{20,16},{24,28},{28,24},{32,36},... | collective-permute-start | bytes 24584 | tf_op jit(solution)/shard_map/ppermute | solution.py:494
  39.9 4.1 %collective-permute-start.13 = (f32[32,128]{1,0:T(8,128)S(1)}, f32[32,128]{1,0:T(8,128)S(1)}, u32[]{:S(2)}, u32[]{:S(2)}) collective-permute-start(f32[32,128]{1,0:T(8,128)S(1)} %get-tuple-element.58.message), channel_id=1, source_target_pairs={{0,2},{2,0},{1,3},{3,1},{4,6},{6,4},{5,7},{7,5},{8,10},{10,8},{9,1... | collective-permute-start | bytes 49160 | tf_op jit(solution)/shard_map/ppermute | solution.py:498

commit v7 on v4

--- a/solution.py
+++ b/solution.py
@@ -254,7 +254,7 @@
     return (a * left[0] + b * right[0], a * left[1] + b * right[1], a * left[2] + b * right[2] + c)
 
 
-def chip_kernel(keep, got, chip, middle):
+def chip_kernel(keep, got, message, middle):
     even = lax.axis_index("gx") % 2 == 0
     mine, other = load(keep), load(got)
     first = [jnp.where(even, m, o) for m, o in zip(mine, other)]
@@ -262,21 +262,15 @@
     tail, start = behind((first[6] + second[5]) * 0.5, second[:5])
     element, end = merge(first[:5], tail)
     for n, value in enumerate((*element, first[5], second[6])):
-        chip[n] = value
+        for m in range(4):
+            message[m, n] = value
     for n, value in enumerate((*end, *start)):
         middle[n] = value
 
 
-def slab_kernel(chip, far1, far2, far3, middle, message, nodes):
+def slab_kernel(got, middle, message, nodes):
     y = lax.axis_index("gx") // 2 % 4
-    arrived = [load(chip), load(far1), load(far2), load(far3)]
-    chips = []
-    for m in range(4):
-        chosen = arrived[0]
-        for shift in range(1, 4):
-            here = (y + shift) % 4 == m
-            chosen = [jnp.where(here, a, c) for a, c in zip(arrived[shift], chosen)]
-        chips.append(chosen)
+    chips = [tuple(got[m, n] for n in range(7)) for m in range(4)]
     element = chips[0][:5]
     inner, fronts = [], []
     for m in range(1, 4):
@@ -388,11 +382,8 @@
 
 
 SLAB_GROUPS = [[8 * b + a for b in range(8)] for a in range(8)]
+CHIP_GROUPS = [[8 * z + 2 * y + c for y in range(4)] for z in range(8) for c in range(2)]
 CORES = [(i, i ^ 1) for i in range(64)]
-
-
-def chips_on(shift):
-    return [(i // 8 * 8 + (i + 2 * shift) % 8, i) for i in range(64)]
 
 
 def local(fields, kappa, vertical):
@@ -424,11 +415,13 @@
     )
     got = lax.ppermute(send, "gx", CORES)
     local_x = call(local_x_kernel, full, [VMEM] * 4, flops=1_000_000, size=1_000_000)(source, ax, bx, qx)
-    chip, middle = call(chip_kernel, (half, shape(6, 8, 128)), [VMEM] * 2)(keep, got)
-    far = [lax.ppermute(chip, "gx", chips_on(shift)) for shift in (2, 1, 3)]
+    message, middle = call(
+        chip_kernel, (shape(4, 7, 8, 128), shape(6, 8, 128)), [VMEM] * 2
+    )(keep, got)
+    got = lax.all_to_all(message, "gx", 0, 0, axis_index_groups=CHIP_GROUPS, tiled=True)
     message, nodes = call(
-        slab_kernel, (shape(8, 7, 8, 128), shape(4, 3, 8, 128)), [VMEM] * 5
-    )(chip, far[1], far[0], far[2], middle)
+        slab_kernel, (shape(8, 7, 8, 128), shape(4, 3, 8, 128)), [VMEM] * 2
+    )(got, middle)
     got = lax.all_to_all(message, "gx", 0, 0, axis_index_groups=SLAB_GROUPS, tiled=True)
     mine, other = call(
         ends_kernel, (shape(2, 8, 128), shape(2, 8, 128)), [VMEM, VMEM]

time: 44.4 us -> 46.1 us (1.038)
  blocking collectives: 17.1 us -> 25.7 us
  starting transfers between devices: 15.9 us -> 10.9 us
  waiting for transfers between devices: 5.12 us -> 3.2 us
    all_to_all x0 -> x1, blocking collectives: none -> 8.66 us  [local(): lax.all_to_all(message, 'gx', 0, 0, axis_index_groups=CHIP_GROUPS, tiled=...]
    ppermute x3 -> x0, starting transfers between devices: 5 us -> none  [local(): far = [lax.ppermute(chip, 'gx', chips_on(shift)) for shift in (2, 1, 3)]]
    ppermute x3 -> x0, waiting for transfers between devices: 1.92 us -> none  [local(): far = [lax.ppermute(chip, 'gx', chips_on(shift)) for shift in (2, 1, 3)]]
  transfers between devices with their start and end apart: 8 -> 5, of which waited for: 6 -> 4; matrix products, arithmetic and copies ran while one was open for 0% -> 0% of each run, Pallas kernels for 11% -> 10%
where the time goes in v7:
time: 46.1 us; the launch traced here: 46 us
  blocking collectives  25.7 us (56%)
  starting transfers between devices  10.9 us (24%)
  Pallas kernels  6.09 us (13%)
  waiting for transfers between devices  3.2 us (7%)
    all_to_all x1, blocking collectives, local(): lax.all_to_all(message, 'gx', 0, 0, axis_index_groups=SLAB_GROUPS, tiled=...  17.1 us
    all_to_all x1, blocking collectives, local(): lax.all_to_all(message, 'gx', 0, 0, axis_index_groups=CHIP_GROUPS, tiled=...  8.66 us
    ppermute x1, starting transfers between devices, local(): other = lax.ppermute(other, 'gx', CORES)  3.19 us
    ppermute x1, starting transfers between devices, local(): got = lax.ppermute(send, 'gx', CORES)  2.87 us
    ppermute x1, starting transfers between devices, local(): far = lax.ppermute(message, 'gy', swap)  2.76 us
    pallas_call x1, Pallas kernels, local(): call(factor_y_kernel, (shape(10, 256, 128), shape(10, 256, 128), standing...  2.14 us
    ppermute x1, starting transfers between devices, local(): fields_far = lax.ppermute(fields, 'gz', swap)  2.04 us
    pallas_call x1, Pallas kernels, local(): call(factor_x_kernel, (full, full, full, shape(4, *grid), shape(4, *grid)...  1.62 us
  transfers between devices with their start and end apart: 5, of which 4 were waited for; matrix products, arithmetic and copies ran while one was open for 0% of the time, Pallas kernels for 10%

profile of v7, /device:TPU:1, one launch (start us, length us, event | category | flops | bytes accessed | tf_op | source)
XLA Modules:
  0.0 46.0 jit_solution(10882613341048791531)
XLA Ops:
  0.0 2.0 %collective-permute-start = (f32[2,1,16,1024]{3,2,1,0:T(8,128)}, f32[2,1,16,1024]{3,2,1,0:T(8,128)S(1)}, u32[]{:S(2)}, u32[]{:S(2)}) collective-permute-start(f32[2,1,16,1024]{3,2,1,0:T(8,128)} %param.3), channel_id=1, source_target_pairs={{0,1},{1,0},{2,3},{3,2},{4,5},{5,4},{6,7},{7,6},{8,9},{9,8},{10,11... | collective-permute-start | bytes 393224 | tf_op jit(solution)/shard_map/ppermute | solution.py:392
  2.0 0.0 collective-permute-start.1
  2.1 1.6 %shard_map.37 = (f32[32,1024]{1,0:T(8,128)S(1)}, f32[32,1024]{1,0:T(8,128)S(1)}, f32[32,1024]{1,0:T(8,128)S(1)}, f32[4,32,1024]{2,1,0:T(8,128)S(1)}, f32[4,32,10...) custom-call(f32[32,1024]{1,0:T(8,128)} %bitcast.11, ...), custom_call_target="tpu_custom_call" | custom-call | flops 4000000 | bytes 2000000 | tf_op jit(solution)/shard_map/pallas_call | solution.py:397
  3.7 2.1 %shard_map.38 = (f32[10,256,128]{2,1,0:T(8,128)S(1)}, f32[10,256,128]{2,1,0:T(8,128)S(1)}, f32[256,128]{1,0:T(8,128)S(1)}, f32[32,1024]{1,0:T(8,128)S(1)}, f32[32,128]{1,0:T(8,128)S(1)}) custom-call(f32[32,1024]{1,0:T(8,128)S(1)} %get-tuple-element.35.kappa), custom_call_target="tpu_custom_call" | custom-call | flops 20000000 | bytes 4000000 | tf_op jit(solution)/shard_map/pallas_call | solution.py:405
  5.8 0.0 collective-permute-done
  5.8 1.2 %collective-permute-done.1 = f32[2,1,16,1024]{3,2,1,0:T(8,128)S(1)} collective-permute-done((f32[2,1,16,1024]{3,2,1,0:T(8,128)}, f32[2,1,16,1024]{3,2,1,0:T(8,128)S(1)}, u32[]{:S(2)}, u32[]{:S(2)}) %collective-permute-start.1) | collective-permute-done | bytes 131104 | tf_op jit(solution)/shard_map/ppermute | solution.py:393
  7.0 0.1 shard_map.39
  7.1 2.9 %collective-permute-start.2 = (f32[7,8,128]{2,1,0:T(8,128)S(1)}, f32[7,8,128]{2,1,0:T(8,128)S(1)}, u32[]{:S(2)}, u32[]{:S(2)}) collective-permute-start(f32[7,8,128]{2,1,0:T(8,128)S(1)} %get-tuple-element.38), channel_id=1, source_target_pairs={{0,4},{4,0},{8,12},{12,8},{16,20},{20,16},{24,28},{28,24},{32,36},... | collective-permute-start | bytes 86024 | tf_op jit(solution)/shard_map/ppermute | solution.py:416
  10.0 0.9 %collective-permute-done.2.got = f32[7,8,128]{2,1,0:T(8,128)S(1)} collective-permute-done((f32[7,8,128]{2,1,0:T(8,128)S(1)}, f32[7,8,128]{2,1,0:T(8,128)S(1)}, u32[]{:S(2)}, u32[]{:S(2)}) %collective-permute-start.2) | collective-permute-done | bytes 28704 | tf_op jit(solution)/shard_map/ppermute | solution.py:416
  10.9 8.7 %all_to_all.10.got = f32[4,7,8,128]{3,2,1,0:T(8,128)S(1)} all-to-all(f32[4,7,8,128]{3,2,1,0:T(8,128)S(1)} %get-tuple-element.39), channel_id=1, replica_groups={{0,8,16,24},{4,12,20,28},{32,40,48,56},{36,44,52,60},{64,72,80,88},{68,..., dimensions={0} | all-to-all | bytes 229376 | tf_op jit(solution)/shard_map/all_to_all | solution.py:421
  19.6 0.1 shard_map.41
  19.6 17.1 %all_to_all.11.got = f32[8,7,8,128]{3,2,1,0:T(8,128)S(1)} all-to-all(f32[8,7,8,128]{3,2,1,0:T(8,128)S(1)} %get-tuple-element.41), channel_id=1, replica_groups={{0,32,64,96,128,160,192,224},{4,36,68,100,132,164,196,228},{8,40,72,104..., dimensions={0} | all-to-all | bytes 458752 | tf_op jit(solution)/shard_map/all_to_all | solution.py:425
  36.7 0.1 shard_map.42
  36.8 3.2 %collective-permute-start.3 = (f32[2,8,128]{2,1,0:T(8,128)S(1)}, f32[2,8,128]{2,1,0:T(8,128)S(1)}, u32[]{:S(2)}, u32[]{:S(2)}) collective-permute-start(f32[2,8,128]{2,1,0:T(8,128)S(1)} %get-tuple-element.44), channel_id=1, source_target_pairs={{0,4},{4,0},{8,12},{12,8},{16,20},{20,16},{24,28},{28,24},{32,36},... | collective-permute-start | bytes 24584 | tf_op jit(solution)/shard_map/ppermute | solution.py:429
  40.0 0.1 shard_map.43.local
  40.1 0.7 %collective-permute-done.3.other = f32[2,8,128]{2,1,0:T(8,128)S(1)} collective-permute-done((f32[2,8,128]{2,1,0:T(8,128)S(1)}, f32[2,8,128]{2,1,0:T(8,128)S(1)}, u32[]{:S(2)}, u32[]{:S(2)}) %collective-permute-start.3) | collective-permute-done | bytes 8224 | tf_op jit(solution)/shard_map/ppermute | solution.py:429
  40.8 0.1 shard_map.44
  41.0 2.8 %collective-permute-start.4 = (f32[32,128]{1,0:T(8,128)S(1)}, f32[32,128]{1,0:T(8,128)S(1)}, u32[]{:S(2)}, u32[]{:S(2)}) collective-permute-start(f32[32,128]{1,0:T(8,128)S(1)} %get-tuple-element.50.message), channel_id=1, source_target_pairs={{0,2},{2,0},{1,3},{3,1},{4,6},{6,4},{5,7},{7,5},{8,10},{10,8},{9,1... | collective-permute-start | bytes 49160 | tf_op jit(solution)/shard_map/ppermute | solution.py:433
  43.7 0.9 %shard_map.45.local = f32[32,1024]{1,0:T(8,128)S(1)} custom-call(f32[32,1024]{1,0:T(8,128)S(1)} %get-tuple-element.51.section, f32[10,256,128]{2,1,0:T(8,128)S(1)} %get-tuple-element.52.ay, f32[10,256,128]{2,1,0:T(8,128)S(1)} %get-tuple-element.53.by, f32[256,128]{1,0:T(8,128)S(1)} %get-tuple-element.54.qy), custom_call_target="tpu_custom_call" | custom-call | flops 4000000 | bytes 3000000 | tf_op jit(solution)/shard_map/pallas_call | solution.py:434
  44.6 0.5 %collective-permute-done.4.far = f32[32,128]{1,0:T(8,128)S(1)} collective-permute-done((f32[32,128]{1,0:T(8,128)S(1)}, f32[32,128]{1,0:T(8,128)S(1)}, u32[]{:S(2)}, u32[]{:S(2)}) %collective-permute-start.4) | collective-permute-done | bytes 16416 | tf_op jit(solution)/shard_map/ppermute | solution.py:433
  45.1 0.9 %shard_map.46 = f32[32,1024]{1,0:T(8,128)} custom-call(f32[32,128]{1,0:T(8,128)S(1)} %get-tuple-element.50.message, f32[32,128]{1,0:T(8,128)S(1)} %collective-permute-done.4.far, f32[32,1024]{1,0:T(8,128)S(1)} %shard_map.45.local, f32[32,1024]{1,0:T(8,128)S(1)} %get-tuple-element.49.hy), custom_call_target="tpu_custom_call" | custom-call | tf_op jit(solution)/shard_map/pallas_call | solution.py:435
  (1 shorter events, 0.0 us)
Async XLA Ops:
  0.0 5.8 %collective-permute-start = (f32[2,1,16,1024]{3,2,1,0:T(8,128)}, f32[2,1,16,1024]{3,2,1,0:T(8,128)S(1)}, u32[]{:S(2)}, u32[]{:S(2)}) collective-permute-start(f32[2,1,16,1024]{3,2,1,0:T(8,128)} %param.3), channel_id=1, source_target_pairs={{0,1},{1,0},{2,3},{3,2},{4,5},{5,4},{6,7},{7,6},{8,9},{9,8},{10,11... | collective-permute-start | bytes 393224 | tf_op jit(solution)/shard_map/ppermute | solution.py:392
  2.0 5.0 %collective-permute-start.1 = (f32[2,1,16,1024]{3,2,1,0:T(8,128)}, f32[2,1,16,1024]{3,2,1,0:T(8,128)S(1)}, u32[]{:S(2)}, u32[]{:S(2)}) collective-permute-start(f32[2,1,16,1024]{3,2,1,0:T(8,128)} %param.5), channel_id=1, source_target_pairs={{0,1},{1,0},{2,3},{3,2},{4,5},{5,4},{6,7},{7,6},{8,9},{9,8},{10,11... | collective-permute-start | bytes 393224 | tf_op jit(solution)/shard_map/ppermute | solution.py:393
  7.1 3.7 %collective-permute-start.2 = (f32[7,8,128]{2,1,0:T(8,128)S(1)}, f32[7,8,128]{2,1,0:T(8,128)S(1)}, u32[]{:S(2)}, u32[]{:S(2)}) collective-permute-start(f32[7,8,128]{2,1,0:T(8,128)S(1)} %get-tuple-element.38), channel_id=1, source_target_pairs={{0,4},{4,0},{8,12},{12,8},{16,20},{20,16},{24,28},{28,24},{32,36},... | collective-permute-start | bytes 86024 | tf_op jit(solution)/shard_map/ppermute | solution.py:416
  36.8 4.0 %collective-permute-start.3 = (f32[2,8,128]{2,1,0:T(8,128)S(1)}, f32[2,8,128]{2,1,0:T(8,128)S(1)}, u32[]{:S(2)}, u32[]{:S(2)}) collective-permute-start(f32[2,8,128]{2,1,0:T(8,128)S(1)} %get-tuple-element.44), channel_id=1, source_target_pairs={{0,4},{4,0},{8,12},{12,8},{16,20},{20,16},{24,28},{28,24},{32,36},... | collective-permute-start | bytes 24584 | tf_op jit(solution)/shard_map/ppermute | solution.py:429
  41.0 4.1 %collective-permute-start.4 = (f32[32,128]{1,0:T(8,128)S(1)}, f32[32,128]{1,0:T(8,128)S(1)}, u32[]{:S(2)}, u32[]{:S(2)}) collective-permute-start(f32[32,128]{1,0:T(8,128)S(1)} %get-tuple-element.50.message), channel_id=1, source_target_pairs={{0,2},{2,0},{1,3},{3,1},{4,6},{6,4},{5,7},{7,5},{8,10},{10,8},{9,1... | collective-permute-start | bytes 49160 | tf_op jit(solution)/shard_map/ppermute | solution.py:433

commit v8 on v4

--- a/solution.py
+++ b/solution.py
@@ -267,15 +267,15 @@
         middle[n] = value
 
 
-def slab_kernel(chip, far1, far2, far3, middle, message, nodes):
+def slab_kernel(chip, far1, far3, far2, middle, message, nodes):
     y = lax.axis_index("gx") // 2 % 4
     arrived = [load(chip), load(far1), load(far2), load(far3)]
     chips = []
     for m in range(4):
         chosen = arrived[0]
-        for shift in range(1, 4):
-            here = (y + shift) % 4 == m
-            chosen = [jnp.where(here, a, c) for a, c in zip(arrived[shift], chosen)]
+        for flip in range(1, 4):
+            here = y ^ flip == m
+            chosen = [jnp.where(here, a, c) for a, c in zip(arrived[flip], chosen)]
         chips.append(chosen)
     element = chips[0][:5]
     inner, fronts = [], []
@@ -391,8 +391,8 @@
 CORES = [(i, i ^ 1) for i in range(64)]
 
 
-def chips_on(shift):
-    return [(i // 8 * 8 + (i + 2 * shift) % 8, i) for i in range(64)]
+def chips_across(flip):
+    return [(i, i ^ 2 * flip) for i in range(64)]
 
 
 def local(fields, kappa, vertical):
@@ -425,10 +425,10 @@
     got = lax.ppermute(send, "gx", CORES)
     local_x = call(local_x_kernel, full, [VMEM] * 4, flops=1_000_000, size=1_000_000)(source, ax, bx, qx)
     chip, middle = call(chip_kernel, (half, shape(6, 8, 128)), [VMEM] * 2)(keep, got)
-    far = [lax.ppermute(chip, "gx", chips_on(shift)) for shift in (2, 1, 3)]
+    far = [lax.ppermute(chip, "gx", chips_across(flip)) for flip in (1, 3, 2)]
     message, nodes = call(
         slab_kernel, (shape(8, 7, 8, 128), shape(4, 3, 8, 128)), [VMEM] * 5
-    )(chip, far[1], far[0], far[2], middle)
+    )(chip, *far, middle)
     got = lax.all_to_all(message, "gx", 0, 0, axis_index_groups=SLAB_GROUPS, tiled=True)
     mine, other = call(
         ends_kernel, (shape(2, 8, 128), shape(2, 8, 128)), [VMEM, VMEM]

time: 44.4 us -> 44.3 us (level)
  starting transfers between devices: 15.9 us -> 14.6 us
  waiting for transfers between devices: 5.12 us -> 6.36 us
    ppermute x3, starting transfers between devices: 5 us -> 3.72 us  [local(): far = [lax.ppermute(chip, 'gx', chips_across(flip)) for flip in (1, 3, 2)]]
    ppermute x3, waiting for transfers between devices: 1.92 us -> 3.16 us  [local(): far = [lax.ppermute(chip, 'gx', chips_across(flip)) for flip in (1, 3, 2)]]
where the time goes in v8:
time: 44.3 us; the launch traced here: 44.2 us
  blocking collectives  17.1 us (39%)
  starting transfers between devices  14.6 us (33%)
  waiting for transfers between devices  6.36 us (14%)
  Pallas kernels  6.11 us (14%)
    all_to_all x1, blocking collectives, local(): lax.all_to_all(message, 'gx', 0, 0, axis_index_groups=SLAB_GROUPS, tiled=...  17.1 us
    ppermute x3, starting transfers between devices, local(): far = [lax.ppermute(chip, 'gx', chips_across(flip)) for flip in (1, 3, 2)]  3.72 us
    ppermute x1, starting transfers between devices, local(): other = lax.ppermute(other, 'gx', CORES)  3.19 us
    ppermute x3, waiting for transfers between devices, local(): far = [lax.ppermute(chip, 'gx', chips_across(flip)) for flip in (1, 3, 2)]  3.16 us
    ppermute x1, starting transfers between devices, local(): got = lax.ppermute(send, 'gx', CORES)  2.87 us
    ppermute x1, starting transfers between devices, local(): far = lax.ppermute(message, 'gy', swap)  2.76 us
    pallas_call x1, Pallas kernels, local(): call(factor_y_kernel, (shape(10, 256, 128), shape(10, 256, 128), standing...  2.14 us
    ppermute x1, starting transfers between devices, local(): fields_far = lax.ppermute(fields, 'gz', swap)  2.04 us
  transfers between devices with their start and end apart: 8, of which 6 were waited for; matrix products, arithmetic and copies ran while one was open for 0% of the time, Pallas kernels for 11%

profile of v8, /device:TPU:1, one launch (start us, length us, event | category | flops | bytes accessed | tf_op | source)
XLA Modules:
  0.0 44.2 jit_solution(16041583728979711158)
XLA Ops:
  0.0 2.0 %collective-permute-start = (f32[2,1,16,1024]{3,2,1,0:T(8,128)}, f32[2,1,16,1024]{3,2,1,0:T(8,128)S(1)}, u32[]{:S(2)}, u32[]{:S(2)}) collective-permute-start(f32[2,1,16,1024]{3,2,1,0:T(8,128)} %param.3), channel_id=1, source_target_pairs={{0,1},{1,0},{2,3},{3,2},{4,5},{5,4},{6,7},{7,6},{8,9},{9,8},{10,11... | collective-permute-start | bytes 393224 | tf_op jit(solution)/shard_map/ppermute | solution.py:401
  2.0 0.0 collective-permute-start.1
  2.1 1.6 %shard_map.37 = (f32[32,1024]{1,0:T(8,128)S(1)}, f32[32,1024]{1,0:T(8,128)S(1)}, f32[32,1024]{1,0:T(8,128)S(1)}, f32[4,32,1024]{2,1,0:T(8,128)S(1)}, f32[4,32,10...) custom-call(f32[32,1024]{1,0:T(8,128)} %bitcast.11, ...), custom_call_target="tpu_custom_call" | custom-call | flops 4000000 | bytes 2000000 | tf_op jit(solution)/shard_map/pallas_call | solution.py:406
  3.7 2.1 %shard_map.38 = (f32[10,256,128]{2,1,0:T(8,128)S(1)}, f32[10,256,128]{2,1,0:T(8,128)S(1)}, f32[256,128]{1,0:T(8,128)S(1)}, f32[32,1024]{1,0:T(8,128)S(1)}, f32[32,128]{1,0:T(8,128)S(1)}) custom-call(f32[32,1024]{1,0:T(8,128)S(1)} %get-tuple-element.35.kappa), custom_call_target="tpu_custom_call" | custom-call | flops 20000000 | bytes 4000000 | tf_op jit(solution)/shard_map/pallas_call | solution.py:414
  5.8 0.0 collective-permute-done
  5.8 1.2 %collective-permute-done.1 = f32[2,1,16,1024]{3,2,1,0:T(8,128)S(1)} collective-permute-done((f32[2,1,16,1024]{3,2,1,0:T(8,128)}, f32[2,1,16,1024]{3,2,1,0:T(8,128)S(1)}, u32[]{:S(2)}, u32[]{:S(2)}) %collective-permute-start.1) | collective-permute-done | bytes 131104 | tf_op jit(solution)/shard_map/ppermute | solution.py:402
  7.0 0.1 shard_map.39
  7.1 2.9 %collective-permute-start.2 = (f32[7,8,128]{2,1,0:T(8,128)S(1)}, f32[7,8,128]{2,1,0:T(8,128)S(1)}, u32[]{:S(2)}, u32[]{:S(2)}) collective-permute-start(f32[7,8,128]{2,1,0:T(8,128)S(1)} %get-tuple-element.38), channel_id=1, source_target_pairs={{0,4},{4,0},{8,12},{12,8},{16,20},{20,16},{24,28},{28,24},{32,36},... | collective-permute-start | bytes 86024 | tf_op jit(solution)/shard_map/ppermute | solution.py:425
  10.0 0.9 %collective-permute-done.2.got = f32[7,8,128]{2,1,0:T(8,128)S(1)} collective-permute-done((f32[7,8,128]{2,1,0:T(8,128)S(1)}, f32[7,8,128]{2,1,0:T(8,128)S(1)}, u32[]{:S(2)}, u32[]{:S(2)}) %collective-permute-start.2) | collective-permute-done | bytes 28704 | tf_op jit(solution)/shard_map/ppermute | solution.py:425
  10.9 2.9 %collective-permute-start.5 = (f32[7,8,128]{2,1,0:T(8,128)S(1)}, f32[7,8,128]{2,1,0:T(8,128)S(1)}, u32[]{:S(2)}, u32[]{:S(2)}) collective-permute-start(f32[7,8,128]{2,1,0:T(8,128)S(1)} %get-tuple-element.39.chip), channel_id=1, source_target_pairs={{0,16},{4,20},{8,24},{12,28},{16,0},{20,4},{24,8},{28,12},{32,48},... | collective-permute-start | bytes 86024 | tf_op jit(solution)/shard_map/ppermute | solution.py:428
  13.8 0.8 %collective-permute-start.4 = (f32[7,8,128]{2,1,0:T(8,128)S(1)}, f32[7,8,128]{2,1,0:T(8,128)S(1)}, u32[]{:S(2)}, u32[]{:S(2)}) collective-permute-start(f32[7,8,128]{2,1,0:T(8,128)S(1)} %get-tuple-element.39.chip), channel_id=1, source_target_pairs={{0,24},{4,28},{8,16},{12,20},{16,8},{20,12},{24,0},{28,4},{32,56},... | collective-permute-start | bytes 86024 | tf_op jit(solution)/shard_map/ppermute | solution.py:428
  14.6 0.0 collective-permute-start.3
  14.6 0.6 %collective-permute-done.5.far2 = f32[7,8,128]{2,1,0:T(8,128)S(1)} collective-permute-done((f32[7,8,128]{2,1,0:T(8,128)S(1)}, f32[7,8,128]{2,1,0:T(8,128)S(1)}, u32[]{:S(2)}, u32[]{:S(2)}) %collective-permute-start.5) | collective-permute-done | bytes 28704 | tf_op jit(solution)/shard_map/ppermute | solution.py:428
  15.2 2.6 %collective-permute-done.4.far3 = f32[7,8,128]{2,1,0:T(8,128)S(1)} collective-permute-done((f32[7,8,128]{2,1,0:T(8,128)S(1)}, f32[7,8,128]{2,1,0:T(8,128)S(1)}, u32[]{:S(2)}, u32[]{:S(2)}) %collective-permute-start.4) | collective-permute-done | bytes 28704 | tf_op jit(solution)/shard_map/ppermute | solution.py:428
  17.8 0.0 collective-permute-done.3.far1
  17.8 0.1 shard_map.41
  17.8 17.1 %all_to_all.5.got = f32[8,7,8,128]{3,2,1,0:T(8,128)S(1)} all-to-all(f32[8,7,8,128]{3,2,1,0:T(8,128)S(1)} %get-tuple-element.41), channel_id=1, replica_groups={{0,32,64,96,128,160,192,224},{4,36,68,100,132,164,196,228},{8,40,72,104..., dimensions={0} | all-to-all | bytes 458752 | tf_op jit(solution)/shard_map/all_to_all | solution.py:432
  34.9 0.1 shard_map.42
  35.0 3.2 %collective-permute-start.6 = (f32[2,8,128]{2,1,0:T(8,128)S(1)}, f32[2,8,128]{2,1,0:T(8,128)S(1)}, u32[]{:S(2)}, u32[]{:S(2)}) collective-permute-start(f32[2,8,128]{2,1,0:T(8,128)S(1)} %get-tuple-element.44), channel_id=1, source_target_pairs={{0,4},{4,0},{8,12},{12,8},{16,20},{20,16},{24,28},{28,24},{32,36},... | collective-permute-start | bytes 24584 | tf_op jit(solution)/shard_map/ppermute | solution.py:436
  38.2 0.1 shard_map.43.local
  38.4 0.7 %collective-permute-done.6.other = f32[2,8,128]{2,1,0:T(8,128)S(1)} collective-permute-done((f32[2,8,128]{2,1,0:T(8,128)S(1)}, f32[2,8,128]{2,1,0:T(8,128)S(1)}, u32[]{:S(2)}, u32[]{:S(2)}) %collective-permute-start.6) | collective-permute-done | bytes 8224 | tf_op jit(solution)/shard_map/ppermute | solution.py:436
  39.1 0.1 shard_map.44
  39.2 2.8 %collective-permute-start.7 = (f32[32,128]{1,0:T(8,128)S(1)}, f32[32,128]{1,0:T(8,128)S(1)}, u32[]{:S(2)}, u32[]{:S(2)}) collective-permute-start(f32[32,128]{1,0:T(8,128)S(1)} %get-tuple-element.50.message), channel_id=1, source_target_pairs={{0,2},{2,0},{1,3},{3,1},{4,6},{6,4},{5,7},{7,5},{8,10},{10,8},{9,1... | collective-permute-start | bytes 49160 | tf_op jit(solution)/shard_map/ppermute | solution.py:440
  42.0 0.9 %shard_map.45.local = f32[32,1024]{1,0:T(8,128)S(1)} custom-call(f32[32,1024]{1,0:T(8,128)S(1)} %get-tuple-element.51.section, f32[10,256,128]{2,1,0:T(8,128)S(1)} %get-tuple-element.52.ay, f32[10,256,128]{2,1,0:T(8,128)S(1)} %get-tuple-element.53.by, f32[256,128]{1,0:T(8,128)S(1)} %get-tuple-element.54.qy), custom_call_target="tpu_custom_call" | custom-call | flops 4000000 | bytes 3000000 | tf_op jit(solution)/shard_map/pallas_call | solution.py:441
  42.8 0.5 %collective-permute-done.7.far = f32[32,128]{1,0:T(8,128)S(1)} collective-permute-done((f32[32,128]{1,0:T(8,128)S(1)}, f32[32,128]{1,0:T(8,128)S(1)}, u32[]{:S(2)}, u32[]{:S(2)}) %collective-permute-start.7) | collective-permute-done | bytes 16416 | tf_op jit(solution)/shard_map/ppermute | solution.py:440
  43.3 0.9 %shard_map.46 = f32[32,1024]{1,0:T(8,128)} custom-call(f32[32,128]{1,0:T(8,128)S(1)} %get-tuple-element.50.message, f32[32,128]{1,0:T(8,128)S(1)} %collective-permute-done.7.far, f32[32,1024]{1,0:T(8,128)S(1)} %shard_map.45.local, f32[32,1024]{1,0:T(8,128)S(1)} %get-tuple-element.49.hy), custom_call_target="tpu_custom_call" | custom-call | tf_op jit(solution)/shard_map/pallas_call | solution.py:442
  (1 shorter events, 0.0 us)
Async XLA Ops:
  0.0 5.8 %collective-permute-start = (f32[2,1,16,1024]{3,2,1,0:T(8,128)}, f32[2,1,16,1024]{3,2,1,0:T(8,128)S(1)}, u32[]{:S(2)}, u32[]{:S(2)}) collective-permute-start(f32[2,1,16,1024]{3,2,1,0:T(8,128)} %param.3), channel_id=1, source_target_pairs={{0,1},{1,0},{2,3},{3,2},{4,5},{5,4},{6,7},{7,6},{8,9},{9,8},{10,11... | collective-permute-start | bytes 393224 | tf_op jit(solution)/shard_map/ppermute | solution.py:401
  2.0 5.0 %collective-permute-start.1 = (f32[2,1,16,1024]{3,2,1,0:T(8,128)}, f32[2,1,16,1024]{3,2,1,0:T(8,128)S(1)}, u32[]{:S(2)}, u32[]{:S(2)}) collective-permute-start(f32[2,1,16,1024]{3,2,1,0:T(8,128)} %param.5), channel_id=1, source_target_pairs={{0,1},{1,0},{2,3},{3,2},{4,5},{5,4},{6,7},{7,6},{8,9},{9,8},{10,11... | collective-permute-start | bytes 393224 | tf_op jit(solution)/shard_map/ppermute | solution.py:402
  7.1 3.7 %collective-permute-start.2 = (f32[7,8,128]{2,1,0:T(8,128)S(1)}, f32[7,8,128]{2,1,0:T(8,128)S(1)}, u32[]{:S(2)}, u32[]{:S(2)}) collective-permute-start(f32[7,8,128]{2,1,0:T(8,128)S(1)} %get-tuple-element.38), channel_id=1, source_target_pairs={{0,4},{4,0},{8,12},{12,8},{16,20},{20,16},{24,28},{28,24},{32,36},... | collective-permute-start | bytes 86024 | tf_op jit(solution)/shard_map/ppermute | solution.py:425
  10.9 4.3 %collective-permute-start.5 = (f32[7,8,128]{2,1,0:T(8,128)S(1)}, f32[7,8,128]{2,1,0:T(8,128)S(1)}, u32[]{:S(2)}, u32[]{:S(2)}) collective-permute-start(f32[7,8,128]{2,1,0:T(8,128)S(1)} %get-tuple-element.39.chip), channel_id=1, source_target_pairs={{0,16},{4,20},{8,24},{12,28},{16,0},{20,4},{24,8},{28,12},{32,48},... | collective-permute-start | bytes 86024 | tf_op jit(solution)/shard_map/ppermute | solution.py:428
  13.8 3.9 %collective-permute-start.4 = (f32[7,8,128]{2,1,0:T(8,128)S(1)}, f32[7,8,128]{2,1,0:T(8,128)S(1)}, u32[]{:S(2)}, u32[]{:S(2)}) collective-permute-start(f32[7,8,128]{2,1,0:T(8,128)S(1)} %get-tuple-element.39.chip), channel_id=1, source_target_pairs={{0,24},{4,28},{8,16},{12,20},{16,8},{20,12},{24,0},{28,4},{32,56},... | collective-permute-start | bytes 86024 | tf_op jit(solution)/shard_map/ppermute | solution.py:428
  14.6 3.2 %collective-permute-start.3 = (f32[7,8,128]{2,1,0:T(8,128)S(1)}, f32[7,8,128]{2,1,0:T(8,128)S(1)}, u32[]{:S(2)}, u32[]{:S(2)}) collective-permute-start(f32[7,8,128]{2,1,0:T(8,128)S(1)} %get-tuple-element.39.chip), channel_id=1, source_target_pairs={{0,8},{4,12},{8,0},{12,4},{16,24},{20,28},{24,16},{28,20},{32,40},... | collective-permute-start | bytes 86024 | tf_op jit(solution)/shard_map/ppermute | solution.py:428
  35.0 4.0 %collective-permute-start.6 = (f32[2,8,128]{2,1,0:T(8,128)S(1)}, f32[2,8,128]{2,1,0:T(8,128)S(1)}, u32[]{:S(2)}, u32[]{:S(2)}) collective-permute-start(f32[2,8,128]{2,1,0:T(8,128)S(1)} %get-tuple-element.44), channel_id=1, source_target_pairs={{0,4},{4,0},{8,12},{12,8},{16,20},{20,16},{24,28},{28,24},{32,36},... | collective-permute-start | bytes 24584 | tf_op jit(solution)/shard_map/ppermute | solution.py:436
  39.2 4.1 %collective-permute-start.7 = (f32[32,128]{1,0:T(8,128)S(1)}, f32[32,128]{1,0:T(8,128)S(1)}, u32[]{:S(2)}, u32[]{:S(2)}) collective-permute-start(f32[32,128]{1,0:T(8,128)S(1)} %get-tuple-element.50.message), channel_id=1, source_target_pairs={{0,2},{2,0},{1,3},{3,1},{4,6},{6,4},{5,7},{7,5},{8,10},{10,8},{9,1... | collective-permute-start | bytes 49160 | tf_op jit(solution)/shard_map/ppermute | solution.py:440

commit v9 on v8

--- a/solution.py
+++ b/solution.py
@@ -193,8 +193,12 @@
     column = lax.broadcasted_iota(jnp.int32, (ALL, COLS), 1)
     total = jnp.sum(profile * jnp.where(column == start, 1.0 + 0.5 * k, 1.0), axis=1, keepdims=True)
     rim = jnp.sum(jnp.where(column == end, k, 0.0), axis=1, keepdims=True)
-    wide = lax.broadcasted_iota(jnp.int32, (ALL, 128), 1)
-    edge[...] = jnp.where(wide == 0, total, jnp.where(wide == 1, rim, 0.0))
+    lane = lax.broadcasted_iota(jnp.int32, (8, 128), 1)
+    tile = jnp.zeros((8, 128), F32)
+    for g in range(ALL // 8):
+        part = slice(8 * g, 8 * g + 8)
+        tile = jnp.where(lane == 4 * g, total[part], jnp.where(lane == 4 * g + 1, rim[part], tile))
+    edge[...] = tile
 
 
 def source_kernel(fields, fields_far, vertical, vertical_far, h1, h2, parts, after, source, keep, send):
@@ -348,7 +352,8 @@
 
 def section_kernel(mine, other, local, h1, h2, hy, edge, section, message):
     core = lax.axis_index("gx") % 2
-    wide = lax.broadcasted_iota(jnp.int32, (8, 128), 1)
+    lane = lax.broadcasted_iota(jnp.int32, (8, 128), 1)
+    tile = edge[...]
     for f in range(2):
         first = jnp.where(core == f, mine[0], other[0])
         last = jnp.where(core == f, mine[1], other[1])
@@ -357,8 +362,8 @@
         section[rows, :] = s
         total = jnp.sum(hy[rows, :] * s, axis=1, keepdims=True)
         for g in range(2):
-            part = slice(f * ROWS + g * 8, f * ROWS + g * 8 + 8)
-            message[part, :] = jnp.where(wide == 2, total[g * 8 : g * 8 + 8], edge[part, :])
+            tile = jnp.where(lane == 4 * (2 * f + g) + 2, total[8 * g : 8 * g + 8], tile)
+    message[...] = tile
 
 
 def local_y_kernel(section, ay, by, qy, out):
@@ -368,11 +373,13 @@
 
 
 def output_kernel(message, far, local, hy, out):
-    e, k, r = (message[:, n : n + 1] for n in range(3))
-    e2, k2, r2 = (far[:, n : n + 1] for n in range(3))
-    c = (k + k2) * 0.5
-    value = ((e2 + c) * r + c * r2) / (e * e2 + c * (e + e2))
-    out[...] = local[...] + hy[...] * value
+    for g in range(ALL // 8):
+        part = slice(8 * g, 8 * g + 8)
+        e, k, r = (message[:, 4 * g + n : 4 * g + n + 1] for n in range(3))
+        e2, k2, r2 = (far[:, 4 * g + n : 4 * g + n + 1] for n in range(3))
+        c = (k + k2) * 0.5
+        value = ((e2 + c) * r + c * r2) / (e * e2 + c * (e + e2))
+        out[part, :] = local[part, :] + hy[part, :] * value
 
 
 def call(kernel, outs, specs, flops=0, size=0, scratch=()):
@@ -413,7 +420,7 @@
     )(*(pltpu.with_memory_space_constraint(x.reshape(grid), pltpu.HBM) for x in (fields, vertical, kappa)))
     ay, by, qy, hy, edge = call(
         factor_y_kernel,
-        (shape(10, 256, 128), shape(10, 256, 128), standing, full, shape(ALL, 128)),
+        (shape(10, 256, 128), shape(10, 256, 128), standing, full, shape(8, 128)),
         [VMEM],
         flops=20_000_000,
         size=4_000_000,
@@ -435,7 +442,7 @@
     )(got, nodes)
     other = lax.ppermute(other, "gx", CORES)
     section, message = call(
-        section_kernel, (full, shape(ALL, 128)), [VMEM] * 7
+        section_kernel, (full, shape(8, 128)), [VMEM] * 7
     )(mine, other, local_x, h1, h2, hy, edge)
     far = lax.ppermute(message, "gy", swap)
     local_y = call(local_y_kernel, full, [VMEM] * 4, flops=4_000_000, size=3_000_000)(section, ay, by, qy)

time: 44.3 us -> 44.2 us (level)
  no operation moved by 1% of the time
where the time goes in v9:
time: 44.2 us; the launch traced here: 44.1 us
  blocking collectives  17.1 us (39%)
  starting transfers between devices  14.6 us (33%)
  waiting for transfers between devices  6.19 us (14%)
  Pallas kernels  6.14 us (14%)
    all_to_all x1, blocking collectives, local(): lax.all_to_all(message, 'gx', 0, 0, axis_index_groups=SLAB_GROUPS, tiled=...  17.1 us
    ppermute x3, starting transfers between devices, local(): far = [lax.ppermute(chip, 'gx', chips_across(flip)) for flip in (1, 3, 2)]  3.72 us
    ppermute x1, starting transfers between devices, local(): other = lax.ppermute(other, 'gx', CORES)  3.19 us
    ppermute x3, waiting for transfers between devices, local(): far = [lax.ppermute(chip, 'gx', chips_across(flip)) for flip in (1, 3, 2)]  3.16 us
    ppermute x1, starting transfers between devices, local(): got = lax.ppermute(send, 'gx', CORES)  2.87 us
    ppermute x1, starting transfers between devices, local(): far = lax.ppermute(message, 'gy', swap)  2.77 us
    pallas_call x1, Pallas kernels, local(): call(factor_y_kernel, (shape(10, 256, 128), shape(10, 256, 128), standing...  2.15 us
    ppermute x1, starting transfers between devices, local(): fields_far = lax.ppermute(fields, 'gz', swap)  2.04 us
  transfers between devices with their start and end apart: 8, of which 6 were waited for; matrix products, arithmetic and copies ran while one was open for 0% of the time, Pallas kernels for 11%

profile of v9, /device:TPU:1, one launch (start us, length us, event | category | flops | bytes accessed | tf_op | source)
XLA Modules:
  0.0 44.1 jit_solution(872499175082667564)
XLA Ops:
  0.0 2.0 %collective-permute-start = (f32[2,1,16,1024]{3,2,1,0:T(8,128)}, f32[2,1,16,1024]{3,2,1,0:T(8,128)S(1)}, u32[]{:S(2)}, u32[]{:S(2)}) collective-permute-start(f32[2,1,16,1024]{3,2,1,0:T(8,128)} %param.3), channel_id=1, source_target_pairs={{0,1},{1,0},{2,3},{3,2},{4,5},{5,4},{6,7},{7,6},{8,9},{9,8},{10,11... | collective-permute-start | bytes 393224 | tf_op jit(solution)/shard_map/ppermute | solution.py:408
  2.0 0.0 collective-permute-start.1
  2.1 1.6 %shard_map.37 = (f32[32,1024]{1,0:T(8,128)S(1)}, f32[32,1024]{1,0:T(8,128)S(1)}, f32[32,1024]{1,0:T(8,128)S(1)}, f32[4,32,1024]{2,1,0:T(8,128)S(1)}, f32[4,32,10...) custom-call(f32[32,1024]{1,0:T(8,128)} %bitcast.11, ...), custom_call_target="tpu_custom_call" | custom-call | flops 4000000 | bytes 2000000 | tf_op jit(solution)/shard_map/pallas_call | solution.py:413
  3.7 2.2 %shard_map.38 = (f32[10,256,128]{2,1,0:T(8,128)S(1)}, f32[10,256,128]{2,1,0:T(8,128)S(1)}, f32[256,128]{1,0:T(8,128)S(1)}, f32[32,1024]{1,0:T(8,128)S(1)}, f32[8,128]{1,0:T(8,128)S(1)}) custom-call(f32[32,1024]{1,0:T(8,128)S(1)} %get-tuple-element.35.kappa), custom_call_target="tpu_custom_call" | custom-call | flops 20000000 | bytes 4000000 | tf_op jit(solution)/shard_map/pallas_call | solution.py:421
  5.9 0.0 collective-permute-done
  5.9 1.2 %collective-permute-done.1 = f32[2,1,16,1024]{3,2,1,0:T(8,128)S(1)} collective-permute-done((f32[2,1,16,1024]{3,2,1,0:T(8,128)}, f32[2,1,16,1024]{3,2,1,0:T(8,128)S(1)}, u32[]{:S(2)}, u32[]{:S(2)}) %collective-permute-start.1) | collective-permute-done | bytes 131104 | tf_op jit(solution)/shard_map/ppermute | solution.py:409
  7.0 0.1 shard_map.39
  7.1 2.9 %collective-permute-start.2 = (f32[7,8,128]{2,1,0:T(8,128)S(1)}, f32[7,8,128]{2,1,0:T(8,128)S(1)}, u32[]{:S(2)}, u32[]{:S(2)}) collective-permute-start(f32[7,8,128]{2,1,0:T(8,128)S(1)} %get-tuple-element.38), channel_id=1, source_target_pairs={{0,4},{4,0},{8,12},{12,8},{16,20},{20,16},{24,28},{28,24},{32,36},... | collective-permute-start | bytes 86024 | tf_op jit(solution)/shard_map/ppermute | solution.py:432
  10.0 0.9 %collective-permute-done.2.got = f32[7,8,128]{2,1,0:T(8,128)S(1)} collective-permute-done((f32[7,8,128]{2,1,0:T(8,128)S(1)}, f32[7,8,128]{2,1,0:T(8,128)S(1)}, u32[]{:S(2)}, u32[]{:S(2)}) %collective-permute-start.2) | collective-permute-done | bytes 28704 | tf_op jit(solution)/shard_map/ppermute | solution.py:432
  10.9 2.9 %collective-permute-start.5 = (f32[7,8,128]{2,1,0:T(8,128)S(1)}, f32[7,8,128]{2,1,0:T(8,128)S(1)}, u32[]{:S(2)}, u32[]{:S(2)}) collective-permute-start(f32[7,8,128]{2,1,0:T(8,128)S(1)} %get-tuple-element.39.chip), channel_id=1, source_target_pairs={{0,16},{4,20},{8,24},{12,28},{16,0},{20,4},{24,8},{28,12},{32,48},... | collective-permute-start | bytes 86024 | tf_op jit(solution)/shard_map/ppermute | solution.py:435
  13.8 0.8 %collective-permute-start.4 = (f32[7,8,128]{2,1,0:T(8,128)S(1)}, f32[7,8,128]{2,1,0:T(8,128)S(1)}, u32[]{:S(2)}, u32[]{:S(2)}) collective-permute-start(f32[7,8,128]{2,1,0:T(8,128)S(1)} %get-tuple-element.39.chip), channel_id=1, source_target_pairs={{0,24},{4,28},{8,16},{12,20},{16,8},{20,12},{24,0},{28,4},{32,56},... | collective-permute-start | bytes 86024 | tf_op jit(solution)/shard_map/ppermute | solution.py:435
  14.6 0.0 collective-permute-start.3
  14.6 0.6 %collective-permute-done.5.far2 = f32[7,8,128]{2,1,0:T(8,128)S(1)} collective-permute-done((f32[7,8,128]{2,1,0:T(8,128)S(1)}, f32[7,8,128]{2,1,0:T(8,128)S(1)}, u32[]{:S(2)}, u32[]{:S(2)}) %collective-permute-start.5) | collective-permute-done | bytes 28704 | tf_op jit(solution)/shard_map/ppermute | solution.py:435
  15.2 2.6 %collective-permute-done.4.far3 = f32[7,8,128]{2,1,0:T(8,128)S(1)} collective-permute-done((f32[7,8,128]{2,1,0:T(8,128)S(1)}, f32[7,8,128]{2,1,0:T(8,128)S(1)}, u32[]{:S(2)}, u32[]{:S(2)}) %collective-permute-start.4) | collective-permute-done | bytes 28704 | tf_op jit(solution)/shard_map/ppermute | solution.py:435
  17.8 0.0 collective-permute-done.3.far1
  17.8 0.1 shard_map.41
  17.9 17.1 %all_to_all.5.got = f32[8,7,8,128]{3,2,1,0:T(8,128)S(1)} all-to-all(f32[8,7,8,128]{3,2,1,0:T(8,128)S(1)} %get-tuple-element.41), channel_id=1, replica_groups={{0,32,64,96,128,160,192,224},{4,36,68,100,132,164,196,228},{8,40,72,104..., dimensions={0} | all-to-all | bytes 458752 | tf_op jit(solution)/shard_map/all_to_all | solution.py:439
  34.9 0.1 shard_map.42
  35.0 3.2 %collective-permute-start.6 = (f32[2,8,128]{2,1,0:T(8,128)S(1)}, f32[2,8,128]{2,1,0:T(8,128)S(1)}, u32[]{:S(2)}, u32[]{:S(2)}) collective-permute-start(f32[2,8,128]{2,1,0:T(8,128)S(1)} %get-tuple-element.44), channel_id=1, source_target_pairs={{0,4},{4,0},{8,12},{12,8},{16,20},{20,16},{24,28},{28,24},{32,36},... | collective-permute-start | bytes 24584 | tf_op jit(solution)/shard_map/ppermute | solution.py:443
  38.2 0.2 shard_map.43.local
  38.4 0.7 %collective-permute-done.6.other = f32[2,8,128]{2,1,0:T(8,128)S(1)} collective-permute-done((f32[2,8,128]{2,1,0:T(8,128)S(1)}, f32[2,8,128]{2,1,0:T(8,128)S(1)}, u32[]{:S(2)}, u32[]{:S(2)}) %collective-permute-start.6) | collective-permute-done | bytes 8224 | tf_op jit(solution)/shard_map/ppermute | solution.py:443
  39.1 0.1 shard_map.44
  39.2 2.8 %collective-permute-start.7 = (f32[8,128]{1,0:T(8,128)S(1)}, f32[8,128]{1,0:T(8,128)S(1)}, u32[]{:S(2)}, u32[]{:S(2)}) collective-permute-start(f32[8,128]{1,0:T(8,128)S(1)} %get-tuple-element.50.message), channel_id=1, source_target_pairs={{0,2},{2,0},{1,3},{3,1},{4,6},{6,4},{5,7},{7,5},{8,10},{10,8},{9,1... | collective-permute-start | bytes 12296 | tf_op jit(solution)/shard_map/ppermute | solution.py:447
  42.0 0.9 %shard_map.45.local = f32[32,1024]{1,0:T(8,128)S(1)} custom-call(f32[32,1024]{1,0:T(8,128)S(1)} %get-tuple-element.51.section, f32[10,256,128]{2,1,0:T(8,128)S(1)} %get-tuple-element.52.ay, f32[10,256,128]{2,1,0:T(8,128)S(1)} %get-tuple-element.53.by, f32[256,128]{1,0:T(8,128)S(1)} %get-tuple-element.54.qy), custom_call_target="tpu_custom_call" | custom-call | flops 4000000 | bytes 3000000 | tf_op jit(solution)/shard_map/pallas_call | solution.py:448
  42.8 0.3 collective-permute-done.7.far
  43.2 0.9 %shard_map.46 = f32[32,1024]{1,0:T(8,128)} custom-call(f32[8,128]{1,0:T(8,128)S(1)} %get-tuple-element.50.message, f32[8,128]{1,0:T(8,128)S(1)} %collective-permute-done.7.far, f32[32,1024]{1,0:T(8,128)S(1)} %shard_map.45.local, f32[32,1024]{1,0:T(8,128)S(1)} %get-tuple-element.49.hy), custom_call_target="tpu_custom_call" | custom-call | tf_op jit(solution)/shard_map/pallas_call | solution.py:449
  (1 shorter events, 0.0 us)
Async XLA Ops:
  0.0 5.9 %collective-permute-start = (f32[2,1,16,1024]{3,2,1,0:T(8,128)}, f32[2,1,16,1024]{3,2,1,0:T(8,128)S(1)}, u32[]{:S(2)}, u32[]{:S(2)}) collective-permute-start(f32[2,1,16,1024]{3,2,1,0:T(8,128)} %param.3), channel_id=1, source_target_pairs={{0,1},{1,0},{2,3},{3,2},{4,5},{5,4},{6,7},{7,6},{8,9},{9,8},{10,11... | collective-permute-start | bytes 393224 | tf_op jit(solution)/shard_map/ppermute | solution.py:408
  2.0 5.0 %collective-permute-start.1 = (f32[2,1,16,1024]{3,2,1,0:T(8,128)}, f32[2,1,16,1024]{3,2,1,0:T(8,128)S(1)}, u32[]{:S(2)}, u32[]{:S(2)}) collective-permute-start(f32[2,1,16,1024]{3,2,1,0:T(8,128)} %param.5), channel_id=1, source_target_pairs={{0,1},{1,0},{2,3},{3,2},{4,5},{5,4},{6,7},{7,6},{8,9},{9,8},{10,11... | collective-permute-start | bytes 393224 | tf_op jit(solution)/shard_map/ppermute | solution.py:409
  7.1 3.7 %collective-permute-start.2 = (f32[7,8,128]{2,1,0:T(8,128)S(1)}, f32[7,8,128]{2,1,0:T(8,128)S(1)}, u32[]{:S(2)}, u32[]{:S(2)}) collective-permute-start(f32[7,8,128]{2,1,0:T(8,128)S(1)} %get-tuple-element.38), channel_id=1, source_target_pairs={{0,4},{4,0},{8,12},{12,8},{16,20},{20,16},{24,28},{28,24},{32,36},... | collective-permute-start | bytes 86024 | tf_op jit(solution)/shard_map/ppermute | solution.py:432
  10.9 4.3 %collective-permute-start.5 = (f32[7,8,128]{2,1,0:T(8,128)S(1)}, f32[7,8,128]{2,1,0:T(8,128)S(1)}, u32[]{:S(2)}, u32[]{:S(2)}) collective-permute-start(f32[7,8,128]{2,1,0:T(8,128)S(1)} %get-tuple-element.39.chip), channel_id=1, source_target_pairs={{0,16},{4,20},{8,24},{12,28},{16,0},{20,4},{24,8},{28,12},{32,48},... | collective-permute-start | bytes 86024 | tf_op jit(solution)/shard_map/ppermute | solution.py:435
  13.8 3.9 %collective-permute-start.4 = (f32[7,8,128]{2,1,0:T(8,128)S(1)}, f32[7,8,128]{2,1,0:T(8,128)S(1)}, u32[]{:S(2)}, u32[]{:S(2)}) collective-permute-start(f32[7,8,128]{2,1,0:T(8,128)S(1)} %get-tuple-element.39.chip), channel_id=1, source_target_pairs={{0,24},{4,28},{8,16},{12,20},{16,8},{20,12},{24,0},{28,4},{32,56},... | collective-permute-start | bytes 86024 | tf_op jit(solution)/shard_map/ppermute | solution.py:435
  14.6 3.2 %collective-permute-start.3 = (f32[7,8,128]{2,1,0:T(8,128)S(1)}, f32[7,8,128]{2,1,0:T(8,128)S(1)}, u32[]{:S(2)}, u32[]{:S(2)}) collective-permute-start(f32[7,8,128]{2,1,0:T(8,128)S(1)} %get-tuple-element.39.chip), channel_id=1, source_target_pairs={{0,8},{4,12},{8,0},{12,4},{16,24},{20,28},{24,16},{28,20},{32,40},... | collective-permute-start | bytes 86024 | tf_op jit(solution)/shard_map/ppermute | solution.py:435
  35.0 4.0 %collective-permute-start.6 = (f32[2,8,128]{2,1,0:T(8,128)S(1)}, f32[2,8,128]{2,1,0:T(8,128)S(1)}, u32[]{:S(2)}, u32[]{:S(2)}) collective-permute-start(f32[2,8,128]{2,1,0:T(8,128)S(1)} %get-tuple-element.44), channel_id=1, source_target_pairs={{0,4},{4,0},{8,12},{12,8},{16,20},{20,16},{24,28},{28,24},{32,36},... | collective-permute-start | bytes 24584 | tf_op jit(solution)/shard_map/ppermute | solution.py:443
  39.2 4.0 %collective-permute-start.7 = (f32[8,128]{1,0:T(8,128)S(1)}, f32[8,128]{1,0:T(8,128)S(1)}, u32[]{:S(2)}, u32[]{:S(2)}) collective-permute-start(f32[8,128]{1,0:T(8,128)S(1)} %get-tuple-element.50.message), channel_id=1, source_target_pairs={{0,2},{2,0},{1,3},{3,1},{4,6},{6,4},{5,7},{7,5},{8,10},{10,8},{9,1... | collective-permute-start | bytes 12296 | tf_op jit(solution)/shard_map/ppermute | solution.py:447

commit v10 on v9

--- a/solution.py
+++ b/solution.py
@@ -372,14 +372,19 @@
     out[...] = lie(r * qy[...])
 
 
-def output_kernel(message, far, local, hy, out):
+def output_kernel(message, far, local, hy, out, rows, done):
+    copies = []
     for g in range(ALL // 8):
-        part = slice(8 * g, 8 * g + 8)
+        part = pl.ds(8 * g, 8)
         e, k, r = (message[:, 4 * g + n : 4 * g + n + 1] for n in range(3))
         e2, k2, r2 = (far[:, 4 * g + n : 4 * g + n + 1] for n in range(3))
         c = (k + k2) * 0.5
         value = ((e2 + c) * r + c * r2) / (e * e2 + c * (e + e2))
-        out[part, :] = local[part, :] + hy[part, :] * value
+        rows[part, :] = local[part, :] + hy[part, :] * value
+        copies.append(pltpu.make_async_copy(rows.at[part], out.at[part], done.at[g]))
+        copies[-1].start()
+    for copy in copies:
+        copy.wait()
 
 
 def call(kernel, outs, specs, flops=0, size=0, scratch=()):
@@ -446,7 +451,14 @@
     )(mine, other, local_x, h1, h2, hy, edge)
     far = lax.ppermute(message, "gy", swap)
     local_y = call(local_y_kernel, full, [VMEM] * 4, flops=4_000_000, size=3_000_000)(section, ay, by, qy)
-    out = call(output_kernel, full, [VMEM] * 4)(message, far, local_y, hy)
+    out = pl.pallas_call(
+        output_kernel,
+        out_shape=full,
+        in_specs=[VMEM] * 4,
+        out_specs=pl.BlockSpec(memory_space=pltpu.HBM),
+        scratch_shapes=[pltpu.VMEM(grid, F32), pltpu.SemaphoreType.DMA((ALL // 8,))],
+        compiler_params=PARAMS,
+    )(message, far, local_y, hy)
     return out.reshape(fields.shape)
 
 

time: 44.2 us -> 44.2 us (level)
  no operation moved by 1% of the time
where the time goes in v10:
time: 44.2 us; the launch traced here: 44.1 us
  blocking collectives  17.1 us (39%)
  starting transfers between devices  14.6 us (33%)
  waiting for transfers between devices  6.19 us (14%)
  Pallas kernels  6.16 us (14%)
    all_to_all x1, blocking collectives, local(): lax.all_to_all(message, 'gx', 0, 0, axis_index_groups=SLAB_GROUPS, tiled=...  17.1 us
    ppermute x3, starting transfers between devices, local(): far = [lax.ppermute(chip, 'gx', chips_across(flip)) for flip in (1, 3, 2)]  3.72 us
    ppermute x1, starting transfers between devices, local(): other = lax.ppermute(other, 'gx', CORES)  3.19 us
    ppermute x3, waiting for transfers between devices, local(): far = [lax.ppermute(chip, 'gx', chips_across(flip)) for flip in (1, 3, 2)]  3.16 us
    ppermute x1, starting transfers between devices, local(): got = lax.ppermute(send, 'gx', CORES)  2.87 us
    ppermute x1, starting transfers between devices, local(): far = lax.ppermute(message, 'gy', swap)  2.77 us
    pallas_call x1, Pallas kernels, local(): call(factor_y_kernel, (shape(10, 256, 128), shape(10, 256, 128), standing...  2.15 us
    ppermute x1, starting transfers between devices, local(): fields_far = lax.ppermute(fields, 'gz', swap)  2.04 us
  transfers between devices with their start and end apart: 8, of which 6 were waited for; matrix products, arithmetic and copies ran while one was open for 0% of the time, Pallas kernels for 11%

profile of v10, /device:TPU:1, one launch (start us, length us, event | category | flops | bytes accessed | tf_op | source)
XLA Modules:
  0.0 44.1 jit_solution(3666027596730004789)
XLA Ops:
  0.0 2.0 %collective-permute-start = (f32[2,1,16,1024]{3,2,1,0:T(8,128)}, f32[2,1,16,1024]{3,2,1,0:T(8,128)S(1)}, u32[]{:S(2)}, u32[]{:S(2)}) collective-permute-start(f32[2,1,16,1024]{3,2,1,0:T(8,128)} %param.3), channel_id=1, source_target_pairs={{0,1},{1,0},{2,3},{3,2},{4,5},{5,4},{6,7},{7,6},{8,9},{9,8},{10,11... | collective-permute-start | bytes 393224 | tf_op jit(solution)/shard_map/ppermute | solution.py:413
  2.0 0.0 collective-permute-start.1
  2.1 1.6 %shard_map.37 = (f32[32,1024]{1,0:T(8,128)S(1)}, f32[32,1024]{1,0:T(8,128)S(1)}, f32[32,1024]{1,0:T(8,128)S(1)}, f32[4,32,1024]{2,1,0:T(8,128)S(1)}, f32[4,32,10...) custom-call(f32[32,1024]{1,0:T(8,128)} %bitcast.11, ...), custom_call_target="tpu_custom_call" | custom-call | flops 4000000 | bytes 2000000 | tf_op jit(solution)/shard_map/pallas_call | solution.py:418
  3.7 2.2 %shard_map.38 = (f32[10,256,128]{2,1,0:T(8,128)S(1)}, f32[10,256,128]{2,1,0:T(8,128)S(1)}, f32[256,128]{1,0:T(8,128)S(1)}, f32[32,1024]{1,0:T(8,128)S(1)}, f32[8,128]{1,0:T(8,128)S(1)}) custom-call(f32[32,1024]{1,0:T(8,128)S(1)} %get-tuple-element.35.kappa), custom_call_target="tpu_custom_call" | custom-call | flops 20000000 | bytes 4000000 | tf_op jit(solution)/shard_map/pallas_call | solution.py:426
  5.9 0.0 collective-permute-done
  5.9 1.2 %collective-permute-done.1 = f32[2,1,16,1024]{3,2,1,0:T(8,128)S(1)} collective-permute-done((f32[2,1,16,1024]{3,2,1,0:T(8,128)}, f32[2,1,16,1024]{3,2,1,0:T(8,128)S(1)}, u32[]{:S(2)}, u32[]{:S(2)}) %collective-permute-start.1) | collective-permute-done | bytes 131104 | tf_op jit(solution)/shard_map/ppermute | solution.py:414
  7.0 0.1 shard_map.39
  7.1 2.9 %collective-permute-start.2 = (f32[7,8,128]{2,1,0:T(8,128)S(1)}, f32[7,8,128]{2,1,0:T(8,128)S(1)}, u32[]{:S(2)}, u32[]{:S(2)}) collective-permute-start(f32[7,8,128]{2,1,0:T(8,128)S(1)} %get-tuple-element.38), channel_id=1, source_target_pairs={{0,4},{4,0},{8,12},{12,8},{16,20},{20,16},{24,28},{28,24},{32,36},... | collective-permute-start | bytes 86024 | tf_op jit(solution)/shard_map/ppermute | solution.py:437
  10.0 0.9 %collective-permute-done.2.got = f32[7,8,128]{2,1,0:T(8,128)S(1)} collective-permute-done((f32[7,8,128]{2,1,0:T(8,128)S(1)}, f32[7,8,128]{2,1,0:T(8,128)S(1)}, u32[]{:S(2)}, u32[]{:S(2)}) %collective-permute-start.2) | collective-permute-done | bytes 28704 | tf_op jit(solution)/shard_map/ppermute | solution.py:437
  10.9 2.9 %collective-permute-start.5 = (f32[7,8,128]{2,1,0:T(8,128)S(1)}, f32[7,8,128]{2,1,0:T(8,128)S(1)}, u32[]{:S(2)}, u32[]{:S(2)}) collective-permute-start(f32[7,8,128]{2,1,0:T(8,128)S(1)} %get-tuple-element.39.chip), channel_id=1, source_target_pairs={{0,16},{4,20},{8,24},{12,28},{16,0},{20,4},{24,8},{28,12},{32,48},... | collective-permute-start | bytes 86024 | tf_op jit(solution)/shard_map/ppermute | solution.py:440
  13.8 0.8 %collective-permute-start.4 = (f32[7,8,128]{2,1,0:T(8,128)S(1)}, f32[7,8,128]{2,1,0:T(8,128)S(1)}, u32[]{:S(2)}, u32[]{:S(2)}) collective-permute-start(f32[7,8,128]{2,1,0:T(8,128)S(1)} %get-tuple-element.39.chip), channel_id=1, source_target_pairs={{0,24},{4,28},{8,16},{12,20},{16,8},{20,12},{24,0},{28,4},{32,56},... | collective-permute-start | bytes 86024 | tf_op jit(solution)/shard_map/ppermute | solution.py:440
  14.6 0.0 collective-permute-start.3
  14.6 0.6 %collective-permute-done.5.far2 = f32[7,8,128]{2,1,0:T(8,128)S(1)} collective-permute-done((f32[7,8,128]{2,1,0:T(8,128)S(1)}, f32[7,8,128]{2,1,0:T(8,128)S(1)}, u32[]{:S(2)}, u32[]{:S(2)}) %collective-permute-start.5) | collective-permute-done | bytes 28704 | tf_op jit(solution)/shard_map/ppermute | solution.py:440
  15.2 2.6 %collective-permute-done.4.far3 = f32[7,8,128]{2,1,0:T(8,128)S(1)} collective-permute-done((f32[7,8,128]{2,1,0:T(8,128)S(1)}, f32[7,8,128]{2,1,0:T(8,128)S(1)}, u32[]{:S(2)}, u32[]{:S(2)}) %collective-permute-start.4) | collective-permute-done | bytes 28704 | tf_op jit(solution)/shard_map/ppermute | solution.py:440
  17.8 0.0 collective-permute-done.3.far1
  17.8 0.1 shard_map.41
  17.9 17.1 %all_to_all.5.got = f32[8,7,8,128]{3,2,1,0:T(8,128)S(1)} all-to-all(f32[8,7,8,128]{3,2,1,0:T(8,128)S(1)} %get-tuple-element.41), channel_id=1, replica_groups={{0,32,64,96,128,160,192,224},{4,36,68,100,132,164,196,228},{8,40,72,104..., dimensions={0} | all-to-all | bytes 458752 | tf_op jit(solution)/shard_map/all_to_all | solution.py:444
  34.9 0.1 shard_map.42
  35.0 3.2 %collective-permute-start.6 = (f32[2,8,128]{2,1,0:T(8,128)S(1)}, f32[2,8,128]{2,1,0:T(8,128)S(1)}, u32[]{:S(2)}, u32[]{:S(2)}) collective-permute-start(f32[2,8,128]{2,1,0:T(8,128)S(1)} %get-tuple-element.44), channel_id=1, source_target_pairs={{0,4},{4,0},{8,12},{12,8},{16,20},{20,16},{24,28},{28,24},{32,36},... | collective-permute-start | bytes 24584 | tf_op jit(solution)/shard_map/ppermute | solution.py:448
  38.2 0.2 shard_map.43.local
  38.4 0.7 %collective-permute-done.6.other = f32[2,8,128]{2,1,0:T(8,128)S(1)} collective-permute-done((f32[2,8,128]{2,1,0:T(8,128)S(1)}, f32[2,8,128]{2,1,0:T(8,128)S(1)}, u32[]{:S(2)}, u32[]{:S(2)}) %collective-permute-start.6) | collective-permute-done | bytes 8224 | tf_op jit(solution)/shard_map/ppermute | solution.py:448
  39.1 0.1 shard_map.44
  39.2 2.8 %collective-permute-start.7 = (f32[8,128]{1,0:T(8,128)S(1)}, f32[8,128]{1,0:T(8,128)S(1)}, u32[]{:S(2)}, u32[]{:S(2)}) collective-permute-start(f32[8,128]{1,0:T(8,128)S(1)} %get-tuple-element.50.message), channel_id=1, source_target_pairs={{0,2},{2,0},{1,3},{3,1},{4,6},{6,4},{5,7},{7,5},{8,10},{10,8},{9,1... | collective-permute-start | bytes 12296 | tf_op jit(solution)/shard_map/ppermute | solution.py:452
  42.0 0.9 %shard_map.45.local = f32[32,1024]{1,0:T(8,128)S(1)} custom-call(f32[32,1024]{1,0:T(8,128)S(1)} %get-tuple-element.51.section, f32[10,256,128]{2,1,0:T(8,128)S(1)} %get-tuple-element.52.ay, f32[10,256,128]{2,1,0:T(8,128)S(1)} %get-tuple-element.53.by, f32[256,128]{1,0:T(8,128)S(1)} %get-tuple-element.54.qy), custom_call_target="tpu_custom_call" | custom-call | flops 4000000 | bytes 3000000 | tf_op jit(solution)/shard_map/pallas_call | solution.py:453
  42.8 0.3 collective-permute-done.7.far
  43.2 0.9 %shard_map.46 = f32[32,1024]{1,0:T(8,128)} custom-call(f32[8,128]{1,0:T(8,128)S(1)} %get-tuple-element.50.message, f32[8,128]{1,0:T(8,128)S(1)} %collective-permute-done.7.far, f32[32,1024]{1,0:T(8,128)S(1)} %shard_map.45.local, f32[32,1024]{1,0:T(8,128)S(1)} %get-tuple-element.49.hy), custom_call_target="tpu_custom_call" | custom-call | tf_op jit(solution)/shard_map/pallas_call | solution.py:454
  (1 shorter events, 0.0 us)
Async XLA Ops:
  0.0 5.9 %collective-permute-start = (f32[2,1,16,1024]{3,2,1,0:T(8,128)}, f32[2,1,16,1024]{3,2,1,0:T(8,128)S(1)}, u32[]{:S(2)}, u32[]{:S(2)}) collective-permute-start(f32[2,1,16,1024]{3,2,1,0:T(8,128)} %param.3), channel_id=1, source_target_pairs={{0,1},{1,0},{2,3},{3,2},{4,5},{5,4},{6,7},{7,6},{8,9},{9,8},{10,11... | collective-permute-start | bytes 393224 | tf_op jit(solution)/shard_map/ppermute | solution.py:413
  2.0 5.0 %collective-permute-start.1 = (f32[2,1,16,1024]{3,2,1,0:T(8,128)}, f32[2,1,16,1024]{3,2,1,0:T(8,128)S(1)}, u32[]{:S(2)}, u32[]{:S(2)}) collective-permute-start(f32[2,1,16,1024]{3,2,1,0:T(8,128)} %param.5), channel_id=1, source_target_pairs={{0,1},{1,0},{2,3},{3,2},{4,5},{5,4},{6,7},{7,6},{8,9},{9,8},{10,11... | collective-permute-start | bytes 393224 | tf_op jit(solution)/shard_map/ppermute | solution.py:414
  7.1 3.7 %collective-permute-start.2 = (f32[7,8,128]{2,1,0:T(8,128)S(1)}, f32[7,8,128]{2,1,0:T(8,128)S(1)}, u32[]{:S(2)}, u32[]{:S(2)}) collective-permute-start(f32[7,8,128]{2,1,0:T(8,128)S(1)} %get-tuple-element.38), channel_id=1, source_target_pairs={{0,4},{4,0},{8,12},{12,8},{16,20},{20,16},{24,28},{28,24},{32,36},... | collective-permute-start | bytes 86024 | tf_op jit(solution)/shard_map/ppermute | solution.py:437
  10.9 4.3 %collective-permute-start.5 = (f32[7,8,128]{2,1,0:T(8,128)S(1)}, f32[7,8,128]{2,1,0:T(8,128)S(1)}, u32[]{:S(2)}, u32[]{:S(2)}) collective-permute-start(f32[7,8,128]{2,1,0:T(8,128)S(1)} %get-tuple-element.39.chip), channel_id=1, source_target_pairs={{0,16},{4,20},{8,24},{12,28},{16,0},{20,4},{24,8},{28,12},{32,48},... | collective-permute-start | bytes 86024 | tf_op jit(solution)/shard_map/ppermute | solution.py:440
  13.8 3.9 %collective-permute-start.4 = (f32[7,8,128]{2,1,0:T(8,128)S(1)}, f32[7,8,128]{2,1,0:T(8,128)S(1)}, u32[]{:S(2)}, u32[]{:S(2)}) collective-permute-start(f32[7,8,128]{2,1,0:T(8,128)S(1)} %get-tuple-element.39.chip), channel_id=1, source_target_pairs={{0,24},{4,28},{8,16},{12,20},{16,8},{20,12},{24,0},{28,4},{32,56},... | collective-permute-start | bytes 86024 | tf_op jit(solution)/shard_map/ppermute | solution.py:440
  14.6 3.2 %collective-permute-start.3 = (f32[7,8,128]{2,1,0:T(8,128)S(1)}, f32[7,8,128]{2,1,0:T(8,128)S(1)}, u32[]{:S(2)}, u32[]{:S(2)}) collective-permute-start(f32[7,8,128]{2,1,0:T(8,128)S(1)} %get-tuple-element.39.chip), channel_id=1, source_target_pairs={{0,8},{4,12},{8,0},{12,4},{16,24},{20,28},{24,16},{28,20},{32,40},... | collective-permute-start | bytes 86024 | tf_op jit(solution)/shard_map/ppermute | solution.py:440
  35.0 4.0 %collective-permute-start.6 = (f32[2,8,128]{2,1,0:T(8,128)S(1)}, f32[2,8,128]{2,1,0:T(8,128)S(1)}, u32[]{:S(2)}, u32[]{:S(2)}) collective-permute-start(f32[2,8,128]{2,1,0:T(8,128)S(1)} %get-tuple-element.44), channel_id=1, source_target_pairs={{0,4},{4,0},{8,12},{12,8},{16,20},{20,16},{24,28},{28,24},{32,36},... | collective-permute-start | bytes 24584 | tf_op jit(solution)/shard_map/ppermute | solution.py:448
  39.2 4.0 %collective-permute-start.7 = (f32[8,128]{1,0:T(8,128)S(1)}, f32[8,128]{1,0:T(8,128)S(1)}, u32[]{:S(2)}, u32[]{:S(2)}) collective-permute-start(f32[8,128]{1,0:T(8,128)S(1)} %get-tuple-element.50.message), channel_id=1, source_target_pairs={{0,2},{2,0},{1,3},{3,1},{4,6},{6,4},{5,7},{7,5},{8,10},{10,8},{9,1... | collective-permute-start | bytes 12296 | tf_op jit(solution)/shard_map/ppermute | solution.py:452

commit v11 on v9

--- a/solution.py
+++ b/solution.py
@@ -13,7 +13,7 @@
 ALL = 2 * ROWS
 VMEM = pl.BlockSpec(memory_space=pltpu.VMEM)
 HBM = pl.BlockSpec(memory_space=pltpu.HBM)
-X_STEPS = (1, 2, 4, 8)
+X_STEPS = (1, 2, 4, 8, 16)
 Y_STEPS = (1, 2, 4, 8, 16, 32, 64, 128, 256, 512)
 PARAMS = pltpu.CompilerParams(vmem_limit_bytes=40 * 1024 * 1024)
 
@@ -119,50 +119,66 @@
     )
 
 
-def factor_x_kernel(
-    fields_arg, vertical_arg, kappa_arg, fields, vertical, kappa, ax, bx, qx, h1, h2, parts, done
-):
-    pairs = ((kappa_arg, kappa), (fields_arg, fields), (vertical_arg, vertical))
+def own(even, mine, other):
+    return jnp.concatenate([jnp.where(even, mine, other), jnp.where(even, other, mine)], axis=0)
+
+
+def input_kernel(fields, vertical, kappa, same, cross, swapped, kappa_own, done):
+    core = lax.axis_index("gx") % 2
+    other = 1 - core
+    pairs = (
+        (fields.at[core], same.at[0]),
+        (vertical.at[core], same.at[1]),
+        (fields.at[other], cross.at[0]),
+        (vertical.at[other], cross.at[1]),
+        (fields.at[other], swapped.at[0]),
+        (vertical.at[other], swapped.at[1]),
+        (kappa.at[other], swapped.at[2]),
+        (kappa.at[core], kappa_own),
+    )
     copies = [pltpu.make_async_copy(a, b, done.at[n]) for n, (a, b) in enumerate(pairs)]
     for copy in copies:
         copy.start()
-    copies[0].wait()
-    half = 512
-    rows = lax.broadcasted_iota(jnp.int32, (ROWS, half), 0)
-    for f in range(2):
-        mine = pl.ds(f * ROWS, ROWS)
-        for c in range(COLS // half):
-            cols = pl.ds(c * half, half)
-            k = kappa[mine, cols]
-            face = (k + turn(k, 1, 0)) * 0.5
-            low = jnp.where((rows >= 2) & (rows <= 14), face, 0.0)
-            first = jnp.where(rows == 1, face, 0.0)
-            last = jnp.where(rows == 14, turn(face, -1, 0), 0.0)
-
-            def keep(index, a, b, mine=mine, cols=cols):
-                ax[index, mine, cols] = a
-                bx[index, mine, cols] = b
-
-            inverse, (one, two) = reduce_matrix(
-                low, 1.0 + first + last, [first, last], X_STEPS, turn_rows, keep
-            )
-            qx[mine, cols] = jnp.where((rows >= 1) & (rows <= 14), inverse, 0.0)
-            one = jnp.where(rows == 0, 1.0, one)
-            two = jnp.where(rows == ROWS - 1, 1.0, two)
-            h1[mine, cols] = one
-            h2[mine, cols] = two
-            sums = (
-                jnp.sum(first * two, axis=0, keepdims=True),
-                jnp.sum(one, axis=0, keepdims=True),
-                jnp.sum(two, axis=0, keepdims=True),
-                k[:1],
-                k[ROWS - 1 :],
-            )
-            for n, row in enumerate(sums):
-                for i in range(half // 128):
-                    parts[n, f, pl.ds(c * (half // 128) + i, 1), :] = row[:, 128 * i : 128 * (i + 1)]
-    copies[1].wait()
-    copies[2].wait()
+    for copy in copies:
+        copy.wait()
+
+
+def factor_x_kernel(kappa_own, swapped, kappa, ax, bx, qx, h1, h2, parts):
+    even = lax.axis_index("gx") % 2 == 0
+    kappa[...] = own(even, kappa_own[...], swapped[2])
+    width = 256
+    rows = lax.broadcasted_iota(jnp.int32, (ALL, width), 0)
+    inside = (rows >= 1) & (rows <= ALL - 2)
+    for c in range(COLS // width):
+        cols = pl.ds(c * width, width)
+        k = kappa[:, cols]
+        face = (k + turn(k, 1, 0)) * 0.5
+        low = jnp.where((rows >= 2) & (rows <= ALL - 2), face, 0.0)
+        first = jnp.where(rows == 1, face, 0.0)
+        last = jnp.where(rows == ALL - 2, turn(face, -1, 0), 0.0)
+
+        def keep(index, a, b, cols=cols):
+            ax[index, :, cols] = a
+            bx[index, :, cols] = b
+
+        inverse, (one, two) = reduce_matrix(
+            low, 1.0 + first + last, [first, last], X_STEPS, turn_rows, keep
+        )
+        qx[:, cols] = jnp.where(inside, inverse, 0.0)
+        one = jnp.where(rows == 0, 1.0, jnp.where(inside, one, 0.0))
+        two = jnp.where(rows == ALL - 1, 1.0, jnp.where(inside, two, 0.0))
+        h1[:, cols] = one
+        h2[:, cols] = two
+        sums = (
+            jnp.sum(first * two, axis=0, keepdims=True),
+            jnp.sum(one, axis=0, keepdims=True),
+            jnp.sum(two, axis=0, keepdims=True),
+            k[:1],
+            k[ALL - 1 :],
+        )
+        for n, row in enumerate(sums):
+            for i in range(width // 128):
+                parts[n, pl.ds(c * (width // 128) + i, 1), :] = row[:, 128 * i : 128 * (i + 1)]
 
 
 def factor_y_kernel(kappa, ay, by, qy, hy, edge):
@@ -201,33 +217,33 @@
     edge[...] = tile
 
 
-def source_kernel(fields, fields_far, vertical, vertical_far, h1, h2, parts, after, source, keep, send):
+def source_kernel(same, swapped, far_same, far_cross, h1, h2, parts, after, source, chip):
     del after
     even = lax.axis_index("gx") % 2 == 0
-    here = fields[...]
-    v = vertical[...]
-    s = here + (v + vertical_far[...]) * 0.5 * (fields_far[...] - here) - v * 0.5 * here
+
+    def flux(here, v, there, v_there):
+        return here + (v + v_there) * 0.5 * (there - here) - v * 0.5 * here
+
+    s = own(
+        even,
+        flux(same[0], same[1], far_same[0], far_same[1]),
+        flux(swapped[0], swapped[1], far_cross[0], far_cross[1]),
+    )
     source[...] = s
-    elements = []
-    for f in range(2):
-        mine = slice(f * ROWS, (f + 1) * ROWS)
-        first = dense(jnp.sum(h1[mine, :] * s[mine, :], axis=0, keepdims=True))
-        last = dense(jnp.sum(h2[mine, :] * s[mine, :], axis=0, keepdims=True))
-        elements.append((parts[0, f], parts[1, f], parts[2, f], first, last, parts[3, f], parts[4, f]))
-    for n, (one, two) in enumerate(zip(*elements)):
-        keep[n] = jnp.where(even, one, two)
-        send[n] = jnp.where(even, two, one)
+    first = dense(jnp.sum(h1[...] * s, axis=0, keepdims=True))
+    last = dense(jnp.sum(h2[...] * s, axis=0, keepdims=True))
+    for n, value in enumerate((parts[0], parts[1], parts[2], first, last, parts[3], parts[4])):
+        chip[n] = value
 
 
 def local_x_kernel(source, ax, bx, qx, out):
-    half = 512
-    for f in range(2):
-        mine = pl.ds(f * ROWS, ROWS)
-        for c in range(COLS // half):
-            cols = pl.ds(c * half, half)
-            r = source[mine, cols]
-            r = reduce_right(r, X_STEPS, turn_rows, lambda i: (ax[i, mine, cols], bx[i, mine, cols]))
-            out[mine, cols] = r * qx[mine, cols]
+    width = 256
+    for c in range(COLS // width):
+        cols = pl.ds(c * width, width)
+        r = reduce_right(
+            source[:, cols], X_STEPS, turn_rows, lambda i: (ax[i, :, cols], bx[i, :, cols])
+        )
+        out[:, cols] = r * qx[:, cols]
 
 
 def merge(one, two):
@@ -258,20 +274,8 @@
     return (a * left[0] + b * right[0], a * left[1] + b * right[1], a * left[2] + b * right[2] + c)
 
 
-def chip_kernel(keep, got, chip, middle):
-    even = lax.axis_index("gx") % 2 == 0
-    mine, other = load(keep), load(got)
-    first = [jnp.where(even, m, o) for m, o in zip(mine, other)]
-    second = [jnp.where(even, o, m) for m, o in zip(mine, other)]
-    tail, start = behind((first[6] + second[5]) * 0.5, second[:5])
-    element, end = merge(first[:5], tail)
-    for n, value in enumerate((*element, first[5], second[6])):
-        chip[n] = value
-    for n, value in enumerate((*end, *start)):
-        middle[n] = value
-
-
-def slab_kernel(chip, far1, far3, far2, middle, message, nodes):
+def slab_kernel(chip, far1, far3, far2, after, message, nodes):
+    del after
     y = lax.axis_index("gx") // 2 % 4
     arrived = [load(chip), load(far1), load(far2), load(far3)]
     chips = []
@@ -302,17 +306,13 @@
     for m in range(1, 4):
         first = [jnp.where(y == m, new, old) for new, old in zip(firsts[m], first)]
         last = [jnp.where(y == m, new, old) for new, old in zip(lasts[m], last)]
-    before = within(tuple(middle[n] for n in range(3)), first, last)
-    second = within(tuple(middle[n] for n in range(3, 6)), before, last)
-    for n, trio in enumerate((first, before, second, last)):
+    for n, trio in enumerate((first, last)):
         for m in range(3):
             nodes[n, m] = trio[m]
 
 
-def ends_kernel(got, nodes, mine, other):
-    gx = lax.axis_index("gx")
-    slab = gx // 8
-    even = gx % 2 == 0
+def ends_kernel(got, nodes, ends):
+    slab = lax.axis_index("gx") // 8
     zero = jnp.zeros((8, 128), F32)
     slabs, fronts = [], []
     for z in range(8):
@@ -344,25 +344,18 @@
         a, b, c = fronts[z]
         first = jnp.where(slab == z, a * values[z] + b * values[z + 1] + c, first)
         last = jnp.where(slab == z, values[z + 1], last)
-    row = [nodes[n, 0] * first + nodes[n, 1] * last + nodes[n, 2] for n in range(4)]
     for n in range(2):
-        mine[n] = jnp.where(even, row[n], row[n + 2])
-        other[n] = jnp.where(even, row[n + 2], row[n])
-
-
-def section_kernel(mine, other, local, h1, h2, hy, edge, section, message):
-    core = lax.axis_index("gx") % 2
+        ends[n] = nodes[n, 0] * first + nodes[n, 1] * last + nodes[n, 2]
+
+
+def section_kernel(ends, local, h1, h2, hy, edge, section, message):
     lane = lax.broadcasted_iota(jnp.int32, (8, 128), 1)
+    s = local[...] + h1[...] * natural(ends[0], ALL) + h2[...] * natural(ends[1], ALL)
+    section[...] = s
+    total = jnp.sum(hy[...] * s, axis=1, keepdims=True)
     tile = edge[...]
-    for f in range(2):
-        first = jnp.where(core == f, mine[0], other[0])
-        last = jnp.where(core == f, mine[1], other[1])
-        rows = slice(f * ROWS, (f + 1) * ROWS)
-        s = local[rows, :] + h1[rows, :] * natural(first, ROWS) + h2[rows, :] * natural(last, ROWS)
-        section[rows, :] = s
-        total = jnp.sum(hy[rows, :] * s, axis=1, keepdims=True)
-        for g in range(2):
-            tile = jnp.where(lane == 4 * (2 * f + g) + 2, total[8 * g : 8 * g + 8], tile)
+    for g in range(ALL // 8):
+        tile = jnp.where(lane == 4 * g + 2, total[8 * g : 8 * g + 8], tile)
     message[...] = tile
 
 
@@ -372,14 +365,25 @@
     out[...] = lie(r * qy[...])
 
 
-def output_kernel(message, far, local, hy, out):
+def result_kernel(message, far, local, hy, mine, ship):
+    even = lax.axis_index("gx") % 2 == 0
+    parts = []
     for g in range(ALL // 8):
         part = slice(8 * g, 8 * g + 8)
         e, k, r = (message[:, 4 * g + n : 4 * g + n + 1] for n in range(3))
         e2, k2, r2 = (far[:, 4 * g + n : 4 * g + n + 1] for n in range(3))
         c = (k + k2) * 0.5
         value = ((e2 + c) * r + c * r2) / (e * e2 + c * (e + e2))
-        out[part, :] = local[part, :] + hy[part, :] * value
+        parts.append(local[part, :] + hy[part, :] * value)
+    for g in range(2):
+        part = slice(8 * g, 8 * g + 8)
+        mine[part, :] = jnp.where(even, parts[g], parts[2 + g])
+        ship[part, :] = jnp.where(even, parts[2 + g], parts[g])
+
+
+def output_kernel(mine, got, out):
+    even = lax.axis_index("gx") % 2 == 0
+    out[...] = own(even, mine[...], got[...])
 
 
 def call(kernel, outs, specs, flops=0, size=0, scratch=()):
@@ -402,51 +406,64 @@
     return [(i, i ^ 2 * flip) for i in range(64)]
 
 
+SAME = [(2 * i + z, 2 * i + 1 - z) for i in range(64) for z in range(2)]
+CROSS = [(2 * i + z, 2 * (i ^ 1) + 1 - z) for i in range(64) for z in range(2)]
+
+
 def local(fields, kappa, vertical):
     grid = (ALL, COLS)
-    swap = [(0, 1), (1, 0)]
-    fields_far = lax.ppermute(fields, "gz", swap)
-    vertical_far = lax.ppermute(vertical, "gz", swap)
     full = shape(*grid)
-    half = shape(7, 8, 128)
-    standing = shape(256, 128)
-    fields_here, vertical_here, kappa_here, ax, bx, qx, h1, h2, parts = call(
+    tile = shape(8, 128)
+    element = shape(7, 8, 128)
+    two = shape(2, ROWS, COLS)
+    three = shape(3, ROWS, COLS)
+    same, cross, swapped, kappa_own = call(
+        input_kernel,
+        (two, two, three, shape(ROWS, COLS)),
+        [HBM] * 3,
+        flops=1_000_000,
+        size=1_000_000,
+        scratch=[pltpu.SemaphoreType.DMA((8,))],
+    )(
+        *(
+            pltpu.with_memory_space_constraint(x.reshape(2, ROWS, COLS), pltpu.HBM)
+            for x in (fields, vertical, kappa)
+        )
+    )
+    far_same = lax.ppermute(same, ("gx", "gz"), SAME)
+    far_cross = lax.ppermute(cross, ("gx", "gz"), CROSS)
+    swapped = lax.ppermute(swapped, "gx", CORES)
+    kappa_here, ax, bx, qx, h1, h2, parts = call(
         factor_x_kernel,
-        (full, full, full, shape(4, *grid), shape(4, *grid), full, full, full, shape(5, 2, 8, 128)),
-        [HBM] * 3,
+        (full, shape(5, *grid), shape(5, *grid), full, full, full, shape(5, 8, 128)),
+        [VMEM] * 2,
         flops=4_000_000,
         size=2_000_000,
-        scratch=[pltpu.SemaphoreType.DMA((3,))],
-    )(*(pltpu.with_memory_space_constraint(x.reshape(grid), pltpu.HBM) for x in (fields, vertical, kappa)))
+    )(kappa_own, swapped)
     ay, by, qy, hy, edge = call(
         factor_y_kernel,
-        (shape(10, 256, 128), shape(10, 256, 128), standing, full, shape(8, 128)),
+        (shape(10, 256, 128), shape(10, 256, 128), shape(256, 128), full, tile),
         [VMEM],
         flops=20_000_000,
         size=4_000_000,
     )(kappa_here)
-    source, keep, send = call(source_kernel, (full, half, half), [VMEM] * 8)(
-        fields_here, fields_far.reshape(grid), vertical_here, vertical_far.reshape(grid),
-        h1, h2, parts, edge,
-    )
-    got = lax.ppermute(send, "gx", CORES)
+    source, chip = call(source_kernel, (full, element), [VMEM] * 8)(
+        same, swapped, far_same, far_cross, h1, h2, parts, edge
+    )
     local_x = call(local_x_kernel, full, [VMEM] * 4, flops=1_000_000, size=1_000_000)(source, ax, bx, qx)
-    chip, middle = call(chip_kernel, (half, shape(6, 8, 128)), [VMEM] * 2)(keep, got)
     far = [lax.ppermute(chip, "gx", chips_across(flip)) for flip in (1, 3, 2)]
     message, nodes = call(
-        slab_kernel, (shape(8, 7, 8, 128), shape(4, 3, 8, 128)), [VMEM] * 5
-    )(chip, *far, middle)
+        slab_kernel, (shape(8, 7, 8, 128), shape(2, 3, 8, 128)), [VMEM] * 5
+    )(chip, *far, local_x)
     got = lax.all_to_all(message, "gx", 0, 0, axis_index_groups=SLAB_GROUPS, tiled=True)
-    mine, other = call(
-        ends_kernel, (shape(2, 8, 128), shape(2, 8, 128)), [VMEM, VMEM]
-    )(got, nodes)
-    other = lax.ppermute(other, "gx", CORES)
-    section, message = call(
-        section_kernel, (full, shape(8, 128)), [VMEM] * 7
-    )(mine, other, local_x, h1, h2, hy, edge)
-    far = lax.ppermute(message, "gy", swap)
+    ends = call(ends_kernel, shape(2, 8, 128), [VMEM] * 2)(got, nodes)
+    section, message = call(section_kernel, (full, tile), [VMEM] * 6)(ends, local_x, h1, h2, hy, edge)
+    far = lax.ppermute(message, "gy", [(0, 1), (1, 0)])
     local_y = call(local_y_kernel, full, [VMEM] * 4, flops=4_000_000, size=3_000_000)(section, ay, by, qy)
-    out = call(output_kernel, full, [VMEM] * 4)(message, far, local_y, hy)
+    rows = shape(ROWS, COLS)
+    mine, ship = call(result_kernel, (rows, rows), [VMEM] * 4)(message, far, local_y, hy)
+    got = lax.ppermute(ship, "gx", CORES)
+    out = call(output_kernel, full, [VMEM] * 2)(mine, got)
     return out.reshape(fields.shape)
 
 

time: 44.2 us -> 45.8 us (1.036)
  waiting for transfers between devices: 6.19 us -> 6.95 us
  starting transfers between devices: 14.6 us -> 15.3 us
    ppermute x5, starting transfers between devices: 10.9 us -> 12.5 us  [the longest x1 4.99 us: local(): got = lax.ppermute(ship, 'gx', CORES)]
    ppermute x5, waiting for transfers between devices: 3.04 us -> 4.65 us  [the longest x1 2 us: local(): far_same = lax.ppermute(same, ('gx', 'gz'), SAME)]
    ppermute x3, starting transfers between devices: 3.72 us -> 2.74 us  [local(): far = [lax.ppermute(chip, 'gx', chips_across(flip)) for flip in (1, 3, 2)]]
    ppermute x3, waiting for transfers between devices: 3.16 us -> 2.3 us  [local(): far = [lax.ppermute(chip, 'gx', chips_across(flip)) for flip in (1, 3, 2)]]
    pallas_call x8 -> x9, Pallas kernels: 5.1 us -> 5.29 us  [the longest x1 2.15 us: local(): call(factor_y_kernel, (shape(10, 256, 128), shape(10, 256, 128), shape(25...]
  transfers between devices with their start and end apart: 8 -> 8, of which waited for: 6 -> 6; matrix products, arithmetic and copies ran while one was open for 0% -> 0% of each run, Pallas kernels for 11% -> 9%
where the time goes in v11:
time: 45.8 us; the launch traced here: 45.6 us
  blocking collectives  17 us (37%)
  starting transfers between devices  15.3 us (33%)
  waiting for transfers between devices  6.95 us (15%)
  Pallas kernels  6.35 us (14%)
    all_to_all x1, blocking collectives, local(): lax.all_to_all(message, 'gx', 0, 0, axis_index_groups=SLAB_GROUPS, tiled=...  17 us
    ppermute x1, starting transfers between devices, local(): got = lax.ppermute(ship, 'gx', CORES)  4.99 us
    ppermute x1, starting transfers between devices, local(): swapped = lax.ppermute(swapped, 'gx', CORES)  3.33 us
    ppermute x1, starting transfers between devices, local(): far = lax.ppermute(message, 'gy', [(0, 1), (1, 0)])  2.77 us
    ppermute x3, starting transfers between devices, local(): far = [lax.ppermute(chip, 'gx', chips_across(flip)) for flip in (1, 3, 2)]  2.74 us
    ppermute x3, waiting for transfers between devices, local(): far = [lax.ppermute(chip, 'gx', chips_across(flip)) for flip in (1, 3, 2)]  2.3 us
    pallas_call x1, Pallas kernels, local(): call(factor_y_kernel, (shape(10, 256, 128), shape(10, 256, 128), shape(25...  2.15 us
    ppermute x1, waiting for transfers between devices, local(): far_same = lax.ppermute(same, ('gx', 'gz'), SAME)  2 us
  transfers between devices with their start and end apart: 8, of which 6 were waited for; matrix products, arithmetic and copies ran while one was open for 0% of the time, Pallas kernels for 9%

profile of v11, /device:TPU:1, one launch (start us, length us, event | category | flops | bytes accessed | tf_op | source)
XLA Modules:
  0.0 45.6 jit_solution(10007640924254324197)
XLA Ops:
  0.0 1.1 %shard_map.37 = (f32[2,16,1024]{2,1,0:T(8,128)S(1)}, f32[2,16,1024]{2,1,0:T(8,128)S(1)}, f32[3,16,1024]{2,1,0:T(8,128)S(1)}, f32[16,1024]{1,0:T(8,128)S(1)}) custom-call(f32[2,16,1024]{2,1,0:T(8,128)} %bitcast.6, f32[2,16,1024]{2,1,0:T(8,128)} %bitcast.7, f32[2,16,1024]{2,1,0:T(8,128)} %bitcast.8), custom_call_target="tpu_custom_call" | custom-call | flops 1000000 | bytes 1000000 | tf_op jit(solution)/shard_map/pallas_call | solution.py:420
  1.1 3.3 %collective-permute-start = (f32[3,16,1024]{2,1,0:T(8,128)S(1)}, f32[3,16,1024]{2,1,0:T(8,128)S(1)}, u32[]{:S(2)}, u32[]{:S(2)}) collective-permute-start(f32[3,16,1024]{2,1,0:T(8,128)S(1)} %get-tuple-element.30), channel_id=1, source_target_pairs={{0,4},{4,0},{8,12},{12,8},{16,20},{20,16},{24,28},{28,24},{32,36},... | collective-permute-start | bytes 589832 | tf_op jit(solution)/shard_map/ppermute | solution.py:435
  4.5 0.0 collective-permute-start.2
  4.5 1.4 %collective-permute-start.1 = (f32[2,16,1024]{2,1,0:T(8,128)S(1)}, f32[2,16,1024]{2,1,0:T(8,128)S(1)}, u32[]{:S(2)}, u32[]{:S(2)}) collective-permute-start(f32[2,16,1024]{2,1,0:T(8,128)S(1)} %get-tuple-element.29.same), channel_id=1, source_target_pairs={{0,1},{1,0},{4,5},{5,4},{8,9},{9,8},{12,13},{13,12},{16,17},{17,16... | collective-permute-start | bytes 393224 | tf_op jit(solution)/shard_map/ppermute | solution.py:433
  5.9 0.0 collective-permute-done.swapped
  5.9 0.7 %shard_map.38 = (f32[32,1024]{1,0:T(8,128)S(1)}, f32[5,32,1024]{2,1,0:T(8,128)S(1)}, f32[5,32,1024]{2,1,0:T(8,128)S(1)}, f32[32,1024]{1,0:T(8,128)S(1)}, f32[32,...) custom-call(f32[16,1024]{1,0:T(8,128)S(1)} %get-tuple-element.32.kappa_own, ...), custom_call_target="tpu_custom_call" | custom-call | flops 4000000 | bytes 2000000 | tf_op jit(solution)/shard_map/pallas_call | solution.py:436
  6.6 2.2 %shard_map.39 = (f32[10,256,128]{2,1,0:T(8,128)S(1)}, f32[10,256,128]{2,1,0:T(8,128)S(1)}, f32[256,128]{1,0:T(8,128)S(1)}, f32[32,1024]{1,0:T(8,128)S(1)}, f32[8,128]{1,0:T(8,128)S(1)}) custom-call(f32[32,1024]{1,0:T(8,128)S(1)} %get-tuple-element.36.kappa), custom_call_target="tpu_custom_call" | custom-call | flops 20000000 | bytes 4000000 | tf_op jit(solution)/shard_map/pallas_call | solution.py:443
  8.8 1.4 %collective-permute-done.2.far_cross = f32[2,16,1024]{2,1,0:T(8,128)S(1)} collective-permute-done((f32[2,16,1024]{2,1,0:T(8,128)S(1)}, f32[2,16,1024]{2,1,0:T(8,128)S(1)}, u32[]{:S(2)}, u32[]{:S(2)}) %collective-permute-start.2) | collective-permute-done | bytes 131104 | tf_op jit(solution)/shard_map/ppermute | solution.py:434
  10.2 2.0 %collective-permute-done.1.far_same = f32[2,16,1024]{2,1,0:T(8,128)S(1)} collective-permute-done((f32[2,16,1024]{2,1,0:T(8,128)S(1)}, f32[2,16,1024]{2,1,0:T(8,128)S(1)}, u32[]{:S(2)}, u32[]{:S(2)}) %collective-permute-start.1) | collective-permute-done | bytes 131104 | tf_op jit(solution)/shard_map/ppermute | solution.py:433
  12.2 0.1 shard_map.40
  12.3 1.3 %collective-permute-start.5 = (f32[7,8,128]{2,1,0:T(8,128)S(1)}, f32[7,8,128]{2,1,0:T(8,128)S(1)}, u32[]{:S(2)}, u32[]{:S(2)}) collective-permute-start(f32[7,8,128]{2,1,0:T(8,128)S(1)} %get-tuple-element.38.chip), channel_id=1, source_target_pairs={{0,16},{4,20},{8,24},{12,28},{16,0},{20,4},{24,8},{28,12},{32,48},... | collective-permute-start | bytes 86024 | tf_op jit(solution)/shard_map/ppermute | solution.py:454
  13.6 0.8 %collective-permute-start.4 = (f32[7,8,128]{2,1,0:T(8,128)S(1)}, f32[7,8,128]{2,1,0:T(8,128)S(1)}, u32[]{:S(2)}, u32[]{:S(2)}) collective-permute-start(f32[7,8,128]{2,1,0:T(8,128)S(1)} %get-tuple-element.38.chip), channel_id=1, source_target_pairs={{0,24},{4,28},{8,16},{12,20},{16,8},{20,12},{24,0},{28,4},{32,56},... | collective-permute-start | bytes 86024 | tf_op jit(solution)/shard_map/ppermute | solution.py:454
  14.3 0.7 %collective-permute-start.3 = (f32[7,8,128]{2,1,0:T(8,128)S(1)}, f32[7,8,128]{2,1,0:T(8,128)S(1)}, u32[]{:S(2)}, u32[]{:S(2)}) collective-permute-start(f32[7,8,128]{2,1,0:T(8,128)S(1)} %get-tuple-element.38.chip), channel_id=1, source_target_pairs={{0,8},{4,12},{8,0},{12,4},{16,24},{20,28},{24,16},{28,20},{32,40},... | collective-permute-start | bytes 86024 | tf_op jit(solution)/shard_map/ppermute | solution.py:454
  15.0 0.2 shard_map.41.after.local
  15.2 1.4 %collective-permute-done.5.far2 = f32[7,8,128]{2,1,0:T(8,128)S(1)} collective-permute-done((f32[7,8,128]{2,1,0:T(8,128)S(1)}, f32[7,8,128]{2,1,0:T(8,128)S(1)}, u32[]{:S(2)}, u32[]{:S(2)}) %collective-permute-start.5) | collective-permute-done | bytes 28704 | tf_op jit(solution)/shard_map/ppermute | solution.py:454
  16.6 0.9 %collective-permute-done.4.far3 = f32[7,8,128]{2,1,0:T(8,128)S(1)} collective-permute-done((f32[7,8,128]{2,1,0:T(8,128)S(1)}, f32[7,8,128]{2,1,0:T(8,128)S(1)}, u32[]{:S(2)}, u32[]{:S(2)}) %collective-permute-start.4) | collective-permute-done | bytes 28704 | tf_op jit(solution)/shard_map/ppermute | solution.py:454
  17.5 0.0 collective-permute-done.3.far1
  17.5 0.1 shard_map.42
  17.6 17.0 %all_to_all.5.got = f32[8,7,8,128]{3,2,1,0:T(8,128)S(1)} all-to-all(f32[8,7,8,128]{3,2,1,0:T(8,128)S(1)} %get-tuple-element.43), channel_id=1, replica_groups={{0,32,64,96,128,160,192,224},{4,36,68,100,132,164,196,228},{8,40,72,104..., dimensions={0} | all-to-all | bytes 458752 | tf_op jit(solution)/shard_map/all_to_all | solution.py:458
  34.6 0.1 shard_map.43.ends
  34.7 0.1 shard_map.44
  34.9 2.8 %collective-permute-start.6 = (f32[8,128]{1,0:T(8,128)S(1)}, f32[8,128]{1,0:T(8,128)S(1)}, u32[]{:S(2)}, u32[]{:S(2)}) collective-permute-start(f32[8,128]{1,0:T(8,128)S(1)} %get-tuple-element.46.message), channel_id=1, source_target_pairs={{0,2},{2,0},{1,3},{3,1},{4,6},{6,4},{5,7},{7,5},{8,10},{10,8},{9,1... | collective-permute-start | bytes 12296 | tf_op jit(solution)/shard_map/ppermute | solution.py:461
  37.6 0.9 %shard_map.45.local = f32[32,1024]{1,0:T(8,128)S(1)} custom-call(f32[32,1024]{1,0:T(8,128)S(1)} %get-tuple-element.47.section, f32[10,256,128]{2,1,0:T(8,128)S(1)} %get-tuple-element.48.ay, f32[10,256,128]{2,1,0:T(8,128)S(1)} %get-tuple-element.49.by, f32[256,128]{1,0:T(8,128)S(1)} %get-tuple-element.50.qy), custom_call_target="tpu_custom_call" | custom-call | flops 4000000 | bytes 3000000 | tf_op jit(solution)/shard_map/pallas_call | solution.py:462
  38.5 0.3 collective-permute-done.6.far
  38.8 0.2 shard_map.46
  39.1 5.0 %collective-permute-start.7 = (f32[16,1024]{1,0:T(8,128)S(1)}, f32[16,1024]{1,0:T(8,128)S(1)}, u32[]{:S(2)}, u32[]{:S(2)}) collective-permute-start(f32[16,1024]{1,0:T(8,128)S(1)} %get-tuple-element.52), channel_id=1, source_target_pairs={{0,4},{4,0},{8,12},{12,8},{16,20},{20,16},{24,28},{28,24},{32,36},... | collective-permute-start | bytes 196616 | tf_op jit(solution)/shard_map/ppermute | solution.py:465
  44.1 0.9 %collective-permute-done.7.got = f32[16,1024]{1,0:T(8,128)S(1)} collective-permute-done((f32[16,1024]{1,0:T(8,128)S(1)}, f32[16,1024]{1,0:T(8,128)S(1)}, u32[]{:S(2)}, u32[]{:S(2)}) %collective-permute-start.7) | collective-permute-done | bytes 65568 | tf_op jit(solution)/shard_map/ppermute | solution.py:465
  45.0 0.7 %shard_map.47 = f32[32,1024]{1,0:T(8,128)} custom-call(f32[16,1024]{1,0:T(8,128)S(1)} %get-tuple-element.51.mine, f32[16,1024]{1,0:T(8,128)S(1)} %collective-permute-done.7.got), custom_call_target="tpu_custom_call" | custom-call | tf_op jit(solution)/shard_map/pallas_call | solution.py:466
Async XLA Ops:
  1.1 4.8 %collective-permute-start = (f32[3,16,1024]{2,1,0:T(8,128)S(1)}, f32[3,16,1024]{2,1,0:T(8,128)S(1)}, u32[]{:S(2)}, u32[]{:S(2)}) collective-permute-start(f32[3,16,1024]{2,1,0:T(8,128)S(1)} %get-tuple-element.30), channel_id=1, source_target_pairs={{0,4},{4,0},{8,12},{12,8},{16,20},{20,16},{24,28},{28,24},{32,36},... | collective-permute-start | bytes 589832 | tf_op jit(solution)/shard_map/ppermute | solution.py:435
  4.5 5.8 %collective-permute-start.2 = (f32[2,16,1024]{2,1,0:T(8,128)S(1)}, f32[2,16,1024]{2,1,0:T(8,128)S(1)}, u32[]{:S(2)}, u32[]{:S(2)}) collective-permute-start(f32[2,16,1024]{2,1,0:T(8,128)S(1)} %get-tuple-element.31), channel_id=1, source_target_pairs={{0,5},{1,4},{4,1},{5,0},{8,13},{9,12},{12,9},{13,8},{16,21},{17,20... | collective-permute-start | bytes 393224 | tf_op jit(solution)/shard_map/ppermute | solution.py:434
  4.5 7.8 %collective-permute-start.1 = (f32[2,16,1024]{2,1,0:T(8,128)S(1)}, f32[2,16,1024]{2,1,0:T(8,128)S(1)}, u32[]{:S(2)}, u32[]{:S(2)}) collective-permute-start(f32[2,16,1024]{2,1,0:T(8,128)S(1)} %get-tuple-element.29.same), channel_id=1, source_target_pairs={{0,1},{1,0},{4,5},{5,4},{8,9},{9,8},{12,13},{13,12},{16,17},{17,16... | collective-permute-start | bytes 393224 | tf_op jit(solution)/shard_map/ppermute | solution.py:433
  12.3 4.3 %collective-permute-start.5 = (f32[7,8,128]{2,1,0:T(8,128)S(1)}, f32[7,8,128]{2,1,0:T(8,128)S(1)}, u32[]{:S(2)}, u32[]{:S(2)}) collective-permute-start(f32[7,8,128]{2,1,0:T(8,128)S(1)} %get-tuple-element.38.chip), channel_id=1, source_target_pairs={{0,16},{4,20},{8,24},{12,28},{16,0},{20,4},{24,8},{28,12},{32,48},... | collective-permute-start | bytes 86024 | tf_op jit(solution)/shard_map/ppermute | solution.py:454
  13.6 3.9 %collective-permute-start.4 = (f32[7,8,128]{2,1,0:T(8,128)S(1)}, f32[7,8,128]{2,1,0:T(8,128)S(1)}, u32[]{:S(2)}, u32[]{:S(2)}) collective-permute-start(f32[7,8,128]{2,1,0:T(8,128)S(1)} %get-tuple-element.38.chip), channel_id=1, source_target_pairs={{0,24},{4,28},{8,16},{12,20},{16,8},{20,12},{24,0},{28,4},{32,56},... | collective-permute-start | bytes 86024 | tf_op jit(solution)/shard_map/ppermute | solution.py:454
  14.3 3.2 %collective-permute-start.3 = (f32[7,8,128]{2,1,0:T(8,128)S(1)}, f32[7,8,128]{2,1,0:T(8,128)S(1)}, u32[]{:S(2)}, u32[]{:S(2)}) collective-permute-start(f32[7,8,128]{2,1,0:T(8,128)S(1)} %get-tuple-element.38.chip), channel_id=1, source_target_pairs={{0,8},{4,12},{8,0},{12,4},{16,24},{20,28},{24,16},{28,20},{32,40},... | collective-permute-start | bytes 86024 | tf_op jit(solution)/shard_map/ppermute | solution.py:454
  34.9 4.0 %collective-permute-start.6 = (f32[8,128]{1,0:T(8,128)S(1)}, f32[8,128]{1,0:T(8,128)S(1)}, u32[]{:S(2)}, u32[]{:S(2)}) collective-permute-start(f32[8,128]{1,0:T(8,128)S(1)} %get-tuple-element.46.message), channel_id=1, source_target_pairs={{0,2},{2,0},{1,3},{3,1},{4,6},{6,4},{5,7},{7,5},{8,10},{10,8},{9,1... | collective-permute-start | bytes 12296 | tf_op jit(solution)/shard_map/ppermute | solution.py:461
  39.1 5.9 %collective-permute-start.7 = (f32[16,1024]{1,0:T(8,128)S(1)}, f32[16,1024]{1,0:T(8,128)S(1)}, u32[]{:S(2)}, u32[]{:S(2)}) collective-permute-start(f32[16,1024]{1,0:T(8,128)S(1)} %get-tuple-element.52), channel_id=1, source_target_pairs={{0,4},{4,0},{8,12},{12,8},{16,20},{20,16},{24,28},{28,24},{32,36},... | collective-permute-start | bytes 196616 | tf_op jit(solution)/shard_map/ppermute | solution.py:465

commit v12 on v9

--- a/solution.py
+++ b/solution.py
@@ -201,22 +201,19 @@
     edge[...] = tile
 
 
-def source_kernel(fields, fields_far, vertical, vertical_far, h1, h2, parts, after, source, keep, send):
+def source_kernel(fields, fields_far, vertical, vertical_far, h1, h2, parts, after, source, elements):
     del after
-    even = lax.axis_index("gx") % 2 == 0
     here = fields[...]
     v = vertical[...]
     s = here + (v + vertical_far[...]) * 0.5 * (fields_far[...] - here) - v * 0.5 * here
     source[...] = s
-    elements = []
     for f in range(2):
         mine = slice(f * ROWS, (f + 1) * ROWS)
         first = dense(jnp.sum(h1[mine, :] * s[mine, :], axis=0, keepdims=True))
         last = dense(jnp.sum(h2[mine, :] * s[mine, :], axis=0, keepdims=True))
-        elements.append((parts[0, f], parts[1, f], parts[2, f], first, last, parts[3, f], parts[4, f]))
-    for n, (one, two) in enumerate(zip(*elements)):
-        keep[n] = jnp.where(even, one, two)
-        send[n] = jnp.where(even, two, one)
+        element = (parts[0, f], parts[1, f], parts[2, f], first, last, parts[3, f], parts[4, f])
+        for n, value in enumerate(element):
+            elements[f, n] = value
 
 
 def local_x_kernel(source, ax, bx, qx, out):
@@ -249,8 +246,8 @@
     return (a * g, a * s, sr + b * s, a * r, rr + b * r), (a, b, r * inverse)
 
 
-def load(ref):
-    return tuple(ref[n] for n in range(7))
+def load(ref, *field):
+    return tuple(ref[(*field, n)] for n in range(7))
 
 
 def within(node, left, right):
@@ -258,22 +255,36 @@
     return (a * left[0] + b * right[0], a * left[1] + b * right[1], a * left[2] + b * right[2] + c)
 
 
-def chip_kernel(keep, got, chip, middle):
+def chip_kernel(mine, other, chips, chip, middle):
     even = lax.axis_index("gx") % 2 == 0
-    mine, other = load(keep), load(got)
-    first = [jnp.where(even, m, o) for m, o in zip(mine, other)]
-    second = [jnp.where(even, o, m) for m, o in zip(mine, other)]
-    tail, start = behind((first[6] + second[5]) * 0.5, second[:5])
-    element, end = merge(first[:5], tail)
-    for n, value in enumerate((*element, first[5], second[6])):
-        chip[n] = value
-    for n, value in enumerate((*end, *start)):
-        middle[n] = value
-
-
-def slab_kernel(chip, far1, far3, far2, middle, message, nodes):
+    fields = []
+    for f in range(2):
+        a, b = load(mine, f), load(other, f)
+        first = [jnp.where(even, m, o) for m, o in zip(a, b)]
+        second = [jnp.where(even, o, m) for m, o in zip(a, b)]
+        tail, start = behind((first[6] + second[5]) * 0.5, second[:5])
+        element, end = merge(first[:5], tail)
+        fields.append(((*element, first[5], second[6]), (*end, *start)))
+        for n, value in enumerate(fields[f][0]):
+            chips[f, n] = value
+    for out, (one, two) in zip((chip, middle), zip(*fields)):
+        for n, (a, b) in enumerate(zip(one, two)):
+            out[n] = jnp.where(even, a, b)
+
+
+def pick_kernel(chips, keep, send):
+    even = lax.axis_index("gx") % 2 == 0
+    for n, (one, two) in enumerate(zip(load(chips, 0), load(chips, 1))):
+        keep[n] = jnp.where(even, one, two)
+        send[n] = jnp.where(even, two, one)
+
+
+def slab_kernel(chip, far1, keep, got, middle, message, nodes):
     y = lax.axis_index("gx") // 2 % 4
-    arrived = [load(chip), load(far1), load(far2), load(far3)]
+    even = lax.axis_index("gx") % 2 == 0
+    far2 = [jnp.where(even, g, k) for k, g in zip(load(keep), load(got))]
+    far3 = [jnp.where(even, k, g) for k, g in zip(load(keep), load(got))]
+    arrived = [load(chip), load(far1), far2, far3]
     chips = []
     for m in range(4):
         chosen = arrived[0]
@@ -398,8 +409,8 @@
 CORES = [(i, i ^ 1) for i in range(64)]
 
 
-def chips_across(flip):
-    return [(i, i ^ 2 * flip) for i in range(64)]
+CHIPS = [(i, i ^ (4 if i % 2 else 6)) for i in range(64)]
+NEXT = [(i, i ^ 2) for i in range(64)]
 
 
 def local(fields, kappa, vertical):
@@ -425,17 +436,21 @@
         flops=20_000_000,
         size=4_000_000,
     )(kappa_here)
-    source, keep, send = call(source_kernel, (full, half, half), [VMEM] * 8)(
+    both = shape(2, 7, 8, 128)
+    source, elements = call(source_kernel, (full, both), [VMEM] * 8)(
         fields_here, fields_far.reshape(grid), vertical_here, vertical_far.reshape(grid),
         h1, h2, parts, edge,
     )
+    got = lax.ppermute(elements, "gx", CORES)
+    local_x = call(local_x_kernel, full, [VMEM] * 4, flops=1_000_000, size=1_000_000)(source, ax, bx, qx)
+    chips, chip, middle = call(chip_kernel, (both, half, shape(6, 8, 128)), [VMEM] * 2)(elements, got)
+    far = lax.ppermute(chips, "gx", CHIPS)
+    far1 = lax.ppermute(chip, "gx", NEXT)
+    keep, send = call(pick_kernel, (half, half), [VMEM])(far)
     got = lax.ppermute(send, "gx", CORES)
-    local_x = call(local_x_kernel, full, [VMEM] * 4, flops=1_000_000, size=1_000_000)(source, ax, bx, qx)
-    chip, middle = call(chip_kernel, (half, shape(6, 8, 128)), [VMEM] * 2)(keep, got)
-    far = [lax.ppermute(chip, "gx", chips_across(flip)) for flip in (1, 3, 2)]
     message, nodes = call(
         slab_kernel, (shape(8, 7, 8, 128), shape(4, 3, 8, 128)), [VMEM] * 5
-    )(chip, *far, middle)
+    )(chip, far1, keep, got, middle)
     got = lax.all_to_all(message, "gx", 0, 0, axis_index_groups=SLAB_GROUPS, tiled=True)
     mine, other = call(
         ends_kernel, (shape(2, 8, 128), shape(2, 8, 128)), [VMEM, VMEM]

time: 44.2 us -> 44.1 us (level)
  waiting for transfers between devices: 6.19 us -> 5.22 us
  blocking collectives: 17.1 us -> 17.9 us
    ppermute x3, starting transfers between devices: 3.72 us -> 6.2 us  [the longest x1 2.94 us: local(): far = lax.ppermute(chips, 'gx', CHIPS)]
    ppermute x1, starting transfers between devices: 2.87 us -> 1.39 us  [local(): got = lax.ppermute(send, 'gx', CORES)]
    ppermute x1, starting transfers between devices: 3.19 us -> 2.19 us  [local(): other = lax.ppermute(other, 'gx', CORES)]
    ppermute x3, waiting for transfers between devices: 3.16 us -> 2.18 us  [the longest x1 1.29 us: local(): far = lax.ppermute(chips, 'gx', CHIPS)]
    all_to_all x1, blocking collectives: 17.1 us -> 17.9 us  [local(): lax.all_to_all(message, 'gx', 0, 0, axis_index_groups=SLAB_GROUPS, tiled=...]
where the time goes in v12:
time: 44.1 us; the launch traced here: 44 us
  blocking collectives  17.9 us (41%)
  starting transfers between devices  14.6 us (33%)
  Pallas kernels  6.15 us (14%)
  waiting for transfers between devices  5.22 us (12%)
    all_to_all x1, blocking collectives, local(): lax.all_to_all(message, 'gx', 0, 0, axis_index_groups=SLAB_GROUPS, tiled=...  17.9 us
    ppermute x1, starting transfers between devices, local(): far = lax.ppermute(chips, 'gx', CHIPS)  2.94 us
    ppermute x1, starting transfers between devices, local(): got = lax.ppermute(elements, 'gx', CORES)  2.87 us
    ppermute x1, starting transfers between devices, local(): far = lax.ppermute(message, 'gy', swap)  2.77 us
    ppermute x1, starting transfers between devices, local(): other = lax.ppermute(other, 'gx', CORES)  2.19 us
    pallas_call x1, Pallas kernels, local(): call(factor_y_kernel, (shape(10, 256, 128), shape(10, 256, 128), standing...  2.15 us
    ppermute x1, starting transfers between devices, local(): fields_far = lax.ppermute(fields, 'gz', swap)  2.04 us
    pallas_call x1, Pallas kernels, local(): call(factor_x_kernel, (full, full, full, shape(4, *grid), shape(4, *grid)...  1.62 us
  transfers between devices with their start and end apart: 8, of which 6 were waited for; matrix products, arithmetic and copies ran while one was open for 0% of the time, Pallas kernels for 11%

profile of v12, /device:TPU:1, one launch (start us, length us, event | category | flops | bytes accessed | tf_op | source)
XLA Modules:
  0.0 44.0 jit_solution(8492917360852446163)
XLA Ops:
  0.0 2.0 %collective-permute-start = (f32[2,1,16,1024]{3,2,1,0:T(8,128)}, f32[2,1,16,1024]{3,2,1,0:T(8,128)S(1)}, u32[]{:S(2)}, u32[]{:S(2)}) collective-permute-start(f32[2,1,16,1024]{3,2,1,0:T(8,128)} %param.3), channel_id=1, source_target_pairs={{0,1},{1,0},{2,3},{3,2},{4,5},{5,4},{6,7},{7,6},{8,9},{9,8},{10,11... | collective-permute-start | bytes 393224 | tf_op jit(solution)/shard_map/ppermute | solution.py:419
  2.0 0.0 collective-permute-start.1
  2.1 1.6 %shard_map.37 = (f32[32,1024]{1,0:T(8,128)S(1)}, f32[32,1024]{1,0:T(8,128)S(1)}, f32[32,1024]{1,0:T(8,128)S(1)}, f32[4,32,1024]{2,1,0:T(8,128)S(1)}, f32[4,32,10...) custom-call(f32[32,1024]{1,0:T(8,128)} %bitcast.11, ...), custom_call_target="tpu_custom_call" | custom-call | flops 4000000 | bytes 2000000 | tf_op jit(solution)/shard_map/pallas_call | solution.py:424
  3.7 2.2 %shard_map.38 = (f32[10,256,128]{2,1,0:T(8,128)S(1)}, f32[10,256,128]{2,1,0:T(8,128)S(1)}, f32[256,128]{1,0:T(8,128)S(1)}, f32[32,1024]{1,0:T(8,128)S(1)}, f32[8,128]{1,0:T(8,128)S(1)}) custom-call(f32[32,1024]{1,0:T(8,128)S(1)} %get-tuple-element.37.kappa), custom_call_target="tpu_custom_call" | custom-call | flops 20000000 | bytes 4000000 | tf_op jit(solution)/shard_map/pallas_call | solution.py:432
  5.9 0.0 collective-permute-done
  5.9 1.2 %collective-permute-done.1 = f32[2,1,16,1024]{3,2,1,0:T(8,128)S(1)} collective-permute-done((f32[2,1,16,1024]{3,2,1,0:T(8,128)}, f32[2,1,16,1024]{3,2,1,0:T(8,128)S(1)}, u32[]{:S(2)}, u32[]{:S(2)}) %collective-permute-start.1) | collective-permute-done | bytes 131104 | tf_op jit(solution)/shard_map/ppermute | solution.py:420
  7.0 0.1 shard_map.39
  7.1 2.9 %collective-permute-start.2 = (f32[2,7,8,128]{3,2,1,0:T(8,128)S(1)}, f32[2,7,8,128]{3,2,1,0:T(8,128)S(1)}, u32[]{:S(2)}, u32[]{:S(2)}) collective-permute-start(f32[2,7,8,128]{3,2,1,0:T(8,128)S(1)} %get-tuple-element.39.mine), channel_id=1, source_target_pairs={{0,4},{4,0},{8,12},{12,8},{16,20},{20,16},{24,28},{28,24},{32,36},... | collective-permute-start | bytes 172040 | tf_op jit(solution)/shard_map/ppermute | solution.py:444
  10.0 0.9 %collective-permute-done.2.other = f32[2,7,8,128]{3,2,1,0:T(8,128)S(1)} collective-permute-done((f32[2,7,8,128]{3,2,1,0:T(8,128)S(1)}, f32[2,7,8,128]{3,2,1,0:T(8,128)S(1)}, u32[]{:S(2)}, u32[]{:S(2)}) %collective-permute-start.2) | collective-permute-done | bytes 57376 | tf_op jit(solution)/shard_map/ppermute | solution.py:444
  10.9 2.9 %collective-permute-start.4 = (f32[2,7,8,128]{3,2,1,0:T(8,128)S(1)}, f32[2,7,8,128]{3,2,1,0:T(8,128)S(1)}, u32[]{:S(2)}, u32[]{:S(2)}) collective-permute-start(f32[2,7,8,128]{3,2,1,0:T(8,128)S(1)} %get-tuple-element.41), channel_id=1, source_target_pairs={{0,24},{4,20},{8,16},{12,28},{16,8},{20,4},{24,0},{28,12},{32,56},... | collective-permute-start | bytes 172040 | tf_op jit(solution)/shard_map/ppermute | solution.py:447
  13.9 0.4 collective-permute-start.3
  14.3 1.3 %collective-permute-done.4.chips = f32[2,7,8,128]{3,2,1,0:T(8,128)S(1)} collective-permute-done((f32[2,7,8,128]{3,2,1,0:T(8,128)S(1)}, f32[2,7,8,128]{3,2,1,0:T(8,128)S(1)}, u32[]{:S(2)}, u32[]{:S(2)}) %collective-permute-start.4) | collective-permute-done | bytes 57376 | tf_op jit(solution)/shard_map/ppermute | solution.py:447
  15.6 1.4 %collective-permute-start.5 = (f32[7,8,128]{2,1,0:T(8,128)S(1)}, f32[7,8,128]{2,1,0:T(8,128)S(1)}, u32[]{:S(2)}, u32[]{:S(2)}) collective-permute-start(f32[7,8,128]{2,1,0:T(8,128)S(1)} %get-tuple-element.43), channel_id=1, source_target_pairs={{0,4},{4,0},{8,12},{12,8},{16,20},{20,16},{24,28},{28,24},{32,36},... | collective-permute-start | bytes 86024 | tf_op jit(solution)/shard_map/ppermute | solution.py:450
  17.0 0.0 collective-permute-done.3.far1
  17.0 0.9 %collective-permute-done.5.got = f32[7,8,128]{2,1,0:T(8,128)S(1)} collective-permute-done((f32[7,8,128]{2,1,0:T(8,128)S(1)}, f32[7,8,128]{2,1,0:T(8,128)S(1)}, u32[]{:S(2)}, u32[]{:S(2)}) %collective-permute-start.5) | collective-permute-done | bytes 28704 | tf_op jit(solution)/shard_map/ppermute | solution.py:450
  17.8 0.1 shard_map.42
  17.9 17.9 %all_to_all.5.got = f32[8,7,8,128]{3,2,1,0:T(8,128)S(1)} all-to-all(f32[8,7,8,128]{3,2,1,0:T(8,128)S(1)} %get-tuple-element.45), channel_id=1, replica_groups={{0,32,64,96,128,160,192,224},{4,36,68,100,132,164,196,228},{8,40,72,104..., dimensions={0} | all-to-all | bytes 458752 | tf_op jit(solution)/shard_map/all_to_all | solution.py:454
  35.8 0.1 shard_map.43
  36.0 2.2 %collective-permute-start.6 = (f32[2,8,128]{2,1,0:T(8,128)S(1)}, f32[2,8,128]{2,1,0:T(8,128)S(1)}, u32[]{:S(2)}, u32[]{:S(2)}) collective-permute-start(f32[2,8,128]{2,1,0:T(8,128)S(1)} %get-tuple-element.48), channel_id=1, source_target_pairs={{0,4},{4,0},{8,12},{12,8},{16,20},{20,16},{24,28},{28,24},{32,36},... | collective-permute-start | bytes 24584 | tf_op jit(solution)/shard_map/ppermute | solution.py:458
  38.2 0.2 shard_map.44.local
  38.3 0.7 %collective-permute-done.6.other = f32[2,8,128]{2,1,0:T(8,128)S(1)} collective-permute-done((f32[2,8,128]{2,1,0:T(8,128)S(1)}, f32[2,8,128]{2,1,0:T(8,128)S(1)}, u32[]{:S(2)}, u32[]{:S(2)}) %collective-permute-start.6) | collective-permute-done | bytes 8224 | tf_op jit(solution)/shard_map/ppermute | solution.py:458
  39.0 0.1 shard_map.45
  39.1 2.8 %collective-permute-start.7 = (f32[8,128]{1,0:T(8,128)S(1)}, f32[8,128]{1,0:T(8,128)S(1)}, u32[]{:S(2)}, u32[]{:S(2)}) collective-permute-start(f32[8,128]{1,0:T(8,128)S(1)} %get-tuple-element.54.message), channel_id=1, source_target_pairs={{0,2},{2,0},{1,3},{3,1},{4,6},{6,4},{5,7},{7,5},{8,10},{10,8},{9,1... | collective-permute-start | bytes 12296 | tf_op jit(solution)/shard_map/ppermute | solution.py:462
  41.9 0.9 %shard_map.46.local = f32[32,1024]{1,0:T(8,128)S(1)} custom-call(f32[32,1024]{1,0:T(8,128)S(1)} %get-tuple-element.55.section, f32[10,256,128]{2,1,0:T(8,128)S(1)} %get-tuple-element.56.ay, f32[10,256,128]{2,1,0:T(8,128)S(1)} %get-tuple-element.57.by, f32[256,128]{1,0:T(8,128)S(1)} %get-tuple-element.58.qy), custom_call_target="tpu_custom_call" | custom-call | flops 4000000 | bytes 3000000 | tf_op jit(solution)/shard_map/pallas_call | solution.py:463
  42.8 0.3 collective-permute-done.7.far
  43.1 0.9 %shard_map.47 = f32[32,1024]{1,0:T(8,128)} custom-call(f32[8,128]{1,0:T(8,128)S(1)} %get-tuple-element.54.message, f32[8,128]{1,0:T(8,128)S(1)} %collective-permute-done.7.far, f32[32,1024]{1,0:T(8,128)S(1)} %shard_map.46.local, f32[32,1024]{1,0:T(8,128)S(1)} %get-tuple-element.53.hy), custom_call_target="tpu_custom_call" | custom-call | tf_op jit(solution)/shard_map/pallas_call | solution.py:464
  (2 shorter events, 0.0 us)
Async XLA Ops:
  0.0 5.9 %collective-permute-start = (f32[2,1,16,1024]{3,2,1,0:T(8,128)}, f32[2,1,16,1024]{3,2,1,0:T(8,128)S(1)}, u32[]{:S(2)}, u32[]{:S(2)}) collective-permute-start(f32[2,1,16,1024]{3,2,1,0:T(8,128)} %param.3), channel_id=1, source_target_pairs={{0,1},{1,0},{2,3},{3,2},{4,5},{5,4},{6,7},{7,6},{8,9},{9,8},{10,11... | collective-permute-start | bytes 393224 | tf_op jit(solution)/shard_map/ppermute | solution.py:419
  2.0 5.0 %collective-permute-start.1 = (f32[2,1,16,1024]{3,2,1,0:T(8,128)}, f32[2,1,16,1024]{3,2,1,0:T(8,128)S(1)}, u32[]{:S(2)}, u32[]{:S(2)}) collective-permute-start(f32[2,1,16,1024]{3,2,1,0:T(8,128)} %param.5), channel_id=1, source_target_pairs={{0,1},{1,0},{2,3},{3,2},{4,5},{5,4},{6,7},{7,6},{8,9},{9,8},{10,11... | collective-permute-start | bytes 393224 | tf_op jit(solution)/shard_map/ppermute | solution.py:420
  7.1 3.8 %collective-permute-start.2 = (f32[2,7,8,128]{3,2,1,0:T(8,128)S(1)}, f32[2,7,8,128]{3,2,1,0:T(8,128)S(1)}, u32[]{:S(2)}, u32[]{:S(2)}) collective-permute-start(f32[2,7,8,128]{3,2,1,0:T(8,128)S(1)} %get-tuple-element.39.mine), channel_id=1, source_target_pairs={{0,4},{4,0},{8,12},{12,8},{16,20},{20,16},{24,28},{28,24},{32,36},... | collective-permute-start | bytes 172040 | tf_op jit(solution)/shard_map/ppermute | solution.py:444
  10.9 4.6 %collective-permute-start.4 = (f32[2,7,8,128]{3,2,1,0:T(8,128)S(1)}, f32[2,7,8,128]{3,2,1,0:T(8,128)S(1)}, u32[]{:S(2)}, u32[]{:S(2)}) collective-permute-start(f32[2,7,8,128]{3,2,1,0:T(8,128)S(1)} %get-tuple-element.41), channel_id=1, source_target_pairs={{0,24},{4,20},{8,16},{12,28},{16,8},{20,4},{24,0},{28,12},{32,56},... | collective-permute-start | bytes 172040 | tf_op jit(solution)/shard_map/ppermute | solution.py:447
  13.9 3.1 %collective-permute-start.3 = (f32[7,8,128]{2,1,0:T(8,128)S(1)}, f32[7,8,128]{2,1,0:T(8,128)S(1)}, u32[]{:S(2)}, u32[]{:S(2)}) collective-permute-start(f32[7,8,128]{2,1,0:T(8,128)S(1)} %get-tuple-element.40.chip), channel_id=1, source_target_pairs={{0,8},{4,12},{8,0},{12,4},{16,24},{20,28},{24,16},{28,20},{32,40},... | collective-permute-start | bytes 86024 | tf_op jit(solution)/shard_map/ppermute | solution.py:448
  15.6 2.2 %collective-permute-start.5 = (f32[7,8,128]{2,1,0:T(8,128)S(1)}, f32[7,8,128]{2,1,0:T(8,128)S(1)}, u32[]{:S(2)}, u32[]{:S(2)}) collective-permute-start(f32[7,8,128]{2,1,0:T(8,128)S(1)} %get-tuple-element.43), channel_id=1, source_target_pairs={{0,4},{4,0},{8,12},{12,8},{16,20},{20,16},{24,28},{28,24},{32,36},... | collective-permute-start | bytes 86024 | tf_op jit(solution)/shard_map/ppermute | solution.py:450
  36.0 3.0 %collective-permute-start.6 = (f32[2,8,128]{2,1,0:T(8,128)S(1)}, f32[2,8,128]{2,1,0:T(8,128)S(1)}, u32[]{:S(2)}, u32[]{:S(2)}) collective-permute-start(f32[2,8,128]{2,1,0:T(8,128)S(1)} %get-tuple-element.48), channel_id=1, source_target_pairs={{0,4},{4,0},{8,12},{12,8},{16,20},{20,16},{24,28},{28,24},{32,36},... | collective-permute-start | bytes 24584 | tf_op jit(solution)/shard_map/ppermute | solution.py:458
  39.1 4.0 %collective-permute-start.7 = (f32[8,128]{1,0:T(8,128)S(1)}, f32[8,128]{1,0:T(8,128)S(1)}, u32[]{:S(2)}, u32[]{:S(2)}) collective-permute-start(f32[8,128]{1,0:T(8,128)S(1)} %get-tuple-element.54.message), channel_id=1, source_target_pairs={{0,2},{2,0},{1,3},{3,1},{4,6},{6,4},{5,7},{7,5},{8,10},{10,8},{9,1... | collective-permute-start | bytes 12296 | tf_op jit(solution)/shard_map/ppermute | solution.py:462

commit v13 on v12

--- a/solution.py
+++ b/solution.py
@@ -119,14 +119,19 @@
     )
 
 
-def factor_x_kernel(
-    fields_arg, vertical_arg, kappa_arg, fields, vertical, kappa, ax, bx, qx, h1, h2, parts, done
-):
+def input_kernel(fields_arg, vertical_arg, kappa_arg, fields, vertical, kappa, rim, done):
     pairs = ((kappa_arg, kappa), (fields_arg, fields), (vertical_arg, vertical))
     copies = [pltpu.make_async_copy(a, b, done.at[n]) for n, (a, b) in enumerate(pairs)]
     for copy in copies:
         copy.start()
     copies[0].wait()
+    for f in range(2):
+        rim[f] = dense(kappa[f * ROWS + ROWS - 1 : f * ROWS + ROWS, :])
+    copies[1].wait()
+    copies[2].wait()
+
+
+def factor_x_kernel(kappa, ax, bx, qx, h1, h2, parts):
     half = 512
     rows = lax.broadcasted_iota(jnp.int32, (ROWS, half), 0)
     for f in range(2):
@@ -161,11 +166,10 @@
             for n, row in enumerate(sums):
                 for i in range(half // 128):
                     parts[n, f, pl.ds(c * (half // 128) + i, 1), :] = row[:, 128 * i : 128 * (i + 1)]
-    copies[1].wait()
-    copies[2].wait()
-
-
-def factor_y_kernel(kappa, ay, by, qy, hy, edge):
+
+
+def factor_y_kernel(kappa, after, ay, by, qy, hy, edge):
+    del after
     gy = lax.axis_index("gy")
     low_side = gy == 0
     end = jnp.where(low_side, COLS - 1, 0)
@@ -201,8 +205,7 @@
     edge[...] = tile
 
 
-def source_kernel(fields, fields_far, vertical, vertical_far, h1, h2, parts, after, source, elements):
-    del after
+def source_kernel(fields, fields_far, vertical, vertical_far, h1, h2, parts, prev, source, elements):
     here = fields[...]
     v = vertical[...]
     s = here + (v + vertical_far[...]) * 0.5 * (fields_far[...] - here) - v * 0.5 * here
@@ -211,7 +214,7 @@
         mine = slice(f * ROWS, (f + 1) * ROWS)
         first = dense(jnp.sum(h1[mine, :] * s[mine, :], axis=0, keepdims=True))
         last = dense(jnp.sum(h2[mine, :] * s[mine, :], axis=0, keepdims=True))
-        element = (parts[0, f], parts[1, f], parts[2, f], first, last, parts[3, f], parts[4, f])
+        element = (parts[0, f], parts[1, f], parts[2, f], first, last, parts[3, f], parts[4, f], prev[f])
         for n, value in enumerate(element):
             elements[f, n] = value
 
@@ -247,7 +250,7 @@
 
 
 def load(ref, *field):
-    return tuple(ref[(*field, n)] for n in range(7))
+    return tuple(ref[(*field, n)] for n in range(8))
 
 
 def within(node, left, right):
@@ -264,7 +267,7 @@
         second = [jnp.where(even, o, m) for m, o in zip(a, b)]
         tail, start = behind((first[6] + second[5]) * 0.5, second[:5])
         element, end = merge(first[:5], tail)
-        fields.append(((*element, first[5], second[6]), (*end, *start)))
+        fields.append(((*element, first[5], *second[6:]), (*end, *start)))
         for n, value in enumerate(fields[f][0]):
             chips[f, n] = value
     for out, (one, two) in zip((chip, middle), zip(*fields)):
@@ -272,7 +275,8 @@
             out[n] = jnp.where(even, a, b)
 
 
-def pick_kernel(chips, keep, send):
+def pick_kernel(chips, after, keep, send):
+    del after
     even = lax.axis_index("gx") % 2 == 0
     for n, (one, two) in enumerate(zip(load(chips, 0), load(chips, 1))):
         keep[n] = jnp.where(even, one, two)
@@ -292,14 +296,21 @@
             here = y ^ flip == m
             chosen = [jnp.where(here, a, c) for a, c in zip(arrived[flip], chosen)]
         chips.append(chosen)
-    element = chips[0][:5]
-    inner, fronts = [], []
-    for m in range(1, 4):
-        tail, front = behind((chips[m - 1][6] + chips[m][5]) * 0.5, chips[m][:5])
-        element, node = merge(element, tail)
-        inner.append(node)
+    slab = lax.axis_index("gx") // 8
+    before = jnp.where(slab == 0, 0.0, chips[3][7])
+    element, inner, fronts = None, [], []
+    for m in range(4):
+        face = ((before if m == 0 else chips[m - 1][6]) + chips[m][5]) * 0.5
+        tail, front = behind(face, chips[m][:5])
         fronts.append(front)
-    for n, value in enumerate((*element, chips[0][5], chips[3][6])):
+        if m == 0:
+            element = tail
+        else:
+            element, node = merge(element, tail)
+            inner.append(node)
+    g, sl, sr, rl, rr = element
+    sr = jnp.where(slab == 7, sr + chips[3][6] * 0.5, sr)
+    for n, value in enumerate((g, sl, sr, rl, rr)):
         for j in range(8):
             message[j, n] = value
     zero, one = jnp.zeros((8, 128), F32), jnp.ones((8, 128), F32)
@@ -307,8 +318,9 @@
     lasts = [(zero, one, zero)]
     for node in inner[::-1]:
         lasts.append(within(node, left, lasts[-1]))
-    lasts = lasts[::-1]
-    firsts = [left] + [within(fronts[m - 1], lasts[m - 1], lasts[m]) for m in range(1, 4)]
+    lasts = [left] + lasts[::-1]
+    firsts = [within(fronts[m], lasts[m], lasts[m + 1]) for m in range(4)]
+    lasts = lasts[1:]
     first, last = firsts[0], lasts[0]
     for m in range(1, 4):
         first = [jnp.where(y == m, new, old) for new, old in zip(firsts[m], first)]
@@ -325,17 +337,11 @@
     slab = gx // 8
     even = gx % 2 == 0
     zero = jnp.zeros((8, 128), F32)
-    slabs, fronts = [], []
-    for z in range(8):
-        face = got[z, 5] * 0.5 if z == 0 else (got[z - 1, 6] + got[z, 5]) * 0.5
-        tail, front = behind(face, tuple(got[z, n] for n in range(5)))
-        slabs.append(tail)
-        fronts.append(front)
-    g, _, conduct, _, right = slabs[0]
-    conduct = conduct + g
+    conduct = got[0, 0] + got[0, 2]
+    right = got[0, 4]
     ratios, offsets = [], []
     for z in range(1, 8):
-        g, sl, sr, rl, rr = slabs[z]
+        g, sl, sr, rl, rr = (got[z, n] for n in range(5))
         conduct = conduct + sl
         right = right + rl
         inverse = 1.0 / (conduct + g)
@@ -344,7 +350,7 @@
         offsets.append(right * inverse)
         conduct = sr + f * conduct
         right = rr + f * right
-    value = right / (conduct + got[7, 6] * 0.5)
+    value = right / conduct
     values = [value]
     for k in range(6, -1, -1):
         value = ratios[k] * value + offsets[k]
@@ -352,8 +358,7 @@
     values = [zero] + values[::-1]
     first, last = zero, zero
     for z in range(8):
-        a, b, c = fronts[z]
-        first = jnp.where(slab == z, a * values[z] + b * values[z + 1] + c, first)
+        first = jnp.where(slab == z, values[z], first)
         last = jnp.where(slab == z, values[z + 1], last)
     row = [nodes[n, 0] * first + nodes[n, 1] * last + nodes[n, 2] for n in range(4)]
     for n in range(2):
@@ -419,37 +424,45 @@
     fields_far = lax.ppermute(fields, "gz", swap)
     vertical_far = lax.ppermute(vertical, "gz", swap)
     full = shape(*grid)
-    half = shape(7, 8, 128)
+    half = shape(8, 8, 128)
     standing = shape(256, 128)
-    fields_here, vertical_here, kappa_here, ax, bx, qx, h1, h2, parts = call(
+    fields_here, vertical_here, kappa_here, rim = call(
+        input_kernel,
+        (full, full, full, shape(2, 8, 128)),
+        [HBM] * 3,
+        flops=1_000_000,
+        size=1_000_000,
+        scratch=[pltpu.SemaphoreType.DMA((3,))],
+    )(*(pltpu.with_memory_space_constraint(x.reshape(grid), pltpu.HBM) for x in (fields, vertical, kappa)))
+    prev = lax.ppermute(rim, "gx", [(i, (i + 8) % 64) for i in range(64)])
+    ax, bx, qx, h1, h2, parts = call(
         factor_x_kernel,
-        (full, full, full, shape(4, *grid), shape(4, *grid), full, full, full, shape(5, 2, 8, 128)),
-        [HBM] * 3,
+        (shape(4, *grid), shape(4, *grid), full, full, full, shape(5, 2, 8, 128)),
+        [VMEM],
         flops=4_000_000,
         size=2_000_000,
-        scratch=[pltpu.SemaphoreType.DMA((3,))],
-    )(*(pltpu.with_memory_space_constraint(x.reshape(grid), pltpu.HBM) for x in (fields, vertical, kappa)))
-    ay, by, qy, hy, edge = call(
-        factor_y_kernel,
-        (shape(10, 256, 128), shape(10, 256, 128), standing, full, shape(8, 128)),
-        [VMEM],
-        flops=20_000_000,
-        size=4_000_000,
     )(kappa_here)
-    both = shape(2, 7, 8, 128)
+    both = shape(2, 8, 8, 128)
     source, elements = call(source_kernel, (full, both), [VMEM] * 8)(
         fields_here, fields_far.reshape(grid), vertical_here, vertical_far.reshape(grid),
-        h1, h2, parts, edge,
+        h1, h2, parts, prev,
     )
     got = lax.ppermute(elements, "gx", CORES)
     local_x = call(local_x_kernel, full, [VMEM] * 4, flops=1_000_000, size=1_000_000)(source, ax, bx, qx)
     chips, chip, middle = call(chip_kernel, (both, half, shape(6, 8, 128)), [VMEM] * 2)(elements, got)
     far = lax.ppermute(chips, "gx", CHIPS)
     far1 = lax.ppermute(chip, "gx", NEXT)
-    keep, send = call(pick_kernel, (half, half), [VMEM])(far)
+    ay, by, qy, hy, edge = call(
+        factor_y_kernel,
+        (shape(10, 256, 128), shape(10, 256, 128), standing, full, shape(8, 128)),
+        [VMEM] * 2,
+        flops=20_000_000,
+        size=4_000_000,
+    )(kappa_here, chip)
+    keep, send = call(pick_kernel, (half, half), [VMEM] * 2)(far, edge)
     got = lax.ppermute(send, "gx", CORES)
     message, nodes = call(
-        slab_kernel, (shape(8, 7, 8, 128), shape(4, 3, 8, 128)), [VMEM] * 5
+        slab_kernel, (shape(8, 5, 8, 128), shape(4, 3, 8, 128)), [VMEM] * 5
     )(chip, far1, keep, got, middle)
     got = lax.all_to_all(message, "gx", 0, 0, axis_index_groups=SLAB_GROUPS, tiled=True)
     mine, other = call(

time: 44.1 us -> 42.9 us (0.973)
  blocking collectives: 17.9 us -> 14.2 us
  waiting for transfers between devices: 5.22 us -> 7.06 us
  starting transfers between devices: 14.6 us -> 15.1 us
    ppermute x0 -> x1, waiting for transfers between devices: none -> 4.28 us  [local(): prev = lax.ppermute(rim, 'gx', [(i, (i + 8) % 64) for i in range(64)])]
    all_to_all x1, blocking collectives: 17.9 us -> 14.2 us  [local(): lax.all_to_all(message, 'gx', 0, 0, axis_index_groups=SLAB_GROUPS, tiled=...]
    ppermute x0 -> x1, starting transfers between devices: none -> 1.94 us  [local(): prev = lax.ppermute(rim, 'gx', [(i, (i + 8) % 64) for i in range(64)])]
    ppermute x1, waiting for transfers between devices: 1.29 us -> 0.01 us  [local(): far = lax.ppermute(chips, 'gx', CHIPS)]
    ppermute x1, waiting for transfers between devices: 1.18 us -> 0.01 us  [local(): vertical_far = lax.ppermute(vertical, 'gz', swap)]
    ppermute x1, starting transfers between devices: 1.39 us -> 0.61 us  [local(): got = lax.ppermute(send, 'gx', CORES)]
    ppermute x1, starting transfers between devices: 2.87 us -> 2.19 us  [local(): got = lax.ppermute(elements, 'gx', CORES)]
    pallas_call x3 -> x4, Pallas kernels: 1.71 us -> 1.86 us  [the longest x1 1.05 us: local(): call(input_kernel, (full, full, full, shape(2, 8, 128)), [HBM] * 3, flops...]
  transfers between devices with their start and end apart: 8 -> 9, of which waited for: 6 -> 5; matrix products, arithmetic and copies ran while one was open for 0% -> 0% of each run, Pallas kernels for 11% -> 12%
where the time goes in v13:
time: 42.9 us; the launch traced here: 42.8 us
  starting transfers between devices  15.1 us (35%)
  blocking collectives  14.2 us (33%)
  waiting for transfers between devices  7.06 us (16%)
  Pallas kernels  6.26 us (15%)
    all_to_all x1, blocking collectives, local(): lax.all_to_all(message, 'gx', 0, 0, axis_index_groups=SLAB_GROUPS, tiled=...  14.2 us
    ppermute x1, waiting for transfers between devices, local(): prev = lax.ppermute(rim, 'gx', [(i, (i + 8) % 64) for i in range(64)])  4.28 us
    ppermute x1, starting transfers between devices, local(): far = lax.ppermute(chips, 'gx', CHIPS)  3 us
    ppermute x1, starting transfers between devices, local(): far = lax.ppermute(message, 'gy', swap)  2.77 us
    ppermute x1, starting transfers between devices, local(): got = lax.ppermute(elements, 'gx', CORES)  2.19 us
    ppermute x1, starting transfers between devices, local(): other = lax.ppermute(other, 'gx', CORES)  2.17 us
    pallas_call x1, Pallas kernels, local(): call(factor_y_kernel, (shape(10, 256, 128), shape(10, 256, 128), standing...  2.15 us
    ppermute x1, starting transfers between devices, local(): fields_far = lax.ppermute(fields, 'gz', swap)  2.04 us
  transfers between devices with their start and end apart: 9, of which 5 were waited for; matrix products, arithmetic and copies ran while one was open for 0% of the time, Pallas kernels for 12%

profile of v13, /device:TPU:1, one launch (start us, length us, event | category | flops | bytes accessed | tf_op | source)
XLA Modules:
  0.0 42.8 jit_solution(6618072126316999213)
XLA Ops:
  0.0 2.0 %collective-permute-start = (f32[2,1,16,1024]{3,2,1,0:T(8,128)}, f32[2,1,16,1024]{3,2,1,0:T(8,128)S(1)}, u32[]{:S(2)}, u32[]{:S(2)}) collective-permute-start(f32[2,1,16,1024]{3,2,1,0:T(8,128)} %param.3), channel_id=1, source_target_pairs={{0,1},{1,0},{2,3},{3,2},{4,5},{5,4},{6,7},{7,6},{8,9},{9,8},{10,11... | collective-permute-start | bytes 393224 | tf_op jit(solution)/shard_map/ppermute | solution.py:424
  2.0 0.0 collective-permute-start.1
  2.1 1.1 %shard_map.37 = (f32[32,1024]{1,0:T(8,128)S(1)}, f32[32,1024]{1,0:T(8,128)S(1)}, f32[32,1024]{1,0:T(8,128)S(1)}, f32[2,8,128]{2,1,0:T(8,128)S(1)}) custom-call(f32[32,1024]{1,0:T(8,128)} %bitcast.11, f32[32,1024]{1,0:T(8,128)} %bitcast.12, f32[32,1024]{1,0:T(8,128)} %bitcast.10), custom_call_target="tpu_custom_call" | custom-call | flops 1000000 | bytes 1000000 | tf_op jit(solution)/shard_map/pallas_call | solution.py:429
  3.1 1.9 %collective-permute-start.2 = (f32[2,8,128]{2,1,0:T(8,128)S(1)}, f32[2,8,128]{2,1,0:T(8,128)S(1)}, u32[]{:S(2)}, u32[]{:S(2)}) collective-permute-start(f32[2,8,128]{2,1,0:T(8,128)S(1)} %get-tuple-element.39), channel_id=1, source_target_pairs={{0,32},{4,36},{8,40},{12,44},{16,48},{20,52},{24,56},{28,60},{32,6... | collective-permute-start | bytes 24584 | tf_op jit(solution)/shard_map/ppermute | solution.py:437
  5.1 0.7 %shard_map.38 = (f32[4,32,1024]{2,1,0:T(8,128)S(1)}, f32[4,32,1024]{2,1,0:T(8,128)S(1)}, f32[32,1024]{1,0:T(8,128)S(1)}, f32[32,1024]{1,0:T(8,128)S(1)}, f32[32,...) custom-call(f32[32,1024]{1,0:T(8,128)S(1)} %get-tuple-element.35.kappa), custom_call_target="tpu_custom_call" | custom-call | flops 4000000 | bytes 2000000 | tf_op jit(solution)/shard_map/pallas_call | solution.py:438
  5.8 4.3 %collective-permute-done.2.prev = f32[2,8,128]{2,1,0:T(8,128)S(1)} collective-permute-done((f32[2,8,128]{2,1,0:T(8,128)S(1)}, f32[2,8,128]{2,1,0:T(8,128)S(1)}, u32[]{:S(2)}, u32[]{:S(2)}) %collective-permute-start.2) | collective-permute-done | bytes 8224 | tf_op jit(solution)/shard_map/ppermute | solution.py:437
  10.1 0.0 collective-permute-done
  10.1 0.0 collective-permute-done.1
  10.1 0.1 shard_map.39
  10.2 2.2 %collective-permute-start.3 = (f32[2,8,8,128]{3,2,1,0:T(8,128)S(1)}, f32[2,8,8,128]{3,2,1,0:T(8,128)S(1)}, u32[]{:S(2)}, u32[]{:S(2)}) collective-permute-start(f32[2,8,8,128]{3,2,1,0:T(8,128)S(1)} %get-tuple-element.40.mine), channel_id=1, source_target_pairs={{0,4},{4,0},{8,12},{12,8},{16,20},{20,16},{24,28},{28,24},{32,36},... | collective-permute-start | bytes 196616 | tf_op jit(solution)/shard_map/ppermute | solution.py:450
  12.3 0.9 %collective-permute-done.3.other = f32[2,8,8,128]{3,2,1,0:T(8,128)S(1)} collective-permute-done((f32[2,8,8,128]{3,2,1,0:T(8,128)S(1)}, f32[2,8,8,128]{3,2,1,0:T(8,128)S(1)}, u32[]{:S(2)}, u32[]{:S(2)}) %collective-permute-start.3) | collective-permute-done | bytes 65568 | tf_op jit(solution)/shard_map/ppermute | solution.py:450
  13.3 3.0 %collective-permute-start.5 = (f32[2,8,8,128]{3,2,1,0:T(8,128)S(1)}, f32[2,8,8,128]{3,2,1,0:T(8,128)S(1)}, u32[]{:S(2)}, u32[]{:S(2)}) collective-permute-start(f32[2,8,8,128]{3,2,1,0:T(8,128)S(1)} %get-tuple-element.42), channel_id=1, source_target_pairs={{0,24},{4,20},{8,16},{12,28},{16,8},{20,4},{24,0},{28,12},{32,56},... | collective-permute-start | bytes 196616 | tf_op jit(solution)/shard_map/ppermute | solution.py:453
  16.3 0.4 collective-permute-start.4
  16.7 2.2 %shard_map.41 = (f32[10,256,128]{2,1,0:T(8,128)S(1)}, f32[10,256,128]{2,1,0:T(8,128)S(1)}, f32[256,128]{1,0:T(8,128)S(1)}, f32[32,1024]{1,0:T(8,128)S(1)}, f32[8,128]{1,0:T(8,128)S(1)}) custom-call(f32[32,1024]{1,0:T(8,128)S(1)} %get-tuple-element.35.kappa, f32[8,8,128]{2,1,0:T(8,128)S(1)} %get-tuple-element.41.after.chip), custom_call_target="tpu_custom_call" | custom-call | flops 20000000 | bytes 4000000 | tf_op jit(solution)/shard_map/pallas_call | solution.py:455
  18.8 0.0 collective-permute-done.5.chips
  18.9 0.6 %collective-permute-start.6 = (f32[8,8,128]{2,1,0:T(8,128)S(1)}, f32[8,8,128]{2,1,0:T(8,128)S(1)}, u32[]{:S(2)}, u32[]{:S(2)}) collective-permute-start(f32[8,8,128]{2,1,0:T(8,128)S(1)} %get-tuple-element.45), channel_id=1, source_target_pairs={{0,4},{4,0},{8,12},{12,8},{16,20},{20,16},{24,28},{28,24},{32,36},... | collective-permute-start | bytes 98312 | tf_op jit(solution)/shard_map/ppermute | solution.py:463
  19.5 0.0 collective-permute-done.4.far1
  19.5 0.9 %collective-permute-done.6.got = f32[8,8,128]{2,1,0:T(8,128)S(1)} collective-permute-done((f32[8,8,128]{2,1,0:T(8,128)S(1)}, f32[8,8,128]{2,1,0:T(8,128)S(1)}, u32[]{:S(2)}, u32[]{:S(2)}) %collective-permute-start.6) | collective-permute-done | bytes 32800 | tf_op jit(solution)/shard_map/ppermute | solution.py:463
  20.3 0.1 shard_map.43
  20.4 14.2 %all_to_all.5.got = f32[8,5,8,128]{3,2,1,0:T(8,128)S(1)} all-to-all(f32[8,5,8,128]{3,2,1,0:T(8,128)S(1)} %get-tuple-element.47), channel_id=1, replica_groups={{0,32,64,96,128,160,192,224},{4,36,68,100,132,164,196,228},{8,40,72,104..., dimensions={0} | all-to-all | bytes 327680 | tf_op jit(solution)/shard_map/all_to_all | solution.py:467
  34.7 0.1 shard_map.44
  34.8 2.2 %collective-permute-start.7 = (f32[2,8,128]{2,1,0:T(8,128)S(1)}, f32[2,8,128]{2,1,0:T(8,128)S(1)}, u32[]{:S(2)}, u32[]{:S(2)}) collective-permute-start(f32[2,8,128]{2,1,0:T(8,128)S(1)} %get-tuple-element.50), channel_id=1, source_target_pairs={{0,4},{4,0},{8,12},{12,8},{16,20},{20,16},{24,28},{28,24},{32,36},... | collective-permute-start | bytes 24584 | tf_op jit(solution)/shard_map/ppermute | solution.py:471
  36.9 0.1 shard_map.45.local
  37.1 0.7 %collective-permute-done.7.other = f32[2,8,128]{2,1,0:T(8,128)S(1)} collective-permute-done((f32[2,8,128]{2,1,0:T(8,128)S(1)}, f32[2,8,128]{2,1,0:T(8,128)S(1)}, u32[]{:S(2)}, u32[]{:S(2)}) %collective-permute-start.7) | collective-permute-done | bytes 8224 | tf_op jit(solution)/shard_map/ppermute | solution.py:471
  37.8 0.1 shard_map.46
  37.9 2.8 %collective-permute-start.8 = (f32[8,128]{1,0:T(8,128)S(1)}, f32[8,128]{1,0:T(8,128)S(1)}, u32[]{:S(2)}, u32[]{:S(2)}) collective-permute-start(f32[8,128]{1,0:T(8,128)S(1)} %get-tuple-element.56.message), channel_id=1, source_target_pairs={{0,2},{2,0},{1,3},{3,1},{4,6},{6,4},{5,7},{7,5},{8,10},{10,8},{9,1... | collective-permute-start | bytes 12296 | tf_op jit(solution)/shard_map/ppermute | solution.py:475
  40.7 0.9 %shard_map.47.local = f32[32,1024]{1,0:T(8,128)S(1)} custom-call(f32[32,1024]{1,0:T(8,128)S(1)} %get-tuple-element.57.section, f32[10,256,128]{2,1,0:T(8,128)S(1)} %get-tuple-element.58.ay, f32[10,256,128]{2,1,0:T(8,128)S(1)} %get-tuple-element.59.by, f32[256,128]{1,0:T(8,128)S(1)} %get-tuple-element.60.qy), custom_call_target="tpu_custom_call" | custom-call | flops 4000000 | bytes 3000000 | tf_op jit(solution)/shard_map/pallas_call | solution.py:476
  41.5 0.3 collective-permute-done.8.far
  41.9 0.9 %shard_map.48 = f32[32,1024]{1,0:T(8,128)} custom-call(f32[8,128]{1,0:T(8,128)S(1)} %get-tuple-element.56.message, f32[8,128]{1,0:T(8,128)S(1)} %collective-permute-done.8.far, f32[32,1024]{1,0:T(8,128)S(1)} %shard_map.47.local, f32[32,1024]{1,0:T(8,128)S(1)} %get-tuple-element.55.hy), custom_call_target="tpu_custom_call" | custom-call | tf_op jit(solution)/shard_map/pallas_call | solution.py:477
  (2 shorter events, 0.1 us)
Async XLA Ops:
  0.0 10.1 %collective-permute-start = (f32[2,1,16,1024]{3,2,1,0:T(8,128)}, f32[2,1,16,1024]{3,2,1,0:T(8,128)S(1)}, u32[]{:S(2)}, u32[]{:S(2)}) collective-permute-start(f32[2,1,16,1024]{3,2,1,0:T(8,128)} %param.3), channel_id=1, source_target_pairs={{0,1},{1,0},{2,3},{3,2},{4,5},{5,4},{6,7},{7,6},{8,9},{9,8},{10,11... | collective-permute-start | bytes 393224 | tf_op jit(solution)/shard_map/ppermute | solution.py:424
  2.0 8.0 %collective-permute-start.1 = (f32[2,1,16,1024]{3,2,1,0:T(8,128)}, f32[2,1,16,1024]{3,2,1,0:T(8,128)S(1)}, u32[]{:S(2)}, u32[]{:S(2)}) collective-permute-start(f32[2,1,16,1024]{3,2,1,0:T(8,128)} %param.5), channel_id=1, source_target_pairs={{0,1},{1,0},{2,3},{3,2},{4,5},{5,4},{6,7},{7,6},{8,9},{9,8},{10,11... | collective-permute-start | bytes 393224 | tf_op jit(solution)/shard_map/ppermute | solution.py:425
  3.1 6.9 %collective-permute-start.2 = (f32[2,8,128]{2,1,0:T(8,128)S(1)}, f32[2,8,128]{2,1,0:T(8,128)S(1)}, u32[]{:S(2)}, u32[]{:S(2)}) collective-permute-start(f32[2,8,128]{2,1,0:T(8,128)S(1)} %get-tuple-element.39), channel_id=1, source_target_pairs={{0,32},{4,36},{8,40},{12,44},{16,48},{20,52},{24,56},{28,60},{32,6... | collective-permute-start | bytes 24584 | tf_op jit(solution)/shard_map/ppermute | solution.py:437
  10.2 3.1 %collective-permute-start.3 = (f32[2,8,8,128]{3,2,1,0:T(8,128)S(1)}, f32[2,8,8,128]{3,2,1,0:T(8,128)S(1)}, u32[]{:S(2)}, u32[]{:S(2)}) collective-permute-start(f32[2,8,8,128]{3,2,1,0:T(8,128)S(1)} %get-tuple-element.40.mine), channel_id=1, source_target_pairs={{0,4},{4,0},{8,12},{12,8},{16,20},{20,16},{24,28},{28,24},{32,36},... | collective-permute-start | bytes 196616 | tf_op jit(solution)/shard_map/ppermute | solution.py:450
  13.3 5.6 %collective-permute-start.5 = (f32[2,8,8,128]{3,2,1,0:T(8,128)S(1)}, f32[2,8,8,128]{3,2,1,0:T(8,128)S(1)}, u32[]{:S(2)}, u32[]{:S(2)}) collective-permute-start(f32[2,8,8,128]{3,2,1,0:T(8,128)S(1)} %get-tuple-element.42), channel_id=1, source_target_pairs={{0,24},{4,20},{8,16},{12,28},{16,8},{20,4},{24,0},{28,12},{32,56},... | collective-permute-start | bytes 196616 | tf_op jit(solution)/shard_map/ppermute | solution.py:453
  16.3 3.2 %collective-permute-start.4 = (f32[8,8,128]{2,1,0:T(8,128)S(1)}, f32[8,8,128]{2,1,0:T(8,128)S(1)}, u32[]{:S(2)}, u32[]{:S(2)}) collective-permute-start(f32[8,8,128]{2,1,0:T(8,128)S(1)} %get-tuple-element.41.after.chip), channel_id=1, source_target_pairs={{0,8},{4,12},{8,0},{12,4},{16,24},{20,28},{24,16},{28,20},{32,40},... | collective-permute-start | bytes 98312 | tf_op jit(solution)/shard_map/ppermute | solution.py:454
  18.9 1.5 %collective-permute-start.6 = (f32[8,8,128]{2,1,0:T(8,128)S(1)}, f32[8,8,128]{2,1,0:T(8,128)S(1)}, u32[]{:S(2)}, u32[]{:S(2)}) collective-permute-start(f32[8,8,128]{2,1,0:T(8,128)S(1)} %get-tuple-element.45), channel_id=1, source_target_pairs={{0,4},{4,0},{8,12},{12,8},{16,20},{20,16},{24,28},{28,24},{32,36},... | collective-permute-start | bytes 98312 | tf_op jit(solution)/shard_map/ppermute | solution.py:463
  34.8 3.0 %collective-permute-start.7 = (f32[2,8,128]{2,1,0:T(8,128)S(1)}, f32[2,8,128]{2,1,0:T(8,128)S(1)}, u32[]{:S(2)}, u32[]{:S(2)}) collective-permute-start(f32[2,8,128]{2,1,0:T(8,128)S(1)} %get-tuple-element.50), channel_id=1, source_target_pairs={{0,4},{4,0},{8,12},{12,8},{16,20},{20,16},{24,28},{28,24},{32,36},... | collective-permute-start | bytes 24584 | tf_op jit(solution)/shard_map/ppermute | solution.py:471
  37.9 4.0 %collective-permute-start.8 = (f32[8,128]{1,0:T(8,128)S(1)}, f32[8,128]{1,0:T(8,128)S(1)}, u32[]{:S(2)}, u32[]{:S(2)}) collective-permute-start(f32[8,128]{1,0:T(8,128)S(1)} %get-tuple-element.56.message), channel_id=1, source_target_pairs={{0,2},{2,0},{1,3},{3,1},{4,6},{6,4},{5,7},{7,5},{8,10},{10,8},{9,1... | collective-permute-start | bytes 12296 | tf_op jit(solution)/shard_map/ppermute | solution.py:475

commit v14 on v13

--- a/solution.py
+++ b/solution.py
@@ -168,8 +168,7 @@
                     parts[n, f, pl.ds(c * (half // 128) + i, 1), :] = row[:, 128 * i : 128 * (i + 1)]
 
 
-def factor_y_kernel(kappa, after, ay, by, qy, hy, edge):
-    del after
+def factor_y_kernel(kappa, ay, by, qy, hy, edge):
     gy = lax.axis_index("gy")
     low_side = gy == 0
     end = jnp.where(low_side, COLS - 1, 0)
@@ -205,7 +204,8 @@
     edge[...] = tile
 
 
-def source_kernel(fields, fields_far, vertical, vertical_far, h1, h2, parts, prev, source, elements):
+def source_kernel(fields, fields_far, vertical, vertical_far, h1, h2, parts, prev, after, source, elements):
+    del after
     here = fields[...]
     v = vertical[...]
     s = here + (v + vertical_far[...]) * 0.5 * (fields_far[...] - here) - v * 0.5 * here
@@ -275,8 +275,7 @@
             out[n] = jnp.where(even, a, b)
 
 
-def pick_kernel(chips, after, keep, send):
-    del after
+def pick_kernel(chips, keep, send):
     even = lax.axis_index("gx") % 2 == 0
     for n, (one, two) in enumerate(zip(load(chips, 0), load(chips, 1))):
         keep[n] = jnp.where(even, one, two)
@@ -442,24 +441,24 @@
         flops=4_000_000,
         size=2_000_000,
     )(kappa_here)
+    ay, by, qy, hy, edge = call(
+        factor_y_kernel,
+        (shape(10, 256, 128), shape(10, 256, 128), standing, full, shape(8, 128)),
+        [VMEM],
+        flops=20_000_000,
+        size=4_000_000,
+    )(kappa_here)
     both = shape(2, 8, 8, 128)
-    source, elements = call(source_kernel, (full, both), [VMEM] * 8)(
+    source, elements = call(source_kernel, (full, both), [VMEM] * 9)(
         fields_here, fields_far.reshape(grid), vertical_here, vertical_far.reshape(grid),
-        h1, h2, parts, prev,
+        h1, h2, parts, prev, edge,
     )
     got = lax.ppermute(elements, "gx", CORES)
     local_x = call(local_x_kernel, full, [VMEM] * 4, flops=1_000_000, size=1_000_000)(source, ax, bx, qx)
     chips, chip, middle = call(chip_kernel, (both, half, shape(6, 8, 128)), [VMEM] * 2)(elements, got)
     far = lax.ppermute(chips, "gx", CHIPS)
     far1 = lax.ppermute(chip, "gx", NEXT)
-    ay, by, qy, hy, edge = call(
-        factor_y_kernel,
-        (shape(10, 256, 128), shape(10, 256, 128), standing, full, shape(8, 128)),
-        [VMEM] * 2,
-        flops=20_000_000,
-        size=4_000_000,
-    )(kappa_here, chip)
-    keep, send = call(pick_kernel, (half, half), [VMEM] * 2)(far, edge)
+    keep, send = call(pick_kernel, (half, half), [VMEM])(far)
     got = lax.ppermute(send, "gx", CORES)
     message, nodes = call(
         slab_kernel, (shape(8, 5, 8, 128), shape(4, 3, 8, 128)), [VMEM] * 5

time: 42.9 us -> 42.9 us (level)
  starting transfers between devices: 15.1 us -> 16 us
  waiting for transfers between devices: 7.06 us -> 6.23 us
    ppermute x1, waiting for transfers between devices: 4.28 us -> 2.13 us  [local(): prev = lax.ppermute(rim, 'gx', [(i, (i + 8) % 64) for i in range(64)])]
    ppermute x1, waiting for transfers between devices: 0.01 us -> 1.32 us  [local(): far = lax.ppermute(chips, 'gx', CHIPS)]
    ppermute x1, starting transfers between devices: 0.61 us -> 1.46 us  [local(): got = lax.ppermute(send, 'gx', CORES)]
  transfers between devices with their start and end apart: 9 -> 9, of which waited for: 5 -> 6; matrix products, arithmetic and copies ran while one was open for 0% -> 0% of each run, Pallas kernels for 12% -> 12%
where the time goes in v14:
time: 42.9 us; the launch traced here: 42.8 us
  starting transfers between devices  16 us (37%)
  blocking collectives  14.2 us (33%)
  Pallas kernels  6.25 us (15%)
  waiting for transfers between devices  6.23 us (15%)
    all_to_all x1, blocking collectives, local(): lax.all_to_all(message, 'gx', 0, 0, axis_index_groups=SLAB_GROUPS, tiled=...  14.2 us
    ppermute x1, starting transfers between devices, local(): far = lax.ppermute(chips, 'gx', CHIPS)  3 us
    ppermute x1, starting transfers between devices, local(): far = lax.ppermute(message, 'gy', swap)  2.77 us
    ppermute x1, starting transfers between devices, local(): got = lax.ppermute(elements, 'gx', CORES)  2.19 us
    ppermute x1, starting transfers between devices, local(): other = lax.ppermute(other, 'gx', CORES)  2.17 us
    pallas_call x1, Pallas kernels, local(): call(factor_y_kernel, (shape(10, 256, 128), shape(10, 256, 128), standing...  2.15 us
    ppermute x1, waiting for transfers between devices, local(): prev = lax.ppermute(rim, 'gx', [(i, (i + 8) % 64) for i in range(64)])  2.13 us
    ppermute x1, starting transfers between devices, local(): fields_far = lax.ppermute(fields, 'gz', swap)  2.04 us
  transfers between devices with their start and end apart: 9, of which 6 were waited for; matrix products, arithmetic and copies ran while one was open for 0% of the time, Pallas kernels for 12%

profile of v14, /device:TPU:1, one launch (start us, length us, event | category | flops | bytes accessed | tf_op | source)
XLA Modules:
  0.0 42.8 jit_solution(17388305309219944441)
XLA Ops:
  0.0 2.0 %collective-permute-start = (f32[2,1,16,1024]{3,2,1,0:T(8,128)}, f32[2,1,16,1024]{3,2,1,0:T(8,128)S(1)}, u32[]{:S(2)}, u32[]{:S(2)}) collective-permute-start(f32[2,1,16,1024]{3,2,1,0:T(8,128)} %param.3), channel_id=1, source_target_pairs={{0,1},{1,0},{2,3},{3,2},{4,5},{5,4},{6,7},{7,6},{8,9},{9,8},{10,11... | collective-permute-start | bytes 393224 | tf_op jit(solution)/shard_map/ppermute | solution.py:423
  2.0 0.0 collective-permute-start.1
  2.1 1.1 %shard_map.37 = (f32[32,1024]{1,0:T(8,128)S(1)}, f32[32,1024]{1,0:T(8,128)S(1)}, f32[32,1024]{1,0:T(8,128)S(1)}, f32[2,8,128]{2,1,0:T(8,128)S(1)}) custom-call(f32[32,1024]{1,0:T(8,128)} %bitcast.11, f32[32,1024]{1,0:T(8,128)} %bitcast.12, f32[32,1024]{1,0:T(8,128)} %bitcast.10), custom_call_target="tpu_custom_call" | custom-call | flops 1000000 | bytes 1000000 | tf_op jit(solution)/shard_map/pallas_call | solution.py:428
  3.1 1.9 %collective-permute-start.2 = (f32[2,8,128]{2,1,0:T(8,128)S(1)}, f32[2,8,128]{2,1,0:T(8,128)S(1)}, u32[]{:S(2)}, u32[]{:S(2)}) collective-permute-start(f32[2,8,128]{2,1,0:T(8,128)S(1)} %get-tuple-element.39), channel_id=1, source_target_pairs={{0,32},{4,36},{8,40},{12,44},{16,48},{20,52},{24,56},{28,60},{32,6... | collective-permute-start | bytes 24584 | tf_op jit(solution)/shard_map/ppermute | solution.py:436
  5.1 0.7 %shard_map.38 = (f32[4,32,1024]{2,1,0:T(8,128)S(1)}, f32[4,32,1024]{2,1,0:T(8,128)S(1)}, f32[32,1024]{1,0:T(8,128)S(1)}, f32[32,1024]{1,0:T(8,128)S(1)}, f32[32,...) custom-call(f32[32,1024]{1,0:T(8,128)S(1)} %get-tuple-element.35.kappa), custom_call_target="tpu_custom_call" | custom-call | flops 4000000 | bytes 2000000 | tf_op jit(solution)/shard_map/pallas_call | solution.py:437
  5.8 2.2 %shard_map.39 = (f32[10,256,128]{2,1,0:T(8,128)S(1)}, f32[10,256,128]{2,1,0:T(8,128)S(1)}, f32[256,128]{1,0:T(8,128)S(1)}, f32[32,1024]{1,0:T(8,128)S(1)}, f32[8,128]{1,0:T(8,128)S(1)}) custom-call(f32[32,1024]{1,0:T(8,128)S(1)} %get-tuple-element.35.kappa), custom_call_target="tpu_custom_call" | custom-call | flops 20000000 | bytes 4000000 | tf_op jit(solution)/shard_map/pallas_call | solution.py:444
  7.9 2.1 %collective-permute-done.2.prev = f32[2,8,128]{2,1,0:T(8,128)S(1)} collective-permute-done((f32[2,8,128]{2,1,0:T(8,128)S(1)}, f32[2,8,128]{2,1,0:T(8,128)S(1)}, u32[]{:S(2)}, u32[]{:S(2)}) %collective-permute-start.2) | collective-permute-done | bytes 8224 | tf_op jit(solution)/shard_map/ppermute | solution.py:436
  10.1 0.0 collective-permute-done
  10.1 0.0 collective-permute-done.1
  10.1 0.1 shard_map.40
  10.2 2.2 %collective-permute-start.3 = (f32[2,8,8,128]{3,2,1,0:T(8,128)S(1)}, f32[2,8,8,128]{3,2,1,0:T(8,128)S(1)}, u32[]{:S(2)}, u32[]{:S(2)}) collective-permute-start(f32[2,8,8,128]{3,2,1,0:T(8,128)S(1)} %get-tuple-element.41.mine), channel_id=1, source_target_pairs={{0,4},{4,0},{8,12},{12,8},{16,20},{20,16},{24,28},{28,24},{32,36},... | collective-permute-start | bytes 196616 | tf_op jit(solution)/shard_map/ppermute | solution.py:456
  12.4 0.9 %collective-permute-done.3.other = f32[2,8,8,128]{3,2,1,0:T(8,128)S(1)} collective-permute-done((f32[2,8,8,128]{3,2,1,0:T(8,128)S(1)}, f32[2,8,8,128]{3,2,1,0:T(8,128)S(1)}, u32[]{:S(2)}, u32[]{:S(2)}) %collective-permute-start.3) | collective-permute-done | bytes 65568 | tf_op jit(solution)/shard_map/ppermute | solution.py:456
  13.3 3.0 %collective-permute-start.5 = (f32[2,8,8,128]{3,2,1,0:T(8,128)S(1)}, f32[2,8,8,128]{3,2,1,0:T(8,128)S(1)}, u32[]{:S(2)}, u32[]{:S(2)}) collective-permute-start(f32[2,8,8,128]{3,2,1,0:T(8,128)S(1)} %get-tuple-element.43), channel_id=1, source_target_pairs={{0,24},{4,20},{8,16},{12,28},{16,8},{20,4},{24,0},{28,12},{32,56},... | collective-permute-start | bytes 196616 | tf_op jit(solution)/shard_map/ppermute | solution.py:459
  16.3 0.4 collective-permute-start.4
  16.7 1.3 %collective-permute-done.5.chips = f32[2,8,8,128]{3,2,1,0:T(8,128)S(1)} collective-permute-done((f32[2,8,8,128]{3,2,1,0:T(8,128)S(1)}, f32[2,8,8,128]{3,2,1,0:T(8,128)S(1)}, u32[]{:S(2)}, u32[]{:S(2)}) %collective-permute-start.5) | collective-permute-done | bytes 65568 | tf_op jit(solution)/shard_map/ppermute | solution.py:459
  18.0 1.5 %collective-permute-start.6 = (f32[8,8,128]{2,1,0:T(8,128)S(1)}, f32[8,8,128]{2,1,0:T(8,128)S(1)}, u32[]{:S(2)}, u32[]{:S(2)}) collective-permute-start(f32[8,8,128]{2,1,0:T(8,128)S(1)} %get-tuple-element.45), channel_id=1, source_target_pairs={{0,4},{4,0},{8,12},{12,8},{16,20},{20,16},{24,28},{28,24},{32,36},... | collective-permute-start | bytes 98312 | tf_op jit(solution)/shard_map/ppermute | solution.py:462
  19.5 0.0 collective-permute-done.4.far1
  19.5 0.9 %collective-permute-done.6.got = f32[8,8,128]{2,1,0:T(8,128)S(1)} collective-permute-done((f32[8,8,128]{2,1,0:T(8,128)S(1)}, f32[8,8,128]{2,1,0:T(8,128)S(1)}, u32[]{:S(2)}, u32[]{:S(2)}) %collective-permute-start.6) | collective-permute-done | bytes 32800 | tf_op jit(solution)/shard_map/ppermute | solution.py:462
  20.3 0.1 shard_map.43
  20.4 14.2 %all_to_all.5.got = f32[8,5,8,128]{3,2,1,0:T(8,128)S(1)} all-to-all(f32[8,5,8,128]{3,2,1,0:T(8,128)S(1)} %get-tuple-element.47), channel_id=1, replica_groups={{0,32,64,96,128,160,192,224},{4,36,68,100,132,164,196,228},{8,40,72,104..., dimensions={0} | all-to-all | bytes 327680 | tf_op jit(solution)/shard_map/all_to_all | solution.py:466
  34.7 0.1 shard_map.44
  34.8 2.2 %collective-permute-start.7 = (f32[2,8,128]{2,1,0:T(8,128)S(1)}, f32[2,8,128]{2,1,0:T(8,128)S(1)}, u32[]{:S(2)}, u32[]{:S(2)}) collective-permute-start(f32[2,8,128]{2,1,0:T(8,128)S(1)} %get-tuple-element.50), channel_id=1, source_target_pairs={{0,4},{4,0},{8,12},{12,8},{16,20},{20,16},{24,28},{28,24},{32,36},... | collective-permute-start | bytes 24584 | tf_op jit(solution)/shard_map/ppermute | solution.py:470
  36.9 0.1 shard_map.45.local
  37.1 0.7 %collective-permute-done.7.other = f32[2,8,128]{2,1,0:T(8,128)S(1)} collective-permute-done((f32[2,8,128]{2,1,0:T(8,128)S(1)}, f32[2,8,128]{2,1,0:T(8,128)S(1)}, u32[]{:S(2)}, u32[]{:S(2)}) %collective-permute-start.7) | collective-permute-done | bytes 8224 | tf_op jit(solution)/shard_map/ppermute | solution.py:470
  37.8 0.1 shard_map.46
  37.9 2.8 %collective-permute-start.8 = (f32[8,128]{1,0:T(8,128)S(1)}, f32[8,128]{1,0:T(8,128)S(1)}, u32[]{:S(2)}, u32[]{:S(2)}) collective-permute-start(f32[8,128]{1,0:T(8,128)S(1)} %get-tuple-element.56.message), channel_id=1, source_target_pairs={{0,2},{2,0},{1,3},{3,1},{4,6},{6,4},{5,7},{7,5},{8,10},{10,8},{9,1... | collective-permute-start | bytes 12296 | tf_op jit(solution)/shard_map/ppermute | solution.py:474
  40.7 0.9 %shard_map.47.local = f32[32,1024]{1,0:T(8,128)S(1)} custom-call(f32[32,1024]{1,0:T(8,128)S(1)} %get-tuple-element.57.section, f32[10,256,128]{2,1,0:T(8,128)S(1)} %get-tuple-element.58.ay, f32[10,256,128]{2,1,0:T(8,128)S(1)} %get-tuple-element.59.by, f32[256,128]{1,0:T(8,128)S(1)} %get-tuple-element.60.qy), custom_call_target="tpu_custom_call" | custom-call | flops 4000000 | bytes 3000000 | tf_op jit(solution)/shard_map/pallas_call | solution.py:475
  41.6 0.3 collective-permute-done.8.far
  41.9 0.9 %shard_map.48 = f32[32,1024]{1,0:T(8,128)} custom-call(f32[8,128]{1,0:T(8,128)S(1)} %get-tuple-element.56.message, f32[8,128]{1,0:T(8,128)S(1)} %collective-permute-done.8.far, f32[32,1024]{1,0:T(8,128)S(1)} %shard_map.47.local, f32[32,1024]{1,0:T(8,128)S(1)} %get-tuple-element.55.hy), custom_call_target="tpu_custom_call" | custom-call | tf_op jit(solution)/shard_map/pallas_call | solution.py:476
  (2 shorter events, 0.0 us)
Async XLA Ops:
  0.0 10.1 %collective-permute-start = (f32[2,1,16,1024]{3,2,1,0:T(8,128)}, f32[2,1,16,1024]{3,2,1,0:T(8,128)S(1)}, u32[]{:S(2)}, u32[]{:S(2)}) collective-permute-start(f32[2,1,16,1024]{3,2,1,0:T(8,128)} %param.3), channel_id=1, source_target_pairs={{0,1},{1,0},{2,3},{3,2},{4,5},{5,4},{6,7},{7,6},{8,9},{9,8},{10,11... | collective-permute-start | bytes 393224 | tf_op jit(solution)/shard_map/ppermute | solution.py:423
  2.0 8.0 %collective-permute-start.1 = (f32[2,1,16,1024]{3,2,1,0:T(8,128)}, f32[2,1,16,1024]{3,2,1,0:T(8,128)S(1)}, u32[]{:S(2)}, u32[]{:S(2)}) collective-permute-start(f32[2,1,16,1024]{3,2,1,0:T(8,128)} %param.5), channel_id=1, source_target_pairs={{0,1},{1,0},{2,3},{3,2},{4,5},{5,4},{6,7},{7,6},{8,9},{9,8},{10,11... | collective-permute-start | bytes 393224 | tf_op jit(solution)/shard_map/ppermute | solution.py:424
  3.1 6.9 %collective-permute-start.2 = (f32[2,8,128]{2,1,0:T(8,128)S(1)}, f32[2,8,128]{2,1,0:T(8,128)S(1)}, u32[]{:S(2)}, u32[]{:S(2)}) collective-permute-start(f32[2,8,128]{2,1,0:T(8,128)S(1)} %get-tuple-element.39), channel_id=1, source_target_pairs={{0,32},{4,36},{8,40},{12,44},{16,48},{20,52},{24,56},{28,60},{32,6... | collective-permute-start | bytes 24584 | tf_op jit(solution)/shard_map/ppermute | solution.py:436
  10.2 3.1 %collective-permute-start.3 = (f32[2,8,8,128]{3,2,1,0:T(8,128)S(1)}, f32[2,8,8,128]{3,2,1,0:T(8,128)S(1)}, u32[]{:S(2)}, u32[]{:S(2)}) collective-permute-start(f32[2,8,8,128]{3,2,1,0:T(8,128)S(1)} %get-tuple-element.41.mine), channel_id=1, source_target_pairs={{0,4},{4,0},{8,12},{12,8},{16,20},{20,16},{24,28},{28,24},{32,36},... | collective-permute-start | bytes 196616 | tf_op jit(solution)/shard_map/ppermute | solution.py:456
  13.3 4.7 %collective-permute-start.5 = (f32[2,8,8,128]{3,2,1,0:T(8,128)S(1)}, f32[2,8,8,128]{3,2,1,0:T(8,128)S(1)}, u32[]{:S(2)}, u32[]{:S(2)}) collective-permute-start(f32[2,8,8,128]{3,2,1,0:T(8,128)S(1)} %get-tuple-element.43), channel_id=1, source_target_pairs={{0,24},{4,20},{8,16},{12,28},{16,8},{20,4},{24,0},{28,12},{32,56},... | collective-permute-start | bytes 196616 | tf_op jit(solution)/shard_map/ppermute | solution.py:459
  16.3 3.2 %collective-permute-start.4 = (f32[8,8,128]{2,1,0:T(8,128)S(1)}, f32[8,8,128]{2,1,0:T(8,128)S(1)}, u32[]{:S(2)}, u32[]{:S(2)}) collective-permute-start(f32[8,8,128]{2,1,0:T(8,128)S(1)} %get-tuple-element.42.chip), channel_id=1, source_target_pairs={{0,8},{4,12},{8,0},{12,4},{16,24},{20,28},{24,16},{28,20},{32,40},... | collective-permute-start | bytes 98312 | tf_op jit(solution)/shard_map/ppermute | solution.py:460
  18.0 2.3 %collective-permute-start.6 = (f32[8,8,128]{2,1,0:T(8,128)S(1)}, f32[8,8,128]{2,1,0:T(8,128)S(1)}, u32[]{:S(2)}, u32[]{:S(2)}) collective-permute-start(f32[8,8,128]{2,1,0:T(8,128)S(1)} %get-tuple-element.45), channel_id=1, source_target_pairs={{0,4},{4,0},{8,12},{12,8},{16,20},{20,16},{24,28},{28,24},{32,36},... | collective-permute-start | bytes 98312 | tf_op jit(solution)/shard_map/ppermute | solution.py:462
  34.8 3.0 %collective-permute-start.7 = (f32[2,8,128]{2,1,0:T(8,128)S(1)}, f32[2,8,128]{2,1,0:T(8,128)S(1)}, u32[]{:S(2)}, u32[]{:S(2)}) collective-permute-start(f32[2,8,128]{2,1,0:T(8,128)S(1)} %get-tuple-element.50), channel_id=1, source_target_pairs={{0,4},{4,0},{8,12},{12,8},{16,20},{20,16},{24,28},{28,24},{32,36},... | collective-permute-start | bytes 24584 | tf_op jit(solution)/shard_map/ppermute | solution.py:470
  37.9 4.0 %collective-permute-start.8 = (f32[8,128]{1,0:T(8,128)S(1)}, f32[8,128]{1,0:T(8,128)S(1)}, u32[]{:S(2)}, u32[]{:S(2)}) collective-permute-start(f32[8,128]{1,0:T(8,128)S(1)} %get-tuple-element.56.message), channel_id=1, source_target_pairs={{0,2},{2,0},{1,3},{3,1},{4,6},{6,4},{5,7},{7,5},{8,10},{10,8},{9,1... | collective-permute-start | bytes 12296 | tf_op jit(solution)/shard_map/ppermute | solution.py:474

commit v15 on v14

--- a/solution.py
+++ b/solution.py
@@ -219,7 +219,20 @@
             elements[f, n] = value
 
 
-def local_x_kernel(source, ax, bx, qx, out):
+def fill(tile, totals):
+    lane = lax.broadcasted_iota(jnp.int32, (8, 128), 1)
+    for g in range(ALL // 8):
+        tile = jnp.where(lane == 4 * g + 2, totals[8 * g : 8 * g + 8], tile)
+    return tile
+
+
+def weights_kernel(h1, h2, hy, after, weights):
+    del after
+    weights[0] = hy[...] * h1[...]
+    weights[1] = hy[...] * h2[...]
+
+
+def local_x_kernel(source, ax, bx, qx, hy, edge, out, tile):
     half = 512
     for f in range(2):
         mine = pl.ds(f * ROWS, ROWS)
@@ -228,6 +241,7 @@
             r = source[mine, cols]
             r = reduce_right(r, X_STEPS, turn_rows, lambda i: (ax[i, mine, cols], bx[i, mine, cols]))
             out[mine, cols] = r * qx[mine, cols]
+    tile[...] = fill(edge[...], jnp.sum(hy[...] * out[...], axis=1, keepdims=True))
 
 
 def merge(one, two):
@@ -282,7 +296,8 @@
         send[n] = jnp.where(even, two, one)
 
 
-def slab_kernel(chip, far1, keep, got, middle, message, nodes):
+def slab_kernel(chip, far1, keep, got, middle, tile, weights, message, nodes):
+    del tile, weights
     y = lax.axis_index("gx") // 2 % 4
     even = lax.axis_index("gx") % 2 == 0
     far2 = [jnp.where(even, g, k) for k, g in zip(load(keep), load(got))]
@@ -331,10 +346,8 @@
             nodes[n, m] = trio[m]
 
 
-def ends_kernel(got, nodes, mine, other):
-    gx = lax.axis_index("gx")
-    slab = gx // 8
-    even = gx % 2 == 0
+def ends_kernel(got, nodes, tile, rows):
+    slab = lax.axis_index("gx") // 8
     zero = jnp.zeros((8, 128), F32)
     conduct = got[0, 0] + got[0, 2]
     right = got[0, 4]
@@ -359,26 +372,40 @@
     for z in range(8):
         first = jnp.where(slab == z, values[z], first)
         last = jnp.where(slab == z, values[z + 1], last)
-    row = [nodes[n, 0] * first + nodes[n, 1] * last + nodes[n, 2] for n in range(4)]
-    for n in range(2):
-        mine[n] = jnp.where(even, row[n], row[n + 2])
-        other[n] = jnp.where(even, row[n + 2], row[n])
+    for n in range(4):
+        rows[n] = nodes[n, 0] * first + nodes[n, 1] * last + nodes[n, 2]
+    rows[4] = tile[...]
+
+
+def ends_of(low, mine, other, f):
+    here = lax.axis_index("gx") % 2 == f
+    row = [jnp.where(here, mine[n], other[n]) for n in range(4)]
+    return jnp.where(low, row[0], row[2]), jnp.where(low, row[1], row[3])
+
+
+def message_kernel(mine, other, weights, message):
+    low = lax.axis_index("gx") % 2 == 1
+    totals = []
+    for f in range(2):
+        first, last = ends_of(low, mine, other, f)
+        rows = slice(f * ROWS, (f + 1) * ROWS)
+        s = weights[0, rows, :] * natural(first, ROWS) + weights[1, rows, :] * natural(last, ROWS)
+        totals.append(jnp.sum(s, axis=1, keepdims=True))
+    totals = jnp.concatenate(totals, axis=0)
+    tile = other[4]
+    message[...] = tile + fill(jnp.zeros((8, 128), F32), totals)
 
 
 def section_kernel(mine, other, local, h1, h2, hy, edge, section, message):
-    core = lax.axis_index("gx") % 2
-    lane = lax.broadcasted_iota(jnp.int32, (8, 128), 1)
-    tile = edge[...]
-    for f in range(2):
-        first = jnp.where(core == f, mine[0], other[0])
-        last = jnp.where(core == f, mine[1], other[1])
+    low = lax.axis_index("gx") % 2 == 0
+    totals = []
+    for f in range(2):
+        first, last = ends_of(low, mine, other, f)
         rows = slice(f * ROWS, (f + 1) * ROWS)
         s = local[rows, :] + h1[rows, :] * natural(first, ROWS) + h2[rows, :] * natural(last, ROWS)
         section[rows, :] = s
-        total = jnp.sum(hy[rows, :] * s, axis=1, keepdims=True)
-        for g in range(2):
-            tile = jnp.where(lane == 4 * (2 * f + g) + 2, total[8 * g : 8 * g + 8], tile)
-    message[...] = tile
+        totals.append(jnp.sum(hy[rows, :] * s, axis=1, keepdims=True))
+    message[...] = fill(edge[...], jnp.concatenate(totals, axis=0))
 
 
 def local_y_kernel(section, ay, by, qy, out):
@@ -414,6 +441,7 @@
 
 
 CHIPS = [(i, i ^ (4 if i % 2 else 6)) for i in range(64)]
+ACROSS = [(2 * i + y, 2 * (i ^ 1) + 1 - y) for i in range(64) for y in range(2)]
 NEXT = [(i, i ^ 2) for i in range(64)]
 
 
@@ -454,24 +482,27 @@
         h1, h2, parts, prev, edge,
     )
     got = lax.ppermute(elements, "gx", CORES)
-    local_x = call(local_x_kernel, full, [VMEM] * 4, flops=1_000_000, size=1_000_000)(source, ax, bx, qx)
+    local_x, tile = call(
+        local_x_kernel, (full, shape(8, 128)), [VMEM] * 6, flops=1_000_000, size=1_000_000
+    )(source, ax, bx, qx, hy, edge)
     chips, chip, middle = call(chip_kernel, (both, half, shape(6, 8, 128)), [VMEM] * 2)(elements, got)
     far = lax.ppermute(chips, "gx", CHIPS)
+    weights = call(weights_kernel, shape(2, *grid), [VMEM] * 4)(h1, h2, hy, chip)
+    weights = lax.ppermute(weights, "gx", CORES)
     far1 = lax.ppermute(chip, "gx", NEXT)
     keep, send = call(pick_kernel, (half, half), [VMEM])(far)
     got = lax.ppermute(send, "gx", CORES)
     message, nodes = call(
-        slab_kernel, (shape(8, 5, 8, 128), shape(4, 3, 8, 128)), [VMEM] * 5
-    )(chip, far1, keep, got, middle)
+        slab_kernel, (shape(8, 5, 8, 128), shape(4, 3, 8, 128)), [VMEM] * 7
+    )(chip, far1, keep, got, middle, tile, weights)
     got = lax.all_to_all(message, "gx", 0, 0, axis_index_groups=SLAB_GROUPS, tiled=True)
-    mine, other = call(
-        ends_kernel, (shape(2, 8, 128), shape(2, 8, 128)), [VMEM, VMEM]
-    )(got, nodes)
-    other = lax.ppermute(other, "gx", CORES)
+    mine = call(ends_kernel, shape(5, 8, 128), [VMEM] * 3)(got, nodes, tile)
+    other = lax.ppermute(mine, "gx", CORES)
+    message = call(message_kernel, shape(8, 128), [VMEM] * 3)(mine, other, weights)
+    far = lax.ppermute(message, ("gx", "gy"), ACROSS)
     section, message = call(
-        section_kernel, (full, shape(8, 128)), [VMEM] * 7
+        section_kernel, (full, shape(8, 128)), [VMEM] * 7, flops=1_000_000, size=1_000_000
     )(mine, other, local_x, h1, h2, hy, edge)
-    far = lax.ppermute(message, "gy", swap)
     local_y = call(local_y_kernel, full, [VMEM] * 4, flops=4_000_000, size=3_000_000)(section, ay, by, qy)
     out = call(output_kernel, full, [VMEM] * 4)(message, far, local_y, hy)
     return out.reshape(fields.shape)

time: 42.9 us -> 43.9 us (1.023)
  starting transfers between devices: 16 us -> 16.6 us
    ppermute x2 -> x3, starting transfers between devices: 4.93 us -> 5.61 us  [the longest x1 2.98 us: local(): far = lax.ppermute(message, ('gx', 'gy'), ACROSS)]
    ppermute x2 -> x3, waiting for transfers between devices: 1.01 us -> 1.32 us  [the longest x1 0.84 us: local(): other = lax.ppermute(mine, 'gx', CORES)]
  transfers between devices with their start and end apart: 9 -> 10, of which waited for: 6 -> 6; matrix products, arithmetic and copies ran while one was open for 0% -> 0% of each run, Pallas kernels for 12% -> 12%
where the time goes in v15:
time: 43.9 us; the launch traced here: 43.8 us
  starting transfers between devices  16.6 us (38%)
  blocking collectives  14.2 us (32%)
  Pallas kernels  6.61 us (15%)
  waiting for transfers between devices  6.34 us (14%)
    all_to_all x1, blocking collectives, local(): lax.all_to_all(message, 'gx', 0, 0, axis_index_groups=SLAB_GROUPS, tiled=...  14.2 us
    ppermute x1, starting transfers between devices, local(): far = lax.ppermute(message, ('gx', 'gy'), ACROSS)  2.98 us
    ppermute x1, starting transfers between devices, local(): far = lax.ppermute(chips, 'gx', CHIPS)  2.91 us
    ppermute x1, starting transfers between devices, local(): other = lax.ppermute(mine, 'gx', CORES)  2.19 us
    ppermute x1, starting transfers between devices, local(): got = lax.ppermute(elements, 'gx', CORES)  2.19 us
    pallas_call x1, Pallas kernels, local(): call(factor_y_kernel, (shape(10, 256, 128), shape(10, 256, 128), standing...  2.15 us
    ppermute x1, waiting for transfers between devices, local(): prev = lax.ppermute(rim, 'gx', [(i, (i + 8) % 64) for i in range(64)])  2.13 us
    ppermute x1, starting transfers between devices, local(): fields_far = lax.ppermute(fields, 'gz', swap)  2.04 us
  transfers between devices with their start and end apart: 10, of which 6 were waited for; matrix products, arithmetic and copies ran while one was open for 0% of the time, Pallas kernels for 12%

profile of v15, /device:TPU:1, one launch (start us, length us, event | category | flops | bytes accessed | tf_op | source)
XLA Modules:
  0.0 43.8 jit_solution(6326419137562581222)
XLA Ops:
  0.0 2.0 %collective-permute-start = (f32[2,1,16,1024]{3,2,1,0:T(8,128)}, f32[2,1,16,1024]{3,2,1,0:T(8,128)S(1)}, u32[]{:S(2)}, u32[]{:S(2)}) collective-permute-start(f32[2,1,16,1024]{3,2,1,0:T(8,128)} %param.3), channel_id=1, source_target_pairs={{0,1},{1,0},{2,3},{3,2},{4,5},{5,4},{6,7},{7,6},{8,9},{9,8},{10,11... | collective-permute-start | bytes 393224 | tf_op jit(solution)/shard_map/ppermute | solution.py:451
  2.0 0.0 collective-permute-start.1
  2.1 1.1 %shard_map.37 = (f32[32,1024]{1,0:T(8,128)S(1)}, f32[32,1024]{1,0:T(8,128)S(1)}, f32[32,1024]{1,0:T(8,128)S(1)}, f32[2,8,128]{2,1,0:T(8,128)S(1)}) custom-call(f32[32,1024]{1,0:T(8,128)} %bitcast.11, f32[32,1024]{1,0:T(8,128)} %bitcast.12, f32[32,1024]{1,0:T(8,128)} %bitcast.10), custom_call_target="tpu_custom_call" | custom-call | flops 1000000 | bytes 1000000 | tf_op jit(solution)/shard_map/pallas_call | solution.py:456
  3.1 1.9 %collective-permute-start.2 = (f32[2,8,128]{2,1,0:T(8,128)S(1)}, f32[2,8,128]{2,1,0:T(8,128)S(1)}, u32[]{:S(2)}, u32[]{:S(2)}) collective-permute-start(f32[2,8,128]{2,1,0:T(8,128)S(1)} %get-tuple-element.39), channel_id=1, source_target_pairs={{0,32},{4,36},{8,40},{12,44},{16,48},{20,52},{24,56},{28,60},{32,6... | collective-permute-start | bytes 24584 | tf_op jit(solution)/shard_map/ppermute | solution.py:464
  5.1 0.7 %shard_map.38 = (f32[4,32,1024]{2,1,0:T(8,128)S(1)}, f32[4,32,1024]{2,1,0:T(8,128)S(1)}, f32[32,1024]{1,0:T(8,128)S(1)}, f32[32,1024]{1,0:T(8,128)S(1)}, f32[32,...) custom-call(f32[32,1024]{1,0:T(8,128)S(1)} %get-tuple-element.35.kappa), custom_call_target="tpu_custom_call" | custom-call | flops 4000000 | bytes 2000000 | tf_op jit(solution)/shard_map/pallas_call | solution.py:465
  5.8 2.2 %shard_map.39 = (f32[10,256,128]{2,1,0:T(8,128)S(1)}, f32[10,256,128]{2,1,0:T(8,128)S(1)}, f32[256,128]{1,0:T(8,128)S(1)}, f32[32,1024]{1,0:T(8,128)S(1)}, f32[8,128]{1,0:T(8,128)S(1)}) custom-call(f32[32,1024]{1,0:T(8,128)S(1)} %get-tuple-element.35.kappa), custom_call_target="tpu_custom_call" | custom-call | flops 20000000 | bytes 4000000 | tf_op jit(solution)/shard_map/pallas_call | solution.py:472
  7.9 2.1 %collective-permute-done.2.prev = f32[2,8,128]{2,1,0:T(8,128)S(1)} collective-permute-done((f32[2,8,128]{2,1,0:T(8,128)S(1)}, f32[2,8,128]{2,1,0:T(8,128)S(1)}, u32[]{:S(2)}, u32[]{:S(2)}) %collective-permute-start.2) | collective-permute-done | bytes 8224 | tf_op jit(solution)/shard_map/ppermute | solution.py:464
  10.1 0.0 collective-permute-done
  10.1 0.0 collective-permute-done.1
  10.1 0.1 shard_map.40
  10.2 2.2 %collective-permute-start.3 = (f32[2,8,8,128]{3,2,1,0:T(8,128)S(1)}, f32[2,8,8,128]{3,2,1,0:T(8,128)S(1)}, u32[]{:S(2)}, u32[]{:S(2)}) collective-permute-start(f32[2,8,8,128]{3,2,1,0:T(8,128)S(1)} %get-tuple-element.41.mine), channel_id=1, source_target_pairs={{0,4},{4,0},{8,12},{12,8},{16,20},{20,16},{24,28},{28,24},{32,36},... | collective-permute-start | bytes 196616 | tf_op jit(solution)/shard_map/ppermute | solution.py:484
  12.4 0.9 %collective-permute-done.3.other = f32[2,8,8,128]{3,2,1,0:T(8,128)S(1)} collective-permute-done((f32[2,8,8,128]{3,2,1,0:T(8,128)S(1)}, f32[2,8,8,128]{3,2,1,0:T(8,128)S(1)}, u32[]{:S(2)}, u32[]{:S(2)}) %collective-permute-start.3) | collective-permute-done | bytes 65568 | tf_op jit(solution)/shard_map/ppermute | solution.py:484
  13.3 0.4 %collective-permute-start.7 = (f32[2,32,1024]{2,1,0:T(8,128)S(1)}, f32[2,32,1024]{2,1,0:T(8,128)S(1)}, u32[]{:S(2)}, u32[]{:S(2)}) collective-permute-start(f32[2,32,1024]{2,1,0:T(8,128)S(1)} %shard_map.44), channel_id=1, source_target_pairs={{0,4},{4,0},{8,12},{12,8},{16,20},{20,16},{24,28},{28,24},{32,36},... | collective-permute-start | bytes 786440 | tf_op jit(solution)/shard_map/ppermute | solution.py:491
  13.8 2.9 %collective-permute-start.5 = (f32[2,8,8,128]{3,2,1,0:T(8,128)S(1)}, f32[2,8,8,128]{3,2,1,0:T(8,128)S(1)}, u32[]{:S(2)}, u32[]{:S(2)}) collective-permute-start(f32[2,8,8,128]{3,2,1,0:T(8,128)S(1)} %get-tuple-element.43), channel_id=1, source_target_pairs={{0,24},{4,20},{8,16},{12,28},{16,8},{20,4},{24,0},{28,12},{32,56},... | collective-permute-start | bytes 196616 | tf_op jit(solution)/shard_map/ppermute | solution.py:489
  16.7 0.4 collective-permute-start.4
  17.1 1.3 %collective-permute-done.5.chips = f32[2,8,8,128]{3,2,1,0:T(8,128)S(1)} collective-permute-done((f32[2,8,8,128]{3,2,1,0:T(8,128)S(1)}, f32[2,8,8,128]{3,2,1,0:T(8,128)S(1)}, u32[]{:S(2)}, u32[]{:S(2)}) %collective-permute-start.5) | collective-permute-done | bytes 65568 | tf_op jit(solution)/shard_map/ppermute | solution.py:489
  18.4 1.4 %collective-permute-start.6 = (f32[8,8,128]{2,1,0:T(8,128)S(1)}, f32[8,8,128]{2,1,0:T(8,128)S(1)}, u32[]{:S(2)}, u32[]{:S(2)}) collective-permute-start(f32[8,8,128]{2,1,0:T(8,128)S(1)} %get-tuple-element.45), channel_id=1, source_target_pairs={{0,4},{4,0},{8,12},{12,8},{16,20},{20,16},{24,28},{28,24},{32,36},... | collective-permute-start | bytes 98312 | tf_op jit(solution)/shard_map/ppermute | solution.py:494
  19.9 0.2 shard_map.43
  20.1 0.0 collective-permute-done.4.far1
  20.1 0.6 %collective-permute-done.6.got = f32[8,8,128]{2,1,0:T(8,128)S(1)} collective-permute-done((f32[8,8,128]{2,1,0:T(8,128)S(1)}, f32[8,8,128]{2,1,0:T(8,128)S(1)}, u32[]{:S(2)}, u32[]{:S(2)}) %collective-permute-start.6) | collective-permute-done | bytes 32800 | tf_op jit(solution)/shard_map/ppermute | solution.py:494
  20.7 0.0 collective-permute-done.7.weights
  20.7 0.1 shard_map.45
  20.8 14.2 %all_to_all.5.got = f32[8,5,8,128]{3,2,1,0:T(8,128)S(1)} all-to-all(f32[8,5,8,128]{3,2,1,0:T(8,128)S(1)} %get-tuple-element.53), channel_id=1, replica_groups={{0,32,64,96,128,160,192,224},{4,36,68,100,132,164,196,228},{8,40,72,104..., dimensions={0} | all-to-all | bytes 327680 | tf_op jit(solution)/shard_map/all_to_all | solution.py:498
  35.0 0.1 shard_map.46.mine
  35.1 2.2 %collective-permute-start.8 = (f32[5,8,128]{2,1,0:T(8,128)S(1)}, f32[5,8,128]{2,1,0:T(8,128)S(1)}, u32[]{:S(2)}, u32[]{:S(2)}) collective-permute-start(f32[5,8,128]{2,1,0:T(8,128)S(1)} %shard_map.46.mine), channel_id=1, source_target_pairs={{0,4},{4,0},{8,12},{12,8},{16,20},{20,16},{24,28},{28,24},{32,36},... | collective-permute-start | bytes 61448 | tf_op jit(solution)/shard_map/ppermute | solution.py:500
  37.3 0.8 %collective-permute-done.8.other = f32[5,8,128]{2,1,0:T(8,128)S(1)} collective-permute-done((f32[5,8,128]{2,1,0:T(8,128)S(1)}, f32[5,8,128]{2,1,0:T(8,128)S(1)}, u32[]{:S(2)}, u32[]{:S(2)}) %collective-permute-start.8) | collective-permute-done | bytes 20512 | tf_op jit(solution)/shard_map/ppermute | solution.py:500
  38.2 0.2 shard_map.48
  38.4 3.0 %collective-permute-start.9 = (f32[8,128]{1,0:T(8,128)S(1)}, f32[8,128]{1,0:T(8,128)S(1)}, u32[]{:S(2)}, u32[]{:S(2)}) collective-permute-start(f32[8,128]{1,0:T(8,128)S(1)} %shard_map.48), channel_id=1, source_target_pairs={{0,6},{2,4},{4,2},{6,0},{8,14},{10,12},{12,10},{14,8},{16,22},{18,... | collective-permute-start | bytes 12296 | tf_op jit(solution)/shard_map/ppermute | solution.py:502
  41.3 0.2 shard_map.47
  41.5 0.9 %shard_map.49.local = f32[32,1024]{1,0:T(8,128)S(1)} custom-call(f32[32,1024]{1,0:T(8,128)S(1)} %get-tuple-element.57.section, f32[10,256,128]{2,1,0:T(8,128)S(1)} %get-tuple-element.58.ay, f32[10,256,128]{2,1,0:T(8,128)S(1)} %get-tuple-element.59.by, f32[256,128]{1,0:T(8,128)S(1)} %get-tuple-element.60.qy), custom_call_target="tpu_custom_call" | custom-call | flops 4000000 | bytes 3000000 | tf_op jit(solution)/shard_map/pallas_call | solution.py:506
  42.4 0.5 %collective-permute-done.9.far = f32[8,128]{1,0:T(8,128)S(1)} collective-permute-done((f32[8,128]{1,0:T(8,128)S(1)}, f32[8,128]{1,0:T(8,128)S(1)}, u32[]{:S(2)}, u32[]{:S(2)}) %collective-permute-start.9) | collective-permute-done | bytes 4128 | tf_op jit(solution)/shard_map/ppermute | solution.py:502
  42.9 0.9 %shard_map.50 = f32[32,1024]{1,0:T(8,128)} custom-call(f32[8,128]{1,0:T(8,128)S(1)} %get-tuple-element.56.message, f32[8,128]{1,0:T(8,128)S(1)} %collective-permute-done.9.far, f32[32,1024]{1,0:T(8,128)S(1)} %shard_map.49.local, f32[32,1024]{1,0:T(8,128)S(1)} %get-tuple-element.51.hy), custom_call_target="tpu_custom_call" | custom-call | tf_op jit(solution)/shard_map/pallas_call | solution.py:507
  (3 shorter events, 0.1 us)
Async XLA Ops:
  0.0 10.1 %collective-permute-start = (f32[2,1,16,1024]{3,2,1,0:T(8,128)}, f32[2,1,16,1024]{3,2,1,0:T(8,128)S(1)}, u32[]{:S(2)}, u32[]{:S(2)}) collective-permute-start(f32[2,1,16,1024]{3,2,1,0:T(8,128)} %param.3), channel_id=1, source_target_pairs={{0,1},{1,0},{2,3},{3,2},{4,5},{5,4},{6,7},{7,6},{8,9},{9,8},{10,11... | collective-permute-start | bytes 393224 | tf_op jit(solution)/shard_map/ppermute | solution.py:451
  2.0 8.0 %collective-permute-start.1 = (f32[2,1,16,1024]{3,2,1,0:T(8,128)}, f32[2,1,16,1024]{3,2,1,0:T(8,128)S(1)}, u32[]{:S(2)}, u32[]{:S(2)}) collective-permute-start(f32[2,1,16,1024]{3,2,1,0:T(8,128)} %param.5), channel_id=1, source_target_pairs={{0,1},{1,0},{2,3},{3,2},{4,5},{5,4},{6,7},{7,6},{8,9},{9,8},{10,11... | collective-permute-start | bytes 393224 | tf_op jit(solution)/shard_map/ppermute | solution.py:452
  3.1 6.9 %collective-permute-start.2 = (f32[2,8,128]{2,1,0:T(8,128)S(1)}, f32[2,8,128]{2,1,0:T(8,128)S(1)}, u32[]{:S(2)}, u32[]{:S(2)}) collective-permute-start(f32[2,8,128]{2,1,0:T(8,128)S(1)} %get-tuple-element.39), channel_id=1, source_target_pairs={{0,32},{4,36},{8,40},{12,44},{16,48},{20,52},{24,56},{28,60},{32,6... | collective-permute-start | bytes 24584 | tf_op jit(solution)/shard_map/ppermute | solution.py:464
  10.2 3.1 %collective-permute-start.3 = (f32[2,8,8,128]{3,2,1,0:T(8,128)S(1)}, f32[2,8,8,128]{3,2,1,0:T(8,128)S(1)}, u32[]{:S(2)}, u32[]{:S(2)}) collective-permute-start(f32[2,8,8,128]{3,2,1,0:T(8,128)S(1)} %get-tuple-element.41.mine), channel_id=1, source_target_pairs={{0,4},{4,0},{8,12},{12,8},{16,20},{20,16},{24,28},{28,24},{32,36},... | collective-permute-start | bytes 196616 | tf_op jit(solution)/shard_map/ppermute | solution.py:484
  13.3 7.4 %collective-permute-start.7 = (f32[2,32,1024]{2,1,0:T(8,128)S(1)}, f32[2,32,1024]{2,1,0:T(8,128)S(1)}, u32[]{:S(2)}, u32[]{:S(2)}) collective-permute-start(f32[2,32,1024]{2,1,0:T(8,128)S(1)} %shard_map.44), channel_id=1, source_target_pairs={{0,4},{4,0},{8,12},{12,8},{16,20},{20,16},{24,28},{28,24},{32,36},... | collective-permute-start | bytes 786440 | tf_op jit(solution)/shard_map/ppermute | solution.py:491
  13.8 4.7 %collective-permute-start.5 = (f32[2,8,8,128]{3,2,1,0:T(8,128)S(1)}, f32[2,8,8,128]{3,2,1,0:T(8,128)S(1)}, u32[]{:S(2)}, u32[]{:S(2)}) collective-permute-start(f32[2,8,8,128]{3,2,1,0:T(8,128)S(1)} %get-tuple-element.43), channel_id=1, source_target_pairs={{0,24},{4,20},{8,16},{12,28},{16,8},{20,4},{24,0},{28,12},{32,56},... | collective-permute-start | bytes 196616 | tf_op jit(solution)/shard_map/ppermute | solution.py:489
  16.7 3.4 %collective-permute-start.4 = (f32[8,8,128]{2,1,0:T(8,128)S(1)}, f32[8,8,128]{2,1,0:T(8,128)S(1)}, u32[]{:S(2)}, u32[]{:S(2)}) collective-permute-start(f32[8,8,128]{2,1,0:T(8,128)S(1)} %get-tuple-element.42.after.chip), channel_id=1, source_target_pairs={{0,8},{4,12},{8,0},{12,4},{16,24},{20,28},{24,16},{28,20},{32,40},... | collective-permute-start | bytes 98312 | tf_op jit(solution)/shard_map/ppermute | solution.py:492
  18.4 2.3 %collective-permute-start.6 = (f32[8,8,128]{2,1,0:T(8,128)S(1)}, f32[8,8,128]{2,1,0:T(8,128)S(1)}, u32[]{:S(2)}, u32[]{:S(2)}) collective-permute-start(f32[8,8,128]{2,1,0:T(8,128)S(1)} %get-tuple-element.45), channel_id=1, source_target_pairs={{0,4},{4,0},{8,12},{12,8},{16,20},{20,16},{24,28},{28,24},{32,36},... | collective-permute-start | bytes 98312 | tf_op jit(solution)/shard_map/ppermute | solution.py:494
  35.1 3.0 %collective-permute-start.8 = (f32[5,8,128]{2,1,0:T(8,128)S(1)}, f32[5,8,128]{2,1,0:T(8,128)S(1)}, u32[]{:S(2)}, u32[]{:S(2)}) collective-permute-start(f32[5,8,128]{2,1,0:T(8,128)S(1)} %shard_map.46.mine), channel_id=1, source_target_pairs={{0,4},{4,0},{8,12},{12,8},{16,20},{20,16},{24,28},{28,24},{32,36},... | collective-permute-start | bytes 61448 | tf_op jit(solution)/shard_map/ppermute | solution.py:500
  38.4 4.5 %collective-permute-start.9 = (f32[8,128]{1,0:T(8,128)S(1)}, f32[8,128]{1,0:T(8,128)S(1)}, u32[]{:S(2)}, u32[]{:S(2)}) collective-permute-start(f32[8,128]{1,0:T(8,128)S(1)} %shard_map.48), channel_id=1, source_target_pairs={{0,6},{2,4},{4,2},{6,0},{8,14},{10,12},{12,10},{14,8},{16,22},{18,... | collective-permute-start | bytes 12296 | tf_op jit(solution)/shard_map/ppermute | solution.py:502

commit v16 on v13

--- a/solution.py
+++ b/solution.py
@@ -206,6 +206,7 @@
 
 
 def source_kernel(fields, fields_far, vertical, vertical_far, h1, h2, parts, prev, source, elements):
+    gx = lax.axis_index("gx")
     here = fields[...]
     v = vertical[...]
     s = here + (v + vertical_far[...]) * 0.5 * (fields_far[...] - here) - v * 0.5 * here
@@ -214,7 +215,10 @@
         mine = slice(f * ROWS, (f + 1) * ROWS)
         first = dense(jnp.sum(h1[mine, :] * s[mine, :], axis=0, keepdims=True))
         last = dense(jnp.sum(h2[mine, :] * s[mine, :], axis=0, keepdims=True))
-        element = (parts[0, f], parts[1, f], parts[2, f], first, last, parts[3, f], parts[4, f], prev[f])
+        rim = parts[4, f]
+        s_last = jnp.where(gx == 63, parts[2, f] + rim * 0.5, parts[2, f])
+        rim = jnp.where(gx % 8 == 7, jnp.where(gx == 7, 0.0, prev[f]), rim)
+        element = (parts[0, f], parts[1, f], s_last, first, last, parts[3, f], rim)
         for n, value in enumerate(element):
             elements[f, n] = value
 
@@ -250,7 +254,7 @@
 
 
 def load(ref, *field):
-    return tuple(ref[(*field, n)] for n in range(8))
+    return tuple(ref[(*field, n)] for n in range(7))
 
 
 def within(node, left, right):
@@ -267,7 +271,7 @@
         second = [jnp.where(even, o, m) for m, o in zip(a, b)]
         tail, start = behind((first[6] + second[5]) * 0.5, second[:5])
         element, end = merge(first[:5], tail)
-        fields.append(((*element, first[5], *second[6:]), (*end, *start)))
+        fields.append(((*element, first[5], second[6]), (*end, *start)))
         for n, value in enumerate(fields[f][0]):
             chips[f, n] = value
     for out, (one, two) in zip((chip, middle), zip(*fields)):
@@ -296,11 +300,9 @@
             here = y ^ flip == m
             chosen = [jnp.where(here, a, c) for a, c in zip(arrived[flip], chosen)]
         chips.append(chosen)
-    slab = lax.axis_index("gx") // 8
-    before = jnp.where(slab == 0, 0.0, chips[3][7])
     element, inner, fronts = None, [], []
     for m in range(4):
-        face = ((before if m == 0 else chips[m - 1][6]) + chips[m][5]) * 0.5
+        face = (chips[m - 1][6] + chips[m][5]) * 0.5
         tail, front = behind(face, chips[m][:5])
         fronts.append(front)
         if m == 0:
@@ -308,9 +310,7 @@
         else:
             element, node = merge(element, tail)
             inner.append(node)
-    g, sl, sr, rl, rr = element
-    sr = jnp.where(slab == 7, sr + chips[3][6] * 0.5, sr)
-    for n, value in enumerate((g, sl, sr, rl, rr)):
+    for n, value in enumerate(element):
         for j in range(8):
             message[j, n] = value
     zero, one = jnp.zeros((8, 128), F32), jnp.ones((8, 128), F32)
@@ -424,7 +424,7 @@
     fields_far = lax.ppermute(fields, "gz", swap)
     vertical_far = lax.ppermute(vertical, "gz", swap)
     full = shape(*grid)
-    half = shape(8, 8, 128)
+    half = shape(7, 8, 128)
     standing = shape(256, 128)
     fields_here, vertical_here, kappa_here, rim = call(
         input_kernel,
@@ -442,7 +442,7 @@
         flops=4_000_000,
         size=2_000_000,
     )(kappa_here)
-    both = shape(2, 8, 8, 128)
+    both = shape(2, 7, 8, 128)
     source, elements = call(source_kernel, (full, both), [VMEM] * 8)(
         fields_here, fields_far.reshape(grid), vertical_here, vertical_far.reshape(grid),
         h1, h2, parts, prev,

time: 42.9 us -> 42.8 us (level)
  no operation moved by 1% of the time
where the time goes in v16:
time: 42.8 us; the launch traced here: 42.6 us
  starting transfers between devices  15.2 us (36%)
  blocking collectives  14 us (33%)
  waiting for transfers between devices  7.06 us (16%)
  Pallas kernels  6.24 us (15%)
    all_to_all x1, blocking collectives, local(): lax.all_to_all(message, 'gx', 0, 0, axis_index_groups=SLAB_GROUPS, tiled=...  14 us
    ppermute x1, waiting for transfers between devices, local(): prev = lax.ppermute(rim, 'gx', [(i, (i + 8) % 64) for i in range(64)])  4.29 us
    ppermute x1, starting transfers between devices, local(): far = lax.ppermute(chips, 'gx', CHIPS)  3 us
    ppermute x1, starting transfers between devices, local(): far = lax.ppermute(message, 'gy', swap)  2.77 us
    ppermute x1, starting transfers between devices, local(): other = lax.ppermute(other, 'gx', CORES)  2.38 us
    ppermute x1, starting transfers between devices, local(): got = lax.ppermute(elements, 'gx', CORES)  2.19 us
    pallas_call x1, Pallas kernels, local(): call(factor_y_kernel, (shape(10, 256, 128), shape(10, 256, 128), standing...  2.14 us
    ppermute x1, starting transfers between devices, local(): fields_far = lax.ppermute(fields, 'gz', swap)  2.04 us
  transfers between devices with their start and end apart: 9, of which 5 were waited for; matrix products, arithmetic and copies ran while one was open for 0% of the time, Pallas kernels for 12%

profile of v16, /device:TPU:1, one launch (start us, length us, event | category | flops | bytes accessed | tf_op | source)
XLA Modules:
  0.0 42.6 jit_solution(8837351818942731833)
XLA Ops:
  0.0 2.0 %collective-permute-start = (f32[2,1,16,1024]{3,2,1,0:T(8,128)}, f32[2,1,16,1024]{3,2,1,0:T(8,128)S(1)}, u32[]{:S(2)}, u32[]{:S(2)}) collective-permute-start(f32[2,1,16,1024]{3,2,1,0:T(8,128)} %param.3), channel_id=1, source_target_pairs={{0,1},{1,0},{2,3},{3,2},{4,5},{5,4},{6,7},{7,6},{8,9},{9,8},{10,11... | collective-permute-start | bytes 393224 | tf_op jit(solution)/shard_map/ppermute | solution.py:424
  2.0 0.0 collective-permute-start.1
  2.1 1.1 %shard_map.37 = (f32[32,1024]{1,0:T(8,128)S(1)}, f32[32,1024]{1,0:T(8,128)S(1)}, f32[32,1024]{1,0:T(8,128)S(1)}, f32[2,8,128]{2,1,0:T(8,128)S(1)}) custom-call(f32[32,1024]{1,0:T(8,128)} %bitcast.11, f32[32,1024]{1,0:T(8,128)} %bitcast.12, f32[32,1024]{1,0:T(8,128)} %bitcast.10), custom_call_target="tpu_custom_call" | custom-call | flops 1000000 | bytes 1000000 | tf_op jit(solution)/shard_map/pallas_call | solution.py:429
  3.1 1.9 %collective-permute-start.2 = (f32[2,8,128]{2,1,0:T(8,128)S(1)}, f32[2,8,128]{2,1,0:T(8,128)S(1)}, u32[]{:S(2)}, u32[]{:S(2)}) collective-permute-start(f32[2,8,128]{2,1,0:T(8,128)S(1)} %get-tuple-element.39), channel_id=1, source_target_pairs={{0,32},{4,36},{8,40},{12,44},{16,48},{20,52},{24,56},{28,60},{32,6... | collective-permute-start | bytes 24584 | tf_op jit(solution)/shard_map/ppermute | solution.py:437
  5.1 0.7 %shard_map.38 = (f32[4,32,1024]{2,1,0:T(8,128)S(1)}, f32[4,32,1024]{2,1,0:T(8,128)S(1)}, f32[32,1024]{1,0:T(8,128)S(1)}, f32[32,1024]{1,0:T(8,128)S(1)}, f32[32,...) custom-call(f32[32,1024]{1,0:T(8,128)S(1)} %get-tuple-element.35.kappa), custom_call_target="tpu_custom_call" | custom-call | flops 4000000 | bytes 2000000 | tf_op jit(solution)/shard_map/pallas_call | solution.py:438
  5.8 4.3 %collective-permute-done.2.prev = f32[2,8,128]{2,1,0:T(8,128)S(1)} collective-permute-done((f32[2,8,128]{2,1,0:T(8,128)S(1)}, f32[2,8,128]{2,1,0:T(8,128)S(1)}, u32[]{:S(2)}, u32[]{:S(2)}) %collective-permute-start.2) | collective-permute-done | bytes 8224 | tf_op jit(solution)/shard_map/ppermute | solution.py:437
  10.1 0.0 collective-permute-done
  10.1 0.0 collective-permute-done.1
  10.1 0.1 shard_map.39
  10.2 2.2 %collective-permute-start.3 = (f32[2,7,8,128]{3,2,1,0:T(8,128)S(1)}, f32[2,7,8,128]{3,2,1,0:T(8,128)S(1)}, u32[]{:S(2)}, u32[]{:S(2)}) collective-permute-start(f32[2,7,8,128]{3,2,1,0:T(8,128)S(1)} %get-tuple-element.40.mine), channel_id=1, source_target_pairs={{0,4},{4,0},{8,12},{12,8},{16,20},{20,16},{24,28},{28,24},{32,36},... | collective-permute-start | bytes 172040 | tf_op jit(solution)/shard_map/ppermute | solution.py:450
  12.3 0.9 %collective-permute-done.3.other = f32[2,7,8,128]{3,2,1,0:T(8,128)S(1)} collective-permute-done((f32[2,7,8,128]{3,2,1,0:T(8,128)S(1)}, f32[2,7,8,128]{3,2,1,0:T(8,128)S(1)}, u32[]{:S(2)}, u32[]{:S(2)}) %collective-permute-start.3) | collective-permute-done | bytes 57376 | tf_op jit(solution)/shard_map/ppermute | solution.py:450
  13.3 3.0 %collective-permute-start.5 = (f32[2,7,8,128]{3,2,1,0:T(8,128)S(1)}, f32[2,7,8,128]{3,2,1,0:T(8,128)S(1)}, u32[]{:S(2)}, u32[]{:S(2)}) collective-permute-start(f32[2,7,8,128]{3,2,1,0:T(8,128)S(1)} %get-tuple-element.42), channel_id=1, source_target_pairs={{0,24},{4,20},{8,16},{12,28},{16,8},{20,4},{24,0},{28,12},{32,56},... | collective-permute-start | bytes 172040 | tf_op jit(solution)/shard_map/ppermute | solution.py:453
  16.3 0.4 collective-permute-start.4
  16.7 2.1 %shard_map.41 = (f32[10,256,128]{2,1,0:T(8,128)S(1)}, f32[10,256,128]{2,1,0:T(8,128)S(1)}, f32[256,128]{1,0:T(8,128)S(1)}, f32[32,1024]{1,0:T(8,128)S(1)}, f32[8,128]{1,0:T(8,128)S(1)}) custom-call(f32[32,1024]{1,0:T(8,128)S(1)} %get-tuple-element.35.kappa, f32[7,8,128]{2,1,0:T(8,128)S(1)} %get-tuple-element.41.after.chip), custom_call_target="tpu_custom_call" | custom-call | flops 20000000 | bytes 4000000 | tf_op jit(solution)/shard_map/pallas_call | solution.py:455
  18.8 0.0 collective-permute-done.5.chips
  18.8 0.4 %collective-permute-start.6 = (f32[7,8,128]{2,1,0:T(8,128)S(1)}, f32[7,8,128]{2,1,0:T(8,128)S(1)}, u32[]{:S(2)}, u32[]{:S(2)}) collective-permute-start(f32[7,8,128]{2,1,0:T(8,128)S(1)} %get-tuple-element.45), channel_id=1, source_target_pairs={{0,4},{4,0},{8,12},{12,8},{16,20},{20,16},{24,28},{28,24},{32,36},... | collective-permute-start | bytes 86024 | tf_op jit(solution)/shard_map/ppermute | solution.py:463
  19.3 0.0 collective-permute-done.4.far1
  19.3 0.9 %collective-permute-done.6.got = f32[7,8,128]{2,1,0:T(8,128)S(1)} collective-permute-done((f32[7,8,128]{2,1,0:T(8,128)S(1)}, f32[7,8,128]{2,1,0:T(8,128)S(1)}, u32[]{:S(2)}, u32[]{:S(2)}) %collective-permute-start.6) | collective-permute-done | bytes 28704 | tf_op jit(solution)/shard_map/ppermute | solution.py:463
  20.2 0.1 shard_map.43
  20.2 14.0 %all_to_all.5.got = f32[8,5,8,128]{3,2,1,0:T(8,128)S(1)} all-to-all(f32[8,5,8,128]{3,2,1,0:T(8,128)S(1)} %get-tuple-element.47), channel_id=1, replica_groups={{0,32,64,96,128,160,192,224},{4,36,68,100,132,164,196,228},{8,40,72,104..., dimensions={0} | all-to-all | bytes 327680 | tf_op jit(solution)/shard_map/all_to_all | solution.py:467
  34.2 0.1 shard_map.44
  34.4 2.4 %collective-permute-start.7 = (f32[2,8,128]{2,1,0:T(8,128)S(1)}, f32[2,8,128]{2,1,0:T(8,128)S(1)}, u32[]{:S(2)}, u32[]{:S(2)}) collective-permute-start(f32[2,8,128]{2,1,0:T(8,128)S(1)} %get-tuple-element.50), channel_id=1, source_target_pairs={{0,4},{4,0},{8,12},{12,8},{16,20},{20,16},{24,28},{28,24},{32,36},... | collective-permute-start | bytes 24584 | tf_op jit(solution)/shard_map/ppermute | solution.py:471
  36.7 0.1 shard_map.45.local
  36.9 0.7 %collective-permute-done.7.other = f32[2,8,128]{2,1,0:T(8,128)S(1)} collective-permute-done((f32[2,8,128]{2,1,0:T(8,128)S(1)}, f32[2,8,128]{2,1,0:T(8,128)S(1)}, u32[]{:S(2)}, u32[]{:S(2)}) %collective-permute-start.7) | collective-permute-done | bytes 8224 | tf_op jit(solution)/shard_map/ppermute | solution.py:471
  37.6 0.1 shard_map.46
  37.7 2.8 %collective-permute-start.8 = (f32[8,128]{1,0:T(8,128)S(1)}, f32[8,128]{1,0:T(8,128)S(1)}, u32[]{:S(2)}, u32[]{:S(2)}) collective-permute-start(f32[8,128]{1,0:T(8,128)S(1)} %get-tuple-element.56.message), channel_id=1, source_target_pairs={{0,2},{2,0},{1,3},{3,1},{4,6},{6,4},{5,7},{7,5},{8,10},{10,8},{9,1... | collective-permute-start | bytes 12296 | tf_op jit(solution)/shard_map/ppermute | solution.py:475
  40.5 0.9 %shard_map.47.local = f32[32,1024]{1,0:T(8,128)S(1)} custom-call(f32[32,1024]{1,0:T(8,128)S(1)} %get-tuple-element.57.section, f32[10,256,128]{2,1,0:T(8,128)S(1)} %get-tuple-element.58.ay, f32[10,256,128]{2,1,0:T(8,128)S(1)} %get-tuple-element.59.by, f32[256,128]{1,0:T(8,128)S(1)} %get-tuple-element.60.qy), custom_call_target="tpu_custom_call" | custom-call | flops 4000000 | bytes 3000000 | tf_op jit(solution)/shard_map/pallas_call | solution.py:476
  41.4 0.3 collective-permute-done.8.far
  41.7 0.9 %shard_map.48 = f32[32,1024]{1,0:T(8,128)} custom-call(f32[8,128]{1,0:T(8,128)S(1)} %get-tuple-element.56.message, f32[8,128]{1,0:T(8,128)S(1)} %collective-permute-done.8.far, f32[32,1024]{1,0:T(8,128)S(1)} %shard_map.47.local, f32[32,1024]{1,0:T(8,128)S(1)} %get-tuple-element.55.hy), custom_call_target="tpu_custom_call" | custom-call | tf_op jit(solution)/shard_map/pallas_call | solution.py:477
  (2 shorter events, 0.0 us)
Async XLA Ops:
  0.0 10.1 %collective-permute-start = (f32[2,1,16,1024]{3,2,1,0:T(8,128)}, f32[2,1,16,1024]{3,2,1,0:T(8,128)S(1)}, u32[]{:S(2)}, u32[]{:S(2)}) collective-permute-start(f32[2,1,16,1024]{3,2,1,0:T(8,128)} %param.3), channel_id=1, source_target_pairs={{0,1},{1,0},{2,3},{3,2},{4,5},{5,4},{6,7},{7,6},{8,9},{9,8},{10,11... | collective-permute-start | bytes 393224 | tf_op jit(solution)/shard_map/ppermute | solution.py:424
  2.0 8.0 %collective-permute-start.1 = (f32[2,1,16,1024]{3,2,1,0:T(8,128)}, f32[2,1,16,1024]{3,2,1,0:T(8,128)S(1)}, u32[]{:S(2)}, u32[]{:S(2)}) collective-permute-start(f32[2,1,16,1024]{3,2,1,0:T(8,128)} %param.5), channel_id=1, source_target_pairs={{0,1},{1,0},{2,3},{3,2},{4,5},{5,4},{6,7},{7,6},{8,9},{9,8},{10,11... | collective-permute-start | bytes 393224 | tf_op jit(solution)/shard_map/ppermute | solution.py:425
  3.1 6.9 %collective-permute-start.2 = (f32[2,8,128]{2,1,0:T(8,128)S(1)}, f32[2,8,128]{2,1,0:T(8,128)S(1)}, u32[]{:S(2)}, u32[]{:S(2)}) collective-permute-start(f32[2,8,128]{2,1,0:T(8,128)S(1)} %get-tuple-element.39), channel_id=1, source_target_pairs={{0,32},{4,36},{8,40},{12,44},{16,48},{20,52},{24,56},{28,60},{32,6... | collective-permute-start | bytes 24584 | tf_op jit(solution)/shard_map/ppermute | solution.py:437
  10.2 3.1 %collective-permute-start.3 = (f32[2,7,8,128]{3,2,1,0:T(8,128)S(1)}, f32[2,7,8,128]{3,2,1,0:T(8,128)S(1)}, u32[]{:S(2)}, u32[]{:S(2)}) collective-permute-start(f32[2,7,8,128]{3,2,1,0:T(8,128)S(1)} %get-tuple-element.40.mine), channel_id=1, source_target_pairs={{0,4},{4,0},{8,12},{12,8},{16,20},{20,16},{24,28},{28,24},{32,36},... | collective-permute-start | bytes 172040 | tf_op jit(solution)/shard_map/ppermute | solution.py:450
  13.3 5.5 %collective-permute-start.5 = (f32[2,7,8,128]{3,2,1,0:T(8,128)S(1)}, f32[2,7,8,128]{3,2,1,0:T(8,128)S(1)}, u32[]{:S(2)}, u32[]{:S(2)}) collective-permute-start(f32[2,7,8,128]{3,2,1,0:T(8,128)S(1)} %get-tuple-element.42), channel_id=1, source_target_pairs={{0,24},{4,20},{8,16},{12,28},{16,8},{20,4},{24,0},{28,12},{32,56},... | collective-permute-start | bytes 172040 | tf_op jit(solution)/shard_map/ppermute | solution.py:453
  16.3 3.0 %collective-permute-start.4 = (f32[7,8,128]{2,1,0:T(8,128)S(1)}, f32[7,8,128]{2,1,0:T(8,128)S(1)}, u32[]{:S(2)}, u32[]{:S(2)}) collective-permute-start(f32[7,8,128]{2,1,0:T(8,128)S(1)} %get-tuple-element.41.after.chip), channel_id=1, source_target_pairs={{0,8},{4,12},{8,0},{12,4},{16,24},{20,28},{24,16},{28,20},{32,40},... | collective-permute-start | bytes 86024 | tf_op jit(solution)/shard_map/ppermute | solution.py:454
  18.8 1.3 %collective-permute-start.6 = (f32[7,8,128]{2,1,0:T(8,128)S(1)}, f32[7,8,128]{2,1,0:T(8,128)S(1)}, u32[]{:S(2)}, u32[]{:S(2)}) collective-permute-start(f32[7,8,128]{2,1,0:T(8,128)S(1)} %get-tuple-element.45), channel_id=1, source_target_pairs={{0,4},{4,0},{8,12},{12,8},{16,20},{20,16},{24,28},{28,24},{32,36},... | collective-permute-start | bytes 86024 | tf_op jit(solution)/shard_map/ppermute | solution.py:463
  34.4 3.2 %collective-permute-start.7 = (f32[2,8,128]{2,1,0:T(8,128)S(1)}, f32[2,8,128]{2,1,0:T(8,128)S(1)}, u32[]{:S(2)}, u32[]{:S(2)}) collective-permute-start(f32[2,8,128]{2,1,0:T(8,128)S(1)} %get-tuple-element.50), channel_id=1, source_target_pairs={{0,4},{4,0},{8,12},{12,8},{16,20},{20,16},{24,28},{28,24},{32,36},... | collective-permute-start | bytes 24584 | tf_op jit(solution)/shard_map/ppermute | solution.py:471
  37.7 4.0 %collective-permute-start.8 = (f32[8,128]{1,0:T(8,128)S(1)}, f32[8,128]{1,0:T(8,128)S(1)}, u32[]{:S(2)}, u32[]{:S(2)}) collective-permute-start(f32[8,128]{1,0:T(8,128)S(1)} %get-tuple-element.56.message), channel_id=1, source_target_pairs={{0,2},{2,0},{1,3},{3,1},{4,6},{6,4},{5,7},{7,5},{8,10},{10,8},{9,1... | collective-permute-start | bytes 12296 | tf_op jit(solution)/shard_map/ppermute | solution.py:475

commit v17 on v16

--- a/solution.py
+++ b/solution.py
@@ -168,8 +168,7 @@
                     parts[n, f, pl.ds(c * (half // 128) + i, 1), :] = row[:, 128 * i : 128 * (i + 1)]
 
 
-def factor_y_kernel(kappa, after, ay, by, qy, hy, edge):
-    del after
+def factor_y(kappa, ay, by, qy, hy, edge):
     gy = lax.axis_index("gy")
     low_side = gy == 0
     end = jnp.where(low_side, COLS - 1, 0)
@@ -203,6 +202,22 @@
         part = slice(8 * g, 8 * g + 8)
         tile = jnp.where(lane == 4 * g, total[part], jnp.where(lane == 4 * g + 1, rim[part], tile))
     edge[...] = tile
+
+
+def factor_y_kernel(kappa, after, *outs):
+    del after
+
+    @pl.when(lax.axis_index("gx") % 2 == 0)
+    def _():
+        factor_y(kappa, *outs)
+
+
+def factor_y_late_kernel(kappa, after, after_too, *refs):
+    del after, after_too
+
+    @pl.when(lax.axis_index("gx") % 2 == 1)
+    def _():
+        factor_y(kappa, *refs[5:])
 
 
 def source_kernel(fields, fields_far, vertical, vertical_far, h1, h2, parts, prev, source, elements):
@@ -287,7 +302,8 @@
         send[n] = jnp.where(even, two, one)
 
 
-def slab_kernel(chip, far1, keep, got, middle, message, nodes):
+def slab_kernel(chip, far1, keep, got, middle, after, message, nodes):
+    del after
     y = lax.axis_index("gx") // 2 % 4
     even = lax.axis_index("gx") % 2 == 0
     far2 = [jnp.where(even, g, k) for k, g in zip(load(keep), load(got))]
@@ -452,18 +468,22 @@
     chips, chip, middle = call(chip_kernel, (both, half, shape(6, 8, 128)), [VMEM] * 2)(elements, got)
     far = lax.ppermute(chips, "gx", CHIPS)
     far1 = lax.ppermute(chip, "gx", NEXT)
-    ay, by, qy, hy, edge = call(
-        factor_y_kernel,
-        (shape(10, 256, 128), shape(10, 256, 128), standing, full, shape(8, 128)),
-        [VMEM] * 2,
-        flops=20_000_000,
-        size=4_000_000,
-    )(kappa_here, chip)
-    keep, send = call(pick_kernel, (half, half), [VMEM] * 2)(far, edge)
+    lines = (shape(10, 256, 128), shape(10, 256, 128), standing, full, shape(8, 128))
+    factors = call(factor_y_kernel, lines, [VMEM] * 2, flops=20_000_000, size=4_000_000)(kappa_here, chip)
+    keep, send = call(pick_kernel, (half, half), [VMEM] * 2)(far, factors[4])
     got = lax.ppermute(send, "gx", CORES)
+    ay, by, qy, hy, edge = pl.pallas_call(
+        factor_y_late_kernel,
+        out_shape=lines,
+        in_specs=[VMEM] * 8,
+        out_specs=(VMEM,) * 5,
+        input_output_aliases={3 + n: n for n in range(5)},
+        compiler_params=PARAMS,
+        cost_estimate=pl.CostEstimate(flops=20_000_000, bytes_accessed=4_000_000, transcendentals=0),
+    )(kappa_here, got, far1, *factors)
     message, nodes = call(
-        slab_kernel, (shape(8, 5, 8, 128), shape(4, 3, 8, 128)), [VMEM] * 5
-    )(chip, far1, keep, got, middle)
+        slab_kernel, (shape(8, 5, 8, 128), shape(4, 3, 8, 128)), [VMEM] * 6
+    )(chip, far1, keep, got, middle, edge)
     got = lax.all_to_all(message, "gx", 0, 0, axis_index_groups=SLAB_GROUPS, tiled=True)
     mine, other = call(
         ends_kernel, (shape(2, 8, 128), shape(2, 8, 128)), [VMEM, VMEM]

time: 42.8 us -> 43.5 us (1.016)
  waiting for transfers between devices: 7.06 us -> 8.59 us
  starting transfers between devices: 15.2 us -> 13.8 us
  blocking collectives: 14 us -> 14.6 us
    ppermute x1, starting transfers between devices: 2.38 us -> 0.09 us  [local(): other = lax.ppermute(other, 'gx', CORES)]
    ppermute x1, waiting for transfers between devices: 0.01 us -> 1.22 us  [local(): far = lax.ppermute(chips, 'gx', CHIPS)]
    ppermute x1, starting transfers between devices: 0.45 us -> 1.39 us  [local(): got = lax.ppermute(send, 'gx', CORES)]
    all_to_all x1, blocking collectives: 14 us -> 14.6 us  [local(): lax.all_to_all(message, 'gx', 0, 0, axis_index_groups=SLAB_GROUPS, tiled=...]
    pallas_call x3 -> x4, Pallas kernels: 2.24 us -> 2.27 us  [the longest x1 2.16 us: local(): pl.pallas_call(factor_y_late_kernel, out_shape=lines, in_specs=[VMEM] * 8...]
  transfers between devices with their start and end apart: 9 -> 9, of which waited for: 5 -> 6; matrix products, arithmetic and copies ran while one was open for 0% -> 0% of each run, Pallas kernels for 12% -> 6%
where the time goes in v17:
time: 43.5 us; the launch traced here: 43.4 us
  blocking collectives  14.6 us (34%)
  starting transfers between devices  13.8 us (32%)
  waiting for transfers between devices  8.59 us (20%)
  Pallas kernels  6.28 us (14%)
    all_to_all x1, blocking collectives, local(): lax.all_to_all(message, 'gx', 0, 0, axis_index_groups=SLAB_GROUPS, tiled=...  14.6 us
    ppermute x1, waiting for transfers between devices, local(): prev = lax.ppermute(rim, 'gx', [(i, (i + 8) % 64) for i in range(64)])  4.28 us
    ppermute x1, starting transfers between devices, local(): far = lax.ppermute(chips, 'gx', CHIPS)  3 us
    ppermute x1, starting transfers between devices, local(): far = lax.ppermute(message, 'gy', swap)  2.77 us
    ppermute x1, starting transfers between devices, local(): got = lax.ppermute(elements, 'gx', CORES)  2.19 us
    pallas_call x1, Pallas kernels, local(): pl.pallas_call(factor_y_late_kernel, out_shape=lines, in_specs=[VMEM] * 8...  2.16 us
    ppermute x1, starting transfers between devices, local(): fields_far = lax.ppermute(fields, 'gz', swap)  2.04 us
    ppermute x1, starting transfers between devices, local(): prev = lax.ppermute(rim, 'gx', [(i, (i + 8) % 64) for i in range(64)])  1.94 us
  transfers between devices with their start and end apart: 9, of which 6 were waited for; matrix products, arithmetic and copies ran while one was open for 0% of the time, Pallas kernels for 6%

profile of v17, /device:TPU:1, one launch (start us, length us, event | category | flops | bytes accessed | tf_op | source)
XLA Modules:
  0.0 43.4 jit_solution(3407458535696268378)
XLA Ops:
  0.0 2.0 %collective-permute-start = (f32[2,1,16,1024]{3,2,1,0:T(8,128)}, f32[2,1,16,1024]{3,2,1,0:T(8,128)S(1)}, u32[]{:S(2)}, u32[]{:S(2)}) collective-permute-start(f32[2,1,16,1024]{3,2,1,0:T(8,128)} %param.3), channel_id=1, source_target_pairs={{0,1},{1,0},{2,3},{3,2},{4,5},{5,4},{6,7},{7,6},{8,9},{9,8},{10,11... | collective-permute-start | bytes 393224 | tf_op jit(solution)/shard_map/ppermute | solution.py:440
  2.0 0.0 collective-permute-start.1
  2.1 1.1 %shard_map.37 = (f32[32,1024]{1,0:T(8,128)S(1)}, f32[32,1024]{1,0:T(8,128)S(1)}, f32[32,1024]{1,0:T(8,128)S(1)}, f32[2,8,128]{2,1,0:T(8,128)S(1)}) custom-call(f32[32,1024]{1,0:T(8,128)} %bitcast.11, f32[32,1024]{1,0:T(8,128)} %bitcast.12, f32[32,1024]{1,0:T(8,128)} %bitcast.10), custom_call_target="tpu_custom_call" | custom-call | flops 1000000 | bytes 1000000 | tf_op jit(solution)/shard_map/pallas_call | solution.py:445
  3.1 1.9 %collective-permute-start.2 = (f32[2,8,128]{2,1,0:T(8,128)S(1)}, f32[2,8,128]{2,1,0:T(8,128)S(1)}, u32[]{:S(2)}, u32[]{:S(2)}) collective-permute-start(f32[2,8,128]{2,1,0:T(8,128)S(1)} %get-tuple-element.44), channel_id=1, source_target_pairs={{0,32},{4,36},{8,40},{12,44},{16,48},{20,52},{24,56},{28,60},{32,6... | collective-permute-start | bytes 24584 | tf_op jit(solution)/shard_map/ppermute | solution.py:453
  5.1 0.7 %shard_map.38 = (f32[4,32,1024]{2,1,0:T(8,128)S(1)}, f32[4,32,1024]{2,1,0:T(8,128)S(1)}, f32[32,1024]{1,0:T(8,128)S(1)}, f32[32,1024]{1,0:T(8,128)S(1)}, f32[32,...) custom-call(f32[32,1024]{1,0:T(8,128)S(1)} %get-tuple-element.40.kappa), custom_call_target="tpu_custom_call" | custom-call | flops 4000000 | bytes 2000000 | tf_op jit(solution)/shard_map/pallas_call | solution.py:454
  5.8 4.3 %collective-permute-done.2.prev = f32[2,8,128]{2,1,0:T(8,128)S(1)} collective-permute-done((f32[2,8,128]{2,1,0:T(8,128)S(1)}, f32[2,8,128]{2,1,0:T(8,128)S(1)}, u32[]{:S(2)}, u32[]{:S(2)}) %collective-permute-start.2) | collective-permute-done | bytes 8224 | tf_op jit(solution)/shard_map/ppermute | solution.py:453
  10.1 0.0 collective-permute-done
  10.1 0.0 collective-permute-done.1
  10.1 0.1 shard_map.39
  10.2 2.2 %collective-permute-start.3 = (f32[2,7,8,128]{3,2,1,0:T(8,128)S(1)}, f32[2,7,8,128]{3,2,1,0:T(8,128)S(1)}, u32[]{:S(2)}, u32[]{:S(2)}) collective-permute-start(f32[2,7,8,128]{3,2,1,0:T(8,128)S(1)} %get-tuple-element.45.mine), channel_id=1, source_target_pairs={{0,4},{4,0},{8,12},{12,8},{16,20},{20,16},{24,28},{28,24},{32,36},... | collective-permute-start | bytes 172040 | tf_op jit(solution)/shard_map/ppermute | solution.py:466
  12.3 0.9 %collective-permute-done.3.other = f32[2,7,8,128]{3,2,1,0:T(8,128)S(1)} collective-permute-done((f32[2,7,8,128]{3,2,1,0:T(8,128)S(1)}, f32[2,7,8,128]{3,2,1,0:T(8,128)S(1)}, u32[]{:S(2)}, u32[]{:S(2)}) %collective-permute-start.3) | collective-permute-done | bytes 57376 | tf_op jit(solution)/shard_map/ppermute | solution.py:466
  13.3 3.0 %collective-permute-start.5 = (f32[2,7,8,128]{3,2,1,0:T(8,128)S(1)}, f32[2,7,8,128]{3,2,1,0:T(8,128)S(1)}, u32[]{:S(2)}, u32[]{:S(2)}) collective-permute-start(f32[2,7,8,128]{3,2,1,0:T(8,128)S(1)} %get-tuple-element.47), channel_id=1, source_target_pairs={{0,24},{4,20},{8,16},{12,28},{16,8},{20,4},{24,0},{28,12},{32,56},... | collective-permute-start | bytes 172040 | tf_op jit(solution)/shard_map/ppermute | solution.py:469
  16.3 0.4 collective-permute-start.4
  16.7 1.2 %collective-permute-done.5.chips = f32[2,7,8,128]{3,2,1,0:T(8,128)S(1)} collective-permute-done((f32[2,7,8,128]{3,2,1,0:T(8,128)S(1)}, f32[2,7,8,128]{3,2,1,0:T(8,128)S(1)}, u32[]{:S(2)}, u32[]{:S(2)}) %collective-permute-start.5) | collective-permute-done | bytes 57376 | tf_op jit(solution)/shard_map/ppermute | solution.py:469
  17.9 1.4 %collective-permute-start.6 = (f32[7,8,128]{2,1,0:T(8,128)S(1)}, f32[7,8,128]{2,1,0:T(8,128)S(1)}, u32[]{:S(2)}, u32[]{:S(2)}) collective-permute-start(f32[7,8,128]{2,1,0:T(8,128)S(1)} %get-tuple-element.50), channel_id=1, source_target_pairs={{0,4},{4,0},{8,12},{12,8},{16,20},{20,16},{24,28},{28,24},{32,36},... | collective-permute-start | bytes 86024 | tf_op jit(solution)/shard_map/ppermute | solution.py:474
  19.3 0.0 collective-permute-done.4.after_too.far1
  19.3 0.9 %collective-permute-done.6.after.got = f32[7,8,128]{2,1,0:T(8,128)S(1)} collective-permute-done((f32[7,8,128]{2,1,0:T(8,128)S(1)}, f32[7,8,128]{2,1,0:T(8,128)S(1)}, u32[]{:S(2)}, u32[]{:S(2)}) %collective-permute-start.6) | collective-permute-done | bytes 28704 | tf_op jit(solution)/shard_map/ppermute | solution.py:474
  20.2 2.2 %shard_map.43 = (f32[10,256,128]{2,1,0:T(8,128)S(1)}, f32[10,256,128]{2,1,0:T(8,128)S(1)}, f32[256,128]{1,0:T(8,128)S(1)}, f32[32,1024]{1,0:T(8,128)S(1)}, f32[8,128]{1,0:T(8,128)S(1)}) custom-call(f32[32,1024]{1,0:T(8,128)S(1)} %get-tuple-element.40.kappa, ...), custom_call_target="tpu_custom_call", output_to_operand_aliasing={{0}: (3, {}), {1}: (4, {}), {2}: (5, {}), {3}: (6, {}), {4}... | custom-call | flops 20000000 | bytes 4000000 | tf_op jit(solution)/shard_map/pallas_call | solution.py:475
  22.3 0.1 shard_map.44
  22.4 14.6 %all_to_all.5.got = f32[8,5,8,128]{3,2,1,0:T(8,128)S(1)} all-to-all(f32[8,5,8,128]{3,2,1,0:T(8,128)S(1)} %get-tuple-element.57), channel_id=1, replica_groups={{0,32,64,96,128,160,192,224},{4,36,68,100,132,164,196,228},{8,40,72,104..., dimensions={0} | all-to-all | bytes 327680 | tf_op jit(solution)/shard_map/all_to_all | solution.py:487
  37.1 0.1 shard_map.45
  37.2 0.1 collective-permute-start.7
  37.3 0.2 shard_map.46.local
  37.4 1.0 %collective-permute-done.7.other = f32[2,8,128]{2,1,0:T(8,128)S(1)} collective-permute-done((f32[2,8,128]{2,1,0:T(8,128)S(1)}, f32[2,8,128]{2,1,0:T(8,128)S(1)}, u32[]{:S(2)}, u32[]{:S(2)}) %collective-permute-start.7) | collective-permute-done | bytes 8224 | tf_op jit(solution)/shard_map/ppermute | solution.py:491
  38.4 0.1 shard_map.47
  38.5 2.8 %collective-permute-start.8 = (f32[8,128]{1,0:T(8,128)S(1)}, f32[8,128]{1,0:T(8,128)S(1)}, u32[]{:S(2)}, u32[]{:S(2)}) collective-permute-start(f32[8,128]{1,0:T(8,128)S(1)} %get-tuple-element.66.message), channel_id=1, source_target_pairs={{0,2},{2,0},{1,3},{3,1},{4,6},{6,4},{5,7},{7,5},{8,10},{10,8},{9,1... | collective-permute-start | bytes 12296 | tf_op jit(solution)/shard_map/ppermute | solution.py:495
  41.3 0.9 %shard_map.48.local = f32[32,1024]{1,0:T(8,128)S(1)} custom-call(f32[32,1024]{1,0:T(8,128)S(1)} %get-tuple-element.67.section, f32[10,256,128]{2,1,0:T(8,128)S(1)} %get-tuple-element.68.ay, f32[10,256,128]{2,1,0:T(8,128)S(1)} %get-tuple-element.69.by, f32[256,128]{1,0:T(8,128)S(1)} %get-tuple-element.70.qy), custom_call_target="tpu_custom_call" | custom-call | flops 4000000 | bytes 3000000 | tf_op jit(solution)/shard_map/pallas_call | solution.py:496
  42.2 0.3 collective-permute-done.8.far
  42.5 0.9 %shard_map.49 = f32[32,1024]{1,0:T(8,128)} custom-call(f32[8,128]{1,0:T(8,128)S(1)} %get-tuple-element.66.message, f32[8,128]{1,0:T(8,128)S(1)} %collective-permute-done.8.far, f32[32,1024]{1,0:T(8,128)S(1)} %shard_map.48.local, f32[32,1024]{1,0:T(8,128)S(1)} %get-tuple-element.65.hy), custom_call_target="tpu_custom_call" | custom-call | tf_op jit(solution)/shard_map/pallas_call | solution.py:497
  (3 shorter events, 0.0 us)
Async XLA Ops:
  0.0 10.1 %collective-permute-start = (f32[2,1,16,1024]{3,2,1,0:T(8,128)}, f32[2,1,16,1024]{3,2,1,0:T(8,128)S(1)}, u32[]{:S(2)}, u32[]{:S(2)}) collective-permute-start(f32[2,1,16,1024]{3,2,1,0:T(8,128)} %param.3), channel_id=1, source_target_pairs={{0,1},{1,0},{2,3},{3,2},{4,5},{5,4},{6,7},{7,6},{8,9},{9,8},{10,11... | collective-permute-start | bytes 393224 | tf_op jit(solution)/shard_map/ppermute | solution.py:440
  2.0 8.0 %collective-permute-start.1 = (f32[2,1,16,1024]{3,2,1,0:T(8,128)}, f32[2,1,16,1024]{3,2,1,0:T(8,128)S(1)}, u32[]{:S(2)}, u32[]{:S(2)}) collective-permute-start(f32[2,1,16,1024]{3,2,1,0:T(8,128)} %param.5), channel_id=1, source_target_pairs={{0,1},{1,0},{2,3},{3,2},{4,5},{5,4},{6,7},{7,6},{8,9},{9,8},{10,11... | collective-permute-start | bytes 393224 | tf_op jit(solution)/shard_map/ppermute | solution.py:441
  3.1 6.9 %collective-permute-start.2 = (f32[2,8,128]{2,1,0:T(8,128)S(1)}, f32[2,8,128]{2,1,0:T(8,128)S(1)}, u32[]{:S(2)}, u32[]{:S(2)}) collective-permute-start(f32[2,8,128]{2,1,0:T(8,128)S(1)} %get-tuple-element.44), channel_id=1, source_target_pairs={{0,32},{4,36},{8,40},{12,44},{16,48},{20,52},{24,56},{28,60},{32,6... | collective-permute-start | bytes 24584 | tf_op jit(solution)/shard_map/ppermute | solution.py:453
  10.2 3.1 %collective-permute-start.3 = (f32[2,7,8,128]{3,2,1,0:T(8,128)S(1)}, f32[2,7,8,128]{3,2,1,0:T(8,128)S(1)}, u32[]{:S(2)}, u32[]{:S(2)}) collective-permute-start(f32[2,7,8,128]{3,2,1,0:T(8,128)S(1)} %get-tuple-element.45.mine), channel_id=1, source_target_pairs={{0,4},{4,0},{8,12},{12,8},{16,20},{20,16},{24,28},{28,24},{32,36},... | collective-permute-start | bytes 172040 | tf_op jit(solution)/shard_map/ppermute | solution.py:466
  13.3 4.6 %collective-permute-start.5 = (f32[2,7,8,128]{3,2,1,0:T(8,128)S(1)}, f32[2,7,8,128]{3,2,1,0:T(8,128)S(1)}, u32[]{:S(2)}, u32[]{:S(2)}) collective-permute-start(f32[2,7,8,128]{3,2,1,0:T(8,128)S(1)} %get-tuple-element.47), channel_id=1, source_target_pairs={{0,24},{4,20},{8,16},{12,28},{16,8},{20,4},{24,0},{28,12},{32,56},... | collective-permute-start | bytes 172040 | tf_op jit(solution)/shard_map/ppermute | solution.py:469
  16.3 3.0 %collective-permute-start.4 = (f32[7,8,128]{2,1,0:T(8,128)S(1)}, f32[7,8,128]{2,1,0:T(8,128)S(1)}, u32[]{:S(2)}, u32[]{:S(2)}) collective-permute-start(f32[7,8,128]{2,1,0:T(8,128)S(1)} %get-tuple-element.46.after.chip), channel_id=1, source_target_pairs={{0,8},{4,12},{8,0},{12,4},{16,24},{20,28},{24,16},{28,20},{32,40},... | collective-permute-start | bytes 86024 | tf_op jit(solution)/shard_map/ppermute | solution.py:470
  17.9 2.2 %collective-permute-start.6 = (f32[7,8,128]{2,1,0:T(8,128)S(1)}, f32[7,8,128]{2,1,0:T(8,128)S(1)}, u32[]{:S(2)}, u32[]{:S(2)}) collective-permute-start(f32[7,8,128]{2,1,0:T(8,128)S(1)} %get-tuple-element.50), channel_id=1, source_target_pairs={{0,4},{4,0},{8,12},{12,8},{16,20},{20,16},{24,28},{28,24},{32,36},... | collective-permute-start | bytes 86024 | tf_op jit(solution)/shard_map/ppermute | solution.py:474
  37.2 1.3 %collective-permute-start.7 = (f32[2,8,128]{2,1,0:T(8,128)S(1)}, f32[2,8,128]{2,1,0:T(8,128)S(1)}, u32[]{:S(2)}, u32[]{:S(2)}) collective-permute-start(f32[2,8,128]{2,1,0:T(8,128)S(1)} %get-tuple-element.60), channel_id=1, source_target_pairs={{0,4},{4,0},{8,12},{12,8},{16,20},{20,16},{24,28},{28,24},{32,36},... | collective-permute-start | bytes 24584 | tf_op jit(solution)/shard_map/ppermute | solution.py:491
  38.5 4.0 %collective-permute-start.8 = (f32[8,128]{1,0:T(8,128)S(1)}, f32[8,128]{1,0:T(8,128)S(1)}, u32[]{:S(2)}, u32[]{:S(2)}) collective-permute-start(f32[8,128]{1,0:T(8,128)S(1)} %get-tuple-element.66.message), channel_id=1, source_target_pairs={{0,2},{2,0},{1,3},{3,1},{4,6},{6,4},{5,7},{7,5},{8,10},{10,8},{9,1... | collective-permute-start | bytes 12296 | tf_op jit(solution)/shard_map/ppermute | solution.py:495

commit v18 on v16

--- a/solution.py
+++ b/solution.py
@@ -290,8 +290,8 @@
 def slab_kernel(chip, far1, keep, got, middle, message, nodes):
     y = lax.axis_index("gx") // 2 % 4
     even = lax.axis_index("gx") % 2 == 0
-    far2 = [jnp.where(even, g, k) for k, g in zip(load(keep), load(got))]
-    far3 = [jnp.where(even, k, g) for k, g in zip(load(keep), load(got))]
+    far2 = [jnp.where(even, k, g) for k, g in zip(load(keep), load(got))]
+    far3 = [jnp.where(even, g, k) for k, g in zip(load(keep), load(got))]
     arrived = [load(chip), load(far1), far2, far3]
     chips = []
     for m in range(4):
@@ -414,7 +414,7 @@
 CORES = [(i, i ^ 1) for i in range(64)]
 
 
-CHIPS = [(i, i ^ (4 if i % 2 else 6)) for i in range(64)]
+CHIPS = [(i, i ^ (5 if i % 2 else 7)) for i in range(64)]
 NEXT = [(i, i ^ 2) for i in range(64)]
 
 

time: 42.8 us -> 42.9 us (level)
  starting transfers between devices: 15.2 us -> 14.5 us
  blocking collectives: 14 us -> 14.6 us
    all_to_all x1, blocking collectives: 14 us -> 14.6 us  [local(): lax.all_to_all(message, 'gx', 0, 0, axis_index_groups=SLAB_GROUPS, tiled=...]
    ppermute x1, starting transfers between devices: 2.38 us -> 1.8 us  [local(): other = lax.ppermute(other, 'gx', CORES)]
where the time goes in v18:
time: 42.9 us; the launch traced here: 42.8 us
  blocking collectives  14.6 us (34%)
  starting transfers between devices  14.5 us (34%)
  waiting for transfers between devices  7.39 us (17%)
  Pallas kernels  6.24 us (15%)
    all_to_all x1, blocking collectives, local(): lax.all_to_all(message, 'gx', 0, 0, axis_index_groups=SLAB_GROUPS, tiled=...  14.6 us
    ppermute x1, waiting for transfers between devices, local(): prev = lax.ppermute(rim, 'gx', [(i, (i + 8) % 64) for i in range(64)])  4.29 us
    ppermute x1, starting transfers between devices, local(): far = lax.ppermute(chips, 'gx', CHIPS)  3.23 us
    ppermute x1, starting transfers between devices, local(): far = lax.ppermute(message, 'gy', swap)  2.77 us
    ppermute x1, starting transfers between devices, local(): got = lax.ppermute(elements, 'gx', CORES)  2.19 us
    pallas_call x1, Pallas kernels, local(): call(factor_y_kernel, (shape(10, 256, 128), shape(10, 256, 128), standing...  2.14 us
    ppermute x1, starting transfers between devices, local(): fields_far = lax.ppermute(fields, 'gz', swap)  2.04 us
    ppermute x1, starting transfers between devices, local(): prev = lax.ppermute(rim, 'gx', [(i, (i + 8) % 64) for i in range(64)])  1.94 us
  transfers between devices with their start and end apart: 9, of which 5 were waited for; matrix products, arithmetic and copies ran while one was open for 0% of the time, Pallas kernels for 12%

profile of v18, /device:TPU:1, one launch (start us, length us, event | category | flops | bytes accessed | tf_op | source)
XLA Modules:
  0.0 42.8 jit_solution(6739966691254826274)
XLA Ops:
  0.0 2.0 %collective-permute-start = (f32[2,1,16,1024]{3,2,1,0:T(8,128)}, f32[2,1,16,1024]{3,2,1,0:T(8,128)S(1)}, u32[]{:S(2)}, u32[]{:S(2)}) collective-permute-start(f32[2,1,16,1024]{3,2,1,0:T(8,128)} %param.3), channel_id=1, source_target_pairs={{0,1},{1,0},{2,3},{3,2},{4,5},{5,4},{6,7},{7,6},{8,9},{9,8},{10,11... | collective-permute-start | bytes 393224 | tf_op jit(solution)/shard_map/ppermute | solution.py:424
  2.0 0.0 collective-permute-start.1
  2.1 1.1 %shard_map.37 = (f32[32,1024]{1,0:T(8,128)S(1)}, f32[32,1024]{1,0:T(8,128)S(1)}, f32[32,1024]{1,0:T(8,128)S(1)}, f32[2,8,128]{2,1,0:T(8,128)S(1)}) custom-call(f32[32,1024]{1,0:T(8,128)} %bitcast.11, f32[32,1024]{1,0:T(8,128)} %bitcast.12, f32[32,1024]{1,0:T(8,128)} %bitcast.10), custom_call_target="tpu_custom_call" | custom-call | flops 1000000 | bytes 1000000 | tf_op jit(solution)/shard_map/pallas_call | solution.py:429
  3.1 1.9 %collective-permute-start.2 = (f32[2,8,128]{2,1,0:T(8,128)S(1)}, f32[2,8,128]{2,1,0:T(8,128)S(1)}, u32[]{:S(2)}, u32[]{:S(2)}) collective-permute-start(f32[2,8,128]{2,1,0:T(8,128)S(1)} %get-tuple-element.39), channel_id=1, source_target_pairs={{0,32},{4,36},{8,40},{12,44},{16,48},{20,52},{24,56},{28,60},{32,6... | collective-permute-start | bytes 24584 | tf_op jit(solution)/shard_map/ppermute | solution.py:437
  5.1 0.7 %shard_map.38 = (f32[4,32,1024]{2,1,0:T(8,128)S(1)}, f32[4,32,1024]{2,1,0:T(8,128)S(1)}, f32[32,1024]{1,0:T(8,128)S(1)}, f32[32,1024]{1,0:T(8,128)S(1)}, f32[32,...) custom-call(f32[32,1024]{1,0:T(8,128)S(1)} %get-tuple-element.35.kappa), custom_call_target="tpu_custom_call" | custom-call | flops 4000000 | bytes 2000000 | tf_op jit(solution)/shard_map/pallas_call | solution.py:438
  5.8 4.3 %collective-permute-done.2.prev = f32[2,8,128]{2,1,0:T(8,128)S(1)} collective-permute-done((f32[2,8,128]{2,1,0:T(8,128)S(1)}, f32[2,8,128]{2,1,0:T(8,128)S(1)}, u32[]{:S(2)}, u32[]{:S(2)}) %collective-permute-start.2) | collective-permute-done | bytes 8224 | tf_op jit(solution)/shard_map/ppermute | solution.py:437
  10.1 0.0 collective-permute-done
  10.1 0.0 collective-permute-done.1
  10.1 0.1 shard_map.39
  10.2 2.2 %collective-permute-start.3 = (f32[2,7,8,128]{3,2,1,0:T(8,128)S(1)}, f32[2,7,8,128]{3,2,1,0:T(8,128)S(1)}, u32[]{:S(2)}, u32[]{:S(2)}) collective-permute-start(f32[2,7,8,128]{3,2,1,0:T(8,128)S(1)} %get-tuple-element.40.mine), channel_id=1, source_target_pairs={{0,4},{4,0},{8,12},{12,8},{16,20},{20,16},{24,28},{28,24},{32,36},... | collective-permute-start | bytes 172040 | tf_op jit(solution)/shard_map/ppermute | solution.py:450
  12.3 0.9 %collective-permute-done.3.other = f32[2,7,8,128]{3,2,1,0:T(8,128)S(1)} collective-permute-done((f32[2,7,8,128]{3,2,1,0:T(8,128)S(1)}, f32[2,7,8,128]{3,2,1,0:T(8,128)S(1)}, u32[]{:S(2)}, u32[]{:S(2)}) %collective-permute-start.3) | collective-permute-done | bytes 57376 | tf_op jit(solution)/shard_map/ppermute | solution.py:450
  13.3 3.2 %collective-permute-start.5 = (f32[2,7,8,128]{3,2,1,0:T(8,128)S(1)}, f32[2,7,8,128]{3,2,1,0:T(8,128)S(1)}, u32[]{:S(2)}, u32[]{:S(2)}) collective-permute-start(f32[2,7,8,128]{3,2,1,0:T(8,128)S(1)} %get-tuple-element.42), channel_id=1, source_target_pairs={{0,28},{4,16},{8,20},{12,24},{16,12},{20,0},{24,4},{28,8},{32,60},... | collective-permute-start | bytes 172040 | tf_op jit(solution)/shard_map/ppermute | solution.py:453
  16.5 0.4 collective-permute-start.4
  16.9 2.1 %shard_map.41 = (f32[10,256,128]{2,1,0:T(8,128)S(1)}, f32[10,256,128]{2,1,0:T(8,128)S(1)}, f32[256,128]{1,0:T(8,128)S(1)}, f32[32,1024]{1,0:T(8,128)S(1)}, f32[8,128]{1,0:T(8,128)S(1)}) custom-call(f32[32,1024]{1,0:T(8,128)S(1)} %get-tuple-element.35.kappa, f32[7,8,128]{2,1,0:T(8,128)S(1)} %get-tuple-element.41.after.chip), custom_call_target="tpu_custom_call" | custom-call | flops 20000000 | bytes 4000000 | tf_op jit(solution)/shard_map/pallas_call | solution.py:455
  19.0 0.0 collective-permute-done.5.chips
  19.1 0.1 collective-permute-start.6
  19.2 0.0 collective-permute-done.4.far1
  19.2 1.1 %collective-permute-done.6.got = f32[7,8,128]{2,1,0:T(8,128)S(1)} collective-permute-done((f32[7,8,128]{2,1,0:T(8,128)S(1)}, f32[7,8,128]{2,1,0:T(8,128)S(1)}, u32[]{:S(2)}, u32[]{:S(2)}) %collective-permute-start.6) | collective-permute-done | bytes 28704 | tf_op jit(solution)/shard_map/ppermute | solution.py:463
  20.4 0.1 shard_map.43
  20.5 14.6 %all_to_all.5.got = f32[8,5,8,128]{3,2,1,0:T(8,128)S(1)} all-to-all(f32[8,5,8,128]{3,2,1,0:T(8,128)S(1)} %get-tuple-element.47), channel_id=1, replica_groups={{0,32,64,96,128,160,192,224},{4,36,68,100,132,164,196,228},{8,40,72,104..., dimensions={0} | all-to-all | bytes 327680 | tf_op jit(solution)/shard_map/all_to_all | solution.py:467
  35.0 0.1 shard_map.44
  35.2 1.8 %collective-permute-start.7 = (f32[2,8,128]{2,1,0:T(8,128)S(1)}, f32[2,8,128]{2,1,0:T(8,128)S(1)}, u32[]{:S(2)}, u32[]{:S(2)}) collective-permute-start(f32[2,8,128]{2,1,0:T(8,128)S(1)} %get-tuple-element.50), channel_id=1, source_target_pairs={{0,4},{4,0},{8,12},{12,8},{16,20},{20,16},{24,28},{28,24},{32,36},... | collective-permute-start | bytes 24584 | tf_op jit(solution)/shard_map/ppermute | solution.py:471
  37.0 0.1 shard_map.45.local
  37.1 0.7 %collective-permute-done.7.other = f32[2,8,128]{2,1,0:T(8,128)S(1)} collective-permute-done((f32[2,8,128]{2,1,0:T(8,128)S(1)}, f32[2,8,128]{2,1,0:T(8,128)S(1)}, u32[]{:S(2)}, u32[]{:S(2)}) %collective-permute-start.7) | collective-permute-done | bytes 8224 | tf_op jit(solution)/shard_map/ppermute | solution.py:471
  37.8 0.1 shard_map.46
  37.9 2.8 %collective-permute-start.8 = (f32[8,128]{1,0:T(8,128)S(1)}, f32[8,128]{1,0:T(8,128)S(1)}, u32[]{:S(2)}, u32[]{:S(2)}) collective-permute-start(f32[8,128]{1,0:T(8,128)S(1)} %get-tuple-element.56.message), channel_id=1, source_target_pairs={{0,2},{2,0},{1,3},{3,1},{4,6},{6,4},{5,7},{7,5},{8,10},{10,8},{9,1... | collective-permute-start | bytes 12296 | tf_op jit(solution)/shard_map/ppermute | solution.py:475
  40.7 0.9 %shard_map.47.local = f32[32,1024]{1,0:T(8,128)S(1)} custom-call(f32[32,1024]{1,0:T(8,128)S(1)} %get-tuple-element.57.section, f32[10,256,128]{2,1,0:T(8,128)S(1)} %get-tuple-element.58.ay, f32[10,256,128]{2,1,0:T(8,128)S(1)} %get-tuple-element.59.by, f32[256,128]{1,0:T(8,128)S(1)} %get-tuple-element.60.qy), custom_call_target="tpu_custom_call" | custom-call | flops 4000000 | bytes 3000000 | tf_op jit(solution)/shard_map/pallas_call | solution.py:476
  41.6 0.3 collective-permute-done.8.far
  41.9 0.9 %shard_map.48 = f32[32,1024]{1,0:T(8,128)} custom-call(f32[8,128]{1,0:T(8,128)S(1)} %get-tuple-element.56.message, f32[8,128]{1,0:T(8,128)S(1)} %collective-permute-done.8.far, f32[32,1024]{1,0:T(8,128)S(1)} %shard_map.47.local, f32[32,1024]{1,0:T(8,128)S(1)} %get-tuple-element.55.hy), custom_call_target="tpu_custom_call" | custom-call | tf_op jit(solution)/shard_map/pallas_call | solution.py:477
  (2 shorter events, 0.0 us)
Async XLA Ops:
  0.0 10.1 %collective-permute-start = (f32[2,1,16,1024]{3,2,1,0:T(8,128)}, f32[2,1,16,1024]{3,2,1,0:T(8,128)S(1)}, u32[]{:S(2)}, u32[]{:S(2)}) collective-permute-start(f32[2,1,16,1024]{3,2,1,0:T(8,128)} %param.3), channel_id=1, source_target_pairs={{0,1},{1,0},{2,3},{3,2},{4,5},{5,4},{6,7},{7,6},{8,9},{9,8},{10,11... | collective-permute-start | bytes 393224 | tf_op jit(solution)/shard_map/ppermute | solution.py:424
  2.0 8.0 %collective-permute-start.1 = (f32[2,1,16,1024]{3,2,1,0:T(8,128)}, f32[2,1,16,1024]{3,2,1,0:T(8,128)S(1)}, u32[]{:S(2)}, u32[]{:S(2)}) collective-permute-start(f32[2,1,16,1024]{3,2,1,0:T(8,128)} %param.5), channel_id=1, source_target_pairs={{0,1},{1,0},{2,3},{3,2},{4,5},{5,4},{6,7},{7,6},{8,9},{9,8},{10,11... | collective-permute-start | bytes 393224 | tf_op jit(solution)/shard_map/ppermute | solution.py:425
  3.1 6.9 %collective-permute-start.2 = (f32[2,8,128]{2,1,0:T(8,128)S(1)}, f32[2,8,128]{2,1,0:T(8,128)S(1)}, u32[]{:S(2)}, u32[]{:S(2)}) collective-permute-start(f32[2,8,128]{2,1,0:T(8,128)S(1)} %get-tuple-element.39), channel_id=1, source_target_pairs={{0,32},{4,36},{8,40},{12,44},{16,48},{20,52},{24,56},{28,60},{32,6... | collective-permute-start | bytes 24584 | tf_op jit(solution)/shard_map/ppermute | solution.py:437
  10.2 3.1 %collective-permute-start.3 = (f32[2,7,8,128]{3,2,1,0:T(8,128)S(1)}, f32[2,7,8,128]{3,2,1,0:T(8,128)S(1)}, u32[]{:S(2)}, u32[]{:S(2)}) collective-permute-start(f32[2,7,8,128]{3,2,1,0:T(8,128)S(1)} %get-tuple-element.40.mine), channel_id=1, source_target_pairs={{0,4},{4,0},{8,12},{12,8},{16,20},{20,16},{24,28},{28,24},{32,36},... | collective-permute-start | bytes 172040 | tf_op jit(solution)/shard_map/ppermute | solution.py:450
  13.3 5.8 %collective-permute-start.5 = (f32[2,7,8,128]{3,2,1,0:T(8,128)S(1)}, f32[2,7,8,128]{3,2,1,0:T(8,128)S(1)}, u32[]{:S(2)}, u32[]{:S(2)}) collective-permute-start(f32[2,7,8,128]{3,2,1,0:T(8,128)S(1)} %get-tuple-element.42), channel_id=1, source_target_pairs={{0,28},{4,16},{8,20},{12,24},{16,12},{20,0},{24,4},{28,8},{32,60},... | collective-permute-start | bytes 172040 | tf_op jit(solution)/shard_map/ppermute | solution.py:453
  16.5 2.7 %collective-permute-start.4 = (f32[7,8,128]{2,1,0:T(8,128)S(1)}, f32[7,8,128]{2,1,0:T(8,128)S(1)}, u32[]{:S(2)}, u32[]{:S(2)}) collective-permute-start(f32[7,8,128]{2,1,0:T(8,128)S(1)} %get-tuple-element.41.after.chip), channel_id=1, source_target_pairs={{0,8},{4,12},{8,0},{12,4},{16,24},{20,28},{24,16},{28,20},{32,40},... | collective-permute-start | bytes 86024 | tf_op jit(solution)/shard_map/ppermute | solution.py:454
  19.1 1.3 %collective-permute-start.6 = (f32[7,8,128]{2,1,0:T(8,128)S(1)}, f32[7,8,128]{2,1,0:T(8,128)S(1)}, u32[]{:S(2)}, u32[]{:S(2)}) collective-permute-start(f32[7,8,128]{2,1,0:T(8,128)S(1)} %get-tuple-element.45), channel_id=1, source_target_pairs={{0,4},{4,0},{8,12},{12,8},{16,20},{20,16},{24,28},{28,24},{32,36},... | collective-permute-start | bytes 86024 | tf_op jit(solution)/shard_map/ppermute | solution.py:463
  35.2 2.6 %collective-permute-start.7 = (f32[2,8,128]{2,1,0:T(8,128)S(1)}, f32[2,8,128]{2,1,0:T(8,128)S(1)}, u32[]{:S(2)}, u32[]{:S(2)}) collective-permute-start(f32[2,8,128]{2,1,0:T(8,128)S(1)} %get-tuple-element.50), channel_id=1, source_target_pairs={{0,4},{4,0},{8,12},{12,8},{16,20},{20,16},{24,28},{28,24},{32,36},... | collective-permute-start | bytes 24584 | tf_op jit(solution)/shard_map/ppermute | solution.py:471
  37.9 4.0 %collective-permute-start.8 = (f32[8,128]{1,0:T(8,128)S(1)}, f32[8,128]{1,0:T(8,128)S(1)}, u32[]{:S(2)}, u32[]{:S(2)}) collective-permute-start(f32[8,128]{1,0:T(8,128)S(1)} %get-tuple-element.56.message), channel_id=1, source_target_pairs={{0,2},{2,0},{1,3},{3,1},{4,6},{6,4},{5,7},{7,5},{8,10},{10,8},{9,1... | collective-permute-start | bytes 12296 | tf_op jit(solution)/shard_map/ppermute | solution.py:475

commit v19 on v14

--- a/solution.py
+++ b/solution.py
@@ -206,6 +206,7 @@
 
 def source_kernel(fields, fields_far, vertical, vertical_far, h1, h2, parts, prev, after, source, elements):
     del after
+    gx = lax.axis_index("gx")
     here = fields[...]
     v = vertical[...]
     s = here + (v + vertical_far[...]) * 0.5 * (fields_far[...] - here) - v * 0.5 * here
@@ -214,7 +215,10 @@
         mine = slice(f * ROWS, (f + 1) * ROWS)
         first = dense(jnp.sum(h1[mine, :] * s[mine, :], axis=0, keepdims=True))
         last = dense(jnp.sum(h2[mine, :] * s[mine, :], axis=0, keepdims=True))
-        element = (parts[0, f], parts[1, f], parts[2, f], first, last, parts[3, f], parts[4, f], prev[f])
+        rim = parts[4, f]
+        s_last = jnp.where(gx == 63, parts[2, f] + rim * 0.5, parts[2, f])
+        rim = jnp.where(gx % 8 == 7, jnp.where(gx == 7, 0.0, prev[f]), rim)
+        element = (parts[0, f], parts[1, f], s_last, first, last, parts[3, f], rim)
         for n, value in enumerate(element):
             elements[f, n] = value
 
@@ -250,7 +254,7 @@
 
 
 def load(ref, *field):
-    return tuple(ref[(*field, n)] for n in range(8))
+    return tuple(ref[(*field, n)] for n in range(7))
 
 
 def within(node, left, right):
@@ -267,7 +271,7 @@
         second = [jnp.where(even, o, m) for m, o in zip(a, b)]
         tail, start = behind((first[6] + second[5]) * 0.5, second[:5])
         element, end = merge(first[:5], tail)
-        fields.append(((*element, first[5], *second[6:]), (*end, *start)))
+        fields.append(((*element, first[5], second[6]), (*end, *start)))
         for n, value in enumerate(fields[f][0]):
             chips[f, n] = value
     for out, (one, two) in zip((chip, middle), zip(*fields)):
@@ -285,8 +289,8 @@
 def slab_kernel(chip, far1, keep, got, middle, message, nodes):
     y = lax.axis_index("gx") // 2 % 4
     even = lax.axis_index("gx") % 2 == 0
-    far2 = [jnp.where(even, g, k) for k, g in zip(load(keep), load(got))]
-    far3 = [jnp.where(even, k, g) for k, g in zip(load(keep), load(got))]
+    far2 = [jnp.where(even, k, g) for k, g in zip(load(keep), load(got))]
+    far3 = [jnp.where(even, g, k) for k, g in zip(load(keep), load(got))]
     arrived = [load(chip), load(far1), far2, far3]
     chips = []
     for m in range(4):
@@ -295,11 +299,9 @@
             here = y ^ flip == m
             chosen = [jnp.where(here, a, c) for a, c in zip(arrived[flip], chosen)]
         chips.append(chosen)
-    slab = lax.axis_index("gx") // 8
-    before = jnp.where(slab == 0, 0.0, chips[3][7])
     element, inner, fronts = None, [], []
     for m in range(4):
-        face = ((before if m == 0 else chips[m - 1][6]) + chips[m][5]) * 0.5
+        face = (chips[m - 1][6] + chips[m][5]) * 0.5
         tail, front = behind(face, chips[m][:5])
         fronts.append(front)
         if m == 0:
@@ -307,9 +309,7 @@
         else:
             element, node = merge(element, tail)
             inner.append(node)
-    g, sl, sr, rl, rr = element
-    sr = jnp.where(slab == 7, sr + chips[3][6] * 0.5, sr)
-    for n, value in enumerate((g, sl, sr, rl, rr)):
+    for n, value in enumerate(element):
         for j in range(8):
             message[j, n] = value
     zero, one = jnp.zeros((8, 128), F32), jnp.ones((8, 128), F32)
@@ -413,7 +413,7 @@
 CORES = [(i, i ^ 1) for i in range(64)]
 
 
-CHIPS = [(i, i ^ (4 if i % 2 else 6)) for i in range(64)]
+CHIPS = [(i, i ^ (5 if i % 2 else 7)) for i in range(64)]
 NEXT = [(i, i ^ 2) for i in range(64)]
 
 
@@ -423,7 +423,7 @@
     fields_far = lax.ppermute(fields, "gz", swap)
     vertical_far = lax.ppermute(vertical, "gz", swap)
     full = shape(*grid)
-    half = shape(8, 8, 128)
+    half = shape(7, 8, 128)
     standing = shape(256, 128)
     fields_here, vertical_here, kappa_here, rim = call(
         input_kernel,
@@ -448,7 +448,7 @@
         flops=20_000_000,
         size=4_000_000,
     )(kappa_here)
-    both = shape(2, 8, 8, 128)
+    both = shape(2, 7, 8, 128)
     source, elements = call(source_kernel, (full, both), [VMEM] * 9)(
         fields_here, fields_far.reshape(grid), vertical_here, vertical_far.reshape(grid),
         h1, h2, parts, prev, edge,

time: 42.9 us -> 42.6 us (level)
  starting transfers between devices: 16 us -> 14.9 us
  waiting for transfers between devices: 6.23 us -> 6.94 us
    ppermute x1, starting transfers between devices: 1.46 us -> 0.22 us  [local(): got = lax.ppermute(send, 'gx', CORES)]
    ppermute x1, waiting for transfers between devices: 1.32 us -> 1.84 us  [local(): far = lax.ppermute(chips, 'gx', CHIPS)]
  transfers between devices with their start and end apart: 9 -> 9, of which waited for: 6 -> 7; matrix products, arithmetic and copies ran while one was open for 0% -> 0% of each run, Pallas kernels for 12% -> 12%
where the time goes in v19:
time: 42.6 us; the launch traced here: 42.4 us
  starting transfers between devices  14.9 us (35%)
  blocking collectives  14.3 us (34%)
  waiting for transfers between devices  6.94 us (16%)
  Pallas kernels  6.25 us (15%)
    all_to_all x1, blocking collectives, local(): lax.all_to_all(message, 'gx', 0, 0, axis_index_groups=SLAB_GROUPS, tiled=...  14.3 us
    ppermute x1, starting transfers between devices, local(): far = lax.ppermute(chips, 'gx', CHIPS)  3.23 us
    ppermute x1, starting transfers between devices, local(): far = lax.ppermute(message, 'gy', swap)  2.77 us
    ppermute x1, starting transfers between devices, local(): got = lax.ppermute(elements, 'gx', CORES)  2.19 us
    pallas_call x1, Pallas kernels, local(): call(factor_y_kernel, (shape(10, 256, 128), shape(10, 256, 128), standing...  2.15 us
    ppermute x1, waiting for transfers between devices, local(): prev = lax.ppermute(rim, 'gx', [(i, (i + 8) % 64) for i in range(64)])  2.13 us
    ppermute x1, starting transfers between devices, local(): other = lax.ppermute(other, 'gx', CORES)  2.12 us
    ppermute x1, starting transfers between devices, local(): fields_far = lax.ppermute(fields, 'gz', swap)  2.04 us
  transfers between devices with their start and end apart: 9, of which 7 were waited for; matrix products, arithmetic and copies ran while one was open for 0% of the time, Pallas kernels for 12%

profile of v19, /device:TPU:1, one launch (start us, length us, event | category | flops | bytes accessed | tf_op | source)
XLA Modules:
  0.0 42.4 jit_solution(4188540281521997528)
XLA Ops:
  0.0 2.0 %collective-permute-start = (f32[2,1,16,1024]{3,2,1,0:T(8,128)}, f32[2,1,16,1024]{3,2,1,0:T(8,128)S(1)}, u32[]{:S(2)}, u32[]{:S(2)}) collective-permute-start(f32[2,1,16,1024]{3,2,1,0:T(8,128)} %param.3), channel_id=1, source_target_pairs={{0,1},{1,0},{2,3},{3,2},{4,5},{5,4},{6,7},{7,6},{8,9},{9,8},{10,11... | collective-permute-start | bytes 393224 | tf_op jit(solution)/shard_map/ppermute | solution.py:423
  2.0 0.0 collective-permute-start.1
  2.1 1.1 %shard_map.37 = (f32[32,1024]{1,0:T(8,128)S(1)}, f32[32,1024]{1,0:T(8,128)S(1)}, f32[32,1024]{1,0:T(8,128)S(1)}, f32[2,8,128]{2,1,0:T(8,128)S(1)}) custom-call(f32[32,1024]{1,0:T(8,128)} %bitcast.11, f32[32,1024]{1,0:T(8,128)} %bitcast.12, f32[32,1024]{1,0:T(8,128)} %bitcast.10), custom_call_target="tpu_custom_call" | custom-call | flops 1000000 | bytes 1000000 | tf_op jit(solution)/shard_map/pallas_call | solution.py:428
  3.1 1.9 %collective-permute-start.2 = (f32[2,8,128]{2,1,0:T(8,128)S(1)}, f32[2,8,128]{2,1,0:T(8,128)S(1)}, u32[]{:S(2)}, u32[]{:S(2)}) collective-permute-start(f32[2,8,128]{2,1,0:T(8,128)S(1)} %get-tuple-element.39), channel_id=1, source_target_pairs={{0,32},{4,36},{8,40},{12,44},{16,48},{20,52},{24,56},{28,60},{32,6... | collective-permute-start | bytes 24584 | tf_op jit(solution)/shard_map/ppermute | solution.py:436
  5.1 0.7 %shard_map.38 = (f32[4,32,1024]{2,1,0:T(8,128)S(1)}, f32[4,32,1024]{2,1,0:T(8,128)S(1)}, f32[32,1024]{1,0:T(8,128)S(1)}, f32[32,1024]{1,0:T(8,128)S(1)}, f32[32,...) custom-call(f32[32,1024]{1,0:T(8,128)S(1)} %get-tuple-element.35.kappa), custom_call_target="tpu_custom_call" | custom-call | flops 4000000 | bytes 2000000 | tf_op jit(solution)/shard_map/pallas_call | solution.py:437
  5.8 2.2 %shard_map.39 = (f32[10,256,128]{2,1,0:T(8,128)S(1)}, f32[10,256,128]{2,1,0:T(8,128)S(1)}, f32[256,128]{1,0:T(8,128)S(1)}, f32[32,1024]{1,0:T(8,128)S(1)}, f32[8,128]{1,0:T(8,128)S(1)}) custom-call(f32[32,1024]{1,0:T(8,128)S(1)} %get-tuple-element.35.kappa), custom_call_target="tpu_custom_call" | custom-call | flops 20000000 | bytes 4000000 | tf_op jit(solution)/shard_map/pallas_call | solution.py:444
  7.9 2.1 %collective-permute-done.2.prev = f32[2,8,128]{2,1,0:T(8,128)S(1)} collective-permute-done((f32[2,8,128]{2,1,0:T(8,128)S(1)}, f32[2,8,128]{2,1,0:T(8,128)S(1)}, u32[]{:S(2)}, u32[]{:S(2)}) %collective-permute-start.2) | collective-permute-done | bytes 8224 | tf_op jit(solution)/shard_map/ppermute | solution.py:436
  10.1 0.0 collective-permute-done
  10.1 0.0 collective-permute-done.1
  10.1 0.1 shard_map.40
  10.2 2.2 %collective-permute-start.3 = (f32[2,7,8,128]{3,2,1,0:T(8,128)S(1)}, f32[2,7,8,128]{3,2,1,0:T(8,128)S(1)}, u32[]{:S(2)}, u32[]{:S(2)}) collective-permute-start(f32[2,7,8,128]{3,2,1,0:T(8,128)S(1)} %get-tuple-element.41.mine), channel_id=1, source_target_pairs={{0,4},{4,0},{8,12},{12,8},{16,20},{20,16},{24,28},{28,24},{32,36},... | collective-permute-start | bytes 172040 | tf_op jit(solution)/shard_map/ppermute | solution.py:456
  12.4 0.9 %collective-permute-done.3.other = f32[2,7,8,128]{3,2,1,0:T(8,128)S(1)} collective-permute-done((f32[2,7,8,128]{3,2,1,0:T(8,128)S(1)}, f32[2,7,8,128]{3,2,1,0:T(8,128)S(1)}, u32[]{:S(2)}, u32[]{:S(2)}) %collective-permute-start.3) | collective-permute-done | bytes 57376 | tf_op jit(solution)/shard_map/ppermute | solution.py:456
  13.3 3.2 %collective-permute-start.5 = (f32[2,7,8,128]{3,2,1,0:T(8,128)S(1)}, f32[2,7,8,128]{3,2,1,0:T(8,128)S(1)}, u32[]{:S(2)}, u32[]{:S(2)}) collective-permute-start(f32[2,7,8,128]{3,2,1,0:T(8,128)S(1)} %get-tuple-element.43), channel_id=1, source_target_pairs={{0,28},{4,16},{8,20},{12,24},{16,12},{20,0},{24,4},{28,8},{32,60},... | collective-permute-start | bytes 172040 | tf_op jit(solution)/shard_map/ppermute | solution.py:459
  16.5 0.4 collective-permute-start.4
  16.9 1.8 %collective-permute-done.5.chips = f32[2,7,8,128]{3,2,1,0:T(8,128)S(1)} collective-permute-done((f32[2,7,8,128]{3,2,1,0:T(8,128)S(1)}, f32[2,7,8,128]{3,2,1,0:T(8,128)S(1)}, u32[]{:S(2)}, u32[]{:S(2)}) %collective-permute-start.5) | collective-permute-done | bytes 57376 | tf_op jit(solution)/shard_map/ppermute | solution.py:459
  18.8 0.2 collective-permute-start.6
  19.0 0.3 collective-permute-done.4.far1
  19.2 0.8 %collective-permute-done.6.got = f32[7,8,128]{2,1,0:T(8,128)S(1)} collective-permute-done((f32[7,8,128]{2,1,0:T(8,128)S(1)}, f32[7,8,128]{2,1,0:T(8,128)S(1)}, u32[]{:S(2)}, u32[]{:S(2)}) %collective-permute-start.6) | collective-permute-done | bytes 28704 | tf_op jit(solution)/shard_map/ppermute | solution.py:462
  20.0 0.1 shard_map.43
  20.1 14.3 %all_to_all.5.got = f32[8,5,8,128]{3,2,1,0:T(8,128)S(1)} all-to-all(f32[8,5,8,128]{3,2,1,0:T(8,128)S(1)} %get-tuple-element.47), channel_id=1, replica_groups={{0,32,64,96,128,160,192,224},{4,36,68,100,132,164,196,228},{8,40,72,104..., dimensions={0} | all-to-all | bytes 327680 | tf_op jit(solution)/shard_map/all_to_all | solution.py:466
  34.4 0.1 shard_map.44
  34.5 2.1 %collective-permute-start.7 = (f32[2,8,128]{2,1,0:T(8,128)S(1)}, f32[2,8,128]{2,1,0:T(8,128)S(1)}, u32[]{:S(2)}, u32[]{:S(2)}) collective-permute-start(f32[2,8,128]{2,1,0:T(8,128)S(1)} %get-tuple-element.50), channel_id=1, source_target_pairs={{0,4},{4,0},{8,12},{12,8},{16,20},{20,16},{24,28},{28,24},{32,36},... | collective-permute-start | bytes 24584 | tf_op jit(solution)/shard_map/ppermute | solution.py:470
  36.6 0.1 shard_map.45.local
  36.8 0.7 %collective-permute-done.7.other = f32[2,8,128]{2,1,0:T(8,128)S(1)} collective-permute-done((f32[2,8,128]{2,1,0:T(8,128)S(1)}, f32[2,8,128]{2,1,0:T(8,128)S(1)}, u32[]{:S(2)}, u32[]{:S(2)}) %collective-permute-start.7) | collective-permute-done | bytes 8224 | tf_op jit(solution)/shard_map/ppermute | solution.py:470
  37.5 0.1 shard_map.46
  37.6 2.8 %collective-permute-start.8 = (f32[8,128]{1,0:T(8,128)S(1)}, f32[8,128]{1,0:T(8,128)S(1)}, u32[]{:S(2)}, u32[]{:S(2)}) collective-permute-start(f32[8,128]{1,0:T(8,128)S(1)} %get-tuple-element.56.message), channel_id=1, source_target_pairs={{0,2},{2,0},{1,3},{3,1},{4,6},{6,4},{5,7},{7,5},{8,10},{10,8},{9,1... | collective-permute-start | bytes 12296 | tf_op jit(solution)/shard_map/ppermute | solution.py:474
  40.3 0.9 %shard_map.47.local = f32[32,1024]{1,0:T(8,128)S(1)} custom-call(f32[32,1024]{1,0:T(8,128)S(1)} %get-tuple-element.57.section, f32[10,256,128]{2,1,0:T(8,128)S(1)} %get-tuple-element.58.ay, f32[10,256,128]{2,1,0:T(8,128)S(1)} %get-tuple-element.59.by, f32[256,128]{1,0:T(8,128)S(1)} %get-tuple-element.60.qy), custom_call_target="tpu_custom_call" | custom-call | flops 4000000 | bytes 3000000 | tf_op jit(solution)/shard_map/pallas_call | solution.py:475
  41.2 0.3 collective-permute-done.8.far
  41.6 0.9 %shard_map.48 = f32[32,1024]{1,0:T(8,128)} custom-call(f32[8,128]{1,0:T(8,128)S(1)} %get-tuple-element.56.message, f32[8,128]{1,0:T(8,128)S(1)} %collective-permute-done.8.far, f32[32,1024]{1,0:T(8,128)S(1)} %shard_map.47.local, f32[32,1024]{1,0:T(8,128)S(1)} %get-tuple-element.55.hy), custom_call_target="tpu_custom_call" | custom-call | tf_op jit(solution)/shard_map/pallas_call | solution.py:476
  (2 shorter events, 0.0 us)
Async XLA Ops:
  0.0 10.1 %collective-permute-start = (f32[2,1,16,1024]{3,2,1,0:T(8,128)}, f32[2,1,16,1024]{3,2,1,0:T(8,128)S(1)}, u32[]{:S(2)}, u32[]{:S(2)}) collective-permute-start(f32[2,1,16,1024]{3,2,1,0:T(8,128)} %param.3), channel_id=1, source_target_pairs={{0,1},{1,0},{2,3},{3,2},{4,5},{5,4},{6,7},{7,6},{8,9},{9,8},{10,11... | collective-permute-start | bytes 393224 | tf_op jit(solution)/shard_map/ppermute | solution.py:423
  2.0 8.0 %collective-permute-start.1 = (f32[2,1,16,1024]{3,2,1,0:T(8,128)}, f32[2,1,16,1024]{3,2,1,0:T(8,128)S(1)}, u32[]{:S(2)}, u32[]{:S(2)}) collective-permute-start(f32[2,1,16,1024]{3,2,1,0:T(8,128)} %param.5), channel_id=1, source_target_pairs={{0,1},{1,0},{2,3},{3,2},{4,5},{5,4},{6,7},{7,6},{8,9},{9,8},{10,11... | collective-permute-start | bytes 393224 | tf_op jit(solution)/shard_map/ppermute | solution.py:424
  3.1 6.9 %collective-permute-start.2 = (f32[2,8,128]{2,1,0:T(8,128)S(1)}, f32[2,8,128]{2,1,0:T(8,128)S(1)}, u32[]{:S(2)}, u32[]{:S(2)}) collective-permute-start(f32[2,8,128]{2,1,0:T(8,128)S(1)} %get-tuple-element.39), channel_id=1, source_target_pairs={{0,32},{4,36},{8,40},{12,44},{16,48},{20,52},{24,56},{28,60},{32,6... | collective-permute-start | bytes 24584 | tf_op jit(solution)/shard_map/ppermute | solution.py:436
  10.2 3.1 %collective-permute-start.3 = (f32[2,7,8,128]{3,2,1,0:T(8,128)S(1)}, f32[2,7,8,128]{3,2,1,0:T(8,128)S(1)}, u32[]{:S(2)}, u32[]{:S(2)}) collective-permute-start(f32[2,7,8,128]{3,2,1,0:T(8,128)S(1)} %get-tuple-element.41.mine), channel_id=1, source_target_pairs={{0,4},{4,0},{8,12},{12,8},{16,20},{20,16},{24,28},{28,24},{32,36},... | collective-permute-start | bytes 172040 | tf_op jit(solution)/shard_map/ppermute | solution.py:456
  13.3 5.5 %collective-permute-start.5 = (f32[2,7,8,128]{3,2,1,0:T(8,128)S(1)}, f32[2,7,8,128]{3,2,1,0:T(8,128)S(1)}, u32[]{:S(2)}, u32[]{:S(2)}) collective-permute-start(f32[2,7,8,128]{3,2,1,0:T(8,128)S(1)} %get-tuple-element.43), channel_id=1, source_target_pairs={{0,28},{4,16},{8,20},{12,24},{16,12},{20,0},{24,4},{28,8},{32,60},... | collective-permute-start | bytes 172040 | tf_op jit(solution)/shard_map/ppermute | solution.py:459
  16.5 2.7 %collective-permute-start.4 = (f32[7,8,128]{2,1,0:T(8,128)S(1)}, f32[7,8,128]{2,1,0:T(8,128)S(1)}, u32[]{:S(2)}, u32[]{:S(2)}) collective-permute-start(f32[7,8,128]{2,1,0:T(8,128)S(1)} %get-tuple-element.42.chip), channel_id=1, source_target_pairs={{0,8},{4,12},{8,0},{12,4},{16,24},{20,28},{24,16},{28,20},{32,40},... | collective-permute-start | bytes 86024 | tf_op jit(solution)/shard_map/ppermute | solution.py:460
  18.8 1.3 %collective-permute-start.6 = (f32[7,8,128]{2,1,0:T(8,128)S(1)}, f32[7,8,128]{2,1,0:T(8,128)S(1)}, u32[]{:S(2)}, u32[]{:S(2)}) collective-permute-start(f32[7,8,128]{2,1,0:T(8,128)S(1)} %get-tuple-element.45), channel_id=1, source_target_pairs={{0,4},{4,0},{8,12},{12,8},{16,20},{20,16},{24,28},{28,24},{32,36},... | collective-permute-start | bytes 86024 | tf_op jit(solution)/shard_map/ppermute | solution.py:462
  34.5 2.9 %collective-permute-start.7 = (f32[2,8,128]{2,1,0:T(8,128)S(1)}, f32[2,8,128]{2,1,0:T(8,128)S(1)}, u32[]{:S(2)}, u32[]{:S(2)}) collective-permute-start(f32[2,8,128]{2,1,0:T(8,128)S(1)} %get-tuple-element.50), channel_id=1, source_target_pairs={{0,4},{4,0},{8,12},{12,8},{16,20},{20,16},{24,28},{28,24},{32,36},... | collective-permute-start | bytes 24584 | tf_op jit(solution)/shard_map/ppermute | solution.py:470
  37.6 4.0 %collective-permute-start.8 = (f32[8,128]{1,0:T(8,128)S(1)}, f32[8,128]{1,0:T(8,128)S(1)}, u32[]{:S(2)}, u32[]{:S(2)}) collective-permute-start(f32[8,128]{1,0:T(8,128)S(1)} %get-tuple-element.56.message), channel_id=1, source_target_pairs={{0,2},{2,0},{1,3},{3,1},{4,6},{6,4},{5,7},{7,5},{8,10},{10,8},{9,1... | collective-permute-start | bytes 12296 | tf_op jit(solution)/shard_map/ppermute | solution.py:474

commit v20 on v19

--- a/solution.py
+++ b/solution.py
@@ -289,8 +289,8 @@
 def slab_kernel(chip, far1, keep, got, middle, message, nodes):
     y = lax.axis_index("gx") // 2 % 4
     even = lax.axis_index("gx") % 2 == 0
-    far2 = [jnp.where(even, k, g) for k, g in zip(load(keep), load(got))]
-    far3 = [jnp.where(even, g, k) for k, g in zip(load(keep), load(got))]
+    far2 = [jnp.where(even, g, k) for k, g in zip(load(keep), load(got))]
+    far3 = [jnp.where(even, k, g) for k, g in zip(load(keep), load(got))]
     arrived = [load(chip), load(far1), far2, far3]
     chips = []
     for m in range(4):
@@ -413,7 +413,7 @@
 CORES = [(i, i ^ 1) for i in range(64)]
 
 
-CHIPS = [(i, i ^ (5 if i % 2 else 7)) for i in range(64)]
+CHIPS = [(i, i ^ (7 if i % 2 else 5)) for i in range(64)]
 NEXT = [(i, i ^ 2) for i in range(64)]
 
 

time: 42.6 us -> 42.4 us (level)
  waiting for transfers between devices: 6.94 us -> 7.49 us
  blocking collectives: 14.3 us -> 13.8 us
    ppermute x1, starting transfers between devices: 2.12 us -> 2.63 us  [local(): other = lax.ppermute(other, 'gx', CORES)]
    all_to_all x1, blocking collectives: 14.3 us -> 13.8 us  [local(): lax.all_to_all(message, 'gx', 0, 0, axis_index_groups=SLAB_GROUPS, tiled=...]
where the time goes in v20:
time: 42.4 us; the launch traced here: 42.3 us
  starting transfers between devices  14.7 us (35%)
  blocking collectives  13.8 us (33%)
  waiting for transfers between devices  7.49 us (18%)
  Pallas kernels  6.25 us (15%)
    all_to_all x1, blocking collectives, local(): lax.all_to_all(message, 'gx', 0, 0, axis_index_groups=SLAB_GROUPS, tiled=...  13.8 us
    ppermute x1, starting transfers between devices, local(): far = lax.ppermute(chips, 'gx', CHIPS)  3.05 us
    ppermute x1, starting transfers between devices, local(): far = lax.ppermute(message, 'gy', swap)  2.77 us
    ppermute x1, starting transfers between devices, local(): other = lax.ppermute(other, 'gx', CORES)  2.63 us
    ppermute x1, waiting for transfers between devices, local(): far = lax.ppermute(chips, 'gx', CHIPS)  2.26 us
    ppermute x1, starting transfers between devices, local(): got = lax.ppermute(elements, 'gx', CORES)  2.19 us
    pallas_call x1, Pallas kernels, local(): call(factor_y_kernel, (shape(10, 256, 128), shape(10, 256, 128), standing...  2.15 us
    ppermute x1, waiting for transfers between devices, local(): prev = lax.ppermute(rim, 'gx', [(i, (i + 8) % 64) for i in range(64)])  2.13 us
  transfers between devices with their start and end apart: 9, of which 7 were waited for; matrix products, arithmetic and copies ran while one was open for 0% of the time, Pallas kernels for 12%

profile of v20, /device:TPU:1, one launch (start us, length us, event | category | flops | bytes accessed | tf_op | source)
XLA Modules:
  0.0 42.3 jit_solution(16870532524380315548)
XLA Ops:
  0.0 2.0 %collective-permute-start = (f32[2,1,16,1024]{3,2,1,0:T(8,128)}, f32[2,1,16,1024]{3,2,1,0:T(8,128)S(1)}, u32[]{:S(2)}, u32[]{:S(2)}) collective-permute-start(f32[2,1,16,1024]{3,2,1,0:T(8,128)} %param.3), channel_id=1, source_target_pairs={{0,1},{1,0},{2,3},{3,2},{4,5},{5,4},{6,7},{7,6},{8,9},{9,8},{10,11... | collective-permute-start | bytes 393224 | tf_op jit(solution)/shard_map/ppermute | solution.py:423
  2.0 0.0 collective-permute-start.1
  2.1 1.1 %shard_map.37 = (f32[32,1024]{1,0:T(8,128)S(1)}, f32[32,1024]{1,0:T(8,128)S(1)}, f32[32,1024]{1,0:T(8,128)S(1)}, f32[2,8,128]{2,1,0:T(8,128)S(1)}) custom-call(f32[32,1024]{1,0:T(8,128)} %bitcast.11, f32[32,1024]{1,0:T(8,128)} %bitcast.12, f32[32,1024]{1,0:T(8,128)} %bitcast.10), custom_call_target="tpu_custom_call" | custom-call | flops 1000000 | bytes 1000000 | tf_op jit(solution)/shard_map/pallas_call | solution.py:428
  3.1 1.9 %collective-permute-start.2 = (f32[2,8,128]{2,1,0:T(8,128)S(1)}, f32[2,8,128]{2,1,0:T(8,128)S(1)}, u32[]{:S(2)}, u32[]{:S(2)}) collective-permute-start(f32[2,8,128]{2,1,0:T(8,128)S(1)} %get-tuple-element.39), channel_id=1, source_target_pairs={{0,32},{4,36},{8,40},{12,44},{16,48},{20,52},{24,56},{28,60},{32,6... | collective-permute-start | bytes 24584 | tf_op jit(solution)/shard_map/ppermute | solution.py:436
  5.1 0.7 %shard_map.38 = (f32[4,32,1024]{2,1,0:T(8,128)S(1)}, f32[4,32,1024]{2,1,0:T(8,128)S(1)}, f32[32,1024]{1,0:T(8,128)S(1)}, f32[32,1024]{1,0:T(8,128)S(1)}, f32[32,...) custom-call(f32[32,1024]{1,0:T(8,128)S(1)} %get-tuple-element.35.kappa), custom_call_target="tpu_custom_call" | custom-call | flops 4000000 | bytes 2000000 | tf_op jit(solution)/shard_map/pallas_call | solution.py:437
  5.8 2.2 %shard_map.39 = (f32[10,256,128]{2,1,0:T(8,128)S(1)}, f32[10,256,128]{2,1,0:T(8,128)S(1)}, f32[256,128]{1,0:T(8,128)S(1)}, f32[32,1024]{1,0:T(8,128)S(1)}, f32[8,128]{1,0:T(8,128)S(1)}) custom-call(f32[32,1024]{1,0:T(8,128)S(1)} %get-tuple-element.35.kappa), custom_call_target="tpu_custom_call" | custom-call | flops 20000000 | bytes 4000000 | tf_op jit(solution)/shard_map/pallas_call | solution.py:444
  7.9 2.1 %collective-permute-done.2.prev = f32[2,8,128]{2,1,0:T(8,128)S(1)} collective-permute-done((f32[2,8,128]{2,1,0:T(8,128)S(1)}, f32[2,8,128]{2,1,0:T(8,128)S(1)}, u32[]{:S(2)}, u32[]{:S(2)}) %collective-permute-start.2) | collective-permute-done | bytes 8224 | tf_op jit(solution)/shard_map/ppermute | solution.py:436
  10.1 0.0 collective-permute-done
  10.1 0.0 collective-permute-done.1
  10.1 0.1 shard_map.40
  10.2 2.2 %collective-permute-start.3 = (f32[2,7,8,128]{3,2,1,0:T(8,128)S(1)}, f32[2,7,8,128]{3,2,1,0:T(8,128)S(1)}, u32[]{:S(2)}, u32[]{:S(2)}) collective-permute-start(f32[2,7,8,128]{3,2,1,0:T(8,128)S(1)} %get-tuple-element.41.mine), channel_id=1, source_target_pairs={{0,4},{4,0},{8,12},{12,8},{16,20},{20,16},{24,28},{28,24},{32,36},... | collective-permute-start | bytes 172040 | tf_op jit(solution)/shard_map/ppermute | solution.py:456
  12.4 0.9 %collective-permute-done.3.other = f32[2,7,8,128]{3,2,1,0:T(8,128)S(1)} collective-permute-done((f32[2,7,8,128]{3,2,1,0:T(8,128)S(1)}, f32[2,7,8,128]{3,2,1,0:T(8,128)S(1)}, u32[]{:S(2)}, u32[]{:S(2)}) %collective-permute-start.3) | collective-permute-done | bytes 57376 | tf_op jit(solution)/shard_map/ppermute | solution.py:456
  13.3 3.0 %collective-permute-start.5 = (f32[2,7,8,128]{3,2,1,0:T(8,128)S(1)}, f32[2,7,8,128]{3,2,1,0:T(8,128)S(1)}, u32[]{:S(2)}, u32[]{:S(2)}) collective-permute-start(f32[2,7,8,128]{3,2,1,0:T(8,128)S(1)} %get-tuple-element.43), channel_id=1, source_target_pairs={{0,20},{4,24},{8,28},{12,16},{16,4},{20,8},{24,12},{28,0},{32,52},... | collective-permute-start | bytes 172040 | tf_op jit(solution)/shard_map/ppermute | solution.py:459
  16.3 0.0 collective-permute-start.4
  16.3 2.3 %collective-permute-done.5.chips = f32[2,7,8,128]{3,2,1,0:T(8,128)S(1)} collective-permute-done((f32[2,7,8,128]{3,2,1,0:T(8,128)S(1)}, f32[2,7,8,128]{3,2,1,0:T(8,128)S(1)}, u32[]{:S(2)}, u32[]{:S(2)}) %collective-permute-start.5) | collective-permute-done | bytes 57376 | tf_op jit(solution)/shard_map/ppermute | solution.py:459
  18.6 0.1 collective-permute-start.6
  18.7 0.4 collective-permute-done.4.far1
  19.1 0.8 %collective-permute-done.6.got = f32[7,8,128]{2,1,0:T(8,128)S(1)} collective-permute-done((f32[7,8,128]{2,1,0:T(8,128)S(1)}, f32[7,8,128]{2,1,0:T(8,128)S(1)}, u32[]{:S(2)}, u32[]{:S(2)}) %collective-permute-start.6) | collective-permute-done | bytes 28704 | tf_op jit(solution)/shard_map/ppermute | solution.py:462
  19.9 0.1 shard_map.43
  20.0 13.8 %all_to_all.5.got = f32[8,5,8,128]{3,2,1,0:T(8,128)S(1)} all-to-all(f32[8,5,8,128]{3,2,1,0:T(8,128)S(1)} %get-tuple-element.47), channel_id=1, replica_groups={{0,32,64,96,128,160,192,224},{4,36,68,100,132,164,196,228},{8,40,72,104..., dimensions={0} | all-to-all | bytes 327680 | tf_op jit(solution)/shard_map/all_to_all | solution.py:466
  33.7 0.1 shard_map.44
  33.9 2.6 %collective-permute-start.7 = (f32[2,8,128]{2,1,0:T(8,128)S(1)}, f32[2,8,128]{2,1,0:T(8,128)S(1)}, u32[]{:S(2)}, u32[]{:S(2)}) collective-permute-start(f32[2,8,128]{2,1,0:T(8,128)S(1)} %get-tuple-element.50), channel_id=1, source_target_pairs={{0,4},{4,0},{8,12},{12,8},{16,20},{20,16},{24,28},{28,24},{32,36},... | collective-permute-start | bytes 24584 | tf_op jit(solution)/shard_map/ppermute | solution.py:470
  36.5 0.1 shard_map.45.local
  36.6 0.7 %collective-permute-done.7.other = f32[2,8,128]{2,1,0:T(8,128)S(1)} collective-permute-done((f32[2,8,128]{2,1,0:T(8,128)S(1)}, f32[2,8,128]{2,1,0:T(8,128)S(1)}, u32[]{:S(2)}, u32[]{:S(2)}) %collective-permute-start.7) | collective-permute-done | bytes 8224 | tf_op jit(solution)/shard_map/ppermute | solution.py:470
  37.3 0.1 shard_map.46
  37.4 2.8 %collective-permute-start.8 = (f32[8,128]{1,0:T(8,128)S(1)}, f32[8,128]{1,0:T(8,128)S(1)}, u32[]{:S(2)}, u32[]{:S(2)}) collective-permute-start(f32[8,128]{1,0:T(8,128)S(1)} %get-tuple-element.56.message), channel_id=1, source_target_pairs={{0,2},{2,0},{1,3},{3,1},{4,6},{6,4},{5,7},{7,5},{8,10},{10,8},{9,1... | collective-permute-start | bytes 12296 | tf_op jit(solution)/shard_map/ppermute | solution.py:474
  40.2 0.9 %shard_map.47.local = f32[32,1024]{1,0:T(8,128)S(1)} custom-call(f32[32,1024]{1,0:T(8,128)S(1)} %get-tuple-element.57.section, f32[10,256,128]{2,1,0:T(8,128)S(1)} %get-tuple-element.58.ay, f32[10,256,128]{2,1,0:T(8,128)S(1)} %get-tuple-element.59.by, f32[256,128]{1,0:T(8,128)S(1)} %get-tuple-element.60.qy), custom_call_target="tpu_custom_call" | custom-call | flops 4000000 | bytes 3000000 | tf_op jit(solution)/shard_map/pallas_call | solution.py:475
  41.1 0.3 collective-permute-done.8.far
  41.4 0.9 %shard_map.48 = f32[32,1024]{1,0:T(8,128)} custom-call(f32[8,128]{1,0:T(8,128)S(1)} %get-tuple-element.56.message, f32[8,128]{1,0:T(8,128)S(1)} %collective-permute-done.8.far, f32[32,1024]{1,0:T(8,128)S(1)} %shard_map.47.local, f32[32,1024]{1,0:T(8,128)S(1)} %get-tuple-element.55.hy), custom_call_target="tpu_custom_call" | custom-call | tf_op jit(solution)/shard_map/pallas_call | solution.py:476
  (2 shorter events, 0.0 us)
Async XLA Ops:
  0.0 10.1 %collective-permute-start = (f32[2,1,16,1024]{3,2,1,0:T(8,128)}, f32[2,1,16,1024]{3,2,1,0:T(8,128)S(1)}, u32[]{:S(2)}, u32[]{:S(2)}) collective-permute-start(f32[2,1,16,1024]{3,2,1,0:T(8,128)} %param.3), channel_id=1, source_target_pairs={{0,1},{1,0},{2,3},{3,2},{4,5},{5,4},{6,7},{7,6},{8,9},{9,8},{10,11... | collective-permute-start | bytes 393224 | tf_op jit(solution)/shard_map/ppermute | solution.py:423
  2.0 8.0 %collective-permute-start.1 = (f32[2,1,16,1024]{3,2,1,0:T(8,128)}, f32[2,1,16,1024]{3,2,1,0:T(8,128)S(1)}, u32[]{:S(2)}, u32[]{:S(2)}) collective-permute-start(f32[2,1,16,1024]{3,2,1,0:T(8,128)} %param.5), channel_id=1, source_target_pairs={{0,1},{1,0},{2,3},{3,2},{4,5},{5,4},{6,7},{7,6},{8,9},{9,8},{10,11... | collective-permute-start | bytes 393224 | tf_op jit(solution)/shard_map/ppermute | solution.py:424
  3.1 6.9 %collective-permute-start.2 = (f32[2,8,128]{2,1,0:T(8,128)S(1)}, f32[2,8,128]{2,1,0:T(8,128)S(1)}, u32[]{:S(2)}, u32[]{:S(2)}) collective-permute-start(f32[2,8,128]{2,1,0:T(8,128)S(1)} %get-tuple-element.39), channel_id=1, source_target_pairs={{0,32},{4,36},{8,40},{12,44},{16,48},{20,52},{24,56},{28,60},{32,6... | collective-permute-start | bytes 24584 | tf_op jit(solution)/shard_map/ppermute | solution.py:436
  10.2 3.1 %collective-permute-start.3 = (f32[2,7,8,128]{3,2,1,0:T(8,128)S(1)}, f32[2,7,8,128]{3,2,1,0:T(8,128)S(1)}, u32[]{:S(2)}, u32[]{:S(2)}) collective-permute-start(f32[2,7,8,128]{3,2,1,0:T(8,128)S(1)} %get-tuple-element.41.mine), channel_id=1, source_target_pairs={{0,4},{4,0},{8,12},{12,8},{16,20},{20,16},{24,28},{28,24},{32,36},... | collective-permute-start | bytes 172040 | tf_op jit(solution)/shard_map/ppermute | solution.py:456
  13.3 5.3 %collective-permute-start.5 = (f32[2,7,8,128]{3,2,1,0:T(8,128)S(1)}, f32[2,7,8,128]{3,2,1,0:T(8,128)S(1)}, u32[]{:S(2)}, u32[]{:S(2)}) collective-permute-start(f32[2,7,8,128]{3,2,1,0:T(8,128)S(1)} %get-tuple-element.43), channel_id=1, source_target_pairs={{0,20},{4,24},{8,28},{12,16},{16,4},{20,8},{24,12},{28,0},{32,52},... | collective-permute-start | bytes 172040 | tf_op jit(solution)/shard_map/ppermute | solution.py:459
  16.3 2.8 %collective-permute-start.4 = (f32[7,8,128]{2,1,0:T(8,128)S(1)}, f32[7,8,128]{2,1,0:T(8,128)S(1)}, u32[]{:S(2)}, u32[]{:S(2)}) collective-permute-start(f32[7,8,128]{2,1,0:T(8,128)S(1)} %get-tuple-element.42.chip), channel_id=1, source_target_pairs={{0,8},{4,12},{8,0},{12,4},{16,24},{20,28},{24,16},{28,20},{32,40},... | collective-permute-start | bytes 86024 | tf_op jit(solution)/shard_map/ppermute | solution.py:460
  18.6 1.3 %collective-permute-start.6 = (f32[7,8,128]{2,1,0:T(8,128)S(1)}, f32[7,8,128]{2,1,0:T(8,128)S(1)}, u32[]{:S(2)}, u32[]{:S(2)}) collective-permute-start(f32[7,8,128]{2,1,0:T(8,128)S(1)} %get-tuple-element.45), channel_id=1, source_target_pairs={{0,4},{4,0},{8,12},{12,8},{16,20},{20,16},{24,28},{28,24},{32,36},... | collective-permute-start | bytes 86024 | tf_op jit(solution)/shard_map/ppermute | solution.py:462
  33.9 3.5 %collective-permute-start.7 = (f32[2,8,128]{2,1,0:T(8,128)S(1)}, f32[2,8,128]{2,1,0:T(8,128)S(1)}, u32[]{:S(2)}, u32[]{:S(2)}) collective-permute-start(f32[2,8,128]{2,1,0:T(8,128)S(1)} %get-tuple-element.50), channel_id=1, source_target_pairs={{0,4},{4,0},{8,12},{12,8},{16,20},{20,16},{24,28},{28,24},{32,36},... | collective-permute-start | bytes 24584 | tf_op jit(solution)/shard_map/ppermute | solution.py:470
  37.4 4.0 %collective-permute-start.8 = (f32[8,128]{1,0:T(8,128)S(1)}, f32[8,128]{1,0:T(8,128)S(1)}, u32[]{:S(2)}, u32[]{:S(2)}) collective-permute-start(f32[8,128]{1,0:T(8,128)S(1)} %get-tuple-element.56.message), channel_id=1, source_target_pairs={{0,2},{2,0},{1,3},{3,1},{4,6},{6,4},{5,7},{7,5},{8,10},{10,8},{9,1... | collective-permute-start | bytes 12296 | tf_op jit(solution)/shard_map/ppermute | solution.py:474

commit v21 on v19

--- a/solution.py
+++ b/solution.py
@@ -286,7 +286,8 @@
         send[n] = jnp.where(even, two, one)
 
 
-def slab_kernel(chip, far1, keep, got, middle, message, nodes):
+def slab_kernel(chip, far1, keep, got, middle, after, message, nodes):
+    del after
     y = lax.axis_index("gx") // 2 % 4
     even = lax.axis_index("gx") % 2 == 0
     far2 = [jnp.where(even, k, g) for k, g in zip(load(keep), load(got))]
@@ -461,8 +462,8 @@
     keep, send = call(pick_kernel, (half, half), [VMEM])(far)
     got = lax.ppermute(send, "gx", CORES)
     message, nodes = call(
-        slab_kernel, (shape(8, 5, 8, 128), shape(4, 3, 8, 128)), [VMEM] * 5
-    )(chip, far1, keep, got, middle)
+        slab_kernel, (shape(8, 5, 8, 128), shape(4, 3, 8, 128)), [VMEM] * 6
+    )(chip, far1, keep, got, middle, local_x)
     got = lax.all_to_all(message, "gx", 0, 0, axis_index_groups=SLAB_GROUPS, tiled=True)
     mine, other = call(
         ends_kernel, (shape(2, 8, 128), shape(2, 8, 128)), [VMEM, VMEM]

time: 42.6 us -> 42.6 us (level)
  no operation moved by 1% of the time
where the time goes in v21:
time: 42.6 us; the launch traced here: 42.5 us
  starting transfers between devices  14.9 us (35%)
  blocking collectives  14.3 us (34%)
  waiting for transfers between devices  6.93 us (16%)
  Pallas kernels  6.26 us (15%)
    all_to_all x1, blocking collectives, local(): lax.all_to_all(message, 'gx', 0, 0, axis_index_groups=SLAB_GROUPS, tiled=...  14.3 us
    ppermute x1, starting transfers between devices, local(): far = lax.ppermute(chips, 'gx', CHIPS)  3.23 us
    ppermute x1, starting transfers between devices, local(): far = lax.ppermute(message, 'gy', swap)  2.77 us
    ppermute x1, starting transfers between devices, local(): got = lax.ppermute(elements, 'gx', CORES)  2.19 us
    pallas_call x1, Pallas kernels, local(): call(factor_y_kernel, (shape(10, 256, 128), shape(10, 256, 128), standing...  2.15 us
    ppermute x1, waiting for transfers between devices, local(): prev = lax.ppermute(rim, 'gx', [(i, (i + 8) % 64) for i in range(64)])  2.13 us
    ppermute x1, starting transfers between devices, local(): other = lax.ppermute(other, 'gx', CORES)  2.12 us
    ppermute x1, starting transfers between devices, local(): fields_far = lax.ppermute(fields, 'gz', swap)  2.04 us
  transfers between devices with their start and end apart: 9, of which 7 were waited for; matrix products, arithmetic and copies ran while one was open for 0% of the time, Pallas kernels for 12%

profile of v21, /device:TPU:1, one launch (start us, length us, event | category | flops | bytes accessed | tf_op | source)
XLA Modules:
  0.0 42.5 jit_solution(14164864553866952499)
XLA Ops:
  0.0 2.0 %collective-permute-start = (f32[2,1,16,1024]{3,2,1,0:T(8,128)}, f32[2,1,16,1024]{3,2,1,0:T(8,128)S(1)}, u32[]{:S(2)}, u32[]{:S(2)}) collective-permute-start(f32[2,1,16,1024]{3,2,1,0:T(8,128)} %param.3), channel_id=1, source_target_pairs={{0,1},{1,0},{2,3},{3,2},{4,5},{5,4},{6,7},{7,6},{8,9},{9,8},{10,11... | collective-permute-start | bytes 393224 | tf_op jit(solution)/shard_map/ppermute | solution.py:424
  2.0 0.0 collective-permute-start.1
  2.1 1.1 %shard_map.37 = (f32[32,1024]{1,0:T(8,128)S(1)}, f32[32,1024]{1,0:T(8,128)S(1)}, f32[32,1024]{1,0:T(8,128)S(1)}, f32[2,8,128]{2,1,0:T(8,128)S(1)}) custom-call(f32[32,1024]{1,0:T(8,128)} %bitcast.11, f32[32,1024]{1,0:T(8,128)} %bitcast.12, f32[32,1024]{1,0:T(8,128)} %bitcast.10), custom_call_target="tpu_custom_call" | custom-call | flops 1000000 | bytes 1000000 | tf_op jit(solution)/shard_map/pallas_call | solution.py:429
  3.1 1.9 %collective-permute-start.2 = (f32[2,8,128]{2,1,0:T(8,128)S(1)}, f32[2,8,128]{2,1,0:T(8,128)S(1)}, u32[]{:S(2)}, u32[]{:S(2)}) collective-permute-start(f32[2,8,128]{2,1,0:T(8,128)S(1)} %get-tuple-element.39), channel_id=1, source_target_pairs={{0,32},{4,36},{8,40},{12,44},{16,48},{20,52},{24,56},{28,60},{32,6... | collective-permute-start | bytes 24584 | tf_op jit(solution)/shard_map/ppermute | solution.py:437
  5.1 0.7 %shard_map.38 = (f32[4,32,1024]{2,1,0:T(8,128)S(1)}, f32[4,32,1024]{2,1,0:T(8,128)S(1)}, f32[32,1024]{1,0:T(8,128)S(1)}, f32[32,1024]{1,0:T(8,128)S(1)}, f32[32,...) custom-call(f32[32,1024]{1,0:T(8,128)S(1)} %get-tuple-element.35.kappa), custom_call_target="tpu_custom_call" | custom-call | flops 4000000 | bytes 2000000 | tf_op jit(solution)/shard_map/pallas_call | solution.py:438
  5.8 2.2 %shard_map.39 = (f32[10,256,128]{2,1,0:T(8,128)S(1)}, f32[10,256,128]{2,1,0:T(8,128)S(1)}, f32[256,128]{1,0:T(8,128)S(1)}, f32[32,1024]{1,0:T(8,128)S(1)}, f32[8,128]{1,0:T(8,128)S(1)}) custom-call(f32[32,1024]{1,0:T(8,128)S(1)} %get-tuple-element.35.kappa), custom_call_target="tpu_custom_call" | custom-call | flops 20000000 | bytes 4000000 | tf_op jit(solution)/shard_map/pallas_call | solution.py:445
  7.9 2.1 %collective-permute-done.2.prev = f32[2,8,128]{2,1,0:T(8,128)S(1)} collective-permute-done((f32[2,8,128]{2,1,0:T(8,128)S(1)}, f32[2,8,128]{2,1,0:T(8,128)S(1)}, u32[]{:S(2)}, u32[]{:S(2)}) %collective-permute-start.2) | collective-permute-done | bytes 8224 | tf_op jit(solution)/shard_map/ppermute | solution.py:437
  10.1 0.0 collective-permute-done
  10.1 0.0 collective-permute-done.1
  10.1 0.1 shard_map.40
  10.2 2.2 %collective-permute-start.3 = (f32[2,7,8,128]{3,2,1,0:T(8,128)S(1)}, f32[2,7,8,128]{3,2,1,0:T(8,128)S(1)}, u32[]{:S(2)}, u32[]{:S(2)}) collective-permute-start(f32[2,7,8,128]{3,2,1,0:T(8,128)S(1)} %get-tuple-element.41.mine), channel_id=1, source_target_pairs={{0,4},{4,0},{8,12},{12,8},{16,20},{20,16},{24,28},{28,24},{32,36},... | collective-permute-start | bytes 172040 | tf_op jit(solution)/shard_map/ppermute | solution.py:457
  12.4 0.9 %collective-permute-done.3.other = f32[2,7,8,128]{3,2,1,0:T(8,128)S(1)} collective-permute-done((f32[2,7,8,128]{3,2,1,0:T(8,128)S(1)}, f32[2,7,8,128]{3,2,1,0:T(8,128)S(1)}, u32[]{:S(2)}, u32[]{:S(2)}) %collective-permute-start.3) | collective-permute-done | bytes 57376 | tf_op jit(solution)/shard_map/ppermute | solution.py:457
  13.3 3.2 %collective-permute-start.5 = (f32[2,7,8,128]{3,2,1,0:T(8,128)S(1)}, f32[2,7,8,128]{3,2,1,0:T(8,128)S(1)}, u32[]{:S(2)}, u32[]{:S(2)}) collective-permute-start(f32[2,7,8,128]{3,2,1,0:T(8,128)S(1)} %get-tuple-element.43), channel_id=1, source_target_pairs={{0,28},{4,16},{8,20},{12,24},{16,12},{20,0},{24,4},{28,8},{32,60},... | collective-permute-start | bytes 172040 | tf_op jit(solution)/shard_map/ppermute | solution.py:460
  16.5 0.4 collective-permute-start.4
  16.9 1.8 %collective-permute-done.5.chips = f32[2,7,8,128]{3,2,1,0:T(8,128)S(1)} collective-permute-done((f32[2,7,8,128]{3,2,1,0:T(8,128)S(1)}, f32[2,7,8,128]{3,2,1,0:T(8,128)S(1)}, u32[]{:S(2)}, u32[]{:S(2)}) %collective-permute-start.5) | collective-permute-done | bytes 57376 | tf_op jit(solution)/shard_map/ppermute | solution.py:460
  18.8 0.2 collective-permute-start.6
  19.0 0.2 shard_map.43.after.local
  19.1 0.1 collective-permute-done.4.far1
  19.2 0.8 %collective-permute-done.6.got = f32[7,8,128]{2,1,0:T(8,128)S(1)} collective-permute-done((f32[7,8,128]{2,1,0:T(8,128)S(1)}, f32[7,8,128]{2,1,0:T(8,128)S(1)}, u32[]{:S(2)}, u32[]{:S(2)}) %collective-permute-start.6) | collective-permute-done | bytes 28704 | tf_op jit(solution)/shard_map/ppermute | solution.py:463
  20.0 0.1 shard_map.44
  20.1 14.3 %all_to_all.5.got = f32[8,5,8,128]{3,2,1,0:T(8,128)S(1)} all-to-all(f32[8,5,8,128]{3,2,1,0:T(8,128)S(1)} %get-tuple-element.51), channel_id=1, replica_groups={{0,32,64,96,128,160,192,224},{4,36,68,100,132,164,196,228},{8,40,72,104..., dimensions={0} | all-to-all | bytes 327680 | tf_op jit(solution)/shard_map/all_to_all | solution.py:467
  34.4 0.1 shard_map.45
  34.5 2.1 %collective-permute-start.7 = (f32[2,8,128]{2,1,0:T(8,128)S(1)}, f32[2,8,128]{2,1,0:T(8,128)S(1)}, u32[]{:S(2)}, u32[]{:S(2)}) collective-permute-start(f32[2,8,128]{2,1,0:T(8,128)S(1)} %get-tuple-element.54), channel_id=1, source_target_pairs={{0,4},{4,0},{8,12},{12,8},{16,20},{20,16},{24,28},{28,24},{32,36},... | collective-permute-start | bytes 24584 | tf_op jit(solution)/shard_map/ppermute | solution.py:471
  36.6 0.8 %collective-permute-done.7.other = f32[2,8,128]{2,1,0:T(8,128)S(1)} collective-permute-done((f32[2,8,128]{2,1,0:T(8,128)S(1)}, f32[2,8,128]{2,1,0:T(8,128)S(1)}, u32[]{:S(2)}, u32[]{:S(2)}) %collective-permute-start.7) | collective-permute-done | bytes 8224 | tf_op jit(solution)/shard_map/ppermute | solution.py:471
  37.5 0.1 shard_map.46
  37.6 2.8 %collective-permute-start.8 = (f32[8,128]{1,0:T(8,128)S(1)}, f32[8,128]{1,0:T(8,128)S(1)}, u32[]{:S(2)}, u32[]{:S(2)}) collective-permute-start(f32[8,128]{1,0:T(8,128)S(1)} %get-tuple-element.56.message), channel_id=1, source_target_pairs={{0,2},{2,0},{1,3},{3,1},{4,6},{6,4},{5,7},{7,5},{8,10},{10,8},{9,1... | collective-permute-start | bytes 12296 | tf_op jit(solution)/shard_map/ppermute | solution.py:475
  40.4 0.9 %shard_map.47.local = f32[32,1024]{1,0:T(8,128)S(1)} custom-call(f32[32,1024]{1,0:T(8,128)S(1)} %get-tuple-element.57.section, f32[10,256,128]{2,1,0:T(8,128)S(1)} %get-tuple-element.58.ay, f32[10,256,128]{2,1,0:T(8,128)S(1)} %get-tuple-element.59.by, f32[256,128]{1,0:T(8,128)S(1)} %get-tuple-element.60.qy), custom_call_target="tpu_custom_call" | custom-call | flops 4000000 | bytes 3000000 | tf_op jit(solution)/shard_map/pallas_call | solution.py:476
  41.2 0.3 collective-permute-done.8.far
  41.6 0.9 %shard_map.48 = f32[32,1024]{1,0:T(8,128)} custom-call(f32[8,128]{1,0:T(8,128)S(1)} %get-tuple-element.56.message, f32[8,128]{1,0:T(8,128)S(1)} %collective-permute-done.8.far, f32[32,1024]{1,0:T(8,128)S(1)} %shard_map.47.local, f32[32,1024]{1,0:T(8,128)S(1)} %get-tuple-element.55.hy), custom_call_target="tpu_custom_call" | custom-call | tf_op jit(solution)/shard_map/pallas_call | solution.py:477
  (2 shorter events, 0.0 us)
Async XLA Ops:
  0.0 10.1 %collective-permute-start = (f32[2,1,16,1024]{3,2,1,0:T(8,128)}, f32[2,1,16,1024]{3,2,1,0:T(8,128)S(1)}, u32[]{:S(2)}, u32[]{:S(2)}) collective-permute-start(f32[2,1,16,1024]{3,2,1,0:T(8,128)} %param.3), channel_id=1, source_target_pairs={{0,1},{1,0},{2,3},{3,2},{4,5},{5,4},{6,7},{7,6},{8,9},{9,8},{10,11... | collective-permute-start | bytes 393224 | tf_op jit(solution)/shard_map/ppermute | solution.py:424
  2.0 8.0 %collective-permute-start.1 = (f32[2,1,16,1024]{3,2,1,0:T(8,128)}, f32[2,1,16,1024]{3,2,1,0:T(8,128)S(1)}, u32[]{:S(2)}, u32[]{:S(2)}) collective-permute-start(f32[2,1,16,1024]{3,2,1,0:T(8,128)} %param.5), channel_id=1, source_target_pairs={{0,1},{1,0},{2,3},{3,2},{4,5},{5,4},{6,7},{7,6},{8,9},{9,8},{10,11... | collective-permute-start | bytes 393224 | tf_op jit(solution)/shard_map/ppermute | solution.py:425
  3.1 6.9 %collective-permute-start.2 = (f32[2,8,128]{2,1,0:T(8,128)S(1)}, f32[2,8,128]{2,1,0:T(8,128)S(1)}, u32[]{:S(2)}, u32[]{:S(2)}) collective-permute-start(f32[2,8,128]{2,1,0:T(8,128)S(1)} %get-tuple-element.39), channel_id=1, source_target_pairs={{0,32},{4,36},{8,40},{12,44},{16,48},{20,52},{24,56},{28,60},{32,6... | collective-permute-start | bytes 24584 | tf_op jit(solution)/shard_map/ppermute | solution.py:437
  10.2 3.1 %collective-permute-start.3 = (f32[2,7,8,128]{3,2,1,0:T(8,128)S(1)}, f32[2,7,8,128]{3,2,1,0:T(8,128)S(1)}, u32[]{:S(2)}, u32[]{:S(2)}) collective-permute-start(f32[2,7,8,128]{3,2,1,0:T(8,128)S(1)} %get-tuple-element.41.mine), channel_id=1, source_target_pairs={{0,4},{4,0},{8,12},{12,8},{16,20},{20,16},{24,28},{28,24},{32,36},... | collective-permute-start | bytes 172040 | tf_op jit(solution)/shard_map/ppermute | solution.py:457
  13.3 5.5 %collective-permute-start.5 = (f32[2,7,8,128]{3,2,1,0:T(8,128)S(1)}, f32[2,7,8,128]{3,2,1,0:T(8,128)S(1)}, u32[]{:S(2)}, u32[]{:S(2)}) collective-permute-start(f32[2,7,8,128]{3,2,1,0:T(8,128)S(1)} %get-tuple-element.43), channel_id=1, source_target_pairs={{0,28},{4,16},{8,20},{12,24},{16,12},{20,0},{24,4},{28,8},{32,60},... | collective-permute-start | bytes 172040 | tf_op jit(solution)/shard_map/ppermute | solution.py:460
  16.5 2.7 %collective-permute-start.4 = (f32[7,8,128]{2,1,0:T(8,128)S(1)}, f32[7,8,128]{2,1,0:T(8,128)S(1)}, u32[]{:S(2)}, u32[]{:S(2)}) collective-permute-start(f32[7,8,128]{2,1,0:T(8,128)S(1)} %get-tuple-element.42.chip), channel_id=1, source_target_pairs={{0,8},{4,12},{8,0},{12,4},{16,24},{20,28},{24,16},{28,20},{32,40},... | collective-permute-start | bytes 86024 | tf_op jit(solution)/shard_map/ppermute | solution.py:461
  18.8 1.3 %collective-permute-start.6 = (f32[7,8,128]{2,1,0:T(8,128)S(1)}, f32[7,8,128]{2,1,0:T(8,128)S(1)}, u32[]{:S(2)}, u32[]{:S(2)}) collective-permute-start(f32[7,8,128]{2,1,0:T(8,128)S(1)} %get-tuple-element.45), channel_id=1, source_target_pairs={{0,4},{4,0},{8,12},{12,8},{16,20},{20,16},{24,28},{28,24},{32,36},... | collective-permute-start | bytes 86024 | tf_op jit(solution)/shard_map/ppermute | solution.py:463
  34.5 2.9 %collective-permute-start.7 = (f32[2,8,128]{2,1,0:T(8,128)S(1)}, f32[2,8,128]{2,1,0:T(8,128)S(1)}, u32[]{:S(2)}, u32[]{:S(2)}) collective-permute-start(f32[2,8,128]{2,1,0:T(8,128)S(1)} %get-tuple-element.54), channel_id=1, source_target_pairs={{0,4},{4,0},{8,12},{12,8},{16,20},{20,16},{24,28},{28,24},{32,36},... | collective-permute-start | bytes 24584 | tf_op jit(solution)/shard_map/ppermute | solution.py:471
  37.6 4.0 %collective-permute-start.8 = (f32[8,128]{1,0:T(8,128)S(1)}, f32[8,128]{1,0:T(8,128)S(1)}, u32[]{:S(2)}, u32[]{:S(2)}) collective-permute-start(f32[8,128]{1,0:T(8,128)S(1)} %get-tuple-element.56.message), channel_id=1, source_target_pairs={{0,2},{2,0},{1,3},{3,1},{4,6},{6,4},{5,7},{7,5},{8,10},{10,8},{9,1... | collective-permute-start | bytes 12296 | tf_op jit(solution)/shard_map/ppermute | solution.py:475
